TPU v7x, 32 devices: a whole 2x2x4 slice. The times are simulated.
32 devices in a mesh: slab: 2 (over y), patch: 4 (over z), atom: 2 (over core), feat: 2 (over x).
Axes of the slice: x: 2, y: 2, z: 4, core: 2. Of those that a mesh axis runs over, the one named last changes fastest.
Arguments:
- patches: bfloat16 [3072, 1728], P(('slab', 'patch'), 'feat'), parts along dimension 0, may hold values from -160 to 160
- dictionary: bfloat16 [1728, 2048], P('feat', 'atom'), may hold values from -0.15625 to 0.15625
- threshold: float32 [2048], P('atom'), may hold values from 0.05 to 0.5
Outputs:
- codes: bfloat16 [3072, 2048], P(('slab', 'patch'), 'atom'), parts along dimension 0
- gram: float32 [4096, 2048], P(('slab', 'atom', 'feat'), 'patch'), parts along dimension 0
- cross: float32 [3456, 2048], P(('slab', 'feat'), ('patch', 'atom')), parts along dimension 0
There are 2 independent parts, one for each index of `slab`. A program takes and returns all parts, laid end to end along the dimension named above; an argument that names none is the same for every part. Nothing has to cross between parts.
All inputs are finite; a program needn't handle non-finite values.
Results may differ from a plain program's by a relative error of at most 0.011.
Values may be sent and summed in bfloat16 or wider, within the bound.
No kernel may reach another device: no remote copies, remote signals or barrier semaphores. Data moves between devices by JAX's collectives and lax.ppermute only.
A program may use at most 64 MiB of HBM per device.

v0:
```python
import jax
import jax.numpy as jnp
from jax import lax
from jax.sharding import PartitionSpec as P

BINS = 8
VOXELS = 216


step_rate = 0.2


def soften(value, level):
    return jnp.sign(value) * jnp.maximum(jnp.abs(value) - level, 0.0)


def on_device(patches, dictionary, threshold):
    values = patches.astype(jnp.float32)
    local_sq = jnp.sum(values * values, axis=1)
    local_first = jnp.dot(patches, dictionary, preferred_element_type=jnp.float32)
    summed, energy = lax.psum((local_first, local_sq), "feat")
    scale = lax.rsqrt(energy[:, None] / (BINS * VOXELS) + 1e-05)
    level = step_rate * threshold[None, :]
    start = soften(step_rate * (scale * summed), level).astype(jnp.bfloat16)
    contract_last = (((1,), (1,)), ((), ()))
    own_part = lax.dot_general(start, dictionary, contract_last, preferred_element_type=jnp.float32)
    rebuilt = lax.psum(own_part, "atom")
    misfit = (scale * values - rebuilt).astype(jnp.bfloat16)
    local_second = jnp.dot(misfit, dictionary, preferred_element_type=jnp.float32)
    second = lax.psum(local_second, "feat")
    codes = soften(start.astype(jnp.float32) + step_rate * second, level).astype(jnp.bfloat16)
    codes_whole = lax.all_gather(codes, "atom", axis=1, tiled=True)
    n_patch = lax.axis_size("patch")
    n_atom = lax.axis_size("atom")
    n_feat = lax.axis_size("feat")
    total_atoms = codes_whole.shape[1]
    count = patches.shape[0] * n_patch
    contract_first = (((0,), (0,)), ((), ()))
    block_rows = total_atoms // (n_atom * n_feat)
    offset = (lax.axis_index("atom") * n_feat + lax.axis_index("feat")) * block_rows
    chosen = lax.dynamic_slice_in_dim(codes_whole, offset, block_rows, 1)
    gram_part = lax.dot_general(
        chosen, codes_whole, contract_first, preferred_element_type=jnp.float32
    )
    gram = (
        lax.psum_scatter(
            gram_part.astype(jnp.bfloat16), "patch", scatter_dimension=1, tiled=True
        ).astype(jnp.float32)
        / count
    )
    width = total_atoms // (n_patch * n_atom)
    arranged = codes_whole.reshape(codes_whole.shape[0], n_patch, n_atom, width)
    picked = lax.dynamic_slice_in_dim(arranged, lax.axis_index("atom"), 1, 2).reshape(
        codes_whole.shape[0], n_patch * width
    )
    normed = (scale * values).astype(jnp.bfloat16)
    cross_part = lax.dot_general(normed, picked, contract_first, preferred_element_type=jnp.float32)
    cross = (
        lax.psum_scatter(
            cross_part.astype(jnp.bfloat16), "patch", scatter_dimension=1, tiled=True
        ).astype(jnp.float32)
        / count
    )
    return (codes, gram, cross)


def solution(mesh):
    in_specs = (P(("slab", "patch"), "feat"), P("feat", "atom"), P("atom"))
    out_specs = (
        P(("slab", "patch"), "atom"),
        P(("slab", "atom", "feat"), "patch"),
        P(("slab", "feat"), ("patch", "atom")),
    )
    return jax.shard_map(
        on_device, mesh=mesh, in_specs=in_specs, out_specs=out_specs, check_vma=False
    )
```

profile of v0, /device:TPU:0, one launch (start us, length us, event | category | flops | bytes accessed | tf_op | source)
XLA Modules:
  0.0 267.7 jit_solution(12650686993985074955)
XLA Ops:
  7.2 0.0 copy-start
  7.2 0.0 all-reduce.4.cloned.1.call-start
  7.2 1.4 copy-done
  8.6 3.3 %fusion.12 = f32[384,1024]{1,0:T(8,128)} fusion(bf16[384,864]{0,1:T(8,128)(2,1)} %param.3, bf16[864,1024]{1,0:T(8,128)(2,1)S(1)} %copy-done), kind=kOutput, calls=%fused_computation.21 | convolution fusion | flops 679477248 | bytes 4005888 | tf_op jit(solution)/shard_map/dot_general | solution.py:20
  11.9 0.0 copy-start.1
  11.9 0.0 copy-start.4
  11.9 0.0 all-reduce.4.cloned.1.call-update
  11.9 0.0 all-reduce.6.cloned.1.call-start
  12.0 1.0 copy-done.1
  13.0 0.2 fusion.3
  13.2 5.8 %psum.28 = f32[384]{0:T(512)S(1)} all-reduce(f32[384]{0:T(512)S(1)} %fusion.3), channel_id=1, replica_groups=mesh['slab'=2,'patch'=4,'atom'=2,'feat'=2] {'feat'}, use_global_device_ids=true, to_apply=%region_1.0 | all-reduce | flops 384 | bytes 3072 | tf_op jit(solution)/shard_map/psum | solution.py:21
  19.0 0.0 copy-done.4
  19.0 47.2 %all-reduce.4.cloned.1.call-done = f32[384,1024]{1,0:T(8,128)} async-done(((f32[384,1024]{1,0:T(8,128)}), f32[384,1024]{1,0:T(8,128)}) %all-reduce.4.cloned.1.call-update) | async-done | bytes 1572880 | tf_op jit(solution)/shard_map/psum | solution.py:21
  66.3 4.0 %fusion.11 = f32[384,864]{0,1:T(8,128)} fusion(bf16[864,1024]{1,0:T(8,128)(2,1)S(1)} %copy-done, f32[384,1024]{1,0:T(8,128)} %all-reduce.4.cloned.1.call-done, f32[1024]{0:T(1024)S(1)} %broadcast_multiply_fusion, f32[384]{0:T(512)S(1)} %add_rsqrt_fusion), kind=kOutput, calls=%fused_computation.20 | convolution fusion | flops 682622976 | bytes 4675072 | tf_op jit(solution)/shard_map/dot_general | solution.py:26
  70.3 0.0 all-reduce.6.cloned.1.call-update
  70.3 0.0 all-reduce.8.cloned.1.call-start
  70.3 20.1 %all-reduce.6.cloned.1.call-done = f32[384,864]{0,1:T(8,128)} async-done(((f32[384,864]{0,1:T(8,128)}), f32[384,864]{0,1:T(8,128)}) %all-reduce.6.cloned.1.call-update) | async-done | bytes 1327120 | tf_op jit(solution)/shard_map/psum | solution.py:27
  90.5 3.5 %fusion.4 = f32[384,1024]{1,0:T(8,128)} fusion(bf16[864,1024]{1,0:T(8,128)(2,1)S(1)} %copy-done, f32[384,864]{0,1:T(8,128)} %all-reduce.6.cloned.1.call-done, bf16[384,864]{0,1:T(8,128)(2,1)S(1)} %copy-done.1, f32[384]{0:T(512)S(1)} %add_rsqrt_fusion), kind=kOutput, calls=%fused_computation.12 | convolution fusion | flops 680804352 | bytes 5334528 | tf_op jit(solution)/shard_map/dot_general | solution.py:29
  93.9 0.0 copy-start.3
  93.9 0.0 all-reduce.8.cloned.1.call-update
  94.0 0.0 all-gather.2.cloned.1.call-start
  94.0 52.8 %all-reduce.8.cloned.1.call-done = f32[384,1024]{1,0:T(8,128)} async-done(((f32[384,1024]{1,0:T(8,128)}), f32[384,1024]{1,0:T(8,128)}) %all-reduce.8.cloned.1.call-update) | async-done | bytes 1572880 | tf_op jit(solution)/shard_map/psum | solution.py:30
  146.8 0.0 copy-done.3
  146.8 3.7 %multiply_convert_fusion = bf16[384,1024]{1,0:T(8,128)(2,1)} fusion(f32[384,1024]{1,0:T(8,128)} %all-reduce.8.cloned.1.call-done, f32[1024]{0:T(1024)S(1)} %broadcast_multiply_fusion, f32[384,1024]{1,0:T(8,128)S(1)} %copy-done.3, f32[384]{0:T(512)S(1)} %add_rsqrt_fusion), kind=kLoop, calls=%fused_computation.6 | loop fusion | flops 6684672 | bytes 3937792 | tf_op jit(solution)/shard_map/convert_element_type | solution.py:31
  150.5 0.0 all-gather.2.cloned.1.call-update
  150.5 0.0 reduce-scatter.5.cloned.1.call-start
  150.6 9.9 %all-gather.2.cloned.1.call-done = bf16[384,2048]{1,0:T(8,128)(2,1)} async-done(((bf16[384,1024]{1,0:T(8,128)(2,1)}), bf16[384,2048]{1,0:T(8,128)(2,1)}) %all-gather.2.cloned.1.call-update) | async-done | bytes 1572880 | tf_op jit(solution)/shard_map/all_gather | solution.py:32
  160.5 3.8 %reshape.18 = bf16[384,4,2,256]{3,2,1,0:T(2,128)(2,1)} reshape(bf16[384,2048]{1,0:T(8,128)(2,1)} %all-gather.2.cloned.1.call-done) | data formatting | bytes 3145728 | tf_op jit(solution)/shard_map/reshape | solution.py:52
  164.3 3.0 %constant_dynamic-slice_fusion = bf16[384,4,1,256]{3,2,1,0:T(2,128)(2,1)S(1)} fusion(bf16[384,4,2,256]{3,2,1,0:T(2,128)(2,1)} %reshape.18, s32[]{:T(128)S(6)} %select_n.7), kind=kLoop, calls=%fused_computation.18 | loop fusion | bytes 1572868 | tf_op jit(solution)/shard_map/dynamic_slice | solution.py:53
  167.4 2.7 %copy.7 = bf16[384,4,1,256]{0,3,1,2:T(8,128)(2,1)} copy(bf16[384,4,1,256]{3,2,1,0:T(2,128)(2,1)S(1)} %constant_dynamic-slice_fusion) | data formatting | bytes 1572864
  170.1 3.7 %convolution_convert_fusion.1 = bf16[864,1024]{1,0:T(8,128)(2,1)} fusion(bf16[384,1024]{0,1:T(8,128)(2,1)} %bitcast.7, bf16[384,864]{0,1:T(8,128)(2,1)} %param.3, f32[384]{0:T(512)S(1)} %add_rsqrt_fusion), kind=kOutput, calls=%fused_computation.1 | convolution fusion | flops 681357312 | bytes 3220992 | tf_op jit(solution)/shard_map/dot_general | solution.py:57
  173.8 0.0 copy-start.2
  173.8 0.0 reduce-scatter.5.cloned.1.call-update
  173.8 0.0 reduce-scatter.3.cloned.1.call-start
  173.9 1.3 copy-done.2
  175.2 2.6 convolution_convert_fusion
  177.8 0.0 reduce-scatter.3.cloned.1.call-update
  177.8 35.7 %reduce-scatter.5.cloned.1.call-done = bf16[864,256]{1,0:T(8,128)(2,1)} async-done(((bf16[864,1024]{1,0:T(8,128)(2,1)}), bf16[864,256]{1,0:T(8,128)(2,1)}) %reduce-scatter.5.cloned.1.call-update) | async-done | bytes 442384 | tf_op jit(solution)/shard_map/reduce_scatter | solution.py:59
  213.5 2.0 convert_multiply_fusion.3
  215.5 43.1 %reduce-scatter.3.cloned.1.call-done = bf16[512,512]{1,0:T(8,128)(2,1)} async-done(((bf16[512,2048]{1,0:T(8,128)(2,1)}), bf16[512,512]{1,0:T(8,128)(2,1)}) %reduce-scatter.3.cloned.1.call-update) | async-done | bytes 524304 | tf_op jit(solution)/shard_map/reduce_scatter | solution.py:46
  258.6 2.2 convert_multiply_fusion.2
  (2 shorter events, 0.0 us)
Async XLA Ops:
  7.2 1.5 copy-start
  7.2 59.1 %all-reduce.4.cloned.1.call-start = ((), (), s32[]{:S(2)}) async-start(), calls=%async_computation.2 | async-start | bytes 3145728 | tf_op jit(solution)/shard_map/psum | solution.py:21
  11.9 1.1 copy-start.1
  11.9 7.1 %copy-start.4 = (f32[1024]{0:T(1024)S(1)}, f32[1024]{0:T(1024)}, u32[]{:S(2)}) copy-start(f32[1024]{0:T(1024)} %param.5) | copy-start | bytes 12292
  11.9 78.5 %all-reduce.6.cloned.1.call-start = ((), (), s32[]{:S(2)}) async-start(), calls=%async_computation.3 | async-start | bytes 2654208 | tf_op jit(solution)/shard_map/psum | solution.py:27
  70.3 76.5 %all-reduce.8.cloned.1.call-start = ((), (), s32[]{:S(2)}) async-start(), calls=%async_computation.4 | async-start | bytes 3145728 | tf_op jit(solution)/shard_map/psum | solution.py:30
  93.9 52.8 %copy-start.3 = (f32[384,1024]{1,0:T(8,128)S(1)}, f32[384,1024]{1,0:T(8,128)}, u32[]{:S(2)}) copy-start(f32[384,1024]{1,0:T(8,128)} %all-reduce.4.cloned.1.call-done) | copy-start | bytes 4718596
  94.0 66.5 %all-gather.2.cloned.1.call-start = ((), (), s32[]{:S(2)}) async-start(), calls=%async_computation.5 | async-start | bytes 2359296 | tf_op jit(solution)/shard_map/all_gather | solution.py:32
  150.5 63.0 %reduce-scatter.5.cloned.1.call-start = ((), (), s32[]{:S(2)}) async-start(), calls=%async_computation.7 | async-start | bytes 2211840 | tf_op jit(solution)/shard_map/reduce_scatter | solution.py:59
  173.8 1.4 copy-start.2
  173.8 84.9 %reduce-scatter.3.cloned.1.call-start = ((), (), s32[]{:S(2)}) async-start(), calls=%async_computation.6 | async-start | bytes 2621440 | tf_op jit(solution)/shard_map/reduce_scatter | solution.py:46
Sparse Core Ops, SparseCore 0:
  12.1 54.1 all-reduce.3
  70.4 20.0 all-reduce.5
  94.1 52.6 all-reduce.7
  150.6 9.8 all-gather.1
  173.9 39.5 reduce-scatter.4
  215.7 42.9 reduce-scatter.2
where the time goes:
time: 268 us
  waiting for transfers between devices  209 us (78%)
  matrix products  17 us (6%)
  between operations  14.1 us (5%)
  local copies, waits for them, and re-layouts  13.4 us (5%)
  other arithmetic  8.07 us (3%)
  blocking collectives  5.83 us (2%)
    psum x1, waiting for transfers between devices, on_device(): second = lax.psum(local_second, 'feat')  52.8 us
    psum x1, waiting for transfers between devices, on_device(): summed, energy = lax.psum((local_first, local_sq), 'feat')  47.2 us
    reduce_scatter x1, waiting for transfers between devices, on_device(): lax.psum_scatter(gram_part.astype(jnp.bfloat16), 'patch', scatter_dimensi...  43.1 us
    reduce_scatter x1, waiting for transfers between devices, on_device(): lax.psum_scatter(cross_part.astype(jnp.bfloat16), 'patch', scatter_dimens...  35.7 us
    psum x1, waiting for transfers between devices, on_device(): rebuilt = lax.psum(own_part, 'atom')  20.1 us
    all_gather x1, waiting for transfers between devices, on_device(): codes_whole = lax.all_gather(codes, 'atom', axis=1, tiled=True)  9.91 us
    unnamed x11, local copies, waits for them, and re-layouts  6.51 us
    psum x1, blocking collectives, on_device(): summed, energy = lax.psum((local_first, local_sq), 'feat')  5.83 us
  transfers between devices with their start and end apart: 6, of which 6 were waited for; matrix products, arithmetic and copies ran while one was open for 2% of the time, Pallas kernels for 0%

commit v1 on v0

--- a/solution.py
+++ b/solution.py
@@ -8,13 +8,14 @@
 
 
 step_rate = 0.2
+CHUNKS = 2
 
 
 def soften(value, level):
     return jnp.sign(value) * jnp.maximum(jnp.abs(value) - level, 0.0)
 
 
-def on_device(patches, dictionary, threshold):
+def general(patches, dictionary, threshold):
     values = patches.astype(jnp.float32)
     local_sq = jnp.sum(values * values, axis=1)
     local_first = jnp.dot(patches, dictionary, preferred_element_type=jnp.float32)
@@ -64,6 +65,97 @@
     return (codes, gram, cross)
 
 
+def swap(value, axis):
+    return lax.ppermute(value, axis, [(0, 1), (1, 0)])
+
+
+def shift(value):
+    n = lax.axis_size("patch")
+    return lax.ppermute(value, "patch", [(i, (i + 1) % n) for i in range(n)])
+
+
+def paired(patches, dictionary, threshold):
+    n_patch = lax.axis_size("patch")
+    plane = lax.axis_index("patch")
+    core = lax.axis_index("atom")
+    half = lax.axis_index("feat")
+    rows = patches.shape[0]
+    count = rows * n_patch
+    block = dictionary.shape[1] // 2
+    step = rows // CHUNKS
+    f32 = jnp.float32
+
+    values = patches.astype(f32)
+    local_sq = jnp.sum(values * values, axis=1)
+    energy = local_sq + swap(local_sq, "feat")
+    scale = lax.rsqrt(energy[:, None] / (BINS * VOXELS) + 1e-05)
+    normed = (scale * values).astype(jnp.bfloat16)
+    normed_of = [normed]
+    level = step_rate * threshold[None, :]
+    mine = half * block
+    theirs = (1 - half) * block
+    keep = lax.dynamic_slice_in_dim(dictionary, mine, block, 1)
+    send = lax.dynamic_slice_in_dim(dictionary, theirs, block, 1)
+    level_keep = lax.dynamic_slice_in_dim(level, mine, block, 1)
+
+    parts = []
+    for c in range(CHUNKS):
+        part = jnp.dot(patches[c * step : (c + 1) * step], dictionary, preferred_element_type=f32)
+        part = part.astype(jnp.bfloat16)
+        parts.append((part, swap(part, "feat")))
+    for k in range(1, n_patch):
+        normed_of.append(shift(normed_of[-1]))
+    codes_of = []
+    for c in range(CHUNKS):
+        window = slice(c * step, (c + 1) * step)
+        part, other = parts[c]
+        summed = part.astype(f32) + other.astype(f32)
+        start = soften(step_rate * (scale[window] * summed), level).astype(jnp.bfloat16)
+        own = lax.dot_general(start, dictionary, (((1,), (1,)), ((), ())), preferred_element_type=f32)
+        rebuilt = own + swap(own, "atom")
+        misfit = (scale[window] * values[window] - rebuilt).astype(jnp.bfloat16)
+        away = jnp.dot(misfit, send, preferred_element_type=f32).astype(jnp.bfloat16)
+        arrived = swap(away, "feat")
+        second = jnp.dot(misfit, keep, preferred_element_type=f32) + arrived.astype(f32)
+        start_keep = lax.dynamic_slice_in_dim(start, mine, block, 1).astype(f32)
+        codes_of.append(soften(start_keep + step_rate * second, level_keep).astype(jnp.bfloat16))
+
+    left = [codes_of]
+    for k in range(1, n_patch):
+        left.append([shift(x) for x in left[-1]])
+    outside = [swap(x, "feat") for x in codes_of]
+    own_rows = jnp.concatenate(codes_of, 0)
+    other_rows = jnp.concatenate(outside, 0)
+    codes = jnp.where(
+        half == 0,
+        jnp.concatenate([own_rows, other_rows], 1),
+        jnp.concatenate([other_rows, own_rows], 1),
+    )
+    home_core = plane // 2
+    home_half = plane % 2
+    over = [((q * 2 + q // 2) * 2 + q % 2, (q * 2 + q // 2) * 2 + 1 - q % 2) for q in range(n_patch)]
+    across = [(q * 2 + q // 2, q * 2 + 1 - q // 2) for q in range(n_patch)]
+    first = (((0,), (0,)), ((), ()))
+    gram = 0.0
+    cross = 0.0
+    for k in range(n_patch):
+        for c in range(CHUNKS):
+            lhs = left[k][c]
+            if k == 0:
+                there = jnp.where(half == home_half, lhs, outside[c])
+            else:
+                there = jnp.where(
+                    half == home_half, lhs, lax.ppermute(lhs, ("patch", "atom", "feat"), over)
+                )
+            rhs = jnp.where(core == home_core, there, lax.ppermute(there, ("patch", "atom"), across))
+            gram += lax.dot_general(lhs, rhs, first, preferred_element_type=f32)
+            narrow = lax.dynamic_slice_in_dim(rhs, core * (block // 2), block // 2, 1)
+            cross += lax.dot_general(
+                normed_of[k][c * step : (c + 1) * step], narrow, first, preferred_element_type=f32
+            )
+    return (codes, gram / count, cross / count)
+
+
 def solution(mesh):
     in_specs = (P(("slab", "patch"), "feat"), P("feat", "atom"), P("atom"))
     out_specs = (
@@ -71,6 +163,8 @@
         P(("slab", "atom", "feat"), "patch"),
         P(("slab", "feat"), ("patch", "atom")),
     )
+    sizes = mesh.shape
+    small = sizes["feat"] == 2 and sizes["atom"] == 2 and sizes["patch"] == 4
     return jax.shard_map(
-        on_device, mesh=mesh, in_specs=in_specs, out_specs=out_specs, check_vma=False
+        paired if small else general, mesh=mesh, in_specs=in_specs, out_specs=out_specs, check_vma=False
     )

time: 268 us -> 118 us (0.44)
  waiting for transfers between devices: 209 us -> 34.7 us
  starting transfers between devices: 0.25 us -> 47.7 us
  between operations: 14.1 us -> 1.13 us
  local copies, waits for them, and re-layouts: 13.4 us -> 2.87 us
  blocking collectives: 5.83 us -> 0 us
  other arithmetic: 8.07 us -> 11.3 us
  matrix products: 17 us -> 20.1 us
    psum x3 -> x0, waiting for transfers between devices: 120 us -> none  [the longest x1 52.8 us: on_device(): second = lax.psum(local_second, 'feat')]
    reduce_scatter x2 -> x0, waiting for transfers between devices: 78.8 us -> none  [the longest x1 43.1 us: on_device(): lax.psum_scatter(gram_part.astype(jnp.bfloat16), 'patch', scatter_dimensi...]
    ppermute x0 -> x32, starting transfers between devices: none -> 47.7 us  [the longest x6 17.7 us: paired(): lax.ppermute(lhs, ('patch', 'atom', 'feat'), over)]
    ppermute x0 -> x32, waiting for transfers between devices: none -> 34.7 us  [the longest x9 23.8 us: swap(): return lax.ppermute(value, axis, [(0, 1), (1, 0)])]
    all_gather x1 -> x0, waiting for transfers between devices: 9.91 us -> none  [on_device(): codes_whole = lax.all_gather(codes, 'atom', axis=1, tiled=True)]
    psum x1 -> x0, blocking collectives: 5.83 us -> none  [on_device(): summed, energy = lax.psum((local_first, local_sq), 'feat')]
    select_n x0 -> x17, other arithmetic: none -> 5.01 us  [the longest x6 2.01 us: paired(): jnp.where(half == home_half, lhs, lax.ppermute(lhs, ('patch', 'atom', 'fe...]
    unnamed x11 -> x13, local copies, waits for them, and re-layouts: 6.51 us -> 1.61 us
  transfers between devices with their start and end apart: 6 -> 32, of which waited for: 6 -> 12; matrix products, arithmetic and copies ran while one was open for 2% -> 25% of each run, Pallas kernels for 0% -> 0%
where the time goes in v1:
time: 118 us
  starting transfers between devices  47.7 us (40%)
  waiting for transfers between devices  34.7 us (29%)
  matrix products  20.1 us (17%)
  other arithmetic  11.3 us (10%)
  local copies, waits for them, and re-layouts  2.87 us (2%)
    ppermute x9, waiting for transfers between devices, swap(): return lax.ppermute(value, axis, [(0, 1), (1, 0)])  23.8 us
    ppermute x6, starting transfers between devices, paired(): lax.ppermute(lhs, ('patch', 'atom', 'feat'), over)  17.7 us
    ppermute x8, starting transfers between devices, paired(): lax.ppermute(there, ('patch', 'atom'), across)  11 us
    ppermute x9, starting transfers between devices, shift(): return lax.ppermute(value, 'patch', [(i, (i + 1) % n) for i in range(n)])  9.97 us
    ppermute x9, starting transfers between devices, swap(): return lax.ppermute(value, axis, [(0, 1), (1, 0)])  9 us
    dot_general x8, matrix products, paired(): lax.dot_general(normed_of[k][c * step:(c + 1) * step], narrow, first, pre...  7.42 us
    ppermute x9, waiting for transfers between devices, shift(): return lax.ppermute(value, 'patch', [(i, (i + 1) % n) for i in range(n)])  5.69 us
    dot_general x8, matrix products, paired(): gram += lax.dot_general(lhs, rhs, first, preferred_element_type=f32)  5.47 us
  transfers between devices with their start and end apart: 32, of which 12 were waited for; matrix products, arithmetic and copies ran while one was open for 25% of the time, Pallas kernels for 0%

profile of v1, /device:TPU:0, one launch (start us, length us, event | category | flops | bytes accessed | tf_op | source)
XLA Modules:
  0.0 117.7 jit_solution(6946021532586709267)
XLA Ops:
  0.7 1.6 %copy.7 = bf16[384,864]{1,0:T(8,128)(2,1)S(1)} copy(bf16[384,864]{0,1:T(8,128)(2,1)} %param.3) | data formatting | bytes 1327104 | tf_op args[0]
  2.5 3.0 %collective-permute-start = (f32[384]{0:T(512)S(1)}, f32[384]{0:T(512)S(1)}, u32[]{:S(2)}, u32[]{:S(2)}) collective-permute-start(f32[384]{0:T(512)S(1)} %multiply_reduce_fusion), channel_id=1, source_target_pairs={{0,1},{1,0},{2,3},{3,2},{4,5},{5,4},{6,7},{7,6},{8,9},{9,8},{10,11... | collective-permute-start | bytes 4616 | tf_op jit(solution)/shard_map/ppermute | solution.py:69
  5.5 0.6 convolution_convert_fusion.1
  6.2 1.4 %convolution_convert_fusion = bf16[192,1024]{1,0:T(8,128)(2,1)} fusion(bf16[864,1024]{1,0:T(8,128)(2,1)S(1)} %copy-done, bf16[384,864]{0,1:T(8,128)(2,1)S(1)} %copy-done.3), kind=kOutput, calls=%fused_computation.18 | convolution fusion | flops 339935232 | bytes 2605056 | tf_op jit(solution)/shard_map/dot_general | solution.py:103
  7.6 2.0 %collective-permute-start.4 = (bf16[192,1024]{1,0:T(8,128)(2,1)}, bf16[192,1024]{1,0:T(8,128)(2,1)}, u32[]{:S(2)}, u32[]{:S(2)}) collective-permute-start(bf16[192,1024]{1,0:T(8,128)(2,1)} %convolution_convert_fusion), channel_id=1, source_target_pairs={{0,1},{1,0},{2,3},{3,2},{4,5},{5,4},{6,7},{7,6},{8,9},{9,8},{10,11... | collective-permute-start | bytes 1179656 | tf_op jit(solution)/shard_map/ppermute | solution.py:69
  9.8 1.1 copy.8
  10.9 1.6 %collective-permute-start.29 = (bf16[384,864]{0,1:T(8,128)(2,1)}, bf16[384,864]{0,1:T(8,128)(2,1)}, u32[]{:S(2)}, u32[]{:S(2)}) collective-permute-start(bf16[384,864]{0,1:T(8,128)(2,1)} %copy.8), channel_id=1, source_target_pairs={{0,4},{4,8},{8,12},{12,0},{1,5},{5,9},{9,13},{13,1},{2,6},{6,10},{... | collective-permute-start | bytes 1990664 | tf_op jit(solution)/shard_map/ppermute | solution.py:74
  12.6 5.7 %collective-permute-done.1 = bf16[192,1024]{1,0:T(8,128)(2,1)} collective-permute-done((bf16[192,1024]{1,0:T(8,128)(2,1)S(1)}, bf16[192,1024]{1,0:T(8,128)(2,1)}, u32[]{:S(2)}, u32[]{:S(2)}) %collective-permute-start.1) | collective-permute-done | bytes 393248 | tf_op jit(solution)/shard_map/ppermute | solution.py:69
  18.3 7.0 %collective-permute-done.4 = bf16[192,1024]{1,0:T(8,128)(2,1)} collective-permute-done((bf16[192,1024]{1,0:T(8,128)(2,1)}, bf16[192,1024]{1,0:T(8,128)(2,1)}, u32[]{:S(2)}, u32[]{:S(2)}) %collective-permute-start.4) | collective-permute-done | bytes 393248 | tf_op jit(solution)/shard_map/ppermute | solution.py:69
  25.3 2.3 %multiply_convert_fusion.1 = (bf16[192,1024]{1,0:T(8,128)(2,1)S(1)}, bf16[192,1024]{1,0:T(8,128)(2,1)S(1)}) fusion(bf16[192,1024]{1,0:T(8,128)(2,1)} %collective-permute-done.4, bf16[192,1024]{1,0:T(8,128)(2,1)} %convolution_convert_fusion, f32[192]{0:T(256)S(1)} %get-tuple-element.11, f32[1024]{0:T(1024)S(1)} %broadcast_multiply_fusion, ...), kind=kLoop, calls=%fused_computation.29 | loop fusion | flops 4325376 | bytes 2364928 | tf_op jit(solution)/shard_map/convert_element_type | solution.py:113
  27.5 1.6 %fusion.62 = f32[192,864]{1,0:T(8,128)} fusion(bf16[192,1024]{1,0:T(8,128)(2,1)S(1)} %get-tuple-element.10, bf16[864,1024]{1,0:T(8,128)(2,1)S(1)} %copy-done), kind=kOutput, calls=%fused_computation.99 | convolution fusion | flops 339738624 | bytes 2826240 | tf_op jit(solution)/shard_map/dot_general | solution.py:114
  29.2 1.6 %fusion.63 = f32[192,864]{1,0:T(8,128)} fusion(bf16[192,1024]{1,0:T(8,128)(2,1)S(1)} %get-tuple-element.9, bf16[864,1024]{1,0:T(8,128)(2,1)S(1)} %copy-done), kind=kOutput, calls=%fused_computation.100 | convolution fusion | flops 339738624 | bytes 2826240 | tf_op jit(solution)/shard_map/dot_general | solution.py:114
  30.8 0.5 collective-permute-start.5
  31.3 1.2 %convert_element_type.60 = f32[384,864]{1,0:T(8,128)} convert(bf16[384,864]{1,0:T(8,128)(2,1)S(1)} %copy.7) | non-fusion elementwise | flops 331776 | bytes 1990656 | tf_op jit(solution)/shard_map/convert_element_type | solution.py:88
  32.6 1.6 %collective-permute-start.30 = (bf16[384,864]{0,1:T(8,128)(2,1)}, bf16[384,864]{0,1:T(8,128)(2,1)}, u32[]{:S(2)}, u32[]{:S(2)}) collective-permute-start(bf16[384,864]{0,1:T(8,128)(2,1)} %collective-permute-done.29), channel_id=1, source_target_pairs={{0,4},{4,8},{8,12},{12,0},{1,5},{5,9},{9,13},{13,1},{2,6},{6,10},{... | collective-permute-start | bytes 1990664 | tf_op jit(solution)/shard_map/ppermute | solution.py:74
  34.2 2.4 %fusion.19 = (bf16[192,864]{1,0:T(8,128)(2,1)S(1)}, bf16[192,864]{1,0:T(8,128)(2,1)S(1)}) fusion(f32[384,864]{1,0:T(8,128)} %convert_element_type.60, f32[192,864]{1,0:T(8,128)} %fusion.63, f32[192,864]{1,0:T(8,128)} %collective-permute-done.5, f32[192]{0:T(256)S(1)} %get-tuple-element.11, f32[192,864]{1,0:T(8,128)} %fusion.62, ...), kind=kLoop, calls=%fused_computation.37 | loop fusion | flops 1327104 | bytes 4646400 | tf_op jit(solution)/shard_map/convert_element_type | solution.py:116
  36.6 0.4 convolution_convert_fusion.3
  37.0 0.6 collective-permute-start.3
  37.6 0.4 convolution_convert_fusion.2
  38.0 1.5 %collective-permute-start.6 = (bf16[192,512]{1,0:T(8,128)(2,1)S(1)}, bf16[192,512]{1,0:T(8,128)(2,1)S(1)}, u32[]{:S(2)}, u32[]{:S(2)}) collective-permute-start(bf16[192,512]{1,0:T(8,128)(2,1)S(1)} %convolution_convert_fusion.2), channel_id=1, source_target_pairs={{0,1},{1,0},{2,3},{3,2},{4,5},{5,4},{6,7},{7,6},{8,9},{9,8},{10,11... | collective-permute-start | bytes 589832 | tf_op jit(solution)/shard_map/ppermute | solution.py:69
  39.5 5.3 %collective-permute-done.3 = bf16[192,512]{1,0:T(8,128)(2,1)S(1)} collective-permute-done((bf16[192,512]{1,0:T(8,128)(2,1)S(1)}, bf16[192,512]{1,0:T(8,128)(2,1)S(1)}, u32[]{:S(2)}, u32[]{:S(2)}) %collective-permute-start.3) | collective-permute-done | bytes 196640 | tf_op jit(solution)/shard_map/ppermute | solution.py:69
  44.8 0.6 multiply_convert_fusion.4
  45.4 0.6 collective-permute-start.7
  46.0 1.6 %collective-permute-start.11 = (bf16[192,512]{1,0:T(8,128)(2,1)S(1)}, bf16[192,512]{1,0:T(8,128)(2,1)}, u32[]{:S(2)}, u32[]{:S(2)}) collective-permute-start(bf16[192,512]{1,0:T(8,128)(2,1)S(1)} %multiply_convert_fusion.4), channel_id=1, source_target_pairs={{0,4},{4,8},{8,12},{12,0},{1,5},{5,9},{9,13},{13,1},{2,6},{6,10},{... | collective-permute-start | bytes 589832 | tf_op jit(solution)/shard_map/ppermute | solution.py:74
  47.6 1.5 %collective-permute-done.6 = bf16[192,512]{1,0:T(8,128)(2,1)S(1)} collective-permute-done((bf16[192,512]{1,0:T(8,128)(2,1)S(1)}, bf16[192,512]{1,0:T(8,128)(2,1)S(1)}, u32[]{:S(2)}, u32[]{:S(2)}) %collective-permute-start.6) | collective-permute-done | bytes 196640 | tf_op jit(solution)/shard_map/ppermute | solution.py:69
  49.0 0.6 multiply_convert_fusion.3
  49.6 0.6 collective-permute-start.8
  50.2 1.6 %collective-permute-start.14 = (bf16[192,512]{1,0:T(8,128)(2,1)S(1)}, bf16[192,512]{1,0:T(8,128)(2,1)}, u32[]{:S(2)}, u32[]{:S(2)}) collective-permute-start(bf16[192,512]{1,0:T(8,128)(2,1)S(1)} %multiply_convert_fusion.3), channel_id=1, source_target_pairs={{0,4},{4,8},{8,12},{12,0},{1,5},{5,9},{9,13},{13,1},{2,6},{6,10},{... | collective-permute-start | bytes 589832 | tf_op jit(solution)/shard_map/ppermute | solution.py:74
  51.8 1.5 %collective-permute-done.7 = bf16[192,512]{1,0:T(8,128)(2,1)S(1)} collective-permute-done((bf16[192,512]{1,0:T(8,128)(2,1)S(1)}, bf16[192,512]{1,0:T(8,128)(2,1)S(1)}, u32[]{:S(2)}, u32[]{:S(2)}) %collective-permute-start.7) | collective-permute-done | bytes 196640 | tf_op jit(solution)/shard_map/ppermute | solution.py:69
  53.3 2.9 %collective-permute-done.8 = bf16[192,512]{1,0:T(8,128)(2,1)S(1)} collective-permute-done((bf16[192,512]{1,0:T(8,128)(2,1)S(1)}, bf16[192,512]{1,0:T(8,128)(2,1)S(1)}, u32[]{:S(2)}, u32[]{:S(2)}) %collective-permute-start.8) | collective-permute-done | bytes 196640 | tf_op jit(solution)/shard_map/ppermute | solution.py:69
  56.2 0.7 broadcast_select_fusion.6
  56.9 2.0 %collective-permute-start.10 = (bf16[192,512]{1,0:T(8,128)(2,1)}, bf16[192,512]{1,0:T(8,128)(2,1)}, u32[]{:S(2)}, u32[]{:S(2)}) collective-permute-start(bf16[192,512]{1,0:T(8,128)(2,1)} %get-tuple-element.7), channel_id=1, source_target_pairs={{0,2},{4,6},{10,8},{14,12},{1,3},{5,7},{11,9},{15,13},{16,18},{20,... | collective-permute-start | bytes 589832 | tf_op jit(solution)/shard_map/ppermute | solution.py:150
  58.9 1.6 %collective-permute-start.31 = (bf16[384,864]{0,1:T(8,128)(2,1)}, bf16[384,864]{0,1:T(8,128)(2,1)S(1)}, u32[]{:S(2)}, u32[]{:S(2)}) collective-permute-start(bf16[384,864]{0,1:T(8,128)(2,1)} %collective-permute-done.30), channel_id=1, source_target_pairs={{0,4},{4,8},{8,12},{12,0},{1,5},{5,9},{9,13},{13,1},{2,6},{6,10},{... | collective-permute-start | bytes 1990664 | tf_op jit(solution)/shard_map/ppermute | solution.py:74
  60.5 1.3 %collective-permute-start.9 = (bf16[192,512]{1,0:T(8,128)(2,1)S(1)}, bf16[192,512]{1,0:T(8,128)(2,1)S(1)}, u32[]{:S(2)}, u32[]{:S(2)}) collective-permute-start(bf16[192,512]{1,0:T(8,128)(2,1)S(1)} %get-tuple-element.5), channel_id=1, source_target_pairs={{0,2},{4,6},{10,8},{14,12},{1,3},{5,7},{11,9},{15,13},{16,18},{20,... | collective-permute-start | bytes 589832 | tf_op jit(solution)/shard_map/ppermute | solution.py:150
  61.8 2.5 %collective-permute-start.12 = (bf16[192,512]{1,0:T(8,128)(2,1)}, bf16[192,512]{1,0:T(8,128)(2,1)S(1)}, u32[]{:S(2)}, u32[]{:S(2)}) collective-permute-start(bf16[192,512]{1,0:T(8,128)(2,1)} %collective-permute-done.11), channel_id=1, source_target_pairs={{0,1},{5,4},{10,11},{15,14},{16,17},{21,20},{26,27},{31,30}} | collective-permute-start | bytes 589832 | tf_op jit(solution)/shard_map/ppermute | solution.py:148
  64.3 1.1 maximum_select_fusion
  65.4 1.8 %collective-permute-start.17 = (bf16[192,512]{1,0:T(8,128)(2,1)}, bf16[192,512]{1,0:T(8,128)(2,1)S(1)}, u32[]{:S(2)}, u32[]{:S(2)}) collective-permute-start(bf16[192,512]{1,0:T(8,128)(2,1)} %collective-permute-done.11), channel_id=1, source_target_pairs={{0,4},{4,8},{8,12},{12,0},{1,5},{5,9},{9,13},{13,1},{2,6},{6,10},{... | collective-permute-start | bytes 589832 | tf_op jit(solution)/shard_map/ppermute | solution.py:74
  67.2 4.6 %collective-permute-start.15 = (bf16[192,512]{1,0:T(8,128)(2,1)}, bf16[192,512]{1,0:T(8,128)(2,1)S(1)}, u32[]{:S(2)}, u32[]{:S(2)}) collective-permute-start(bf16[192,512]{1,0:T(8,128)(2,1)} %collective-permute-done.14), channel_id=1, source_target_pairs={{0,1},{5,4},{10,11},{15,14},{16,17},{21,20},{26,27},{31,30}} | collective-permute-start | bytes 589832 | tf_op jit(solution)/shard_map/ppermute | solution.py:148
  71.8 1.0 broadcast_select_fusion.14
  73.5 1.0 broadcast_select_fusion.5
  74.4 0.8 collective-permute-done.15
  75.2 1.3 %collective-permute-start.13 = (bf16[192,512]{1,0:T(8,128)(2,1)S(1)}, bf16[192,512]{1,0:T(8,128)(2,1)S(1)}, u32[]{:S(2)}, u32[]{:S(2)}) collective-permute-start(bf16[192,512]{1,0:T(8,128)(2,1)S(1)} %broadcast_select_fusion.5), channel_id=1, source_target_pairs={{0,2},{4,6},{10,8},{14,12},{1,3},{5,7},{11,9},{15,13},{16,18},{20,... | collective-permute-start | bytes 589832 | tf_op jit(solution)/shard_map/ppermute | solution.py:150
  76.5 1.0 broadcast_select_fusion.4
  77.5 1.3 %collective-permute-start.16 = (bf16[192,512]{1,0:T(8,128)(2,1)S(1)}, bf16[192,512]{1,0:T(8,128)(2,1)S(1)}, u32[]{:S(2)}, u32[]{:S(2)}) collective-permute-start(bf16[192,512]{1,0:T(8,128)(2,1)S(1)} %broadcast_select_fusion.4), channel_id=1, source_target_pairs={{0,2},{4,6},{10,8},{14,12},{1,3},{5,7},{11,9},{15,13},{16,18},{20,... | collective-permute-start | bytes 589832 | tf_op jit(solution)/shard_map/ppermute | solution.py:150
  78.8 4.0 %collective-permute-done.17 = bf16[192,512]{1,0:T(8,128)(2,1)S(1)} collective-permute-done((bf16[192,512]{1,0:T(8,128)(2,1)}, bf16[192,512]{1,0:T(8,128)(2,1)S(1)}, u32[]{:S(2)}, u32[]{:S(2)}) %collective-permute-start.17) | collective-permute-done | bytes 196640 | tf_op jit(solution)/shard_map/ppermute | solution.py:74
  82.8 2.5 %collective-permute-start.18 = (bf16[192,512]{1,0:T(8,128)(2,1)S(1)}, bf16[192,512]{1,0:T(8,128)(2,1)S(1)}, u32[]{:S(2)}, u32[]{:S(2)}) collective-permute-start(bf16[192,512]{1,0:T(8,128)(2,1)S(1)} %collective-permute-done.17), channel_id=1, source_target_pairs={{0,1},{5,4},{10,11},{15,14},{16,17},{21,20},{26,27},{31,30}} | collective-permute-start | bytes 589832 | tf_op jit(solution)/shard_map/ppermute | solution.py:148
  85.3 1.7 %collective-permute-done.20 = bf16[192,512]{1,0:T(8,128)(2,1)S(1)} collective-permute-done((bf16[192,512]{1,0:T(8,128)(2,1)}, bf16[192,512]{1,0:T(8,128)(2,1)S(1)}, u32[]{:S(2)}, u32[]{:S(2)}) %collective-permute-start.20) | collective-permute-done | bytes 196640 | tf_op jit(solution)/shard_map/ppermute | solution.py:74
  87.0 2.5 %collective-permute-start.21 = (bf16[192,512]{1,0:T(8,128)(2,1)S(1)}, bf16[192,512]{1,0:T(8,128)(2,1)S(1)}, u32[]{:S(2)}, u32[]{:S(2)}) collective-permute-start(bf16[192,512]{1,0:T(8,128)(2,1)S(1)} %collective-permute-done.20), channel_id=1, source_target_pairs={{0,1},{5,4},{10,11},{15,14},{16,17},{21,20},{26,27},{31,30}} | collective-permute-start | bytes 589832 | tf_op jit(solution)/shard_map/ppermute | solution.py:148
  89.7 2.9 %collective-permute-done.21 = bf16[192,512]{1,0:T(8,128)(2,1)S(1)} collective-permute-done((bf16[192,512]{1,0:T(8,128)(2,1)S(1)}, bf16[192,512]{1,0:T(8,128)(2,1)S(1)}, u32[]{:S(2)}, u32[]{:S(2)}) %collective-permute-start.21) | collective-permute-done | bytes 196640 | tf_op jit(solution)/shard_map/ppermute | solution.py:148
  92.6 1.3 %collective-permute-start.19 = (bf16[192,512]{1,0:T(8,128)(2,1)S(1)}, bf16[192,512]{1,0:T(8,128)(2,1)S(1)}, u32[]{:S(2)}, u32[]{:S(2)}) collective-permute-start(bf16[192,512]{1,0:T(8,128)(2,1)S(1)} %broadcast_select_fusion.3), channel_id=1, source_target_pairs={{0,2},{4,6},{10,8},{14,12},{1,3},{5,7},{11,9},{15,13},{16,18},{20,... | collective-permute-start | bytes 589832 | tf_op jit(solution)/shard_map/ppermute | solution.py:150
  94.0 1.3 %collective-permute-start.22 = (bf16[192,512]{1,0:T(8,128)(2,1)S(1)}, bf16[192,512]{1,0:T(8,128)(2,1)S(1)}, u32[]{:S(2)}, u32[]{:S(2)}) collective-permute-start(bf16[192,512]{1,0:T(8,128)(2,1)S(1)} %broadcast_select_fusion.2), channel_id=1, source_target_pairs={{0,2},{4,6},{10,8},{14,12},{1,3},{5,7},{11,9},{15,13},{16,18},{20,... | collective-permute-start | bytes 589832 | tf_op jit(solution)/shard_map/ppermute | solution.py:150
  95.3 1.3 %fusion.65 = f32[512,512]{1,0:T(8,128)S(1)} fusion(bf16[192,512]{1,0:T(8,128)(2,1)} %collective-permute-done.11, bf16[192,512]{1,0:T(8,128)(2,1)S(1)} %broadcast_select_fusion.13), kind=kOutput, calls=%fused_computation.102 | convolution fusion | flops 100663296 | bytes 1441792 | tf_op jit(solution)/shard_map/dot_general | solution.py:151
  96.6 1.3 %fusion.66 = f32[512,512]{1,0:T(8,128)S(1)} fusion(bf16[192,512]{1,0:T(8,128)(2,1)} %collective-permute-done.14, bf16[192,512]{1,0:T(8,128)(2,1)S(1)} %broadcast_select_fusion.12), kind=kOutput, calls=%fused_computation.103 | convolution fusion | flops 100663296 | bytes 1441792 | tf_op jit(solution)/shard_map/dot_general | solution.py:151
  98.2 1.3 %fusion.30 = f32[864,256]{1,0:T(8,128)S(1)} fusion(bf16[384,864]{0,1:T(8,128)(2,1)} %collective-permute-done.29, bf16[192,512]{1,0:T(8,128)(2,1)S(1)} %broadcast_select_fusion.13, s32[]{:T(128)S(6)} %select_n.132), kind=kOutput, calls=%fused_computation.49 | convolution fusion | flops 84934656 | bytes 1425412 | tf_op jit(solution)/shard_map/dot_general | solution.py:153
  99.5 4.4 %collective-permute-start.24 = (bf16[192,512]{1,0:T(8,128)(2,1)S(1)}, bf16[192,512]{1,0:T(8,128)(2,1)S(1)}, u32[]{:S(2)}, u32[]{:S(2)}) collective-permute-start(bf16[192,512]{1,0:T(8,128)(2,1)S(1)} %collective-permute-done.23), channel_id=1, source_target_pairs={{0,1},{5,4},{10,11},{15,14},{16,17},{21,20},{26,27},{31,30}} | collective-permute-start | bytes 589832 | tf_op jit(solution)/shard_map/ppermute | solution.py:148
  103.9 1.3 %fusion.28 = f32[864,256]{1,0:T(8,128)S(1)} fusion(bf16[384,864]{0,1:T(8,128)(2,1)} %collective-permute-done.29, bf16[192,512]{1,0:T(8,128)(2,1)S(1)} %broadcast_select_fusion.12, s32[]{:T(128)S(6)} %select_n.132), kind=kOutput, calls=%fused_computation.47 | convolution fusion | flops 84934656 | bytes 1425412 | tf_op jit(solution)/shard_map/dot_general | solution.py:153
  105.2 1.3 %collective-permute-start.27 = (bf16[192,512]{1,0:T(8,128)(2,1)S(1)}, bf16[192,512]{1,0:T(8,128)(2,1)S(1)}, u32[]{:S(2)}, u32[]{:S(2)}) collective-permute-start(bf16[192,512]{1,0:T(8,128)(2,1)S(1)} %collective-permute-done.26), channel_id=1, source_target_pairs={{0,1},{5,4},{10,11},{15,14},{16,17},{21,20},{26,27},{31,30}} | collective-permute-start | bytes 589832 | tf_op jit(solution)/shard_map/ppermute | solution.py:148
  107.1 1.3 %collective-permute-start.25 = (bf16[192,512]{1,0:T(8,128)(2,1)S(1)}, bf16[192,512]{1,0:T(8,128)(2,1)S(1)}, u32[]{:S(2)}, u32[]{:S(2)}) collective-permute-start(bf16[192,512]{1,0:T(8,128)(2,1)S(1)} %broadcast_select_fusion.1), channel_id=1, source_target_pairs={{0,2},{4,6},{10,8},{14,12},{1,3},{5,7},{11,9},{15,13},{16,18},{20,... | collective-permute-start | bytes 589832 | tf_op jit(solution)/shard_map/ppermute | solution.py:150
  108.4 1.3 %collective-permute-done.27 = bf16[192,512]{1,0:T(8,128)(2,1)S(1)} collective-permute-done((bf16[192,512]{1,0:T(8,128)(2,1)S(1)}, bf16[192,512]{1,0:T(8,128)(2,1)S(1)}, u32[]{:S(2)}, u32[]{:S(2)}) %collective-permute-start.27) | collective-permute-done | bytes 196640 | tf_op jit(solution)/shard_map/ppermute | solution.py:148
  109.7 1.3 %collective-permute-start.28 = (bf16[192,512]{1,0:T(8,128)(2,1)S(1)}, bf16[192,512]{1,0:T(8,128)(2,1)S(1)}, u32[]{:S(2)}, u32[]{:S(2)}) collective-permute-start(bf16[192,512]{1,0:T(8,128)(2,1)S(1)} %broadcast_select_fusion), channel_id=1, source_target_pairs={{0,2},{4,6},{10,8},{14,12},{1,3},{5,7},{11,9},{15,13},{16,18},{20,... | collective-permute-start | bytes 589832 | tf_op jit(solution)/shard_map/ppermute | solution.py:150
  111.4 1.3 %fusion.25 = f32[864,256]{1,0:T(8,128)S(1)} fusion(bf16[384,864]{0,1:T(8,128)(2,1)} %collective-permute-done.30, bf16[192,512]{1,0:T(8,128)(2,1)S(1)} %broadcast_select_fusion.10, s32[]{:T(128)S(6)} %select_n.132), kind=kOutput, calls=%fused_computation.44 | convolution fusion | flops 84934656 | bytes 1425412 | tf_op jit(solution)/shard_map/dot_general | solution.py:153
  113.2 1.3 %fusion.7 = f32[864,256]{1,0:T(8,128)S(1)} fusion(f32[864,256]{1,0:T(8,128)S(1)} %fusion.25, f32[864,256]{1,0:T(8,128)S(1)} %fusion.9, bf16[384,864]{0,1:T(8,128)(2,1)} %collective-permute-done.30, bf16[192,512]{1,0:T(8,128)(2,1)S(1)} %broadcast_select_fusion.11, s32[]{:T(128)S(6)} %select_n.132), kind=kOutput, calls=%fused_computation.14 | convolution fusion | flops 85377024 | bytes 3194884 | tf_op jit(solution)/shard_map/dot_general | solution.py:153
  115.2 1.2 %fusion.6 = f32[864,256]{1,0:T(8,128)} fusion(f32[864,256]{1,0:T(8,128)S(1)} %fusion.22, f32[864,256]{1,0:T(8,128)S(1)} %fusion.7, bf16[384,864]{0,1:T(8,128)(2,1)S(1)} %collective-permute-done.31, bf16[192,512]{1,0:T(8,128)(2,1)S(1)} %broadcast_select_fusion.9, s32[]{:T(128)S(6)} %select_n.132), kind=kOutput, calls=%fused_computation.12 | convolution fusion | flops 85598208 | bytes 3194884 | tf_op jit(solution)/shard_map/dot_general | solution.py:153
  116.4 1.3 %fusion.1 = f32[512,512]{1,0:T(8,128)} fusion(f32[512,512]{1,0:T(8,128)S(1)} %fusion.68, f32[512,512]{1,0:T(8,128)S(1)} %fusion.2, bf16[192,512]{1,0:T(8,128)(2,1)S(1)} %collective-permute-done.23, bf16[192,512]{1,0:T(8,128)(2,1)S(1)} %broadcast_select_fusion.9), kind=kOutput, calls=%fused_computation.4 | convolution fusion | flops 101449728 | bytes 3538944 | tf_op jit(solution)/shard_map/dot_general | solution.py:151
  (64 shorter events, 4.1 us)
Async XLA Ops:
  0.6 4.8 %copy-start = (bf16[864,1024]{1,0:T(8,128)(2,1)S(1)}, bf16[864,1024]{1,0:T(8,128)(2,1)}, u32[]{:S(2)}) copy-start(bf16[864,1024]{1,0:T(8,128)(2,1)} %param.4) | copy-start | bytes 5308420
  0.6 4.8 %copy-start.3 = (bf16[384,864]{0,1:T(8,128)(2,1)S(1)}, bf16[384,864]{0,1:T(8,128)(2,1)}, u32[]{:S(2)}) copy-start(bf16[384,864]{0,1:T(8,128)(2,1)} %param.3) | copy-start | bytes 1990660
  2.5 7.2 %collective-permute-start = (f32[384]{0:T(512)S(1)}, f32[384]{0:T(512)S(1)}, u32[]{:S(2)}, u32[]{:S(2)}) collective-permute-start(f32[384]{0:T(512)S(1)} %multiply_reduce_fusion), channel_id=1, source_target_pairs={{0,1},{1,0},{2,3},{3,2},{4,5},{5,4},{6,7},{7,6},{8,9},{9,8},{10,11... | collective-permute-start | bytes 4616 | tf_op jit(solution)/shard_map/ppermute | solution.py:69
  6.1 19.2 %copy-start.4 = (bf16[192,1024]{1,0:T(8,128)(2,1)}, bf16[192,1024]{1,0:T(8,128)(2,1)S(1)}, u32[]{:S(2)}) copy-start(bf16[192,1024]{1,0:T(8,128)(2,1)S(1)} %convolution_convert_fusion.1) | copy-start | bytes 1179652
  6.1 3.5 %copy-start.5 = (f32[1024]{0:T(1024)S(1)}, f32[1024]{0:T(1024)}, u32[]{:S(2)}) copy-start(f32[1024]{0:T(1024)} %param.5) | copy-start | bytes 12292
  6.1 12.2 %collective-permute-start.1 = (bf16[192,1024]{1,0:T(8,128)(2,1)S(1)}, bf16[192,1024]{1,0:T(8,128)(2,1)}, u32[]{:S(2)}, u32[]{:S(2)}) collective-permute-start(bf16[192,1024]{1,0:T(8,128)(2,1)S(1)} %convolution_convert_fusion.1), channel_id=1, source_target_pairs={{0,1},{1,0},{2,3},{3,2},{4,5},{5,4},{6,7},{7,6},{8,9},{9,8},{10,11... | collective-permute-start | bytes 1179656 | tf_op jit(solution)/shard_map/ppermute | solution.py:69
  7.6 17.6 %collective-permute-start.4 = (bf16[192,1024]{1,0:T(8,128)(2,1)}, bf16[192,1024]{1,0:T(8,128)(2,1)}, u32[]{:S(2)}, u32[]{:S(2)}) collective-permute-start(bf16[192,1024]{1,0:T(8,128)(2,1)} %convolution_convert_fusion), channel_id=1, source_target_pairs={{0,1},{1,0},{2,3},{3,2},{4,5},{5,4},{6,7},{7,6},{8,9},{9,8},{10,11... | collective-permute-start | bytes 1179656 | tf_op jit(solution)/shard_map/ppermute | solution.py:69
  10.9 21.6 %collective-permute-start.29 = (bf16[384,864]{0,1:T(8,128)(2,1)}, bf16[384,864]{0,1:T(8,128)(2,1)}, u32[]{:S(2)}, u32[]{:S(2)}) collective-permute-start(bf16[384,864]{0,1:T(8,128)(2,1)} %copy.8), channel_id=1, source_target_pairs={{0,4},{4,8},{8,12},{12,0},{1,5},{5,9},{9,13},{13,1},{2,6},{6,10},{... | collective-permute-start | bytes 1990664 | tf_op jit(solution)/shard_map/ppermute | solution.py:74
  27.5 3.3 %copy-start.1 = (bf16[192,1024]{1,0:T(8,128)(2,1)}, bf16[192,1024]{1,0:T(8,128)(2,1)S(1)}, u32[]{:S(2)}) copy-start(bf16[192,1024]{1,0:T(8,128)(2,1)S(1)} %get-tuple-element.10) | copy-start | bytes 1179652
  29.2 5.0 %collective-permute-start.2 = (f32[192,864]{1,0:T(8,128)}, f32[192,864]{1,0:T(8,128)}, u32[]{:S(2)}, u32[]{:S(2)}) collective-permute-start(f32[192,864]{1,0:T(8,128)} %fusion.62), channel_id=1, source_target_pairs={{0,2},{2,0},{1,3},{3,1},{4,6},{6,4},{5,7},{7,5},{8,10},{10,8},{9,1... | collective-permute-start | bytes 1990664 | tf_op jit(solution)/shard_map/ppermute | solution.py:69
  30.8 3.4 %collective-permute-start.5 = (f32[192,864]{1,0:T(8,128)}, f32[192,864]{1,0:T(8,128)}, u32[]{:S(2)}, u32[]{:S(2)}) collective-permute-start(f32[192,864]{1,0:T(8,128)} %fusion.63), channel_id=1, source_target_pairs={{0,2},{2,0},{1,3},{3,1},{4,6},{6,4},{5,7},{7,5},{8,10},{10,8},{9,1... | collective-permute-start | bytes 1990664 | tf_op jit(solution)/shard_map/ppermute | solution.py:69
  32.6 26.3 %collective-permute-start.30 = (bf16[384,864]{0,1:T(8,128)(2,1)}, bf16[384,864]{0,1:T(8,128)(2,1)}, u32[]{:S(2)}, u32[]{:S(2)}) collective-permute-start(bf16[384,864]{0,1:T(8,128)(2,1)} %collective-permute-done.29), channel_id=1, source_target_pairs={{0,4},{4,8},{8,12},{12,0},{1,5},{5,9},{9,13},{13,1},{2,6},{6,10},{... | collective-permute-start | bytes 1990664 | tf_op jit(solution)/shard_map/ppermute | solution.py:74
  36.6 8.3 %copy-start.2 = (bf16[192,1024]{1,0:T(8,128)(2,1)S(1)}, bf16[192,1024]{1,0:T(8,128)(2,1)}, u32[]{:S(2)}) copy-start(bf16[192,1024]{1,0:T(8,128)(2,1)} %copy-done.1) | copy-start | bytes 1179652
  37.0 7.9 %collective-permute-start.3 = (bf16[192,512]{1,0:T(8,128)(2,1)S(1)}, bf16[192,512]{1,0:T(8,128)(2,1)S(1)}, u32[]{:S(2)}, u32[]{:S(2)}) collective-permute-start(bf16[192,512]{1,0:T(8,128)(2,1)S(1)} %convolution_convert_fusion.3), channel_id=1, source_target_pairs={{0,1},{1,0},{2,3},{3,2},{4,5},{5,4},{6,7},{7,6},{8,9},{9,8},{10,11... | collective-permute-start | bytes 589832 | tf_op jit(solution)/shard_map/ppermute | solution.py:69
  38.0 11.1 %collective-permute-start.6 = (bf16[192,512]{1,0:T(8,128)(2,1)S(1)}, bf16[192,512]{1,0:T(8,128)(2,1)S(1)}, u32[]{:S(2)}, u32[]{:S(2)}) collective-permute-start(bf16[192,512]{1,0:T(8,128)(2,1)S(1)} %convolution_convert_fusion.2), channel_id=1, source_target_pairs={{0,1},{1,0},{2,3},{3,2},{4,5},{5,4},{6,7},{7,6},{8,9},{9,8},{10,11... | collective-permute-start | bytes 589832 | tf_op jit(solution)/shard_map/ppermute | solution.py:69
  45.4 7.9 %collective-permute-start.7 = (bf16[192,512]{1,0:T(8,128)(2,1)S(1)}, bf16[192,512]{1,0:T(8,128)(2,1)S(1)}, u32[]{:S(2)}, u32[]{:S(2)}) collective-permute-start(bf16[192,512]{1,0:T(8,128)(2,1)S(1)} %multiply_convert_fusion.4), channel_id=1, source_target_pairs={{0,1},{1,0},{2,3},{3,2},{4,5},{5,4},{6,7},{7,6},{8,9},{9,8},{10,11... | collective-permute-start | bytes 589832 | tf_op jit(solution)/shard_map/ppermute | solution.py:69
  46.0 15.8 %collective-permute-start.11 = (bf16[192,512]{1,0:T(8,128)(2,1)S(1)}, bf16[192,512]{1,0:T(8,128)(2,1)}, u32[]{:S(2)}, u32[]{:S(2)}) collective-permute-start(bf16[192,512]{1,0:T(8,128)(2,1)S(1)} %multiply_convert_fusion.4), channel_id=1, source_target_pairs={{0,4},{4,8},{8,12},{12,0},{1,5},{5,9},{9,13},{13,1},{2,6},{6,10},{... | collective-permute-start | bytes 589832 | tf_op jit(solution)/shard_map/ppermute | solution.py:74
  49.6 6.6 %collective-permute-start.8 = (bf16[192,512]{1,0:T(8,128)(2,1)S(1)}, bf16[192,512]{1,0:T(8,128)(2,1)S(1)}, u32[]{:S(2)}, u32[]{:S(2)}) collective-permute-start(bf16[192,512]{1,0:T(8,128)(2,1)S(1)} %multiply_convert_fusion.3), channel_id=1, source_target_pairs={{0,1},{1,0},{2,3},{3,2},{4,5},{5,4},{6,7},{7,6},{8,9},{9,8},{10,11... | collective-permute-start | bytes 589832 | tf_op jit(solution)/shard_map/ppermute | solution.py:69
  50.2 15.1 %collective-permute-start.14 = (bf16[192,512]{1,0:T(8,128)(2,1)S(1)}, bf16[192,512]{1,0:T(8,128)(2,1)}, u32[]{:S(2)}, u32[]{:S(2)}) collective-permute-start(bf16[192,512]{1,0:T(8,128)(2,1)S(1)} %multiply_convert_fusion.3), channel_id=1, source_target_pairs={{0,4},{4,8},{8,12},{12,0},{1,5},{5,9},{9,13},{13,1},{2,6},{6,10},{... | collective-permute-start | bytes 589832 | tf_op jit(solution)/shard_map/ppermute | solution.py:74
  56.9 10.3 %collective-permute-start.10 = (bf16[192,512]{1,0:T(8,128)(2,1)}, bf16[192,512]{1,0:T(8,128)(2,1)}, u32[]{:S(2)}, u32[]{:S(2)}) collective-permute-start(bf16[192,512]{1,0:T(8,128)(2,1)} %get-tuple-element.7), channel_id=1, source_target_pairs={{0,2},{4,6},{10,8},{14,12},{1,3},{5,7},{11,9},{15,13},{16,18},{20,... | collective-permute-start | bytes 589832 | tf_op jit(solution)/shard_map/ppermute | solution.py:150
  58.9 56.0 %collective-permute-start.31 = (bf16[384,864]{0,1:T(8,128)(2,1)}, bf16[384,864]{0,1:T(8,128)(2,1)S(1)}, u32[]{:S(2)}, u32[]{:S(2)}) collective-permute-start(bf16[384,864]{0,1:T(8,128)(2,1)} %collective-permute-done.30), channel_id=1, source_target_pairs={{0,4},{4,8},{8,12},{12,0},{1,5},{5,9},{9,13},{13,1},{2,6},{6,10},{... | collective-permute-start | bytes 1990664 | tf_op jit(solution)/shard_map/ppermute | solution.py:74
  60.5 17.0 %collective-permute-start.9 = (bf16[192,512]{1,0:T(8,128)(2,1)S(1)}, bf16[192,512]{1,0:T(8,128)(2,1)S(1)}, u32[]{:S(2)}, u32[]{:S(2)}) collective-permute-start(bf16[192,512]{1,0:T(8,128)(2,1)S(1)} %get-tuple-element.5), channel_id=1, source_target_pairs={{0,2},{4,6},{10,8},{14,12},{1,3},{5,7},{11,9},{15,13},{16,18},{20,... | collective-permute-start | bytes 589832 | tf_op jit(solution)/shard_map/ppermute | solution.py:150
  61.8 11.6 %collective-permute-start.12 = (bf16[192,512]{1,0:T(8,128)(2,1)}, bf16[192,512]{1,0:T(8,128)(2,1)S(1)}, u32[]{:S(2)}, u32[]{:S(2)}) collective-permute-start(bf16[192,512]{1,0:T(8,128)(2,1)} %collective-permute-done.11), channel_id=1, source_target_pairs={{0,1},{5,4},{10,11},{15,14},{16,17},{21,20},{26,27},{31,30}} | collective-permute-start | bytes 589832 | tf_op jit(solution)/shard_map/ppermute | solution.py:148
  65.4 17.4 %collective-permute-start.17 = (bf16[192,512]{1,0:T(8,128)(2,1)}, bf16[192,512]{1,0:T(8,128)(2,1)S(1)}, u32[]{:S(2)}, u32[]{:S(2)}) collective-permute-start(bf16[192,512]{1,0:T(8,128)(2,1)} %collective-permute-done.11), channel_id=1, source_target_pairs={{0,4},{4,8},{8,12},{12,0},{1,5},{5,9},{9,13},{13,1},{2,6},{6,10},{... | collective-permute-start | bytes 589832 | tf_op jit(solution)/shard_map/ppermute | solution.py:74
  67.2 8.0 %collective-permute-start.15 = (bf16[192,512]{1,0:T(8,128)(2,1)}, bf16[192,512]{1,0:T(8,128)(2,1)S(1)}, u32[]{:S(2)}, u32[]{:S(2)}) collective-permute-start(bf16[192,512]{1,0:T(8,128)(2,1)} %collective-permute-done.14), channel_id=1, source_target_pairs={{0,1},{5,4},{10,11},{15,14},{16,17},{21,20},{26,27},{31,30}} | collective-permute-start | bytes 589832 | tf_op jit(solution)/shard_map/ppermute | solution.py:148
  73.4 13.6 %collective-permute-start.20 = (bf16[192,512]{1,0:T(8,128)(2,1)}, bf16[192,512]{1,0:T(8,128)(2,1)S(1)}, u32[]{:S(2)}, u32[]{:S(2)}) collective-permute-start(bf16[192,512]{1,0:T(8,128)(2,1)} %collective-permute-done.14), channel_id=1, source_target_pairs={{0,4},{4,8},{8,12},{12,0},{1,5},{5,9},{9,13},{13,1},{2,6},{6,10},{... | collective-permute-start | bytes 589832 | tf_op jit(solution)/shard_map/ppermute | solution.py:74
  75.2 11.8 %collective-permute-start.13 = (bf16[192,512]{1,0:T(8,128)(2,1)S(1)}, bf16[192,512]{1,0:T(8,128)(2,1)S(1)}, u32[]{:S(2)}, u32[]{:S(2)}) collective-permute-start(bf16[192,512]{1,0:T(8,128)(2,1)S(1)} %broadcast_select_fusion.5), channel_id=1, source_target_pairs={{0,2},{4,6},{10,8},{14,12},{1,3},{5,7},{11,9},{15,13},{16,18},{20,... | collective-permute-start | bytes 589832 | tf_op jit(solution)/shard_map/ppermute | solution.py:150
  77.5 16.5 %collective-permute-start.16 = (bf16[192,512]{1,0:T(8,128)(2,1)S(1)}, bf16[192,512]{1,0:T(8,128)(2,1)S(1)}, u32[]{:S(2)}, u32[]{:S(2)}) collective-permute-start(bf16[192,512]{1,0:T(8,128)(2,1)S(1)} %broadcast_select_fusion.4), channel_id=1, source_target_pairs={{0,2},{4,6},{10,8},{14,12},{1,3},{5,7},{11,9},{15,13},{16,18},{20,... | collective-permute-start | bytes 589832 | tf_op jit(solution)/shard_map/ppermute | solution.py:150
  82.8 6.7 %collective-permute-start.18 = (bf16[192,512]{1,0:T(8,128)(2,1)S(1)}, bf16[192,512]{1,0:T(8,128)(2,1)S(1)}, u32[]{:S(2)}, u32[]{:S(2)}) collective-permute-start(bf16[192,512]{1,0:T(8,128)(2,1)S(1)} %collective-permute-done.17), channel_id=1, source_target_pairs={{0,1},{5,4},{10,11},{15,14},{16,17},{21,20},{26,27},{31,30}} | collective-permute-start | bytes 589832 | tf_op jit(solution)/shard_map/ppermute | solution.py:148
  87.0 12.5 %collective-permute-start.23 = (bf16[192,512]{1,0:T(8,128)(2,1)S(1)}, bf16[192,512]{1,0:T(8,128)(2,1)S(1)}, u32[]{:S(2)}, u32[]{:S(2)}) collective-permute-start(bf16[192,512]{1,0:T(8,128)(2,1)S(1)} %collective-permute-done.17), channel_id=1, source_target_pairs={{0,4},{4,8},{8,12},{12,0},{1,5},{5,9},{9,13},{13,1},{2,6},{6,10},{... | collective-permute-start | bytes 589832 | tf_op jit(solution)/shard_map/ppermute | solution.py:74
  87.0 5.6 %collective-permute-start.21 = (bf16[192,512]{1,0:T(8,128)(2,1)S(1)}, bf16[192,512]{1,0:T(8,128)(2,1)S(1)}, u32[]{:S(2)}, u32[]{:S(2)}) collective-permute-start(bf16[192,512]{1,0:T(8,128)(2,1)S(1)} %collective-permute-done.20), channel_id=1, source_target_pairs={{0,1},{5,4},{10,11},{15,14},{16,17},{21,20},{26,27},{31,30}} | collective-permute-start | bytes 589832 | tf_op jit(solution)/shard_map/ppermute | solution.py:148
  89.5 15.7 %collective-permute-start.26 = (bf16[192,512]{1,0:T(8,128)(2,1)S(1)}, bf16[192,512]{1,0:T(8,128)(2,1)S(1)}, u32[]{:S(2)}, u32[]{:S(2)}) collective-permute-start(bf16[192,512]{1,0:T(8,128)(2,1)S(1)} %collective-permute-done.20), channel_id=1, source_target_pairs={{0,4},{4,8},{8,12},{12,0},{1,5},{5,9},{9,13},{13,1},{2,6},{6,10},{... | collective-permute-start | bytes 589832 | tf_op jit(solution)/shard_map/ppermute | solution.py:74
  92.6 20.1 %collective-permute-start.19 = (bf16[192,512]{1,0:T(8,128)(2,1)S(1)}, bf16[192,512]{1,0:T(8,128)(2,1)S(1)}, u32[]{:S(2)}, u32[]{:S(2)}) collective-permute-start(bf16[192,512]{1,0:T(8,128)(2,1)S(1)} %broadcast_select_fusion.3), channel_id=1, source_target_pairs={{0,2},{4,6},{10,8},{14,12},{1,3},{5,7},{11,9},{15,13},{16,18},{20,... | collective-permute-start | bytes 589832 | tf_op jit(solution)/shard_map/ppermute | solution.py:150
  94.0 17.1 %collective-permute-start.22 = (bf16[192,512]{1,0:T(8,128)(2,1)S(1)}, bf16[192,512]{1,0:T(8,128)(2,1)S(1)}, u32[]{:S(2)}, u32[]{:S(2)}) collective-permute-start(bf16[192,512]{1,0:T(8,128)(2,1)S(1)} %broadcast_select_fusion.2), channel_id=1, source_target_pairs={{0,2},{4,6},{10,8},{14,12},{1,3},{5,7},{11,9},{15,13},{16,18},{20,... | collective-permute-start | bytes 589832 | tf_op jit(solution)/shard_map/ppermute | solution.py:150
  99.5 7.6 %collective-permute-start.24 = (bf16[192,512]{1,0:T(8,128)(2,1)S(1)}, bf16[192,512]{1,0:T(8,128)(2,1)S(1)}, u32[]{:S(2)}, u32[]{:S(2)}) collective-permute-start(bf16[192,512]{1,0:T(8,128)(2,1)S(1)} %collective-permute-done.23), channel_id=1, source_target_pairs={{0,1},{5,4},{10,11},{15,14},{16,17},{21,20},{26,27},{31,30}} | collective-permute-start | bytes 589832 | tf_op jit(solution)/shard_map/ppermute | solution.py:148
  105.2 4.5 %collective-permute-start.27 = (bf16[192,512]{1,0:T(8,128)(2,1)S(1)}, bf16[192,512]{1,0:T(8,128)(2,1)S(1)}, u32[]{:S(2)}, u32[]{:S(2)}) collective-permute-start(bf16[192,512]{1,0:T(8,128)(2,1)S(1)} %collective-permute-done.26), channel_id=1, source_target_pairs={{0,1},{5,4},{10,11},{15,14},{16,17},{21,20},{26,27},{31,30}} | collective-permute-start | bytes 589832 | tf_op jit(solution)/shard_map/ppermute | solution.py:148
  107.1 7.4 %collective-permute-start.25 = (bf16[192,512]{1,0:T(8,128)(2,1)S(1)}, bf16[192,512]{1,0:T(8,128)(2,1)S(1)}, u32[]{:S(2)}, u32[]{:S(2)}) collective-permute-start(bf16[192,512]{1,0:T(8,128)(2,1)S(1)} %broadcast_select_fusion.1), channel_id=1, source_target_pairs={{0,2},{4,6},{10,8},{14,12},{1,3},{5,7},{11,9},{15,13},{16,18},{20,... | collective-permute-start | bytes 589832 | tf_op jit(solution)/shard_map/ppermute | solution.py:150
  109.7 4.8 %collective-permute-start.28 = (bf16[192,512]{1,0:T(8,128)(2,1)S(1)}, bf16[192,512]{1,0:T(8,128)(2,1)S(1)}, u32[]{:S(2)}, u32[]{:S(2)}) collective-permute-start(bf16[192,512]{1,0:T(8,128)(2,1)S(1)} %broadcast_select_fusion), channel_id=1, source_target_pairs={{0,2},{4,6},{10,8},{14,12},{1,3},{5,7},{11,9},{15,13},{16,18},{20,... | collective-permute-start | bytes 589832 | tf_op jit(solution)/shard_map/ppermute | solution.py:150

commit v2 on v0

--- a/solution.py
+++ b/solution.py
@@ -8,13 +8,14 @@
 
 
 step_rate = 0.2
+CHUNKS = 2
 
 
 def soften(value, level):
     return jnp.sign(value) * jnp.maximum(jnp.abs(value) - level, 0.0)
 
 
-def on_device(patches, dictionary, threshold):
+def general(patches, dictionary, threshold):
     values = patches.astype(jnp.float32)
     local_sq = jnp.sum(values * values, axis=1)
     local_first = jnp.dot(patches, dictionary, preferred_element_type=jnp.float32)
@@ -64,6 +65,112 @@
     return (codes, gram, cross)
 
 
+def swap(value, axis):
+    return lax.ppermute(value, axis, [(0, 1), (1, 0)])
+
+
+def shift(value):
+    n = lax.axis_size("patch")
+    return lax.ppermute(value, "patch", [(i, (i + 1) % n) for i in range(n)])
+
+
+def after(value, earlier):
+    return lax.optimization_barrier((value, earlier))[0]
+
+
+def paired(patches, dictionary, threshold):
+    n_patch = lax.axis_size("patch")
+    plane = lax.axis_index("patch")
+    core = lax.axis_index("atom")
+    half = lax.axis_index("feat")
+    count = patches.shape[0] * n_patch
+    rows = patches.shape[0] // 2
+    block = dictionary.shape[1] // 2
+    step = rows // CHUNKS
+    f32, bf16 = jnp.float32, jnp.bfloat16
+    last = (((1,), (1,)), ((), ()))
+    first = (((0,), (0,)), ((), ()))
+
+    def blocks(array, which):
+        return lax.dynamic_slice_in_dim(array, which * block, block, 1)
+
+    dictionary2 = swap(dictionary, "atom")
+    level = step_rate * threshold[None, :]
+    level2 = swap(level, "atom")
+    mine = lax.dynamic_slice_in_dim(patches, core * rows, rows, 0)
+    part = jnp.dot(mine, dictionary, preferred_element_type=f32).astype(bf16)
+    other = swap(part, "feat")
+    values = mine.astype(f32)
+    local_sq = jnp.sum(values * values, axis=1)
+    energy = local_sq + swap(local_sq, "feat")
+    scale = lax.rsqrt(energy[:, None] / (BINS * VOXELS) + 1e-05)
+    normed = (scale * values).astype(bf16)
+    part2, other2 = [], []
+    for c in range(CHUNKS):
+        window = slice(c * step, (c + 1) * step)
+        part2.append(jnp.dot(mine[window], dictionary2, preferred_element_type=f32).astype(bf16))
+        other2.append(swap(part2[c], "feat"))
+    start = soften(step_rate * (scale * (part.astype(f32) + other.astype(f32))), level).astype(bf16)
+    built = lax.dot_general(start, dictionary, last, preferred_element_type=f32)
+    normed_of = [normed]
+    for k in range(1, n_patch):
+        normed_of.append(shift(normed_of[-1]))
+
+    codes_of = []
+    done = built
+    for c in range(CHUNKS):
+        window = slice(c * step, (c + 1) * step)
+        arrived = after(other2[c], done).astype(f32)
+        start2 = soften(step_rate * (scale[window] * (part2[c].astype(f32) + arrived)), level2).astype(bf16)
+        rebuilt = built[window] + lax.dot_general(start2, dictionary2, last, preferred_element_type=f32)
+        misfit = (scale[window] * values[window] - rebuilt).astype(bf16)
+        away = jnp.concatenate(
+            [
+                jnp.dot(misfit, blocks(d, 1 - half), preferred_element_type=f32).astype(bf16)
+                for d in (dictionary, dictionary2)
+            ],
+            1,
+        )
+        done = away
+        back = swap(away, "feat").astype(f32)
+        pieces = []
+        for i, (d, s, t) in enumerate(((dictionary, start[window], level), (dictionary2, start2, level2))):
+            second = jnp.dot(misfit, blocks(d, half), preferred_element_type=f32)
+            second += back[:, i * block : (i + 1) * block]
+            pieces.append(soften(blocks(s, half).astype(f32) + step_rate * second, blocks(t, half)).astype(bf16))
+        codes_of.append(jnp.concatenate(pieces, 1))
+
+    left = [codes_of]
+    for k in range(1, n_patch):
+        left.append([shift(x) for x in left[-1]])
+    left = [jnp.concatenate(x, 0) for x in left]
+    inside = left[0]
+    outside = swap(inside, "feat")
+    both = [jnp.where(half == 0, inside, outside), jnp.where(half == 0, outside, inside)]
+    upper = jnp.concatenate([x[:, :block] for x in both], 1)
+    lower = swap(jnp.concatenate([x[:, block:] for x in both], 1), "atom")
+    codes = jnp.where(
+        core == 0, jnp.concatenate([upper, lower], 0), jnp.concatenate([lower, upper], 0)
+    )
+    home_core = plane // 2
+    home_half = plane % 2
+    place = jnp.where(core == home_core, 0, 1)
+    over = [(q * 2 + q % 2, q * 2 + 1 - q % 2) for q in range(n_patch)]
+    products = 0.0
+    for k in range(n_patch):
+        here = blocks(left[k], place)
+        there = blocks(outside, place) if k == 0 else lax.ppermute(here, ("patch", "feat"), over)
+        right = jnp.where(half == home_half, here, there)
+        sides = jnp.concatenate([left[k], normed_of[k]], 1)
+        products += lax.dot_general(sides, right, first, preferred_element_type=f32)
+    width = block // 2
+    gram = products[:block] + swap(products[block : 2 * block], "atom")
+    cross = lax.dynamic_slice_in_dim(products[2 * block :], core * width, width, 1) + swap(
+        lax.dynamic_slice_in_dim(products[2 * block :], (1 - core) * width, width, 1), "atom"
+    )
+    return (codes, gram / count, cross / count)
+
+
 def solution(mesh):
     in_specs = (P(("slab", "patch"), "feat"), P("feat", "atom"), P("atom"))
     out_specs = (
@@ -71,6 +178,8 @@
         P(("slab", "atom", "feat"), "patch"),
         P(("slab", "feat"), ("patch", "atom")),
     )
+    sizes = mesh.shape
+    small = sizes["feat"] == 2 and sizes["atom"] == 2 and sizes["patch"] == 4
     return jax.shard_map(
-        on_device, mesh=mesh, in_specs=in_specs, out_specs=out_specs, check_vma=False
+        paired if small else general, mesh=mesh, in_specs=in_specs, out_specs=out_specs, check_vma=False
     )

time: 268 us -> 109 us (0.41)
  waiting for transfers between devices: 209 us -> 53.6 us
  starting transfers between devices: 0.25 us -> 24 us
  between operations: 14.1 us -> 1.08 us
  local copies, waits for them, and re-layouts: 13.4 us -> 5.3 us
  blocking collectives: 5.83 us -> 0 us
  matrix products: 17 us -> 13.5 us
  other arithmetic: 8.07 us -> 10.8 us
    psum x3 -> x0, waiting for transfers between devices: 120 us -> none  [the longest x1 52.8 us: on_device(): second = lax.psum(local_second, 'feat')]
    reduce_scatter x2 -> x0, waiting for transfers between devices: 78.8 us -> none  [the longest x1 43.1 us: on_device(): lax.psum_scatter(gram_part.astype(jnp.bfloat16), 'patch', scatter_dimensi...]
    ppermute x0 -> x24, waiting for transfers between devices: none -> 53.6 us  [the longest x9 33.1 us: shift(): return lax.ppermute(value, 'patch', [(i, (i + 1) % n) for i in range(n)])]
    ppermute x0 -> x24, starting transfers between devices: none -> 24 us  [the longest x12 10.5 us: swap(): return lax.ppermute(value, axis, [(0, 1), (1, 0)])]
    all_gather x1 -> x0, waiting for transfers between devices: 9.91 us -> none  [on_device(): codes_whole = lax.all_gather(codes, 'atom', axis=1, tiled=True)]
    psum x1 -> x0, blocking collectives: 5.83 us -> none  [on_device(): summed, energy = lax.psum((local_first, local_sq), 'feat')]
    unnamed x11 -> x17, local copies, waits for them, and re-layouts: 6.51 us -> 1.93 us
    reshape x1 -> x0, local copies, waits for them, and re-layouts: 3.84 us -> none  [on_device(): arranged = codes_whole.reshape(codes_whole.shape[0], n_patch, n_atom, width)]
  transfers between devices with their start and end apart: 6 -> 24, of which waited for: 6 -> 14; matrix products, arithmetic and copies ran while one was open for 2% -> 21% of each run, Pallas kernels for 0% -> 0%
where the time goes in v2:
time: 109 us; the launch traced here: 108 us
  waiting for transfers between devices  53.6 us (49%)
  starting transfers between devices  24 us (22%)
  matrix products  13.5 us (12%)
  other arithmetic  10.8 us (10%)
  local copies, waits for them, and re-layouts  5.3 us (5%)
    ppermute x9, waiting for transfers between devices, shift(): return lax.ppermute(value, 'patch', [(i, (i + 1) % n) for i in range(n)])  33.1 us
    ppermute x12, waiting for transfers between devices, swap(): return lax.ppermute(value, axis, [(0, 1), (1, 0)])  19.3 us
    ppermute x12, starting transfers between devices, swap(): return lax.ppermute(value, axis, [(0, 1), (1, 0)])  10.5 us
    ppermute x3, starting transfers between devices, paired(): lax.ppermute(here, ('patch', 'feat'), over)  7.85 us
    ppermute x9, starting transfers between devices, shift(): return lax.ppermute(value, 'patch', [(i, (i + 1) % n) for i in range(n)])  5.66 us
    dot_general x4, matrix products, paired(): products += lax.dot_general(sides, right, first, preferred_element_type=f32)  4.83 us
    div x2, other arithmetic, paired(): return (codes, gram / count, cross / count)  4.74 us
    dot_general x1, matrix products, paired(): part = jnp.dot(mine, dictionary, preferred_element_type=f32).astype(bf16)  2.85 us
  transfers between devices with their start and end apart: 24, of which 14 were waited for; matrix products, arithmetic and copies ran while one was open for 21% of the time, Pallas kernels for 0%

profile of v2, /device:TPU:0, one launch (start us, length us, event | category | flops | bytes accessed | tf_op | source)
XLA Modules:
  0.0 108.3 jit_solution(16088931736635581386)
XLA Ops:
  0.6 0.5 collective-permute-start.2
  1.2 0.6 copy-done
  1.7 0.2 constant_dynamic-slice_fusion.5
  1.9 2.9 %convolution_convert_fusion = bf16[192,1024]{1,0:T(8,128)(2,1)} fusion(bf16[192,864]{0,1:T(8,128)(2,1)S(1)} %constant_dynamic-slice_fusion.5, bf16[864,1024]{1,0:T(8,128)(2,1)} %param.4), kind=kOutput, calls=%fused_computation.1 | convolution fusion | flops 339935232 | bytes 2494464 | tf_op jit(solution)/shard_map/dot_general | solution.py:101
  4.8 2.9 %collective-permute-start.1 = (bf16[192,1024]{1,0:T(8,128)(2,1)}, bf16[192,1024]{1,0:T(8,128)(2,1)}, u32[]{:S(2)}, u32[]{:S(2)}) collective-permute-start(bf16[192,1024]{1,0:T(8,128)(2,1)} %convolution_convert_fusion), channel_id=1, source_target_pairs={{0,1},{1,0},{2,3},{3,2},{4,5},{5,4},{6,7},{7,6},{8,9},{9,8},{10,11... | collective-permute-start | bytes 1179656 | tf_op jit(solution)/shard_map/ppermute | solution.py:69
  7.7 0.2 copy.7
  7.9 0.2 multiply_reduce_fusion
  8.4 8.8 %collective-permute-done = f32[192]{0:T(256)S(1)} collective-permute-done((f32[192]{0:T(256)S(1)}, f32[192]{0:T(256)S(1)}, u32[]{:S(2)}, u32[]{:S(2)}) %collective-permute-start) | collective-permute-done | bytes 800 | tf_op jit(solution)/shard_map/ppermute | solution.py:69
  17.3 1.9 %collective-permute-start.12 = (bf16[192,864]{1,0:T(8,128)(2,1)S(1)}, bf16[192,864]{1,0:T(8,128)(2,1)}, u32[]{:S(2)}, u32[]{:S(2)}) collective-permute-start(bf16[192,864]{1,0:T(8,128)(2,1)S(1)} %multiply_convert_fusion.1), channel_id=1, source_target_pairs={{0,4},{4,8},{8,12},{12,0},{1,5},{5,9},{9,13},{13,1},{2,6},{6,10},{... | collective-permute-start | bytes 995336 | tf_op jit(solution)/shard_map/ppermute | solution.py:74
  19.3 9.3 %collective-permute-done.12 = bf16[192,864]{1,0:T(8,128)(2,1)} collective-permute-done((bf16[192,864]{1,0:T(8,128)(2,1)S(1)}, bf16[192,864]{1,0:T(8,128)(2,1)}, u32[]{:S(2)}, u32[]{:S(2)}) %collective-permute-start.12) | collective-permute-done | bytes 331808 | tf_op jit(solution)/shard_map/ppermute | solution.py:74
  28.5 1.6 %multiply_convert_fusion = bf16[192,1024]{1,0:T(8,128)(2,1)S(1)} fusion(bf16[192,1024]{1,0:T(8,128)(2,1)} %collective-permute-done.1, bf16[192,1024]{1,0:T(8,128)(2,1)} %convolution_convert_fusion, f32[1024]{0:T(1024)S(1)} %broadcast_multiply_fusion, f32[192]{0:T(256)S(1)} %add_rsqrt_fusion), kind=kLoop, calls=%fused_computation.24 | loop fusion | flops 2162688 | bytes 1184512 | tf_op jit(solution)/shard_map/convert_element_type | solution.py:113
  30.2 0.8 fusion.84
  31.0 0.4 convolution_convert_fusion.2
  31.4 1.6 %collective-permute-start.3 = (bf16[96,1024]{1,0:T(8,128)(2,1)S(1)}, bf16[96,1024]{1,0:T(8,128)(2,1)S(1)}, u32[]{:S(2)}, u32[]{:S(2)}) collective-permute-start(bf16[96,1024]{1,0:T(8,128)(2,1)S(1)} %convolution_convert_fusion.2), channel_id=1, source_target_pairs={{0,1},{1,0},{2,3},{3,2},{4,5},{5,4},{6,7},{7,6},{8,9},{9,8},{10,11... | collective-permute-start | bytes 589832 | tf_op jit(solution)/shard_map/ppermute | solution.py:69
  33.0 0.4 convolution_convert_fusion.1
  33.4 0.6 collective-permute-start.6
  34.0 4.7 %collective-permute-done.3 = bf16[96,1024]{1,0:T(8,128)(2,1)S(1)} collective-permute-done((bf16[96,1024]{1,0:T(8,128)(2,1)S(1)}, bf16[96,1024]{1,0:T(8,128)(2,1)S(1)}, u32[]{:S(2)}, u32[]{:S(2)}) %collective-permute-start.3) | collective-permute-done | bytes 196640 | tf_op jit(solution)/shard_map/ppermute | solution.py:69
  38.7 0.3 multiply_convert_fusion.3
  39.0 0.7 fusion.2
  39.7 0.3 convolution_convert_fusion.6
  40.0 0.3 convolution_convert_fusion.5
  40.4 1.3 %collective-permute-start.5 = (bf16[96,1024]{1,0:T(8,128)(2,1)S(1)}, bf16[96,1024]{1,0:T(8,128)(2,1)S(1)}, u32[]{:S(2)}, u32[]{:S(2)}) collective-permute-start(bf16[96,1024]{1,0:T(8,128)(2,1)S(1)} %pad_maximum_fusion.1), channel_id=1, source_target_pairs={{0,1},{1,0},{2,3},{3,2},{4,5},{5,4},{6,7},{7,6},{8,9},{9,8},{10,11... | collective-permute-start | bytes 589832 | tf_op jit(solution)/shard_map/ppermute | solution.py:69
  41.7 0.9 collective-permute-done.6
  42.6 0.3 multiply_convert_fusion.2
  42.9 0.7 fusion.3
  43.6 0.3 convolution_convert_fusion.4
  43.9 0.3 convolution_convert_fusion.3
  44.2 1.3 %collective-permute-start.7 = (bf16[96,1024]{1,0:T(8,128)(2,1)S(1)}, bf16[96,1024]{1,0:T(8,128)(2,1)S(1)}, u32[]{:S(2)}, u32[]{:S(2)}) collective-permute-start(bf16[96,1024]{1,0:T(8,128)(2,1)S(1)} %pad_maximum_fusion.3), channel_id=1, source_target_pairs={{0,1},{1,0},{2,3},{3,2},{4,5},{5,4},{6,7},{7,6},{8,9},{9,8},{10,11... | collective-permute-start | bytes 589832 | tf_op jit(solution)/shard_map/ppermute | solution.py:69
  45.6 1.6 %collective-permute-done.5 = bf16[96,1024]{1,0:T(8,128)(2,1)S(1)} collective-permute-done((bf16[96,1024]{1,0:T(8,128)(2,1)S(1)}, bf16[96,1024]{1,0:T(8,128)(2,1)S(1)}, u32[]{:S(2)}, u32[]{:S(2)}) %collective-permute-start.5) | collective-permute-done | bytes 196640 | tf_op jit(solution)/shard_map/ppermute | solution.py:69
  47.2 0.4 multiply_convert_fusion.7
  47.6 0.4 multiply_convert_fusion.6
  48.0 0.8 collective-permute-start.10
  48.8 1.2 %collective-permute-done.7 = bf16[96,1024]{1,0:T(8,128)(2,1)S(1)} collective-permute-done((bf16[96,1024]{1,0:T(8,128)(2,1)S(1)}, bf16[96,1024]{1,0:T(8,128)(2,1)S(1)}, u32[]{:S(2)}, u32[]{:S(2)}) %collective-permute-start.7) | collective-permute-done | bytes 196640 | tf_op jit(solution)/shard_map/ppermute | solution.py:69
  50.0 0.4 multiply_convert_fusion.5
  50.4 0.4 multiply_convert_fusion.4
  50.8 0.8 collective-permute-start.11
  51.6 1.6 %collective-permute-start.8 = (bf16[192,1024]{1,0:T(8,128)(2,1)S(1)}, bf16[192,1024]{1,0:T(8,128)(2,1)S(1)}, u32[]{:S(2)}, u32[]{:S(2)}) collective-permute-start(bf16[192,1024]{1,0:T(8,128)(2,1)S(1)} %maximum_maximum_fusion), channel_id=1, source_target_pairs={{0,1},{1,0},{2,3},{3,2},{4,5},{5,4},{6,7},{7,6},{8,9},{9,8},{10,11... | collective-permute-start | bytes 1179656 | tf_op jit(solution)/shard_map/ppermute | solution.py:69
  53.2 1.8 %collective-permute-start.20 = (bf16[192,864]{1,0:T(8,128)(2,1)}, bf16[192,864]{1,0:T(8,128)(2,1)S(1)}, u32[]{:S(2)}, u32[]{:S(2)}) collective-permute-start(bf16[192,864]{1,0:T(8,128)(2,1)} %collective-permute-done.16), channel_id=1, source_target_pairs={{0,4},{4,8},{8,12},{12,0},{1,5},{5,9},{9,13},{13,1},{2,6},{6,10},{... | collective-permute-start | bytes 995336 | tf_op jit(solution)/shard_map/ppermute | solution.py:74
  55.0 2.7 %collective-permute-done.10 = bf16[96,1024]{1,0:T(8,128)(2,1)S(1)} collective-permute-done((bf16[96,1024]{1,0:T(8,128)(2,1)S(1)}, bf16[96,1024]{1,0:T(8,128)(2,1)S(1)}, u32[]{:S(2)}, u32[]{:S(2)}) %collective-permute-start.10) | collective-permute-done | bytes 196640 | tf_op jit(solution)/shard_map/ppermute | solution.py:74
  57.7 4.0 %collective-permute-done.11 = bf16[96,1024]{1,0:T(8,128)(2,1)S(1)} collective-permute-done((bf16[96,1024]{1,0:T(8,128)(2,1)S(1)}, bf16[96,1024]{1,0:T(8,128)(2,1)S(1)}, u32[]{:S(2)}, u32[]{:S(2)}) %collective-permute-start.11) | collective-permute-done | bytes 196640 | tf_op jit(solution)/shard_map/ppermute | solution.py:74
  61.8 3.4 %collective-permute-start.13 = (bf16[192,512]{1,0:T(8,128)(2,1)S(1)}, bf16[192,512]{1,0:T(8,128)(2,1)S(1)}, u32[]{:S(2)}, u32[]{:S(2)}) collective-permute-start(bf16[192,512]{1,0:T(8,128)(2,1)S(1)} %constant_dynamic-slice_fusion.3), channel_id=1, source_target_pairs={{0,1},{5,4},{8,9},{13,12},{2,3},{7,6},{10,11},{15,14},{16,17},{21,... | collective-permute-start | bytes 589832 | tf_op jit(solution)/shard_map/ppermute | solution.py:162
  65.2 0.4 collective-permute-start.15
  65.6 0.2 broadcast_select_fusion.1
  65.8 0.7 fusion.19
  66.5 8.2 %collective-permute-done.14 = bf16[96,1024]{1,0:T(8,128)(2,1)S(1)} collective-permute-done((bf16[96,1024]{1,0:T(8,128)(2,1)S(1)}, bf16[96,1024]{1,0:T(8,128)(2,1)S(1)}, u32[]{:S(2)}, u32[]{:S(2)}) %collective-permute-start.14) | collective-permute-done | bytes 196640 | tf_op jit(solution)/shard_map/ppermute | solution.py:74
  74.7 3.7 %collective-permute-done.15 = bf16[96,1024]{1,0:T(8,128)(2,1)S(1)} collective-permute-done((bf16[96,1024]{1,0:T(8,128)(2,1)S(1)}, bf16[96,1024]{1,0:T(8,128)(2,1)S(1)}, u32[]{:S(2)}, u32[]{:S(2)}) %collective-permute-start.15) | collective-permute-done | bytes 196640 | tf_op jit(solution)/shard_map/ppermute | solution.py:74
  78.4 2.2 %collective-permute-start.17 = (bf16[192,512]{1,0:T(8,128)(2,1)S(1)}, bf16[192,512]{1,0:T(8,128)(2,1)S(1)}, u32[]{:S(2)}, u32[]{:S(2)}) collective-permute-start(bf16[192,512]{1,0:T(8,128)(2,1)S(1)} %constant_dynamic-slice_fusion.2), channel_id=1, source_target_pairs={{0,1},{5,4},{8,9},{13,12},{2,3},{7,6},{10,11},{15,14},{16,17},{21,... | collective-permute-start | bytes 589832 | tf_op jit(solution)/shard_map/ppermute | solution.py:162
  80.6 1.5 %collective-permute-done.18 = bf16[96,1024]{1,0:T(8,128)(2,1)S(1)} collective-permute-done((bf16[96,1024]{1,0:T(8,128)(2,1)S(1)}, bf16[96,1024]{1,0:T(8,128)(2,1)S(1)}, u32[]{:S(2)}, u32[]{:S(2)}) %collective-permute-start.18) | collective-permute-done | bytes 196640 | tf_op jit(solution)/shard_map/ppermute | solution.py:74
  82.2 3.7 %collective-permute-done.19 = bf16[96,1024]{1,0:T(8,128)(2,1)S(1)} collective-permute-done((bf16[96,1024]{1,0:T(8,128)(2,1)S(1)}, bf16[96,1024]{1,0:T(8,128)(2,1)S(1)}, u32[]{:S(2)}, u32[]{:S(2)}) %collective-permute-start.19) | collective-permute-done | bytes 196640 | tf_op jit(solution)/shard_map/ppermute | solution.py:74
  85.9 2.3 %collective-permute-start.21 = (bf16[192,512]{1,0:T(8,128)(2,1)S(1)}, bf16[192,512]{1,0:T(8,128)(2,1)S(1)}, u32[]{:S(2)}, u32[]{:S(2)}) collective-permute-start(bf16[192,512]{1,0:T(8,128)(2,1)S(1)} %constant_dynamic-slice_fusion.1), channel_id=1, source_target_pairs={{0,1},{5,4},{8,9},{13,12},{2,3},{7,6},{10,11},{15,14},{16,17},{21,... | collective-permute-start | bytes 589832 | tf_op jit(solution)/shard_map/ppermute | solution.py:162
  88.3 1.7 %fusion.29 = f32[1888,512]{1,0:T(8,128)S(1)} fusion(bf16[192,864]{1,0:T(8,128)(2,1)} %collective-permute-done.12, bf16[192,1024]{1,0:T(8,128)(2,1)S(1)} %constant_dynamic-update-slice_fusion, bf16[192,512]{1,0:T(8,128)(2,1)S(1)} %constant_dynamic-slice_fusion.3, bf16[192,512]{1,0:T(8,128)(2,1)S(1)} %collective-permute-done.13, pred[]{:T(512)S(6)} %eq.20), kind=kOutput, calls=%fused_computation.45 | convolution fusion | flops 372744192 | bytes 4984833 | tf_op jit(solution)/shard_map/dot_general | solution.py:165
  90.0 1.3 %collective-permute-done.21 = bf16[192,512]{1,0:T(8,128)(2,1)S(1)} collective-permute-done((bf16[192,512]{1,0:T(8,128)(2,1)S(1)}, bf16[192,512]{1,0:T(8,128)(2,1)S(1)}, u32[]{:S(2)}, u32[]{:S(2)}) %collective-permute-start.21) | collective-permute-done | bytes 196640 | tf_op jit(solution)/shard_map/ppermute | solution.py:162
  91.2 0.7 fusion.39
  91.9 1.7 %add_add_fusion = f32[1888,512]{1,0:T(8,128)S(1)} fusion(f32[1888,512]{1,0:T(8,128)S(1)} %fusion.39, f32[1888,512]{1,0:T(8,128)S(1)} %fusion.19, f32[1888,512]{1,0:T(8,128)S(1)} %fusion.29, bf16[192,864]{1,0:T(8,128)(2,1)} %collective-permute-done.16, bf16[192,1024]{1,0:T(8,128)(2,1)S(1)} %constant_dynamic-update-slice_fusion.2, ...), kind=kOutput, calls=%fused_computation | convolution fusion | flops 375644160 | bytes 16584705 | tf_op jit(solution)/shard_map/dot_general | solution.py:165
  93.7 1.1 %slice.106 = f32[512,512]{1,0:T(8,128)} slice(f32[1888,512]{1,0:T(8,128)S(1)} %add_add_fusion), slice={[512:1024], [0:512]} | slice | bytes 2097152 | tf_op jit(solution)/shard_map/slice | solution.py:167
  95.0 0.9 copy-done.2
  95.9 1.0 constant_dynamic-slice_fusion
  96.9 0.5 collective-permute-start.23
  97.4 0.8 fusion.80
  98.2 0.8 pad_maximum_fusion
  99.0 2.1 %collective-permute-done.9 = bf16[192,1024]{1,0:T(8,128)(2,1)} collective-permute-done((bf16[192,1024]{1,0:T(8,128)(2,1)}, bf16[192,1024]{1,0:T(8,128)(2,1)}, u32[]{:S(2)}, u32[]{:S(2)}) %collective-permute-start.9) | collective-permute-done | bytes 393248 | tf_op jit(solution)/shard_map/ppermute | solution.py:69
  101.1 2.5 %maximum_select_fusion = bf16[384,1024]{1,0:T(8,128)(2,1)} fusion(bf16[192,1024]{1,0:T(8,128)(2,1)} %collective-permute-done.9, bf16[192,512]{1,0:T(8,128)(2,1)} %get-tuple-element.18, bf16[192,512]{1,0:T(8,128)(2,1)} %get-tuple-element.9, pred[]{:T(512)S(6)} %eq.18), kind=kLoop, calls=%fused_computation.23 | loop fusion | flops 5111808 | bytes 1572865 | tf_op jit(solution)/shard_map/jit(_where)/select_n | solution.py:152
  103.6 2.3 %add_multiply_fusion = f32[864,256]{1,0:T(8,128)} fusion(f32[864,256]{1,0:T(8,128)} %collective-permute-done.23, f32[864,512]{1,0:T(8,128)S(1)} %slice.107, s32[]{:T(128)S(6)} %select_n.108), kind=kLoop, calls=%fused_computation.22 | loop fusion | flops 442368 | bytes 2654212 | tf_op jit(solution)/shard_map/div | solution.py:171
  105.9 2.4 %fusion.8 = f32[512,512]{1,0:T(8,128)} fusion(f32[512,512]{1,0:T(8,128)S(1)} %collective-permute-done.22, f32[1888,512]{1,0:T(8,128)} %copy-done.2), kind=kLoop, calls=%fused_computation.21 | loop fusion | flops 524288 | bytes 3145728 | tf_op jit(solution)/shard_map/div | solution.py:171
  (53 shorter events, 1.1 us)
Async XLA Ops:
  0.6 1.1 %copy-start = (bf16[384,864]{0,1:T(8,128)(2,1)S(1)}, bf16[384,864]{0,1:T(8,128)(2,1)}, u32[]{:S(2)}) copy-start(bf16[384,864]{0,1:T(8,128)(2,1)} %param.3) | copy-start | bytes 1990660
  0.6 30.3 %collective-permute-start.2 = (bf16[864,1024]{1,0:T(8,128)(2,1)}, bf16[864,1024]{1,0:T(8,128)(2,1)S(1)}, u32[]{:S(2)}, u32[]{:S(2)}) collective-permute-start(bf16[864,1024]{1,0:T(8,128)(2,1)} %param.4), channel_id=1, source_target_pairs={{0,2},{2,0},{1,3},{3,1},{4,6},{6,4},{5,7},{7,5},{8,10},{10,8},{9,1... | collective-permute-start | bytes 5308424 | tf_op jit(solution)/shard_map/ppermute | solution.py:69
  1.9 6.2 %copy-start.5 = (f32[1024]{0:T(1024)S(1)}, f32[1024]{0:T(1024)}, u32[]{:S(2)}) copy-start(f32[1024]{0:T(1024)} %param.5) | copy-start | bytes 12292
  4.8 23.8 %collective-permute-start.1 = (bf16[192,1024]{1,0:T(8,128)(2,1)}, bf16[192,1024]{1,0:T(8,128)(2,1)}, u32[]{:S(2)}, u32[]{:S(2)}) collective-permute-start(bf16[192,1024]{1,0:T(8,128)(2,1)} %convolution_convert_fusion), channel_id=1, source_target_pairs={{0,1},{1,0},{2,3},{3,2},{4,5},{5,4},{6,7},{7,6},{8,9},{9,8},{10,11... | collective-permute-start | bytes 1179656 | tf_op jit(solution)/shard_map/ppermute | solution.py:69
  8.1 9.1 %collective-permute-start = (f32[192]{0:T(256)S(1)}, f32[192]{0:T(256)S(1)}, u32[]{:S(2)}, u32[]{:S(2)}) collective-permute-start(f32[192]{0:T(256)S(1)} %multiply_reduce_fusion), channel_id=1, source_target_pairs={{0,1},{1,0},{2,3},{3,2},{4,5},{5,4},{6,7},{7,6},{8,9},{9,8},{10,11... | collective-permute-start | bytes 2312 | tf_op jit(solution)/shard_map/ppermute | solution.py:69
  8.2 11.1 %collective-permute-start.4 = (f32[1,1024]{1,0:T(1,128)S(1)}, f32[1,1024]{1,0:T(1,128)S(1)}, u32[]{:S(2)}, u32[]{:S(2)}) collective-permute-start(f32[1,1024]{1,0:T(1,128)S(1)} %bitcast.23), channel_id=1, source_target_pairs={{0,2},{2,0},{1,3},{3,1},{4,6},{6,4},{5,7},{7,5},{8,10},{10,8},{9,1... | collective-permute-start | bytes 12296 | tf_op jit(solution)/shard_map/ppermute | solution.py:69
  8.4 21.8 %copy-start.1 = (bf16[864,1024]{1,0:T(8,128)(2,1)S(1)}, bf16[864,1024]{1,0:T(8,128)(2,1)}, u32[]{:S(2)}) copy-start(bf16[864,1024]{1,0:T(8,128)(2,1)} %param.4) | copy-start | bytes 5308420
  17.3 11.2 %copy-start.3 = (bf16[192,864]{1,0:T(8,128)(2,1)}, bf16[192,864]{1,0:T(8,128)(2,1)S(1)}, u32[]{:S(2)}) copy-start(bf16[192,864]{1,0:T(8,128)(2,1)S(1)} %multiply_convert_fusion.1) | copy-start | bytes 995332
  17.3 11.2 %collective-permute-start.12 = (bf16[192,864]{1,0:T(8,128)(2,1)S(1)}, bf16[192,864]{1,0:T(8,128)(2,1)}, u32[]{:S(2)}, u32[]{:S(2)}) collective-permute-start(bf16[192,864]{1,0:T(8,128)(2,1)S(1)} %multiply_convert_fusion.1), channel_id=1, source_target_pairs={{0,4},{4,8},{8,12},{12,0},{1,5},{5,9},{9,13},{13,1},{2,6},{6,10},{... | collective-permute-start | bytes 995336 | tf_op jit(solution)/shard_map/ppermute | solution.py:74
  28.5 24.7 %collective-permute-start.16 = (bf16[192,864]{1,0:T(8,128)(2,1)}, bf16[192,864]{1,0:T(8,128)(2,1)}, u32[]{:S(2)}, u32[]{:S(2)}) collective-permute-start(bf16[192,864]{1,0:T(8,128)(2,1)} %collective-permute-done.12), channel_id=1, source_target_pairs={{0,4},{4,8},{8,12},{12,0},{1,5},{5,9},{9,13},{13,1},{2,6},{6,10},{... | collective-permute-start | bytes 995336 | tf_op jit(solution)/shard_map/ppermute | solution.py:74
  31.4 7.3 %collective-permute-start.3 = (bf16[96,1024]{1,0:T(8,128)(2,1)S(1)}, bf16[96,1024]{1,0:T(8,128)(2,1)S(1)}, u32[]{:S(2)}, u32[]{:S(2)}) collective-permute-start(bf16[96,1024]{1,0:T(8,128)(2,1)S(1)} %convolution_convert_fusion.2), channel_id=1, source_target_pairs={{0,1},{1,0},{2,3},{3,2},{4,5},{5,4},{6,7},{7,6},{8,9},{9,8},{10,11... | collective-permute-start | bytes 589832 | tf_op jit(solution)/shard_map/ppermute | solution.py:69
  33.4 9.2 %collective-permute-start.6 = (bf16[96,1024]{1,0:T(8,128)(2,1)S(1)}, bf16[96,1024]{1,0:T(8,128)(2,1)S(1)}, u32[]{:S(2)}, u32[]{:S(2)}) collective-permute-start(bf16[96,1024]{1,0:T(8,128)(2,1)S(1)} %convolution_convert_fusion.1), channel_id=1, source_target_pairs={{0,1},{1,0},{2,3},{3,2},{4,5},{5,4},{6,7},{7,6},{8,9},{9,8},{10,11... | collective-permute-start | bytes 589832 | tf_op jit(solution)/shard_map/ppermute | solution.py:69
  40.4 6.8 %collective-permute-start.5 = (bf16[96,1024]{1,0:T(8,128)(2,1)S(1)}, bf16[96,1024]{1,0:T(8,128)(2,1)S(1)}, u32[]{:S(2)}, u32[]{:S(2)}) collective-permute-start(bf16[96,1024]{1,0:T(8,128)(2,1)S(1)} %pad_maximum_fusion.1), channel_id=1, source_target_pairs={{0,1},{1,0},{2,3},{3,2},{4,5},{5,4},{6,7},{7,6},{8,9},{9,8},{10,11... | collective-permute-start | bytes 589832 | tf_op jit(solution)/shard_map/ppermute | solution.py:69
  44.2 5.7 %collective-permute-start.7 = (bf16[96,1024]{1,0:T(8,128)(2,1)S(1)}, bf16[96,1024]{1,0:T(8,128)(2,1)S(1)}, u32[]{:S(2)}, u32[]{:S(2)}) collective-permute-start(bf16[96,1024]{1,0:T(8,128)(2,1)S(1)} %pad_maximum_fusion.3), channel_id=1, source_target_pairs={{0,1},{1,0},{2,3},{3,2},{4,5},{5,4},{6,7},{7,6},{8,9},{9,8},{10,11... | collective-permute-start | bytes 589832 | tf_op jit(solution)/shard_map/ppermute | solution.py:69
  48.0 9.7 %collective-permute-start.10 = (bf16[96,1024]{1,0:T(8,128)(2,1)S(1)}, bf16[96,1024]{1,0:T(8,128)(2,1)S(1)}, u32[]{:S(2)}, u32[]{:S(2)}) collective-permute-start(bf16[96,1024]{1,0:T(8,128)(2,1)S(1)} %pad_maximum_fusion.2), channel_id=1, source_target_pairs={{0,4},{4,8},{8,12},{12,0},{1,5},{5,9},{9,13},{13,1},{2,6},{6,10},{... | collective-permute-start | bytes 589832 | tf_op jit(solution)/shard_map/ppermute | solution.py:74
  50.8 15.0 %copy-start.4 = (bf16[192,864]{1,0:T(8,128)(2,1)S(1)}, bf16[192,864]{1,0:T(8,128)(2,1)}, u32[]{:S(2)}) copy-start(bf16[192,864]{1,0:T(8,128)(2,1)} %copy-done.3) | copy-start | bytes 995332
  50.8 10.9 %collective-permute-start.11 = (bf16[96,1024]{1,0:T(8,128)(2,1)S(1)}, bf16[96,1024]{1,0:T(8,128)(2,1)S(1)}, u32[]{:S(2)}, u32[]{:S(2)}) collective-permute-start(bf16[96,1024]{1,0:T(8,128)(2,1)S(1)} %pad_maximum_fusion.4), channel_id=1, source_target_pairs={{0,4},{4,8},{8,12},{12,0},{1,5},{5,9},{9,13},{13,1},{2,6},{6,10},{... | collective-permute-start | bytes 589832 | tf_op jit(solution)/shard_map/ppermute | solution.py:74
  51.6 14.0 %collective-permute-start.8 = (bf16[192,1024]{1,0:T(8,128)(2,1)S(1)}, bf16[192,1024]{1,0:T(8,128)(2,1)S(1)}, u32[]{:S(2)}, u32[]{:S(2)}) collective-permute-start(bf16[192,1024]{1,0:T(8,128)(2,1)S(1)} %maximum_maximum_fusion), channel_id=1, source_target_pairs={{0,1},{1,0},{2,3},{3,2},{4,5},{5,4},{6,7},{7,6},{8,9},{9,8},{10,11... | collective-permute-start | bytes 1179656 | tf_op jit(solution)/shard_map/ppermute | solution.py:69
  53.2 36.8 %collective-permute-start.20 = (bf16[192,864]{1,0:T(8,128)(2,1)}, bf16[192,864]{1,0:T(8,128)(2,1)S(1)}, u32[]{:S(2)}, u32[]{:S(2)}) collective-permute-start(bf16[192,864]{1,0:T(8,128)(2,1)} %collective-permute-done.16), channel_id=1, source_target_pairs={{0,4},{4,8},{8,12},{12,0},{1,5},{5,9},{9,13},{13,1},{2,6},{6,10},{... | collective-permute-start | bytes 995336 | tf_op jit(solution)/shard_map/ppermute | solution.py:74
  61.8 26.5 %collective-permute-start.13 = (bf16[192,512]{1,0:T(8,128)(2,1)S(1)}, bf16[192,512]{1,0:T(8,128)(2,1)S(1)}, u32[]{:S(2)}, u32[]{:S(2)}) collective-permute-start(bf16[192,512]{1,0:T(8,128)(2,1)S(1)} %constant_dynamic-slice_fusion.3), channel_id=1, source_target_pairs={{0,1},{5,4},{8,9},{13,12},{2,3},{7,6},{10,11},{15,14},{16,17},{21,... | collective-permute-start | bytes 589832 | tf_op jit(solution)/shard_map/ppermute | solution.py:162
  65.2 9.5 %collective-permute-start.14 = (bf16[96,1024]{1,0:T(8,128)(2,1)S(1)}, bf16[96,1024]{1,0:T(8,128)(2,1)S(1)}, u32[]{:S(2)}, u32[]{:S(2)}) collective-permute-start(bf16[96,1024]{1,0:T(8,128)(2,1)S(1)} %collective-permute-done.10), channel_id=1, source_target_pairs={{0,4},{4,8},{8,12},{12,0},{1,5},{5,9},{9,13},{13,1},{2,6},{6,10},{... | collective-permute-start | bytes 589832 | tf_op jit(solution)/shard_map/ppermute | solution.py:74
  65.2 13.2 %collective-permute-start.15 = (bf16[96,1024]{1,0:T(8,128)(2,1)S(1)}, bf16[96,1024]{1,0:T(8,128)(2,1)S(1)}, u32[]{:S(2)}, u32[]{:S(2)}) collective-permute-start(bf16[96,1024]{1,0:T(8,128)(2,1)S(1)} %collective-permute-done.11), channel_id=1, source_target_pairs={{0,4},{4,8},{8,12},{12,0},{1,5},{5,9},{9,13},{13,1},{2,6},{6,10},{... | collective-permute-start | bytes 589832 | tf_op jit(solution)/shard_map/ppermute | solution.py:74
  74.7 7.5 %collective-permute-start.18 = (bf16[96,1024]{1,0:T(8,128)(2,1)S(1)}, bf16[96,1024]{1,0:T(8,128)(2,1)S(1)}, u32[]{:S(2)}, u32[]{:S(2)}) collective-permute-start(bf16[96,1024]{1,0:T(8,128)(2,1)S(1)} %collective-permute-done.14), channel_id=1, source_target_pairs={{0,4},{4,8},{8,12},{12,0},{1,5},{5,9},{9,13},{13,1},{2,6},{6,10},{... | collective-permute-start | bytes 589832 | tf_op jit(solution)/shard_map/ppermute | solution.py:74
  78.4 7.5 %collective-permute-start.19 = (bf16[96,1024]{1,0:T(8,128)(2,1)S(1)}, bf16[96,1024]{1,0:T(8,128)(2,1)S(1)}, u32[]{:S(2)}, u32[]{:S(2)}) collective-permute-start(bf16[96,1024]{1,0:T(8,128)(2,1)S(1)} %collective-permute-done.15), channel_id=1, source_target_pairs={{0,4},{4,8},{8,12},{12,0},{1,5},{5,9},{9,13},{13,1},{2,6},{6,10},{... | collective-permute-start | bytes 589832 | tf_op jit(solution)/shard_map/ppermute | solution.py:74
  78.4 13.5 %collective-permute-start.17 = (bf16[192,512]{1,0:T(8,128)(2,1)S(1)}, bf16[192,512]{1,0:T(8,128)(2,1)S(1)}, u32[]{:S(2)}, u32[]{:S(2)}) collective-permute-start(bf16[192,512]{1,0:T(8,128)(2,1)S(1)} %constant_dynamic-slice_fusion.2), channel_id=1, source_target_pairs={{0,1},{5,4},{8,9},{13,12},{2,3},{7,6},{10,11},{15,14},{16,17},{21,... | collective-permute-start | bytes 589832 | tf_op jit(solution)/shard_map/ppermute | solution.py:162
  85.9 5.3 %collective-permute-start.21 = (bf16[192,512]{1,0:T(8,128)(2,1)S(1)}, bf16[192,512]{1,0:T(8,128)(2,1)S(1)}, u32[]{:S(2)}, u32[]{:S(2)}) collective-permute-start(bf16[192,512]{1,0:T(8,128)(2,1)S(1)} %constant_dynamic-slice_fusion.1), channel_id=1, source_target_pairs={{0,1},{5,4},{8,9},{13,12},{2,3},{7,6},{10,11},{15,14},{16,17},{21,... | collective-permute-start | bytes 589832 | tf_op jit(solution)/shard_map/ppermute | solution.py:162
  93.7 2.2 %copy-start.2 = (f32[1888,512]{1,0:T(8,128)}, f32[1888,512]{1,0:T(8,128)S(1)}, u32[]{:S(2)}) copy-start(f32[1888,512]{1,0:T(8,128)S(1)} %add_add_fusion) | copy-start | bytes 11599876
  95.9 10.0 %collective-permute-start.22 = (f32[512,512]{1,0:T(8,128)}, f32[512,512]{1,0:T(8,128)S(1)}, u32[]{:S(2)}, u32[]{:S(2)}) collective-permute-start(f32[512,512]{1,0:T(8,128)} %slice.106), channel_id=1, source_target_pairs={{0,2},{2,0},{1,3},{3,1},{4,6},{6,4},{5,7},{7,5},{8,10},{10,8},{9,1... | collective-permute-start | bytes 3145736 | tf_op jit(solution)/shard_map/ppermute | solution.py:69
  96.9 6.7 %collective-permute-start.23 = (f32[864,256]{1,0:T(8,128)}, f32[864,256]{1,0:T(8,128)}, u32[]{:S(2)}, u32[]{:S(2)}) collective-permute-start(f32[864,256]{1,0:T(8,128)} %constant_dynamic-slice_fusion), channel_id=1, source_target_pairs={{0,2},{2,0},{1,3},{3,1},{4,6},{6,4},{5,7},{7,5},{8,10},{10,8},{9,1... | collective-permute-start | bytes 2654216 | tf_op jit(solution)/shard_map/ppermute | solution.py:69
  99.0 2.1 %collective-permute-start.9 = (bf16[192,1024]{1,0:T(8,128)(2,1)}, bf16[192,1024]{1,0:T(8,128)(2,1)}, u32[]{:S(2)}, u32[]{:S(2)}) collective-permute-start(bf16[192,1024]{1,0:T(8,128)(2,1)} %pad_maximum_fusion), channel_id=1, source_target_pairs={{0,2},{2,0},{1,3},{3,1},{4,6},{6,4},{5,7},{7,5},{8,10},{10,8},{9,1... | collective-permute-start | bytes 1179656 | tf_op jit(solution)/shard_map/ppermute | solution.py:69

commit v3 on v0

--- a/solution.py
+++ b/solution.py
@@ -8,13 +8,14 @@
 
 
 step_rate = 0.2
+CHUNKS = 2
 
 
 def soften(value, level):
     return jnp.sign(value) * jnp.maximum(jnp.abs(value) - level, 0.0)
 
 
-def on_device(patches, dictionary, threshold):
+def general(patches, dictionary, threshold):
     values = patches.astype(jnp.float32)
     local_sq = jnp.sum(values * values, axis=1)
     local_first = jnp.dot(patches, dictionary, preferred_element_type=jnp.float32)
@@ -64,6 +65,133 @@
     return (codes, gram, cross)
 
 
+def swap(value, axis):
+    return lax.ppermute(value, axis, [(0, 1), (1, 0)])
+
+
+def shift(value):
+    n = lax.axis_size("patch")
+    return lax.ppermute(value, "patch", [(i, (i + 1) % n) for i in range(n)])
+
+
+def after(value, earlier):
+    return lax.optimization_barrier((value, earlier))[0]
+
+
+def paired(patches, dictionary, threshold):
+    n_patch = lax.axis_size("patch")
+    plane = lax.axis_index("patch")
+    core = lax.axis_index("atom")
+    half = lax.axis_index("feat")
+    count = patches.shape[0] * n_patch
+    rows = patches.shape[0] // 2
+    atoms = dictionary.shape[1]
+    block = atoms // 2
+    step = rows // CHUNKS
+    f32, bf16 = jnp.float32, jnp.bfloat16
+    last = (((1,), (1,)), ((), ()))
+    first = (((0,), (0,)), ((), ()))
+
+    def blocks(array, which):
+        return lax.dynamic_slice_in_dim(array, which * block, block, 1)
+
+    mine = lax.dynamic_slice_in_dim(patches, core * rows, rows, 0)
+    values = mine.astype(f32)
+    local_sq = jnp.sum(values * values, axis=1)
+    other_sq = swap(local_sq, "feat")
+    dictionary2 = swap(dictionary, "atom")
+    windows = [slice(c * step, (c + 1) * step) for c in range(CHUNKS)]
+    parts = []
+    for w in windows:
+        parts.append([jnp.dot(mine[w], d, preferred_element_type=f32).astype(bf16) for d in (dictionary, dictionary2)])
+    others = [swap(jnp.concatenate(p, 1), "feat") for p in parts]
+    level = step_rate * threshold[None, :]
+    level2 = swap(level, "atom")
+    energy = local_sq + after(other_sq, parts)
+    scale = lax.rsqrt(energy[:, None] / (BINS * VOXELS) + 1e-05)
+    normed = (scale * values).astype(bf16)
+    normed_of = [normed, shift(normed)]
+
+    starts, backs, kept = [], [], []
+    done = normed
+    for c, w in enumerate(windows):
+        other = after(others[c], done).astype(f32)
+        start = []
+        for i, t in enumerate((level, level2)):
+            summed = parts[c][i].astype(f32) + other[:, i * atoms : (i + 1) * atoms]
+            start.append(soften(step_rate * (scale[w] * summed), t).astype(bf16))
+        rebuilt = lax.dot_general(start[0], dictionary, last, preferred_element_type=f32)
+        rebuilt += lax.dot_general(start[1], dictionary2, last, preferred_element_type=f32)
+        misfit = (scale[w] * values[w] - rebuilt).astype(bf16)
+        away = [
+            jnp.dot(misfit, blocks(d, 1 - half), preferred_element_type=f32).astype(bf16)
+            for d in (dictionary, dictionary2)
+        ]
+        done = away
+        starts.append(start)
+        backs.append(swap(jnp.concatenate(away, 1), "feat"))
+        kept.append(
+            [jnp.dot(misfit, blocks(d, half), preferred_element_type=f32) for d in (dictionary, dictionary2)]
+        )
+        normed_of.append(shift(after(normed_of[-1], away)))
+
+    codes_of = []
+    for c, w in enumerate(windows):
+        back = after(backs[c], done).astype(f32)
+        pieces = []
+        for i, t in enumerate((level, level2)):
+            second = kept[c][i] + back[:, i * block : (i + 1) * block]
+            base = blocks(starts[c][i], half).astype(f32)
+            pieces.append(soften(base + step_rate * second, blocks(t, half)).astype(bf16))
+        codes_of.append(jnp.concatenate(pieces, 1))
+        done = codes_of[c]
+
+    rings = [codes_of]
+    for k in range(1, n_patch):
+        rings.append([shift(x) for x in rings[-1]])
+    left = [jnp.concatenate(x, 0) for x in rings]
+    inside = left[0]
+    outside = swap(inside, "feat")
+
+    home_core = plane // 2
+    home_half = plane % 2
+    place = jnp.where(core == home_core, 0, 1)
+    here = [blocks(x, place) for x in left]
+    over = [(q * 2 + q % 2, q * 2 + 1 - q % 2) for q in range(n_patch)]
+    middle = lax.ppermute(jnp.concatenate(here[1:-1], 0), ("patch", "feat"), over)
+    below = (plane + n_patch - 1) % n_patch
+    place_below = jnp.where(core == below // 2, 0, 1)
+    down = [
+        (q * 2 + 1 - (q - 1) % n_patch % 2, (q - 1) % n_patch * 2 + 1 - (q - 1) % n_patch % 2) for q in range(n_patch)
+    ]
+    final = lax.ppermute(blocks(outside, place_below), ("patch", "feat"), down)
+    there = [blocks(outside, place), middle[:rows], middle[rows:], final]
+    right = [jnp.where(half == home_half, h, t) for h, t in zip(here, there)]
+
+    both = [jnp.where(half == 0, inside, outside), jnp.where(half == 0, outside, inside)]
+    upper = jnp.concatenate([x[:, :block] for x in both], 1)
+    lower = after(jnp.concatenate([x[:, block:] for x in both], 1), rings[1])
+    lower = after(swap(lower, "atom"), rings[2])
+    codes = jnp.where(
+        core == 0, jnp.concatenate([upper, lower], 0), jnp.concatenate([lower, upper], 0)
+    )
+
+    gram_part = 0.0
+    cross_part = 0.0
+    for k in range(n_patch):
+        gram_part += lax.dot_general(left[k], right[k], first, preferred_element_type=f32)
+        cross_part += lax.dot_general(normed_of[k], right[k], first, preferred_element_type=f32)
+        if k == n_patch - 2:
+            gram_part, cross_part, codes = lax.optimization_barrier((gram_part, cross_part, codes))
+    width = block // 2
+    gram = gram_part[:block] + swap(gram_part[block:].astype(bf16), "atom").astype(f32)
+    cross = lax.dynamic_slice_in_dim(cross_part, core * width, width, 1)
+    cross += swap(
+        lax.dynamic_slice_in_dim(cross_part, (1 - core) * width, width, 1).astype(bf16), "atom"
+    ).astype(f32)
+    return (codes, gram / count, cross / count)
+
+
 def solution(mesh):
     in_specs = (P(("slab", "patch"), "feat"), P("feat", "atom"), P("atom"))
     out_specs = (
@@ -71,6 +199,8 @@
         P(("slab", "atom", "feat"), "patch"),
         P(("slab", "feat"), ("patch", "atom")),
     )
+    sizes = mesh.shape
+    small = sizes["feat"] == 2 and sizes["atom"] == 2 and sizes["patch"] == 4
     return jax.shard_map(
-        on_device, mesh=mesh, in_specs=in_specs, out_specs=out_specs, check_vma=False
-    )
+        paired if small else general, mesh=mesh, in_specs=in_specs, out_specs=out_specs, check_vma=False
+    )

time: 268 us -> 106 us (0.40)
  waiting for transfers between devices: 209 us -> 39.2 us
  starting transfers between devices: 0.25 us -> 30.6 us
  between operations: 14.1 us -> 1.18 us
  local copies, waits for them, and re-layouts: 13.4 us -> 3.12 us
  matrix products: 17 us -> 23.8 us
  blocking collectives: 5.83 us -> 0 us
    psum x3 -> x0, waiting for transfers between devices: 120 us -> none  [the longest x1 52.8 us: on_device(): second = lax.psum(local_second, 'feat')]
    reduce_scatter x2 -> x0, waiting for transfers between devices: 78.8 us -> none  [the longest x1 43.1 us: on_device(): lax.psum_scatter(gram_part.astype(jnp.bfloat16), 'patch', scatter_dimensi...]
    ppermute x0 -> x22, waiting for transfers between devices: none -> 39.2 us  [the longest x9 18.6 us: shift(): return lax.ppermute(value, 'patch', [(i, (i + 1) % n) for i in range(n)])]
    ppermute x0 -> x22, starting transfers between devices: none -> 30.6 us  [the longest x9 10.7 us: shift(): return lax.ppermute(value, 'patch', [(i, (i + 1) % n) for i in range(n)])]
    all_gather x1 -> x0, waiting for transfers between devices: 9.91 us -> none  [on_device(): codes_whole = lax.all_gather(codes, 'atom', axis=1, tiled=True)]
    dot_general x5 -> x24, matrix products: 17 us -> 23.8 us  [the longest x4 6.15 us: paired(): jnp.dot(mine[w], d, preferred_element_type=f32).astype(bf16)]
    psum x1 -> x0, blocking collectives: 5.83 us -> none  [on_device(): summed, energy = lax.psum((local_first, local_sq), 'feat')]
    unnamed x11 -> x20, local copies, waits for them, and re-layouts: 6.51 us -> 0.86 us
  transfers between devices with their start and end apart: 6 -> 22, of which waited for: 6 -> 10; matrix products, arithmetic and copies ran while one was open for 2% -> 27% of each run, Pallas kernels for 0% -> 0%
where the time goes in v3:
time: 106 us; the launch traced here: 105 us
  waiting for transfers between devices  39.2 us (37%)
  starting transfers between devices  30.6 us (29%)
  matrix products  23.8 us (22%)
  other arithmetic  7.53 us (7%)
  local copies, waits for them, and re-layouts  3.12 us (3%)
  between operations  1.18 us (1%)
    ppermute x9, waiting for transfers between devices, shift(): return lax.ppermute(value, 'patch', [(i, (i + 1) % n) for i in range(n)])  18.6 us
    ppermute x11, waiting for transfers between devices, swap(): return lax.ppermute(value, axis, [(0, 1), (1, 0)])  17 us
    ppermute x9, starting transfers between devices, shift(): return lax.ppermute(value, 'patch', [(i, (i + 1) % n) for i in range(n)])  10.7 us
    ppermute x11, starting transfers between devices, swap(): return lax.ppermute(value, axis, [(0, 1), (1, 0)])  9.03 us
    dot_general x4, matrix products, paired(): jnp.dot(mine[w], d, preferred_element_type=f32).astype(bf16)  6.15 us
    ppermute x1, starting transfers between devices, paired(): final = lax.ppermute(blocks(outside, place_below), ('patch', 'feat'), down)  5.74 us
    ppermute x1, starting transfers between devices, paired(): lax.ppermute(jnp.concatenate(here[1:-1], 0), ('patch', 'feat'), over)  5.13 us
    dot_general x2, matrix products, paired(): lax.dot_general(start[1], dictionary2, last, preferred_element_type=f32)  4.31 us
  transfers between devices with their start and end apart: 22, of which 10 were waited for; matrix products, arithmetic and copies ran while one was open for 27% of the time, Pallas kernels for 0%

profile of v3, /device:TPU:0, one launch (start us, length us, event | category | flops | bytes accessed | tf_op | source)
XLA Modules:
  0.0 105.4 jit_solution(3172909602059651150)
XLA Ops:
  0.7 0.5 collective-permute-start.1
  1.2 0.6 copy-done
  1.7 0.2 constant_dynamic-slice_fusion.4
  1.9 0.2 copy.7
  2.2 0.2 multiply_reduce_fusion
  2.3 3.0 %collective-permute-start = (f32[192]{0:T(256)S(1)}, f32[192]{0:T(256)S(1)}, u32[]{:S(2)}, u32[]{:S(2)}) collective-permute-start(f32[192]{0:T(256)S(1)} %multiply_reduce_fusion), channel_id=1, source_target_pairs={{0,1},{1,0},{2,3},{3,2},{4,5},{5,4},{6,7},{7,6},{8,9},{9,8},{10,11... | collective-permute-start | bytes 2312 | tf_op jit(solution)/shard_map/ppermute | solution.py:69
  5.3 1.1 %convolution_convert_fusion.1 = bf16[96,1024]{1,0:T(8,128)(2,1)} fusion(bf16[864,1024]{1,0:T(8,128)(2,1)S(1)} %copy-done.1, bf16[192,864]{1,0:T(8,128)(2,1)S(1)} %copy.7), kind=kOutput, calls=%fused_computation.8 | convolution fusion | flops 169967616 | bytes 2138112 | tf_op jit(solution)/shard_map/dot_general | solution.py:106
  6.4 1.1 %convolution_convert_fusion.3 = bf16[96,1024]{1,0:T(8,128)(2,1)} fusion(bf16[864,1024]{1,0:T(8,128)(2,1)S(1)} %copy-done.1, bf16[192,864]{1,0:T(8,128)(2,1)S(1)} %copy.7), kind=kOutput, calls=%fused_computation.10 | convolution fusion | flops 169967616 | bytes 2138112 | tf_op jit(solution)/shard_map/dot_general | solution.py:106
  7.7 2.0 %convolution_convert_fusion = bf16[96,1024]{1,0:T(8,128)(2,1)S(1)} fusion(bf16[864,1024]{1,0:T(8,128)(2,1)} %collective-permute-done.1, bf16[192,864]{1,0:T(8,128)(2,1)S(1)} %copy.7), kind=kOutput, calls=%fused_computation.7 | convolution fusion | flops 169967616 | bytes 2138112 | tf_op jit(solution)/shard_map/dot_general | solution.py:106
  9.8 0.2 collective-permute-start.5
  9.9 1.9 %convolution_convert_fusion.2 = bf16[96,1024]{1,0:T(8,128)(2,1)S(1)} fusion(bf16[864,1024]{1,0:T(8,128)(2,1)} %collective-permute-done.1, bf16[192,864]{1,0:T(8,128)(2,1)S(1)} %copy.7), kind=kOutput, calls=%fused_computation.9 | convolution fusion | flops 169967616 | bytes 2138112 | tf_op jit(solution)/shard_map/dot_general | solution.py:106
  11.9 2.0 %collective-permute-start.2 = (bf16[96,2048]{1,0:T(8,128)(2,1)S(1)}, bf16[96,2048]{1,0:T(8,128)(2,1)S(1)}, u32[]{:S(2)}, u32[]{:S(2)}) collective-permute-start(bf16[96,2048]{1,0:T(8,128)(2,1)S(1)} %pad_maximum_fusion), channel_id=1, source_target_pairs={{0,1},{1,0},{2,3},{3,2},{4,5},{5,4},{6,7},{7,6},{8,9},{9,8},{10,11... | collective-permute-start | bytes 1179656 | tf_op jit(solution)/shard_map/ppermute | solution.py:69
  14.1 1.6 %collective-permute-start.13 = (bf16[192,864]{1,0:T(8,128)(2,1)S(1)}, bf16[192,864]{1,0:T(8,128)(2,1)}, u32[]{:S(2)}, u32[]{:S(2)}) collective-permute-start(bf16[192,864]{1,0:T(8,128)(2,1)S(1)} %multiply_convert_fusion), channel_id=1, source_target_pairs={{0,4},{4,8},{8,12},{12,0},{1,5},{5,9},{9,13},{13,1},{2,6},{6,10},{... | collective-permute-start | bytes 995336 | tf_op jit(solution)/shard_map/ppermute | solution.py:74
  15.8 14.0 %collective-permute-done.2 = bf16[96,2048]{1,0:T(8,128)(2,1)S(1)} collective-permute-done((bf16[96,2048]{1,0:T(8,128)(2,1)S(1)}, bf16[96,2048]{1,0:T(8,128)(2,1)S(1)}, u32[]{:S(2)}, u32[]{:S(2)}) %collective-permute-start.2) | collective-permute-done | bytes 393248 | tf_op jit(solution)/shard_map/ppermute | solution.py:69
  29.8 0.5 multiply_convert_fusion.3
  30.3 0.7 fusion.64
  31.0 2.2 %fusion.2 = bf16[96,864]{1,0:T(8,128)(2,1)S(1)} fusion(f32[96,864]{1,0:T(8,128)S(1)} %fusion.64, bf16[96,1024]{1,0:T(8,128)(2,1)S(1)} %get-tuple-element.29, bf16[864,1024]{1,0:T(8,128)(2,1)} %collective-permute-done.1, f32[192,864]{1,0:T(8,128)S(1)} %convert_element_type.106, f32[96]{0:T(128)S(1)} %get-tuple-element.38), kind=kOutput, calls=%fused_computation.11 | convolution fusion | flops 170201088 | bytes 2795904 | tf_op jit(solution)/shard_map/dot_general | solution.py:124
  33.1 0.3 convolution_convert_fusion.7
  33.5 1.5 %convolution_convert_fusion.6 = bf16[96,512]{1,0:T(8,128)(2,1)S(1)} fusion(bf16[96,864]{1,0:T(8,128)(2,1)S(1)} %fusion.2, bf16[864,1024]{1,0:T(8,128)(2,1)} %collective-permute-done.1, s32[]{:T(128)S(6)} %select_n.106), kind=kOutput, calls=%fused_computation.21 | convolution fusion | flops 84983808 | bytes 1148932 | tf_op jit(solution)/shard_map/dot_general | solution.py:127
  35.0 0.5 multiply_convert_fusion.1
  35.5 0.7 fusion.65
  36.2 2.2 %fusion.3 = bf16[96,864]{1,0:T(8,128)(2,1)S(1)} fusion(f32[96,864]{1,0:T(8,128)S(1)} %fusion.65, bf16[96,1024]{1,0:T(8,128)(2,1)S(1)} %get-tuple-element.27, bf16[864,1024]{1,0:T(8,128)(2,1)} %collective-permute-done.1, f32[192,864]{1,0:T(8,128)S(1)} %convert_element_type.106, f32[96]{0:T(128)S(1)} %get-tuple-element.37), kind=kOutput, calls=%fused_computation.12 | convolution fusion | flops 170201088 | bytes 2795904 | tf_op jit(solution)/shard_map/dot_general | solution.py:124
  38.3 0.3 convolution_convert_fusion.5
  38.6 0.3 collective-permute-start.4
  39.0 1.5 %convolution_convert_fusion.4 = bf16[96,512]{1,0:T(8,128)(2,1)S(1)} fusion(bf16[96,864]{1,0:T(8,128)(2,1)S(1)} %fusion.3, bf16[864,1024]{1,0:T(8,128)(2,1)} %collective-permute-done.1, s32[]{:T(128)S(6)} %select_n.106), kind=kOutput, calls=%fused_computation.19 | convolution fusion | flops 84983808 | bytes 1148932 | tf_op jit(solution)/shard_map/dot_general | solution.py:127
  40.5 1.8 %collective-permute-start.6 = (bf16[96,1024]{1,0:T(8,128)(2,1)S(1)}, bf16[96,1024]{1,0:T(8,128)(2,1)S(1)}, u32[]{:S(2)}, u32[]{:S(2)}) collective-permute-start(bf16[96,1024]{1,0:T(8,128)(2,1)S(1)} %pad_maximum_fusion.6), channel_id=1, source_target_pairs={{0,1},{1,0},{2,3},{3,2},{4,5},{5,4},{6,7},{7,6},{8,9},{9,8},{10,11... | collective-permute-start | bytes 589832 | tf_op jit(solution)/shard_map/ppermute | solution.py:69
  42.3 1.6 %collective-permute-start.14 = (bf16[192,864]{1,0:T(8,128)(2,1)}, bf16[192,864]{1,0:T(8,128)(2,1)S(1)}, u32[]{:S(2)}, u32[]{:S(2)}) collective-permute-start(bf16[192,864]{1,0:T(8,128)(2,1)} %collective-permute-done.13), channel_id=1, source_target_pairs={{0,4},{4,8},{8,12},{12,0},{1,5},{5,9},{9,13},{13,1},{2,6},{6,10},{... | collective-permute-start | bytes 995336 | tf_op jit(solution)/shard_map/ppermute | solution.py:74
  43.9 2.7 %collective-permute-done.4 = bf16[96,1024]{1,0:T(8,128)(2,1)S(1)} collective-permute-done((bf16[96,1024]{1,0:T(8,128)(2,1)S(1)}, bf16[96,1024]{1,0:T(8,128)(2,1)S(1)}, u32[]{:S(2)}, u32[]{:S(2)}) %collective-permute-start.4) | collective-permute-done | bytes 196640 | tf_op jit(solution)/shard_map/ppermute | solution.py:69
  46.6 0.4 multiply_convert_fusion.8
  46.9 1.5 %multiply_convert_fusion.7 = bf16[96,512]{1,0:T(8,128)(2,1)S(1)} fusion(f32[96,1024]{1,0:T(8,128)S(1)} %convert_element_type.129, bf16[96,864]{1,0:T(8,128)(2,1)S(1)} %fusion.2, bf16[864,1024]{1,0:T(8,128)(2,1)} %collective-permute-done.1, s32[]{:T(128)S(6)} %select_n.105, f32[512]{0:T(512)S(1)} %bitcast.34, bf16[96,1024]{1,0:T(8,128)(2,1)S(1)} %get-tuple-element.29), kind=kOutput, calls=%fused_computation.82 | convolution fusion | flops 85426176 | bytes 1446912 | tf_op jit(solution)/shard_map/dot_general | solution.py:134
  48.5 0.7 pad_maximum_fusion.5
  49.2 1.6 %collective-permute-start.8 = (bf16[96,1024]{1,0:T(8,128)(2,1)}, bf16[96,1024]{1,0:T(8,128)(2,1)S(1)}, u32[]{:S(2)}, u32[]{:S(2)}) collective-permute-start(bf16[96,1024]{1,0:T(8,128)(2,1)} %pad_maximum_fusion.5), channel_id=1, source_target_pairs={{0,4},{4,8},{8,12},{12,0},{1,5},{5,9},{9,13},{13,1},{2,6},{6,10},{... | collective-permute-start | bytes 589832 | tf_op jit(solution)/shard_map/ppermute | solution.py:74
  50.8 0.4 multiply_convert_fusion.6
  51.2 1.5 %multiply_convert_fusion.5 = bf16[96,512]{1,0:T(8,128)(2,1)S(1)} fusion(f32[96,1024]{1,0:T(8,128)S(1)} %convert_element_type.134, bf16[96,864]{1,0:T(8,128)(2,1)S(1)} %fusion.3, bf16[864,1024]{1,0:T(8,128)(2,1)} %collective-permute-done.1, s32[]{:T(128)S(6)} %select_n.105, bf16[96,1024]{1,0:T(8,128)(2,1)S(1)} %get-tuple-element.27, f32[512]{0:T(512)S(1)} %bitcast.35), kind=kOutput, calls=%fused_computation.80 | convolution fusion | flops 85426176 | bytes 1446912 | tf_op jit(solution)/shard_map/dot_general | solution.py:134
  52.8 1.6 %collective-permute-start.9 = (bf16[96,1024]{1,0:T(8,128)(2,1)S(1)}, bf16[96,1024]{1,0:T(8,128)(2,1)S(1)}, u32[]{:S(2)}, u32[]{:S(2)}) collective-permute-start(bf16[96,1024]{1,0:T(8,128)(2,1)S(1)} %pad_maximum_fusion.7), channel_id=1, source_target_pairs={{0,4},{4,8},{8,12},{12,0},{1,5},{5,9},{9,13},{13,1},{2,6},{6,10},{... | collective-permute-start | bytes 589832 | tf_op jit(solution)/shard_map/ppermute | solution.py:74
  54.4 0.6 collective-permute-start.7
  55.1 0.2 collective-permute-done.14
  55.3 1.3 %collective-permute-start.20 = (bf16[192,864]{1,0:T(8,128)(2,1)S(1)}, bf16[192,864]{1,0:T(8,128)(2,1)S(1)}, u32[]{:S(2)}, u32[]{:S(2)}) collective-permute-start(bf16[192,864]{1,0:T(8,128)(2,1)S(1)} %collective-permute-done.14), channel_id=1, source_target_pairs={{0,4},{4,8},{8,12},{12,0},{1,5},{5,9},{9,13},{13,1},{2,6},{6,10},{... | collective-permute-start | bytes 995336 | tf_op jit(solution)/shard_map/ppermute | solution.py:74
  56.6 2.9 %collective-permute-done.8 = bf16[96,1024]{1,0:T(8,128)(2,1)S(1)} collective-permute-done((bf16[96,1024]{1,0:T(8,128)(2,1)}, bf16[96,1024]{1,0:T(8,128)(2,1)S(1)}, u32[]{:S(2)}, u32[]{:S(2)}) %collective-permute-start.8) | collective-permute-done | bytes 196640 | tf_op jit(solution)/shard_map/ppermute | solution.py:74
  59.5 4.2 %collective-permute-done.9 = bf16[96,1024]{1,0:T(8,128)(2,1)S(1)} collective-permute-done((bf16[96,1024]{1,0:T(8,128)(2,1)S(1)}, bf16[96,1024]{1,0:T(8,128)(2,1)S(1)}, u32[]{:S(2)}, u32[]{:S(2)}) %collective-permute-start.9) | collective-permute-done | bytes 196640 | tf_op jit(solution)/shard_map/ppermute | solution.py:74
  63.8 0.2 broadcast_select_fusion.1
  64.2 5.7 %collective-permute-start.18 = (bf16[192,512]{1,0:T(8,128)(2,1)S(1)}, bf16[192,512]{1,0:T(8,128)(2,1)S(1)}, u32[]{:S(2)}, u32[]{:S(2)}) collective-permute-start(bf16[192,512]{1,0:T(8,128)(2,1)S(1)} %constant_dynamic-slice_fusion), channel_id=1, source_target_pairs={{0,12},{5,1},{8,4},{13,9},{2,14},{7,3},{10,6},{15,11},{16,28},{21,... | collective-permute-start | bytes 589832 | tf_op jit(solution)/shard_map/ppermute | solution.py:167
  70.0 0.5 fusion.44
  70.5 0.4 fusion.43
  70.9 4.5 %collective-permute-done.10 = bf16[96,1024]{1,0:T(8,128)(2,1)S(1)} collective-permute-done((bf16[96,1024]{1,0:T(8,128)(2,1)S(1)}, bf16[96,1024]{1,0:T(8,128)(2,1)S(1)}, u32[]{:S(2)}, u32[]{:S(2)}) %collective-permute-start.10) | collective-permute-done | bytes 196640 | tf_op jit(solution)/shard_map/ppermute | solution.py:74
  75.4 3.9 %collective-permute-done.11 = bf16[96,1024]{1,0:T(8,128)(2,1)S(1)} collective-permute-done((bf16[96,1024]{1,0:T(8,128)(2,1)S(1)}, bf16[96,1024]{1,0:T(8,128)(2,1)S(1)}, u32[]{:S(2)}, u32[]{:S(2)}) %collective-permute-start.11) | collective-permute-done | bytes 196640 | tf_op jit(solution)/shard_map/ppermute | solution.py:74
  79.3 2.9 %collective-permute-start.17 = (bf16[96,1024]{1,0:T(8,128)(2,1)S(1)}, bf16[96,1024]{1,0:T(8,128)(2,1)S(1)}, u32[]{:S(2)}, u32[]{:S(2)}) collective-permute-start(bf16[96,1024]{1,0:T(8,128)(2,1)S(1)} %collective-permute-done.11), channel_id=1, source_target_pairs={{0,4},{4,8},{8,12},{12,0},{1,5},{5,9},{9,13},{13,1},{2,6},{6,10},{... | collective-permute-start | bytes 589832 | tf_op jit(solution)/shard_map/ppermute | solution.py:74
  82.3 2.9 %collective-permute-done.16 = bf16[96,1024]{1,0:T(8,128)(2,1)S(1)} collective-permute-done((bf16[96,1024]{1,0:T(8,128)(2,1)S(1)}, bf16[96,1024]{1,0:T(8,128)(2,1)S(1)}, u32[]{:S(2)}, u32[]{:S(2)}) %collective-permute-start.16) | collective-permute-done | bytes 196640 | tf_op jit(solution)/shard_map/ppermute | solution.py:74
  85.2 5.1 %collective-permute-start.12 = (bf16[384,512]{1,0:T(8,128)(2,1)S(1)}, bf16[384,512]{1,0:T(8,128)(2,1)S(1)}, u32[]{:S(2)}, u32[]{:S(2)}) collective-permute-start(bf16[384,512]{1,0:T(8,128)(2,1)S(1)} %pad_maximum_fusion.2), channel_id=1, source_target_pairs={{0,1},{5,4},{8,9},{13,12},{2,3},{7,6},{10,11},{15,14},{16,17},{21,... | collective-permute-start | bytes 1179656 | tf_op jit(solution)/shard_map/ppermute | solution.py:161
  90.5 0.4 fusion.42
  90.9 1.2 %maximum_select_fusion = bf16[384,1024]{1,0:T(8,128)(2,1)} fusion(bf16[192,1024]{1,0:T(8,128)(2,1)S(1)} %collective-permute-done.15, bf16[192,512]{1,0:T(8,128)(2,1)S(1)} %get-tuple-element.40, bf16[192,512]{1,0:T(8,128)(2,1)S(1)} %get-tuple-element.33, pred[]{:T(512)S(6)} %eq.24), kind=kLoop, calls=%fused_computation.28 | loop fusion | flops 5111808 | bytes 1572865 | tf_op jit(solution)/shard_map/jit(_where)/select_n | solution.py:175
  92.1 3.6 %collective-permute-done.12 = bf16[384,512]{1,0:T(8,128)(2,1)S(1)} collective-permute-done((bf16[384,512]{1,0:T(8,128)(2,1)S(1)}, bf16[384,512]{1,0:T(8,128)(2,1)S(1)}, u32[]{:S(2)}, u32[]{:S(2)}) %collective-permute-start.12) | collective-permute-done | bytes 393248 | tf_op jit(solution)/shard_map/ppermute | solution.py:161
  95.7 0.5 fusion.40
  96.1 1.4 %fusion.39 = f32[864,512]{1,0:T(8,128)S(1)} fusion(bf16[192,864]{1,0:T(8,128)(2,1)} %collective-permute-done.13, bf16[192,512]{1,0:T(8,128)(2,1)S(1)} %constant_dynamic-slice_fusion.2, bf16[384,512]{1,0:T(8,128)(2,1)S(1)} %collective-permute-done.12, pred[]{:T(512)S(6)} %eq.22), kind=kOutput, calls=%fused_computation.88 | convolution fusion | flops 169967616 | bytes 2494465 | tf_op jit(solution)/shard_map/dot_general | solution.py:183
  97.5 0.5 add_add_fusion
  98.0 0.4 add_add_fusion.1
  98.5 0.4 add.158
  98.9 0.9 dynamic-slice_convert_fusion
  99.8 0.5 convolution_add_fusion
  100.3 0.9 slice.191
  101.1 0.5 collective-permute-start.19
  101.6 0.3 collective-permute-done.21
  101.9 2.3 %add_multiply_fusion = f32[864,256]{1,0:T(8,128)} fusion(bf16[864,256]{1,0:T(8,128)(2,1)} %collective-permute-done.21, f32[864,512]{1,0:T(8,128)} %copy-done.2, s32[]{:T(128)S(6)} %select_n.125), kind=kLoop, calls=%fused_computation.26 | loop fusion | flops 663552 | bytes 2211844 | tf_op jit(solution)/shard_map/div | solution.py:192
  104.2 1.1 %fusion.8 = f32[512,512]{1,0:T(8,128)} fusion(f32[1024,512]{1,0:T(8,128)S(1)} %convolution_add_fusion, bf16[512,512]{1,0:T(8,128)(2,1)S(1)} %collective-permute-done.19), kind=kLoop, calls=%fused_computation.25 | loop fusion | flops 786432 | bytes 2621440 | tf_op jit(solution)/shard_map/div | solution.py:192
  (62 shorter events, 1.1 us)
Async XLA Ops:
  0.6 1.1 %copy-start = (bf16[384,864]{0,1:T(8,128)(2,1)S(1)}, bf16[384,864]{0,1:T(8,128)(2,1)}, u32[]{:S(2)}) copy-start(bf16[384,864]{0,1:T(8,128)(2,1)} %param.3) | copy-start | bytes 1990660
  0.6 4.7 %copy-start.1 = (bf16[864,1024]{1,0:T(8,128)(2,1)S(1)}, bf16[864,1024]{1,0:T(8,128)(2,1)}, u32[]{:S(2)}) copy-start(bf16[864,1024]{1,0:T(8,128)(2,1)} %param.4) | copy-start | bytes 5308420
  0.7 4.7 %copy-start.7 = (f32[1024]{0:T(1024)S(1)}, f32[1024]{0:T(1024)}, u32[]{:S(2)}) copy-start(f32[1024]{0:T(1024)} %param.5) | copy-start | bytes 12292
  0.7 7.0 %collective-permute-start.1 = (bf16[864,1024]{1,0:T(8,128)(2,1)}, bf16[864,1024]{1,0:T(8,128)(2,1)}, u32[]{:S(2)}, u32[]{:S(2)}) collective-permute-start(bf16[864,1024]{1,0:T(8,128)(2,1)} %param.4), channel_id=1, source_target_pairs={{0,2},{2,0},{1,3},{3,1},{4,6},{6,4},{5,7},{7,5},{8,10},{10,8},{9,1... | collective-permute-start | bytes 5308424 | tf_op jit(solution)/shard_map/ppermute | solution.py:69
  2.3 11.6 %collective-permute-start = (f32[192]{0:T(256)S(1)}, f32[192]{0:T(256)S(1)}, u32[]{:S(2)}, u32[]{:S(2)}) collective-permute-start(f32[192]{0:T(256)S(1)} %multiply_reduce_fusion), channel_id=1, source_target_pairs={{0,1},{1,0},{2,3},{3,2},{4,5},{5,4},{6,7},{7,6},{8,9},{9,8},{10,11... | collective-permute-start | bytes 2312 | tf_op jit(solution)/shard_map/ppermute | solution.py:69
  5.3 2.4 %collective-permute-start.3 = (f32[1,1024]{1,0:T(1,128)S(1)}, f32[1,1024]{1,0:T(1,128)S(1)}, u32[]{:S(2)}, u32[]{:S(2)}) collective-permute-start(f32[1,1024]{1,0:T(1,128)S(1)} %bitcast.31), channel_id=1, source_target_pairs={{0,2},{2,0},{1,3},{3,1},{4,6},{6,4},{5,7},{7,5},{8,10},{10,8},{9,1... | collective-permute-start | bytes 12296 | tf_op jit(solution)/shard_map/ppermute | solution.py:69
  7.7 2.0 %copy-start.3 = (bf16[96,1024]{1,0:T(8,128)(2,1)S(1)}, bf16[96,1024]{1,0:T(8,128)(2,1)}, u32[]{:S(2)}) copy-start(bf16[96,1024]{1,0:T(8,128)(2,1)} %convolution_convert_fusion.1) | copy-start | bytes 589828
  9.7 2.1 %copy-start.4 = (bf16[96,1024]{1,0:T(8,128)(2,1)S(1)}, bf16[96,1024]{1,0:T(8,128)(2,1)}, u32[]{:S(2)}) copy-start(bf16[96,1024]{1,0:T(8,128)(2,1)} %convolution_convert_fusion.3) | copy-start | bytes 589828
  9.8 25.2 %collective-permute-start.5 = (bf16[96,2048]{1,0:T(8,128)(2,1)S(1)}, bf16[96,2048]{1,0:T(8,128)(2,1)S(1)}, u32[]{:S(2)}, u32[]{:S(2)}) collective-permute-start(bf16[96,2048]{1,0:T(8,128)(2,1)S(1)} %pad_maximum_fusion.1), channel_id=1, source_target_pairs={{0,1},{1,0},{2,3},{3,2},{4,5},{5,4},{6,7},{7,6},{8,9},{9,8},{10,11... | collective-permute-start | bytes 1179656 | tf_op jit(solution)/shard_map/ppermute | solution.py:69
  11.9 17.9 %collective-permute-start.2 = (bf16[96,2048]{1,0:T(8,128)(2,1)S(1)}, bf16[96,2048]{1,0:T(8,128)(2,1)S(1)}, u32[]{:S(2)}, u32[]{:S(2)}) collective-permute-start(bf16[96,2048]{1,0:T(8,128)(2,1)S(1)} %pad_maximum_fusion), channel_id=1, source_target_pairs={{0,1},{1,0},{2,3},{3,2},{4,5},{5,4},{6,7},{7,6},{8,9},{9,8},{10,11... | collective-permute-start | bytes 1179656 | tf_op jit(solution)/shard_map/ppermute | solution.py:69
  14.0 16.9 %copy-start.5 = (bf16[192,864]{1,0:T(8,128)(2,1)}, bf16[192,864]{1,0:T(8,128)(2,1)S(1)}, u32[]{:S(2)}) copy-start(bf16[192,864]{1,0:T(8,128)(2,1)S(1)} %multiply_convert_fusion) | copy-start | bytes 995332
  14.1 28.2 %collective-permute-start.13 = (bf16[192,864]{1,0:T(8,128)(2,1)S(1)}, bf16[192,864]{1,0:T(8,128)(2,1)}, u32[]{:S(2)}, u32[]{:S(2)}) collective-permute-start(bf16[192,864]{1,0:T(8,128)(2,1)S(1)} %multiply_convert_fusion), channel_id=1, source_target_pairs={{0,4},{4,8},{8,12},{12,0},{1,5},{5,9},{9,13},{13,1},{2,6},{6,10},{... | collective-permute-start | bytes 995336 | tf_op jit(solution)/shard_map/ppermute | solution.py:74
  38.6 7.9 %collective-permute-start.4 = (bf16[96,1024]{1,0:T(8,128)(2,1)S(1)}, bf16[96,1024]{1,0:T(8,128)(2,1)S(1)}, u32[]{:S(2)}, u32[]{:S(2)}) collective-permute-start(bf16[96,1024]{1,0:T(8,128)(2,1)S(1)} %pad_maximum_fusion.4), channel_id=1, source_target_pairs={{0,1},{1,0},{2,3},{3,2},{4,5},{5,4},{6,7},{7,6},{8,9},{9,8},{10,11... | collective-permute-start | bytes 589832 | tf_op jit(solution)/shard_map/ppermute | solution.py:69
  40.5 10.3 %collective-permute-start.6 = (bf16[96,1024]{1,0:T(8,128)(2,1)S(1)}, bf16[96,1024]{1,0:T(8,128)(2,1)S(1)}, u32[]{:S(2)}, u32[]{:S(2)}) collective-permute-start(bf16[96,1024]{1,0:T(8,128)(2,1)S(1)} %pad_maximum_fusion.6), channel_id=1, source_target_pairs={{0,1},{1,0},{2,3},{3,2},{4,5},{5,4},{6,7},{7,6},{8,9},{9,8},{10,11... | collective-permute-start | bytes 589832 | tf_op jit(solution)/shard_map/ppermute | solution.py:69
  42.3 13.0 %collective-permute-start.14 = (bf16[192,864]{1,0:T(8,128)(2,1)}, bf16[192,864]{1,0:T(8,128)(2,1)S(1)}, u32[]{:S(2)}, u32[]{:S(2)}) collective-permute-start(bf16[192,864]{1,0:T(8,128)(2,1)} %collective-permute-done.13), channel_id=1, source_target_pairs={{0,4},{4,8},{8,12},{12,0},{1,5},{5,9},{9,13},{13,1},{2,6},{6,10},{... | collective-permute-start | bytes 995336 | tf_op jit(solution)/shard_map/ppermute | solution.py:74
  49.2 10.3 %collective-permute-start.8 = (bf16[96,1024]{1,0:T(8,128)(2,1)}, bf16[96,1024]{1,0:T(8,128)(2,1)S(1)}, u32[]{:S(2)}, u32[]{:S(2)}) collective-permute-start(bf16[96,1024]{1,0:T(8,128)(2,1)} %pad_maximum_fusion.5), channel_id=1, source_target_pairs={{0,4},{4,8},{8,12},{12,0},{1,5},{5,9},{9,13},{13,1},{2,6},{6,10},{... | collective-permute-start | bytes 589832 | tf_op jit(solution)/shard_map/ppermute | solution.py:74
  52.8 11.0 %collective-permute-start.9 = (bf16[96,1024]{1,0:T(8,128)(2,1)S(1)}, bf16[96,1024]{1,0:T(8,128)(2,1)S(1)}, u32[]{:S(2)}, u32[]{:S(2)}) collective-permute-start(bf16[96,1024]{1,0:T(8,128)(2,1)S(1)} %pad_maximum_fusion.7), channel_id=1, source_target_pairs={{0,4},{4,8},{8,12},{12,0},{1,5},{5,9},{9,13},{13,1},{2,6},{6,10},{... | collective-permute-start | bytes 589832 | tf_op jit(solution)/shard_map/ppermute | solution.py:74
  54.4 9.4 %collective-permute-start.7 = (bf16[192,1024]{1,0:T(8,128)(2,1)S(1)}, bf16[192,1024]{1,0:T(8,128)(2,1)S(1)}, u32[]{:S(2)}, u32[]{:S(2)}) collective-permute-start(bf16[192,1024]{1,0:T(8,128)(2,1)S(1)} %maximum_maximum_fusion), channel_id=1, source_target_pairs={{0,1},{1,0},{2,3},{3,2},{4,5},{5,4},{6,7},{7,6},{8,9},{9,8},{10,11... | collective-permute-start | bytes 1179656 | tf_op jit(solution)/shard_map/ppermute | solution.py:69
  55.3 35.1 %collective-permute-start.20 = (bf16[192,864]{1,0:T(8,128)(2,1)S(1)}, bf16[192,864]{1,0:T(8,128)(2,1)S(1)}, u32[]{:S(2)}, u32[]{:S(2)}) collective-permute-start(bf16[192,864]{1,0:T(8,128)(2,1)S(1)} %collective-permute-done.14), channel_id=1, source_target_pairs={{0,4},{4,8},{8,12},{12,0},{1,5},{5,9},{9,13},{13,1},{2,6},{6,10},{... | collective-permute-start | bytes 995336 | tf_op jit(solution)/shard_map/ppermute | solution.py:74
  59.5 15.9 %collective-permute-start.10 = (bf16[96,1024]{1,0:T(8,128)(2,1)S(1)}, bf16[96,1024]{1,0:T(8,128)(2,1)S(1)}, u32[]{:S(2)}, u32[]{:S(2)}) collective-permute-start(bf16[96,1024]{1,0:T(8,128)(2,1)S(1)} %collective-permute-done.8), channel_id=1, source_target_pairs={{0,4},{4,8},{8,12},{12,0},{1,5},{5,9},{9,13},{13,1},{2,6},{6,10},{... | collective-permute-start | bytes 589832 | tf_op jit(solution)/shard_map/ppermute | solution.py:74
  63.7 15.6 %collective-permute-start.11 = (bf16[96,1024]{1,0:T(8,128)(2,1)S(1)}, bf16[96,1024]{1,0:T(8,128)(2,1)S(1)}, u32[]{:S(2)}, u32[]{:S(2)}) collective-permute-start(bf16[96,1024]{1,0:T(8,128)(2,1)S(1)} %collective-permute-done.9), channel_id=1, source_target_pairs={{0,4},{4,8},{8,12},{12,0},{1,5},{5,9},{9,13},{13,1},{2,6},{6,10},{... | collective-permute-start | bytes 589832 | tf_op jit(solution)/shard_map/ppermute | solution.py:74
  64.1 6.4 %copy-start.6 = (bf16[192,864]{1,0:T(8,128)(2,1)S(1)}, bf16[192,864]{1,0:T(8,128)(2,1)}, u32[]{:S(2)}) copy-start(bf16[192,864]{1,0:T(8,128)(2,1)} %copy-done.5) | copy-start | bytes 995332
  64.1 26.8 %collective-permute-start.15 = (bf16[192,1024]{1,0:T(8,128)(2,1)S(1)}, bf16[192,1024]{1,0:T(8,128)(2,1)S(1)}, u32[]{:S(2)}, u32[]{:S(2)}) collective-permute-start(bf16[192,1024]{1,0:T(8,128)(2,1)S(1)} %pad_maximum_fusion.3), channel_id=1, source_target_pairs={{0,2},{2,0},{1,3},{3,1},{4,6},{6,4},{5,7},{7,5},{8,10},{10,8},{9,1... | collective-permute-start | bytes 1179656 | tf_op jit(solution)/shard_map/ppermute | solution.py:69
  64.2 26.2 %collective-permute-start.18 = (bf16[192,512]{1,0:T(8,128)(2,1)S(1)}, bf16[192,512]{1,0:T(8,128)(2,1)S(1)}, u32[]{:S(2)}, u32[]{:S(2)}) collective-permute-start(bf16[192,512]{1,0:T(8,128)(2,1)S(1)} %constant_dynamic-slice_fusion), channel_id=1, source_target_pairs={{0,12},{5,1},{8,4},{13,9},{2,14},{7,3},{10,6},{15,11},{16,28},{21,... | collective-permute-start | bytes 589832 | tf_op jit(solution)/shard_map/ppermute | solution.py:167
  75.4 9.8 %collective-permute-start.16 = (bf16[96,1024]{1,0:T(8,128)(2,1)S(1)}, bf16[96,1024]{1,0:T(8,128)(2,1)S(1)}, u32[]{:S(2)}, u32[]{:S(2)}) collective-permute-start(bf16[96,1024]{1,0:T(8,128)(2,1)S(1)} %collective-permute-done.10), channel_id=1, source_target_pairs={{0,4},{4,8},{8,12},{12,0},{1,5},{5,9},{9,13},{13,1},{2,6},{6,10},{... | collective-permute-start | bytes 589832 | tf_op jit(solution)/shard_map/ppermute | solution.py:74
  79.3 11.1 %collective-permute-start.17 = (bf16[96,1024]{1,0:T(8,128)(2,1)S(1)}, bf16[96,1024]{1,0:T(8,128)(2,1)S(1)}, u32[]{:S(2)}, u32[]{:S(2)}) collective-permute-start(bf16[96,1024]{1,0:T(8,128)(2,1)S(1)} %collective-permute-done.11), channel_id=1, source_target_pairs={{0,4},{4,8},{8,12},{12,0},{1,5},{5,9},{9,13},{13,1},{2,6},{6,10},{... | collective-permute-start | bytes 589832 | tf_op jit(solution)/shard_map/ppermute | solution.py:74
  85.2 10.4 %collective-permute-start.12 = (bf16[384,512]{1,0:T(8,128)(2,1)S(1)}, bf16[384,512]{1,0:T(8,128)(2,1)S(1)}, u32[]{:S(2)}, u32[]{:S(2)}) collective-permute-start(bf16[384,512]{1,0:T(8,128)(2,1)S(1)} %pad_maximum_fusion.2), channel_id=1, source_target_pairs={{0,1},{5,4},{8,9},{13,12},{2,3},{7,6},{10,11},{15,14},{16,17},{21,... | collective-permute-start | bytes 1179656 | tf_op jit(solution)/shard_map/ppermute | solution.py:161
  98.9 1.4 %copy-start.2 = (f32[864,512]{1,0:T(8,128)}, f32[864,512]{1,0:T(8,128)S(1)}, u32[]{:S(2)}) copy-start(f32[864,512]{1,0:T(8,128)S(1)} %add.158) | copy-start | bytes 5308420
  99.8 2.1 %collective-permute-start.21 = (bf16[864,256]{1,0:T(8,128)(2,1)}, bf16[864,256]{1,0:T(8,128)(2,1)}, u32[]{:S(2)}, u32[]{:S(2)}) collective-permute-start(bf16[864,256]{1,0:T(8,128)(2,1)} %dynamic-slice_convert_fusion), channel_id=1, source_target_pairs={{0,2},{2,0},{1,3},{3,1},{4,6},{6,4},{5,7},{7,5},{8,10},{10,8},{9,1... | collective-permute-start | bytes 1327112 | tf_op jit(solution)/shard_map/ppermute | solution.py:69
  101.1 3.1 %collective-permute-start.19 = (bf16[512,512]{1,0:T(8,128)(2,1)}, bf16[512,512]{1,0:T(8,128)(2,1)S(1)}, u32[]{:S(2)}, u32[]{:S(2)}) collective-permute-start(bf16[512,512]{1,0:T(8,128)(2,1)} %slice.191), channel_id=1, source_target_pairs={{0,2},{2,0},{1,3},{3,1},{4,6},{6,4},{5,7},{7,5},{8,10},{10,8},{9,1... | collective-permute-start | bytes 1572872 | tf_op jit(solution)/shard_map/ppermute | solution.py:69

commit v4 on v3

--- a/solution.py
+++ b/solution.py
@@ -87,63 +87,63 @@
     rows = patches.shape[0] // 2
     atoms = dictionary.shape[1]
     block = atoms // 2
+    width = block // 2
     step = rows // CHUNKS
     f32, bf16 = jnp.float32, jnp.bfloat16
     last = (((1,), (1,)), ((), ()))
     first = (((0,), (0,)), ((), ()))
 
-    def blocks(array, which):
-        return lax.dynamic_slice_in_dim(array, which * block, block, 1)
+    def blocks(array, which, size=block):
+        return lax.dynamic_slice_in_dim(array, which * size, size, 1)
+
+    def group(own, other, which):
+        return jnp.concatenate([blocks(own, which), blocks(other, which)], 1)
+
+    def times(a, b):
+        return jnp.dot(a, b, preferred_element_type=f32)
 
     mine = lax.dynamic_slice_in_dim(patches, core * rows, rows, 0)
     values = mine.astype(f32)
     local_sq = jnp.sum(values * values, axis=1)
     other_sq = swap(local_sq, "feat")
     dictionary2 = swap(dictionary, "atom")
+    near = group(dictionary, dictionary2, half)
+    far = group(dictionary, dictionary2, 1 - half)
     windows = [slice(c * step, (c + 1) * step) for c in range(CHUNKS)]
-    parts = []
+    parts, others = [], []
+    done = ()
     for w in windows:
-        parts.append([jnp.dot(mine[w], d, preferred_element_type=f32).astype(bf16) for d in (dictionary, dictionary2)])
-    others = [swap(jnp.concatenate(p, 1), "feat") for p in parts]
+        piece = after(mine[w], done)
+        parts.append([times(piece, d).astype(bf16) for d in (near, far)])
+        done = parts[-1]
+        others.append(swap(jnp.concatenate(parts[-1], 1), "feat"))
     level = step_rate * threshold[None, :]
-    level2 = swap(level, "atom")
-    energy = local_sq + after(other_sq, parts)
+    level2 = swap(after(level, done), "atom")
+    levels = [group(level, level2, half), group(level, level2, 1 - half)]
+    energy = local_sq + after(other_sq, done)
     scale = lax.rsqrt(energy[:, None] / (BINS * VOXELS) + 1e-05)
     normed = (scale * values).astype(bf16)
     normed_of = [normed, shift(normed)]
 
-    starts, backs, kept = [], [], []
-    done = normed
+    base, backs = [], []
+    done = normed_of
     for c, w in enumerate(windows):
         other = after(others[c], done).astype(f32)
-        start = []
-        for i, t in enumerate((level, level2)):
-            summed = parts[c][i].astype(f32) + other[:, i * atoms : (i + 1) * atoms]
-            start.append(soften(step_rate * (scale[w] * summed), t).astype(bf16))
-        rebuilt = lax.dot_general(start[0], dictionary, last, preferred_element_type=f32)
-        rebuilt += lax.dot_general(start[1], dictionary2, last, preferred_element_type=f32)
+        summed = [parts[c][0].astype(f32) + other[:, atoms:], parts[c][1].astype(f32) + other[:, :atoms]]
+        start = [soften(step_rate * (scale[w] * x), t).astype(bf16) for x, t in zip(summed, levels)]
+        rebuilt = sum(
+            lax.dot_general(x, d, last, preferred_element_type=f32) for x, d in zip(start, (near, far))
+        )
         misfit = (scale[w] * values[w] - rebuilt).astype(bf16)
-        away = [
-            jnp.dot(misfit, blocks(d, 1 - half), preferred_element_type=f32).astype(bf16)
-            for d in (dictionary, dictionary2)
-        ]
-        done = away
-        starts.append(start)
-        backs.append(swap(jnp.concatenate(away, 1), "feat"))
-        kept.append(
-            [jnp.dot(misfit, blocks(d, half), preferred_element_type=f32) for d in (dictionary, dictionary2)]
-        )
-        normed_of.append(shift(after(normed_of[-1], away)))
+        backs.append(swap(times(misfit, far).astype(bf16), "feat"))
+        base.append(start[0].astype(f32) + step_rate * times(misfit, near))
+        normed_of.append(shift(after(normed_of[-1], start)))
+        done = (backs[-1], normed_of[-1]) if c == 0 else (misfit,)
 
     codes_of = []
     for c, w in enumerate(windows):
         back = after(backs[c], done).astype(f32)
-        pieces = []
-        for i, t in enumerate((level, level2)):
-            second = kept[c][i] + back[:, i * block : (i + 1) * block]
-            base = blocks(starts[c][i], half).astype(f32)
-            pieces.append(soften(base + step_rate * second, blocks(t, half)).astype(bf16))
-        codes_of.append(jnp.concatenate(pieces, 1))
+        codes_of.append(soften(base[c] + step_rate * back, levels[0]).astype(bf16))
         done = codes_of[c]
 
     rings = [codes_of]
@@ -153,42 +153,50 @@
     inside = left[0]
     outside = swap(inside, "feat")
 
-    home_core = plane // 2
     home_half = plane % 2
-    place = jnp.where(core == home_core, 0, 1)
+    place = jnp.where(core == plane // 2, 0, 1)
     here = [blocks(x, place) for x in left]
     over = [(q * 2 + q % 2, q * 2 + 1 - q % 2) for q in range(n_patch)]
-    middle = lax.ppermute(jnp.concatenate(here[1:-1], 0), ("patch", "feat"), over)
     below = (plane + n_patch - 1) % n_patch
     place_below = jnp.where(core == below // 2, 0, 1)
     down = [
         (q * 2 + 1 - (q - 1) % n_patch % 2, (q - 1) % n_patch * 2 + 1 - (q - 1) % n_patch % 2) for q in range(n_patch)
     ]
-    final = lax.ppermute(blocks(outside, place_below), ("patch", "feat"), down)
-    there = [blocks(outside, place), middle[:rows], middle[rows:], final]
+    there = [blocks(outside, place)]
+    for k in range(1, n_patch - 1):
+        there.append(lax.ppermute(here[k], ("patch", "feat"), over))
+    there.append(lax.ppermute(blocks(outside, place_below), ("patch", "feat"), down))
     right = [jnp.where(half == home_half, h, t) for h, t in zip(here, there)]
 
     both = [jnp.where(half == 0, inside, outside), jnp.where(half == 0, outside, inside)]
     upper = jnp.concatenate([x[:, :block] for x in both], 1)
-    lower = after(jnp.concatenate([x[:, block:] for x in both], 1), rings[1])
-    lower = after(swap(lower, "atom"), rings[2])
+    lower = swap(jnp.concatenate([x[:, block:] for x in both], 1), "atom")
+    lower = after(lower, rings[1])
     codes = jnp.where(
         core == 0, jnp.concatenate([upper, lower], 0), jnp.concatenate([lower, upper], 0)
     )
 
-    gram_part = 0.0
-    cross_part = 0.0
-    for k in range(n_patch):
-        gram_part += lax.dot_general(left[k], right[k], first, preferred_element_type=f32)
-        cross_part += lax.dot_general(normed_of[k], right[k], first, preferred_element_type=f32)
-        if k == n_patch - 2:
-            gram_part, cross_part, codes = lax.optimization_barrier((gram_part, cross_part, codes))
-    width = block // 2
-    gram = gram_part[:block] + swap(gram_part[block:].astype(bf16), "atom").astype(f32)
-    cross = lax.dynamic_slice_in_dim(cross_part, core * width, width, 1)
-    cross += swap(
-        lax.dynamic_slice_in_dim(cross_part, (1 - core) * width, width, 1).astype(bf16), "atom"
-    ).astype(f32)
+    def product(lhs, rhs):
+        return lax.dot_general(lhs, rhs, first, preferred_element_type=f32)
+
+    steps = range(n_patch - 1)
+    gram_send = sum(product(left[k][:, block:], right[k]) for k in steps).astype(bf16)
+    cross_send = sum(product(normed_of[k], blocks(right[k], 1 - core, width)) for k in steps).astype(bf16)
+    gram = sum(product(left[k][:, :block], right[k]) for k in steps)
+    cross = sum(product(normed_of[k], blocks(right[k], core, width)) for k in steps)
+    gram += swap(gram_send, "atom").astype(f32)
+    cross += swap(cross_send, "atom").astype(f32)
+    late = jnp.concatenate([rings[-1][-1][:, block:], right[-1][-step:]], 1)
+    early = jnp.concatenate([rings[-1][0][:, block:], right[-1][:-step]], 1)
+    early = swap(early, "atom")
+    normed_last = swap(after(normed_of[-1], rings[1]), "atom")
+    codes, gram, cross, late, normed_last = lax.optimization_barrier((codes, gram, cross, late, normed_last))
+    late = swap(late, "atom")
+    gram += product(left[-1][:, :block], right[-1])
+    cross += product(normed_of[-1], blocks(right[-1], core, width))
+    for c, x in enumerate((early, late)):
+        gram += product(x[:, :block], x[:, block:])
+        cross += product(normed_last[windows[c]], blocks(x[:, block:], core, width))
     return (codes, gram / count, cross / count)
 
 

time: 106 us -> 95.2 us (0.90)
  matrix products: 23.8 us -> 15.7 us
  starting transfers between devices: 30.6 us -> 26.3 us
  waiting for transfers between devices: 39.2 us -> 40.8 us
    ppermute x9, waiting for transfers between devices: 18.6 us -> 27.7 us  [shift(): return lax.ppermute(value, 'patch', [(i, (i + 1) % n) for i in range(n)])]
    dot_general x24 -> x30, matrix products: 23.8 us -> 15.7 us  [the longest x18 7.79 us: product(): return lax.dot_general(lhs, rhs, first, preferred_element_type=f32)]
    ppermute x11 -> x14, waiting for transfers between devices: 17 us -> 10.8 us  [swap(): return lax.ppermute(value, axis, [(0, 1), (1, 0)])]
    div x2 -> x0, other arithmetic: 3.46 us -> none  [paired(): return (codes, gram / count, cross / count)]
    dynamic_slice x4 -> x5, local copies, waits for them, and re-layouts: 0.07 us -> 2.42 us  [blocks(): return lax.dynamic_slice_in_dim(array, which * size, size, 1)]
    ppermute x2 -> x3, starting transfers between devices: 10.9 us -> 8.82 us  [the longest x1 5.1 us: paired(): lax.ppermute(blocks(outside, place_below), ('patch', 'feat'), down)]
    ppermute x9, starting transfers between devices: 10.7 us -> 9 us  [shift(): return lax.ppermute(value, 'patch', [(i, (i + 1) % n) for i in range(n)])]
    ppermute x2 -> x3, waiting for transfers between devices: 3.59 us -> 2.26 us  [the longest x2 2.25 us: paired(): there.append(lax.ppermute(here[k], ('patch', 'feat'), over))]
  transfers between devices with their start and end apart: 22 -> 26, of which waited for: 10 -> 13; matrix products, arithmetic and copies ran while one was open for 27% -> 21% of each run, Pallas kernels for 0% -> 0%
where the time goes in v4:
time: 95.2 us; the launch traced here: 94.8 us
  waiting for transfers between devices  40.8 us (43%)
  starting transfers between devices  26.3 us (28%)
  matrix products  15.7 us (16%)
  other arithmetic  6.8 us (7%)
  local copies, waits for them, and re-layouts  3.83 us (4%)
  between operations  1.34 us (1%)
    ppermute x9, waiting for transfers between devices, shift(): return lax.ppermute(value, 'patch', [(i, (i + 1) % n) for i in range(n)])  27.7 us
    ppermute x14, waiting for transfers between devices, swap(): return lax.ppermute(value, axis, [(0, 1), (1, 0)])  10.8 us
    ppermute x9, starting transfers between devices, shift(): return lax.ppermute(value, 'patch', [(i, (i + 1) % n) for i in range(n)])  9 us
    ppermute x14, starting transfers between devices, swap(): return lax.ppermute(value, axis, [(0, 1), (1, 0)])  8.49 us
    dot_general x18, matrix products, product(): return lax.dot_general(lhs, rhs, first, preferred_element_type=f32)  7.79 us
    dot_general x8, matrix products, times(): return jnp.dot(a, b, preferred_element_type=f32)  5.27 us
    ppermute x1, starting transfers between devices, paired(): lax.ppermute(blocks(outside, place_below), ('patch', 'feat'), down)  5.1 us
    ppermute x2, starting transfers between devices, paired(): there.append(lax.ppermute(here[k], ('patch', 'feat'), over))  3.72 us
  transfers between devices with their start and end apart: 26, of which 13 were waited for; matrix products, arithmetic and copies ran while one was open for 21% of the time, Pallas kernels for 0%

profile of v4, /device:TPU:0, one launch (start us, length us, event | category | flops | bytes accessed | tf_op | source)
XLA Modules:
  0.0 94.8 jit_solution(1110959039446754881)
XLA Ops:
  0.6 0.5 collective-permute-start.1
  1.2 0.6 copy-done
  2.3 3.0 %collective-permute-start = (f32[192]{0:T(256)S(1)}, f32[192]{0:T(256)S(1)}, u32[]{:S(2)}, u32[]{:S(2)}) collective-permute-start(f32[192]{0:T(256)S(1)} %multiply_reduce_fusion), channel_id=1, source_target_pairs={{0,1},{1,0},{2,3},{3,2},{4,5},{5,4},{6,7},{7,6},{8,9},{9,8},{10,11... | collective-permute-start | bytes 2312 | tf_op jit(solution)/shard_map/ppermute | solution.py:69
  5.3 0.9 convert_element_type.90
  6.6 2.2 %constant_dynamic-slice_fusion.5 = (bf16[864,512]{1,0:T(8,128)(2,1)S(1)}, bf16[864,512]{1,0:T(8,128)(2,1)S(1)}) fusion(bf16[864,1024]{1,0:T(8,128)(2,1)} %collective-permute-done.1, s32[]{:T(128)S(6)} %select_n.107, s32[]{:T(128)S(6)} %select_n.106), kind=kLoop, calls=%fused_computation.130 | loop fusion | bytes 3538952 | tf_op jit(solution)/shard_map/dynamic_slice | solution.py:97
  8.7 0.4 convolution_convert_fusion.4
  9.2 0.4 convolution_convert_fusion.5
  9.6 0.4 convolution_convert_fusion.3
  10.1 0.4 convolution_convert_fusion.2
  10.6 0.8 pad_maximum_fusion.4
  11.5 1.6 %collective-permute-start.3 = (bf16[192,864]{1,0:T(8,128)(2,1)S(1)}, bf16[192,864]{1,0:T(8,128)(2,1)S(1)}, u32[]{:S(2)}, u32[]{:S(2)}) collective-permute-start(bf16[192,864]{1,0:T(8,128)(2,1)S(1)} %multiply_convert_fusion), channel_id=1, source_target_pairs={{0,4},{4,8},{8,12},{12,0},{1,5},{5,9},{9,13},{13,1},{2,6},{6,10},{... | collective-permute-start | bytes 995336 | tf_op jit(solution)/shard_map/ppermute | solution.py:74
  13.2 0.7 collective-permute-start.2
  13.9 1.4 %collective-permute-start.6 = (bf16[96,2048]{1,0:T(8,128)(2,1)}, bf16[96,2048]{1,0:T(8,128)(2,1)}, u32[]{:S(2)}, u32[]{:S(2)}) collective-permute-start(bf16[96,2048]{1,0:T(8,128)(2,1)} %pad_maximum_fusion.4), channel_id=1, source_target_pairs={{0,1},{1,0},{2,3},{3,2},{4,5},{5,4},{6,7},{7,6},{8,9},{9,8},{10,11... | collective-permute-start | bytes 1179656 | tf_op jit(solution)/shard_map/ppermute | solution.py:69
  15.3 8.7 %collective-permute-done.3 = bf16[192,864]{1,0:T(8,128)(2,1)S(1)} collective-permute-done((bf16[192,864]{1,0:T(8,128)(2,1)S(1)}, bf16[192,864]{1,0:T(8,128)(2,1)S(1)}, u32[]{:S(2)}, u32[]{:S(2)}) %collective-permute-start.3) | collective-permute-done | bytes 331808 | tf_op jit(solution)/shard_map/ppermute | solution.py:74
  24.0 1.2 %collective-permute-done.2 = bf16[96,2048]{1,0:T(8,128)(2,1)S(1)} collective-permute-done((bf16[96,2048]{1,0:T(8,128)(2,1)S(1)}, bf16[96,2048]{1,0:T(8,128)(2,1)S(1)}, u32[]{:S(2)}, u32[]{:S(2)}) %collective-permute-start.2) | collective-permute-done | bytes 393248 | tf_op jit(solution)/shard_map/ppermute | solution.py:69
  25.2 0.5 multiply_convert_fusion.6
  25.7 0.7 fusion.80
  26.4 1.6 %collective-permute-start.7 = (bf16[192,864]{1,0:T(8,128)(2,1)S(1)}, bf16[192,864]{1,0:T(8,128)(2,1)S(1)}, u32[]{:S(2)}, u32[]{:S(2)}) collective-permute-start(bf16[192,864]{1,0:T(8,128)(2,1)S(1)} %collective-permute-done.3), channel_id=1, source_target_pairs={{0,4},{4,8},{8,12},{12,0},{1,5},{5,9},{9,13},{13,1},{2,6},{6,10},{... | collective-permute-start | bytes 995336 | tf_op jit(solution)/shard_map/ppermute | solution.py:74
  28.0 0.7 fusion.14
  28.7 1.1 %convolution_convert_fusion.1 = bf16[96,1024]{1,0:T(8,128)(2,1)} fusion(bf16[96,864]{1,0:T(8,128)(2,1)S(1)} %fusion.14, bf16[864,512]{1,0:T(8,128)(2,1)S(1)} %get-tuple-element.37, bf16[864,512]{1,0:T(8,128)(2,1)S(1)} %get-tuple-element.35), kind=kOutput, calls=%fused_computation.25 | convolution fusion | flops 173506560 | bytes 2131968 | tf_op jit(solution)/shard_map/dot_general | solution.py:103
  29.8 0.7 collective-permute-start.5
  30.5 3.1 %collective-permute-done.6 = bf16[96,2048]{1,0:T(8,128)(2,1)} collective-permute-done((bf16[96,2048]{1,0:T(8,128)(2,1)}, bf16[96,2048]{1,0:T(8,128)(2,1)}, u32[]{:S(2)}, u32[]{:S(2)}) %collective-permute-start.6) | collective-permute-done | bytes 393248 | tf_op jit(solution)/shard_map/ppermute | solution.py:69
  33.7 3.5 %collective-permute-done.5 = bf16[96,1024]{1,0:T(8,128)(2,1)} collective-permute-done((bf16[96,1024]{1,0:T(8,128)(2,1)}, bf16[96,1024]{1,0:T(8,128)(2,1)}, u32[]{:S(2)}, u32[]{:S(2)}) %collective-permute-start.5) | collective-permute-done | bytes 196640 | tf_op jit(solution)/shard_map/ppermute | solution.py:69
  37.2 1.1 %convert_element_type.105 = f32[96,2048]{1,0:T(8,128)S(1)} convert(bf16[96,2048]{1,0:T(8,128)(2,1)} %collective-permute-done.6) | non-fusion elementwise | flops 196608 | bytes 1179648 | tf_op jit(solution)/shard_map/convert_element_type | solution.py:131
  38.2 1.5 %multiply_convert_fusion.4 = (bf16[96,1024]{1,0:T(8,128)(2,1)S(1)}, bf16[96,1024]{1,0:T(8,128)(2,1)S(1)}) fusion(f32[96,2048]{1,0:T(8,128)S(1)} %convert_element_type.105, bf16[96,1024]{1,0:T(8,128)(2,1)} %copy-done.8, f32[96]{0:T(128)S(1)} %get-tuple-element.59, f32[1024]{0:T(1024)S(1)} %bitcast.32, f32[1024]{0:T(1024)S(1)} %bitcast.36, ...), kind=kLoop, calls=%fused_computation.62 | loop fusion | flops 1966080 | bytes 1581440 | tf_op jit(solution)/shard_map/convert_element_type | solution.py:133
  39.8 0.7 fusion.79
  40.4 1.6 %collective-permute-start.22 = (bf16[192,864]{1,0:T(8,128)(2,1)S(1)}, bf16[192,864]{1,0:T(8,128)(2,1)S(1)}, u32[]{:S(2)}, u32[]{:S(2)}) collective-permute-start(bf16[192,864]{1,0:T(8,128)(2,1)S(1)} %collective-permute-done.7), channel_id=1, source_target_pairs={{0,4},{4,8},{8,12},{12,0},{1,5},{5,9},{9,13},{13,1},{2,6},{6,10},{... | collective-permute-start | bytes 995336 | tf_op jit(solution)/shard_map/ppermute | solution.py:74
  42.1 0.7 fusion.15
  42.8 0.4 convolution_convert_fusion
  43.2 0.6 collective-permute-start.8
  43.8 1.4 %multiply_convert_fusion.2 = bf16[96,1024]{1,0:T(8,128)(2,1)S(1)} fusion(bf16[96,864]{1,0:T(8,128)(2,1)S(1)} %copy-done.18, bf16[96,1024]{1,0:T(8,128)(2,1)} %collective-permute-done.5, bf16[96,1024]{1,0:T(8,128)(2,1)S(1)} %copy-done.15, f32[1024]{0:T(1024)S(1)} %bitcast.33, bf16[864,512]{1,0:T(8,128)(2,1)S(1)} %get-tuple-element.38, ...), kind=kOutput, calls=%fused_computation.60 | convolution fusion | flops 174587904 | bytes 2529280 | tf_op jit(solution)/shard_map/dot_general | solution.py:103
  45.3 1.6 %collective-permute-start.11 = (bf16[96,1024]{1,0:T(8,128)(2,1)S(1)}, bf16[96,1024]{1,0:T(8,128)(2,1)S(1)}, u32[]{:S(2)}, u32[]{:S(2)}) collective-permute-start(bf16[96,1024]{1,0:T(8,128)(2,1)S(1)} %multiply_convert_fusion.2), channel_id=1, source_target_pairs={{0,4},{4,8},{8,12},{12,0},{1,5},{5,9},{9,13},{13,1},{2,6},{6,10},{... | collective-permute-start | bytes 589832 | tf_op jit(solution)/shard_map/ppermute | solution.py:74
  46.9 2.2 %collective-permute-done.8 = bf16[96,1024]{1,0:T(8,128)(2,1)S(1)} collective-permute-done((bf16[96,1024]{1,0:T(8,128)(2,1)S(1)}, bf16[96,1024]{1,0:T(8,128)(2,1)S(1)}, u32[]{:S(2)}, u32[]{:S(2)}) %collective-permute-start.8) | collective-permute-done | bytes 196640 | tf_op jit(solution)/shard_map/ppermute | solution.py:69
  49.1 0.5 multiply_convert_fusion.1
  49.6 1.8 %collective-permute-start.12 = (bf16[96,1024]{1,0:T(8,128)(2,1)S(1)}, bf16[96,1024]{1,0:T(8,128)(2,1)S(1)}, u32[]{:S(2)}, u32[]{:S(2)}) collective-permute-start(bf16[96,1024]{1,0:T(8,128)(2,1)S(1)} %multiply_convert_fusion.1), channel_id=1, source_target_pairs={{0,4},{4,8},{8,12},{12,0},{1,5},{5,9},{9,13},{13,1},{2,6},{6,10},{... | collective-permute-start | bytes 589832 | tf_op jit(solution)/shard_map/ppermute | solution.py:74
  51.4 0.4 collective-permute-start.9
  51.8 5.7 %collective-permute-done.11 = bf16[96,1024]{1,0:T(8,128)(2,1)S(1)} collective-permute-done((bf16[96,1024]{1,0:T(8,128)(2,1)S(1)}, bf16[96,1024]{1,0:T(8,128)(2,1)S(1)}, u32[]{:S(2)}, u32[]{:S(2)}) %collective-permute-start.11) | collective-permute-done | bytes 196640 | tf_op jit(solution)/shard_map/ppermute | solution.py:74
  57.5 3.8 %collective-permute-done.12 = bf16[96,1024]{1,0:T(8,128)(2,1)S(1)} collective-permute-done((bf16[96,1024]{1,0:T(8,128)(2,1)S(1)}, bf16[96,1024]{1,0:T(8,128)(2,1)S(1)}, u32[]{:S(2)}, u32[]{:S(2)}) %collective-permute-start.12) | collective-permute-done | bytes 196640 | tf_op jit(solution)/shard_map/ppermute | solution.py:74
  61.4 2.4 %collective-permute-start.13 = (bf16[192,512]{1,0:T(8,128)(2,1)S(1)}, bf16[192,512]{1,0:T(8,128)(2,1)S(1)}, u32[]{:S(2)}, u32[]{:S(2)}) collective-permute-start(bf16[192,512]{1,0:T(8,128)(2,1)S(1)} %constant_dynamic-slice_fusion.2), channel_id=1, source_target_pairs={{0,1},{5,4},{8,9},{13,12},{2,3},{7,6},{10,11},{15,14},{16,17},{21,... | collective-permute-start | bytes 589832 | tf_op jit(solution)/shard_map/ppermute | solution.py:167
  63.9 1.1 %collective-permute-done.14 = bf16[96,1024]{1,0:T(8,128)(2,1)S(1)} collective-permute-done((bf16[96,1024]{1,0:T(8,128)(2,1)S(1)}, bf16[96,1024]{1,0:T(8,128)(2,1)S(1)}, u32[]{:S(2)}, u32[]{:S(2)}) %collective-permute-start.14) | collective-permute-done | bytes 196640 | tf_op jit(solution)/shard_map/ppermute | solution.py:74
  65.0 0.6 collective-permute-start.20
  65.7 5.1 %collective-permute-start.21 = (bf16[192,512]{1,0:T(8,128)(2,1)S(1)}, bf16[192,512]{1,0:T(8,128)(2,1)S(1)}, u32[]{:S(2)}, u32[]{:S(2)}) collective-permute-start(bf16[192,512]{1,0:T(8,128)(2,1)S(1)} %get-tuple-element.45), channel_id=1, source_target_pairs={{0,12},{5,1},{8,4},{13,9},{2,14},{7,3},{10,6},{15,11},{16,28},{21,... | collective-permute-start | bytes 589832 | tf_op jit(solution)/shard_map/ppermute | solution.py:168
  71.1 2.4 %collective-permute-done.15 = bf16[96,1024]{1,0:T(8,128)(2,1)S(1)} collective-permute-done((bf16[96,1024]{1,0:T(8,128)(2,1)S(1)}, bf16[96,1024]{1,0:T(8,128)(2,1)S(1)}, u32[]{:S(2)}, u32[]{:S(2)}) %collective-permute-start.15) | collective-permute-done | bytes 196640 | tf_op jit(solution)/shard_map/ppermute | solution.py:74
  73.6 1.3 %collective-permute-start.16 = (bf16[192,512]{1,0:T(8,128)(2,1)S(1)}, bf16[192,512]{1,0:T(8,128)(2,1)S(1)}, u32[]{:S(2)}, u32[]{:S(2)}) collective-permute-start(bf16[192,512]{1,0:T(8,128)(2,1)S(1)} %constant_dynamic-slice_fusion.1), channel_id=1, source_target_pairs={{0,1},{5,4},{8,9},{13,12},{2,3},{7,6},{10,11},{15,14},{16,17},{21,... | collective-permute-start | bytes 589832 | tf_op jit(solution)/shard_map/ppermute | solution.py:167
  75.0 0.3 fusion.36
  75.3 0.3 fusion.40
  75.6 1.4 %collective-permute-done.20 = bf16[96,1024]{1,0:T(8,128)(2,1)S(1)} collective-permute-done((bf16[96,1024]{1,0:T(8,128)(2,1)S(1)}, bf16[96,1024]{1,0:T(8,128)(2,1)S(1)}, u32[]{:S(2)}, u32[]{:S(2)}) %collective-permute-start.20) | collective-permute-done | bytes 196640 | tf_op jit(solution)/shard_map/ppermute | solution.py:74
  77.1 0.3 fusion.56
  77.4 0.3 fusion.61
  77.7 2.3 %collective-permute-done.16 = bf16[192,512]{1,0:T(8,128)(2,1)S(1)} collective-permute-done((bf16[192,512]{1,0:T(8,128)(2,1)S(1)}, bf16[192,512]{1,0:T(8,128)(2,1)S(1)}, u32[]{:S(2)}, u32[]{:S(2)}) %collective-permute-start.16) | collective-permute-done | bytes 196640 | tf_op jit(solution)/shard_map/ppermute | solution.py:167
  80.0 0.3 fusion.34
  80.4 4.7 %collective-permute-done.19 = bf16[96,1024]{1,0:T(8,128)(2,1)S(1)} collective-permute-done((bf16[96,1024]{1,0:T(8,128)(2,1)S(1)}, bf16[96,1024]{1,0:T(8,128)(2,1)S(1)}, u32[]{:S(2)}, u32[]{:S(2)}) %collective-permute-start.19) | collective-permute-done | bytes 196640 | tf_op jit(solution)/shard_map/ppermute | solution.py:74
  85.1 0.3 fusion.38
  86.0 0.3 fusion.7
  86.3 0.6 collective-permute-start.18
  86.9 0.3 fusion.6
  87.6 0.3 fusion.59
  88.0 1.2 %maximum_select_fusion = bf16[384,1024]{1,0:T(8,128)(2,1)} fusion(bf16[192,1024]{1,0:T(8,128)(2,1)S(1)} %collective-permute-done.10, bf16[192,512]{1,0:T(8,128)(2,1)S(1)} %get-tuple-element.49, bf16[192,512]{1,0:T(8,128)(2,1)S(1)} %get-tuple-element.47, pred[]{:T(512)S(6)} %eq.22), kind=kLoop, calls=%fused_computation.34 | loop fusion | flops 5111808 | bytes 1572865 | tf_op jit(solution)/shard_map/jit(_where)/select_n | solution.py:175
  89.5 0.3 fusion.5
  89.9 0.3 fusion.2
  90.2 0.6 collective-permute-start.25
  91.1 0.8 collective-permute-done.25
  92.2 1.3 %add_multiply_fusion = f32[512,512]{1,0:T(8,128)} fusion(f32[512,512]{1,0:T(8,128)S(1)} %fusion.48, f32[512,512]{1,0:T(8,128)S(1)} %fusion.50, f32[512,512]{1,0:T(8,128)S(1)} %fusion.2, bf16[192,512]{1,0:T(8,128)(2,1)S(1)} %dynamic-slice_select_fusion, bf16[192,1024]{1,0:T(8,128)(2,1)S(1)} %constant_dynamic-update-slice_fusion.4), kind=kOutput, calls=%fused_computation.32 | convolution fusion | flops 101711872 | bytes 4587520 | tf_op jit(solution)/shard_map/dot_general | solution.py:180
  93.5 1.3 %add_multiply_fusion.1 = f32[864,256]{1,0:T(8,128)} fusion(f32[864,256]{1,0:T(8,128)S(1)} %fusion.46, f32[864,256]{1,0:T(8,128)S(1)} %fusion.5, f32[864,256]{1,0:T(8,128)S(1)} %fusion.52, bf16[192,864]{1,0:T(8,128)(2,1)S(1)} %collective-permute-done.23, bf16[96,512]{1,0:T(8,128)(2,1)S(1)} %slice.160, s32[]{:T(128)S(6)} %select_n.119), kind=kOutput, calls=%fused_computation.33 | convolution fusion | flops 43352064 | bytes 3760132 | tf_op jit(solution)/shard_map/dot_general | solution.py:180
  (103 shorter events, 3.9 us)
Async XLA Ops:
  0.6 1.1 %copy-start = (bf16[384,864]{0,1:T(8,128)(2,1)S(1)}, bf16[384,864]{0,1:T(8,128)(2,1)}, u32[]{:S(2)}) copy-start(bf16[384,864]{0,1:T(8,128)(2,1)} %param.3) | copy-start | bytes 1990660
  0.6 5.9 %collective-permute-start.1 = (bf16[864,1024]{1,0:T(8,128)(2,1)}, bf16[864,1024]{1,0:T(8,128)(2,1)}, u32[]{:S(2)}, u32[]{:S(2)}) collective-permute-start(bf16[864,1024]{1,0:T(8,128)(2,1)} %param.4), channel_id=1, source_target_pairs={{0,2},{2,0},{1,3},{3,1},{4,6},{6,4},{5,7},{7,5},{8,10},{10,8},{9,1... | collective-permute-start | bytes 5308424 | tf_op jit(solution)/shard_map/ppermute | solution.py:69
  1.7 4.5 %copy-start.16 = (f32[1024]{0:T(1024)S(1)}, f32[1024]{0:T(1024)}, u32[]{:S(2)}) copy-start(f32[1024]{0:T(1024)} %param.5) | copy-start | bytes 12292
  1.7 4.6 %copy-start.1 = (bf16[864,1024]{1,0:T(8,128)(2,1)S(1)}, bf16[864,1024]{1,0:T(8,128)(2,1)}, u32[]{:S(2)}) copy-start(bf16[864,1024]{1,0:T(8,128)(2,1)} %param.4) | copy-start | bytes 5308420
  2.3 9.1 %collective-permute-start = (f32[192]{0:T(256)S(1)}, f32[192]{0:T(256)S(1)}, u32[]{:S(2)}, u32[]{:S(2)}) collective-permute-start(f32[192]{0:T(256)S(1)} %multiply_reduce_fusion), channel_id=1, source_target_pairs={{0,1},{1,0},{2,3},{3,2},{4,5},{5,4},{6,7},{7,6},{8,9},{9,8},{10,11... | collective-permute-start | bytes 2312 | tf_op jit(solution)/shard_map/ppermute | solution.py:69
  6.5 21.5 %copy-start.2 = (bf16[864,512]{1,0:T(8,128)(2,1)}, bf16[864,512]{1,0:T(8,128)(2,1)S(1)}, u32[]{:S(2)}) copy-start(bf16[864,512]{1,0:T(8,128)(2,1)S(1)} %get-tuple-element.36) | copy-start | bytes 2654212
  6.5 22.1 %copy-start.4 = (bf16[864,512]{1,0:T(8,128)(2,1)}, bf16[864,512]{1,0:T(8,128)(2,1)S(1)}, u32[]{:S(2)}) copy-start(bf16[864,512]{1,0:T(8,128)(2,1)S(1)} %get-tuple-element.35) | copy-start | bytes 2654212
  8.7 20.0 %copy-start.6 = (bf16[864,512]{1,0:T(8,128)(2,1)}, bf16[864,512]{1,0:T(8,128)(2,1)S(1)}, u32[]{:S(2)}) copy-start(bf16[864,512]{1,0:T(8,128)(2,1)S(1)} %get-tuple-element.37) | copy-start | bytes 2654212
  10.1 1.3 %copy-start.8 = (bf16[96,1024]{1,0:T(8,128)(2,1)}, bf16[96,1024]{1,0:T(8,128)(2,1)S(1)}, u32[]{:S(2)}) copy-start(bf16[96,1024]{1,0:T(8,128)(2,1)S(1)} %convolution_convert_fusion.3) | copy-start | bytes 589828
  10.5 0.9 copy-start.9
  11.4 3.9 %collective-permute-start.4 = (f32[1,1024]{1,0:T(1,128)S(1)}, f32[1,1024]{1,0:T(1,128)S(1)}, u32[]{:S(2)}, u32[]{:S(2)}) collective-permute-start(f32[1,1024]{1,0:T(1,128)S(1)} %bitcast.37), channel_id=1, source_target_pairs={{0,2},{2,0},{1,3},{3,1},{4,6},{6,4},{5,7},{7,5},{8,10},{10,8},{9,1... | collective-permute-start | bytes 12296 | tf_op jit(solution)/shard_map/ppermute | solution.py:69
  11.5 12.4 %collective-permute-start.3 = (bf16[192,864]{1,0:T(8,128)(2,1)S(1)}, bf16[192,864]{1,0:T(8,128)(2,1)S(1)}, u32[]{:S(2)}, u32[]{:S(2)}) collective-permute-start(bf16[192,864]{1,0:T(8,128)(2,1)S(1)} %multiply_convert_fusion), channel_id=1, source_target_pairs={{0,4},{4,8},{8,12},{12,0},{1,5},{5,9},{9,13},{13,1},{2,6},{6,10},{... | collective-permute-start | bytes 995336 | tf_op jit(solution)/shard_map/ppermute | solution.py:74
  13.2 11.9 %collective-permute-start.2 = (bf16[96,2048]{1,0:T(8,128)(2,1)S(1)}, bf16[96,2048]{1,0:T(8,128)(2,1)S(1)}, u32[]{:S(2)}, u32[]{:S(2)}) collective-permute-start(bf16[96,2048]{1,0:T(8,128)(2,1)S(1)} %pad_maximum_fusion.3), channel_id=1, source_target_pairs={{0,1},{1,0},{2,3},{3,2},{4,5},{5,4},{6,7},{7,6},{8,9},{9,8},{10,11... | collective-permute-start | bytes 1179656 | tf_op jit(solution)/shard_map/ppermute | solution.py:69
  13.9 19.8 %collective-permute-start.6 = (bf16[96,2048]{1,0:T(8,128)(2,1)}, bf16[96,2048]{1,0:T(8,128)(2,1)}, u32[]{:S(2)}, u32[]{:S(2)}) collective-permute-start(bf16[96,2048]{1,0:T(8,128)(2,1)} %pad_maximum_fusion.4), channel_id=1, source_target_pairs={{0,1},{1,0},{2,3},{3,2},{4,5},{5,4},{6,7},{7,6},{8,9},{9,8},{10,11... | collective-permute-start | bytes 1179656 | tf_op jit(solution)/shard_map/ppermute | solution.py:69
  25.7 3.0 %copy-start.14 = (bf16[96,1024]{1,0:T(8,128)(2,1)}, bf16[96,1024]{1,0:T(8,128)(2,1)S(1)}, u32[]{:S(2)}) copy-start(bf16[96,1024]{1,0:T(8,128)(2,1)S(1)} %get-tuple-element.41) | copy-start | bytes 589828
  25.7 2.3 %copy-start.10 = (f32[192,864]{1,0:T(8,128)S(1)}, f32[192,864]{1,0:T(8,128)}, u32[]{:S(2)}) copy-start(f32[192,864]{1,0:T(8,128)} %convert_element_type.90) | copy-start | bytes 1990660
  26.4 10.8 %collective-permute-start.7 = (bf16[192,864]{1,0:T(8,128)(2,1)S(1)}, bf16[192,864]{1,0:T(8,128)(2,1)S(1)}, u32[]{:S(2)}, u32[]{:S(2)}) collective-permute-start(bf16[192,864]{1,0:T(8,128)(2,1)S(1)} %collective-permute-done.3), channel_id=1, source_target_pairs={{0,4},{4,8},{8,12},{12,0},{1,5},{5,9},{9,13},{13,1},{2,6},{6,10},{... | collective-permute-start | bytes 995336 | tf_op jit(solution)/shard_map/ppermute | solution.py:74
  28.7 1.1 %copy-start.17 = (bf16[96,864]{1,0:T(8,128)(2,1)}, bf16[96,864]{1,0:T(8,128)(2,1)S(1)}, u32[]{:S(2)}) copy-start(bf16[96,864]{1,0:T(8,128)(2,1)S(1)} %fusion.14) | copy-start | bytes 497668
  29.8 9.9 %copy-start.5 = (bf16[864,512]{1,0:T(8,128)(2,1)S(1)}, bf16[864,512]{1,0:T(8,128)(2,1)}, u32[]{:S(2)}) copy-start(bf16[864,512]{1,0:T(8,128)(2,1)} %copy-done.4) | copy-start | bytes 2654212
  29.8 7.3 %collective-permute-start.5 = (bf16[96,1024]{1,0:T(8,128)(2,1)}, bf16[96,1024]{1,0:T(8,128)(2,1)}, u32[]{:S(2)}, u32[]{:S(2)}) collective-permute-start(bf16[96,1024]{1,0:T(8,128)(2,1)} %convolution_convert_fusion.1), channel_id=1, source_target_pairs={{0,1},{1,0},{2,3},{3,2},{4,5},{5,4},{6,7},{7,6},{8,9},{9,8},{10,11... | collective-permute-start | bytes 589832 | tf_op jit(solution)/shard_map/ppermute | solution.py:69
  30.5 9.2 %copy-start.7 = (bf16[864,512]{1,0:T(8,128)(2,1)S(1)}, bf16[864,512]{1,0:T(8,128)(2,1)}, u32[]{:S(2)}) copy-start(bf16[864,512]{1,0:T(8,128)(2,1)} %copy-done.6) | copy-start | bytes 2654212
  39.7 2.4 %copy-start.3 = (bf16[864,512]{1,0:T(8,128)(2,1)S(1)}, bf16[864,512]{1,0:T(8,128)(2,1)}, u32[]{:S(2)}) copy-start(bf16[864,512]{1,0:T(8,128)(2,1)} %copy-done.2) | copy-start | bytes 2654212
  39.7 2.3 %copy-start.11 = (f32[192,864]{1,0:T(8,128)S(1)}, f32[192,864]{1,0:T(8,128)}, u32[]{:S(2)}) copy-start(f32[192,864]{1,0:T(8,128)} %convert_element_type.90) | copy-start | bytes 1990660
  40.4 17.1 %collective-permute-start.22 = (bf16[192,864]{1,0:T(8,128)(2,1)S(1)}, bf16[192,864]{1,0:T(8,128)(2,1)S(1)}, u32[]{:S(2)}, u32[]{:S(2)}) collective-permute-start(bf16[192,864]{1,0:T(8,128)(2,1)S(1)} %collective-permute-done.7), channel_id=1, source_target_pairs={{0,4},{4,8},{8,12},{12,0},{1,5},{5,9},{9,13},{13,1},{2,6},{6,10},{... | collective-permute-start | bytes 995336 | tf_op jit(solution)/shard_map/ppermute | solution.py:74
  42.8 1.1 %copy-start.15 = (bf16[96,1024]{1,0:T(8,128)(2,1)S(1)}, bf16[96,1024]{1,0:T(8,128)(2,1)}, u32[]{:S(2)}) copy-start(bf16[96,1024]{1,0:T(8,128)(2,1)} %copy-done.14) | copy-start | bytes 589828
  42.8 1.1 %copy-start.18 = (bf16[96,864]{1,0:T(8,128)(2,1)S(1)}, bf16[96,864]{1,0:T(8,128)(2,1)}, u32[]{:S(2)}) copy-start(bf16[96,864]{1,0:T(8,128)(2,1)} %copy-done.17) | copy-start | bytes 497668
  43.2 5.9 %collective-permute-start.8 = (bf16[96,1024]{1,0:T(8,128)(2,1)S(1)}, bf16[96,1024]{1,0:T(8,128)(2,1)S(1)}, u32[]{:S(2)}, u32[]{:S(2)}) collective-permute-start(bf16[96,1024]{1,0:T(8,128)(2,1)S(1)} %convolution_convert_fusion), channel_id=1, source_target_pairs={{0,1},{1,0},{2,3},{3,2},{4,5},{5,4},{6,7},{7,6},{8,9},{9,8},{10,11... | collective-permute-start | bytes 589832 | tf_op jit(solution)/shard_map/ppermute | solution.py:69
  45.3 12.2 %collective-permute-start.11 = (bf16[96,1024]{1,0:T(8,128)(2,1)S(1)}, bf16[96,1024]{1,0:T(8,128)(2,1)S(1)}, u32[]{:S(2)}, u32[]{:S(2)}) collective-permute-start(bf16[96,1024]{1,0:T(8,128)(2,1)S(1)} %multiply_convert_fusion.2), channel_id=1, source_target_pairs={{0,4},{4,8},{8,12},{12,0},{1,5},{5,9},{9,13},{13,1},{2,6},{6,10},{... | collective-permute-start | bytes 589832 | tf_op jit(solution)/shard_map/ppermute | solution.py:74
  49.6 11.7 %collective-permute-start.12 = (bf16[96,1024]{1,0:T(8,128)(2,1)S(1)}, bf16[96,1024]{1,0:T(8,128)(2,1)S(1)}, u32[]{:S(2)}, u32[]{:S(2)}) collective-permute-start(bf16[96,1024]{1,0:T(8,128)(2,1)S(1)} %multiply_convert_fusion.1), channel_id=1, source_target_pairs={{0,4},{4,8},{8,12},{12,0},{1,5},{5,9},{9,13},{13,1},{2,6},{6,10},{... | collective-permute-start | bytes 589832 | tf_op jit(solution)/shard_map/ppermute | solution.py:74
  51.4 14.2 %collective-permute-start.9 = (bf16[192,1024]{1,0:T(8,128)(2,1)S(1)}, bf16[192,1024]{1,0:T(8,128)(2,1)S(1)}, u32[]{:S(2)}, u32[]{:S(2)}) collective-permute-start(bf16[192,1024]{1,0:T(8,128)(2,1)S(1)} %pad_maximum_fusion.2), channel_id=1, source_target_pairs={{0,1},{1,0},{2,3},{3,2},{4,5},{5,4},{6,7},{7,6},{8,9},{9,8},{10,11... | collective-permute-start | bytes 1179656 | tf_op jit(solution)/shard_map/ppermute | solution.py:69
  57.5 7.5 %collective-permute-start.14 = (bf16[96,1024]{1,0:T(8,128)(2,1)S(1)}, bf16[96,1024]{1,0:T(8,128)(2,1)S(1)}, u32[]{:S(2)}, u32[]{:S(2)}) collective-permute-start(bf16[96,1024]{1,0:T(8,128)(2,1)S(1)} %collective-permute-done.11), channel_id=1, source_target_pairs={{0,4},{4,8},{8,12},{12,0},{1,5},{5,9},{9,13},{13,1},{2,6},{6,10},{... | collective-permute-start | bytes 589832 | tf_op jit(solution)/shard_map/ppermute | solution.py:74
  61.4 28.9 %collective-permute-start.23 = (bf16[192,864]{1,0:T(8,128)(2,1)S(1)}, bf16[192,864]{1,0:T(8,128)(2,1)S(1)}, u32[]{:S(2)}, u32[]{:S(2)}) collective-permute-start(bf16[192,864]{1,0:T(8,128)(2,1)S(1)} %collective-permute-done.22), channel_id=1, source_target_pairs={{0,2},{2,0},{1,3},{3,1},{4,6},{6,4},{5,7},{7,5},{8,10},{10,8},{9,1... | collective-permute-start | bytes 995336 | tf_op jit(solution)/shard_map/ppermute | solution.py:69
  61.4 12.2 %collective-permute-start.13 = (bf16[192,512]{1,0:T(8,128)(2,1)S(1)}, bf16[192,512]{1,0:T(8,128)(2,1)S(1)}, u32[]{:S(2)}, u32[]{:S(2)}) collective-permute-start(bf16[192,512]{1,0:T(8,128)(2,1)S(1)} %constant_dynamic-slice_fusion.2), channel_id=1, source_target_pairs={{0,1},{5,4},{8,9},{13,12},{2,3},{7,6},{10,11},{15,14},{16,17},{21,... | collective-permute-start | bytes 589832 | tf_op jit(solution)/shard_map/ppermute | solution.py:167
  63.8 9.7 %collective-permute-start.15 = (bf16[96,1024]{1,0:T(8,128)(2,1)S(1)}, bf16[96,1024]{1,0:T(8,128)(2,1)S(1)}, u32[]{:S(2)}, u32[]{:S(2)}) collective-permute-start(bf16[96,1024]{1,0:T(8,128)(2,1)S(1)} %collective-permute-done.12), channel_id=1, source_target_pairs={{0,4},{4,8},{8,12},{12,0},{1,5},{5,9},{9,13},{13,1},{2,6},{6,10},{... | collective-permute-start | bytes 589832 | tf_op jit(solution)/shard_map/ppermute | solution.py:74
  65.0 12.1 %collective-permute-start.20 = (bf16[96,1024]{1,0:T(8,128)(2,1)S(1)}, bf16[96,1024]{1,0:T(8,128)(2,1)S(1)}, u32[]{:S(2)}, u32[]{:S(2)}) collective-permute-start(bf16[96,1024]{1,0:T(8,128)(2,1)S(1)} %collective-permute-done.14), channel_id=1, source_target_pairs={{0,4},{4,8},{8,12},{12,0},{1,5},{5,9},{9,13},{13,1},{2,6},{6,10},{... | collective-permute-start | bytes 589832 | tf_op jit(solution)/shard_map/ppermute | solution.py:74
  65.7 19.7 %collective-permute-start.21 = (bf16[192,512]{1,0:T(8,128)(2,1)S(1)}, bf16[192,512]{1,0:T(8,128)(2,1)S(1)}, u32[]{:S(2)}, u32[]{:S(2)}) collective-permute-start(bf16[192,512]{1,0:T(8,128)(2,1)S(1)} %get-tuple-element.45), channel_id=1, source_target_pairs={{0,12},{5,1},{8,4},{13,9},{2,14},{7,3},{10,6},{15,11},{16,28},{21,... | collective-permute-start | bytes 589832 | tf_op jit(solution)/shard_map/ppermute | solution.py:168
  73.5 14.5 %collective-permute-start.10 = (bf16[192,1024]{1,0:T(8,128)(2,1)S(1)}, bf16[192,1024]{1,0:T(8,128)(2,1)S(1)}, u32[]{:S(2)}, u32[]{:S(2)}) collective-permute-start(bf16[192,1024]{1,0:T(8,128)(2,1)S(1)} %pad_maximum_fusion.5), channel_id=1, source_target_pairs={{0,2},{2,0},{1,3},{3,1},{4,6},{6,4},{5,7},{7,5},{8,10},{10,8},{9,1... | collective-permute-start | bytes 1179656 | tf_op jit(solution)/shard_map/ppermute | solution.py:69
  73.6 6.4 %collective-permute-start.16 = (bf16[192,512]{1,0:T(8,128)(2,1)S(1)}, bf16[192,512]{1,0:T(8,128)(2,1)S(1)}, u32[]{:S(2)}, u32[]{:S(2)}) collective-permute-start(bf16[192,512]{1,0:T(8,128)(2,1)S(1)} %constant_dynamic-slice_fusion.1), channel_id=1, source_target_pairs={{0,1},{5,4},{8,9},{13,12},{2,3},{7,6},{10,11},{15,14},{16,17},{21,... | collective-permute-start | bytes 589832 | tf_op jit(solution)/shard_map/ppermute | solution.py:167
  77.0 3.0 %copy-start.13 = (bf16[96,1024]{1,0:T(8,128)(2,1)}, bf16[96,1024]{1,0:T(8,128)(2,1)S(1)}, u32[]{:S(2)}) copy-start(bf16[96,1024]{1,0:T(8,128)(2,1)S(1)} %collective-permute-done.20) | copy-start | bytes 589828
  77.0 8.1 %collective-permute-start.19 = (bf16[96,1024]{1,0:T(8,128)(2,1)S(1)}, bf16[96,1024]{1,0:T(8,128)(2,1)S(1)}, u32[]{:S(2)}, u32[]{:S(2)}) collective-permute-start(bf16[96,1024]{1,0:T(8,128)(2,1)S(1)} %collective-permute-done.15), channel_id=1, source_target_pairs={{0,4},{4,8},{8,12},{12,0},{1,5},{5,9},{9,13},{13,1},{2,6},{6,10},{... | collective-permute-start | bytes 589832 | tf_op jit(solution)/shard_map/ppermute | solution.py:74
  80.4 5.2 %slice-start.1 = ((bf16[96,1024]{1,0:T(8,128)(2,1)}), bf16[96,512]{1,0:T(8,128)(2,1)S(1)}, s32[]{:S(2)}) async-start(bf16[96,1024]{1,0:T(8,128)(2,1)} %copy-done.13), calls=%async_computation.1 | async-start | bytes 196608 | tf_op jit(solution)/shard_map/slice | solution.py:190
  85.6 2.4 %collective-permute-start.24 = (bf16[96,1024]{1,0:T(8,128)(2,1)S(1)}, bf16[96,1024]{1,0:T(8,128)(2,1)S(1)}, u32[]{:S(2)}, u32[]{:S(2)}) collective-permute-start(bf16[96,1024]{1,0:T(8,128)(2,1)S(1)} %pad_maximum_fusion.7), channel_id=1, source_target_pairs={{0,2},{2,0},{1,3},{3,1},{4,6},{6,4},{5,7},{7,5},{8,10},{10,8},{9,1... | collective-permute-start | bytes 589832 | tf_op jit(solution)/shard_map/ppermute | solution.py:69
  86.3 3.2 %collective-permute-start.18 = (bf16[864,256]{1,0:T(8,128)(2,1)S(1)}, bf16[864,256]{1,0:T(8,128)(2,1)S(1)}, u32[]{:S(2)}, u32[]{:S(2)}) collective-permute-start(bf16[864,256]{1,0:T(8,128)(2,1)S(1)} %fusion.7), channel_id=1, source_target_pairs={{0,2},{2,0},{1,3},{3,1},{4,6},{6,4},{5,7},{7,5},{8,10},{10,8},{9,1... | collective-permute-start | bytes 1327112 | tf_op jit(solution)/shard_map/ppermute | solution.py:69
  87.2 2.6 %collective-permute-start.17 = (bf16[512,512]{1,0:T(8,128)(2,1)S(1)}, bf16[512,512]{1,0:T(8,128)(2,1)S(1)}, u32[]{:S(2)}, u32[]{:S(2)}) collective-permute-start(bf16[512,512]{1,0:T(8,128)(2,1)S(1)} %fusion.6), channel_id=1, source_target_pairs={{0,2},{2,0},{1,3},{3,1},{4,6},{6,4},{5,7},{7,5},{8,10},{10,8},{9,1... | collective-permute-start | bytes 1572872 | tf_op jit(solution)/shard_map/ppermute | solution.py:69
  88.0 1.8 %copy-start.12 = (bf16[96,1024]{1,0:T(8,128)(2,1)}, bf16[96,1024]{1,0:T(8,128)(2,1)S(1)}, u32[]{:S(2)}) copy-start(bf16[96,1024]{1,0:T(8,128)(2,1)S(1)} %collective-permute-done.24) | copy-start | bytes 589828
  89.9 0.9 slice-start
  90.2 1.6 %collective-permute-start.25 = (bf16[96,1024]{1,0:T(8,128)(2,1)S(1)}, bf16[96,1024]{1,0:T(8,128)(2,1)S(1)}, u32[]{:S(2)}, u32[]{:S(2)}) collective-permute-start(bf16[96,1024]{1,0:T(8,128)(2,1)S(1)} %pad_maximum_fusion.6), channel_id=1, source_target_pairs={{0,2},{2,0},{1,3},{3,1},{4,6},{6,4},{5,7},{7,5},{8,10},{10,8},{9,1... | collective-permute-start | bytes 589832 | tf_op jit(solution)/shard_map/ppermute | solution.py:69

commit v5 on v0

--- a/solution.py
+++ b/solution.py
@@ -1,6 +1,10 @@
+import functools
+
 import jax
 import jax.numpy as jnp
 from jax import lax
+from jax.experimental import pallas as pl
+from jax.experimental.pallas import tpu as pltpu
 from jax.sharding import PartitionSpec as P
 
 BINS = 8
@@ -14,7 +18,7 @@
     return jnp.sign(value) * jnp.maximum(jnp.abs(value) - level, 0.0)
 
 
-def on_device(patches, dictionary, threshold):
+def general(patches, dictionary, threshold):
     values = patches.astype(jnp.float32)
     local_sq = jnp.sum(values * values, axis=1)
     local_first = jnp.dot(patches, dictionary, preferred_element_type=jnp.float32)
@@ -64,6 +68,264 @@
     return (codes, gram, cross)
 
 
+def swap(value, axis):
+    return lax.ppermute(value, axis, [(0, 1), (1, 0)])
+
+
+def shift(value):
+    n = lax.axis_size("patch")
+    return lax.ppermute(value, "patch", [(i, (i + 1) % n) for i in range(n)])
+
+
+def after(value, earlier):
+    return lax.optimization_barrier((value, earlier))[0]
+
+
+f32, bf16 = jnp.float32, jnp.bfloat16
+contract_last = (((1,), (1,)), ((), ()))
+contract_first = (((0,), (0,)), ((), ()))
+
+
+def soft(value, level):
+    return jnp.where(value > level, value - level, jnp.where(value < -level, value + level, 0.0))
+
+
+def run(body, outs, scalars, arrays, scratch=()):
+    fast = pl.BlockSpec(memory_space=pltpu.VMEM)
+    slow = pl.BlockSpec(memory_space=pltpu.SMEM)
+    return pl.pallas_call(
+        body,
+        out_shape=outs,
+        in_specs=[slow] + [fast] * len(arrays),
+        out_specs=jax.tree.map(lambda _: fast, outs),
+        scratch_shapes=scratch,
+        compiler_params=pltpu.CompilerParams(vmem_limit_bytes=24 << 20),
+        cost_estimate=pl.CostEstimate(flops=1000, bytes_accessed=1000, transcendentals=0),
+    )(jnp.stack([x.astype(jnp.int32) for x in scalars]), *arrays)
+
+
+def first_body(_, mine, own, other, out):
+    atoms = own.shape[1]
+    for i, d in enumerate((own, other)):
+        out[:, i * atoms : (i + 1) * atoms] = jnp.dot(mine[...], d[...], preferred_element_type=f32).astype(bf16)
+
+
+def second_body(where, part, arrived, mine, scale, threshold, own, other, away, base, start):
+    atoms = own.shape[1]
+    block = atoms // 2
+    near = pl.multiple_of(where[0] * block, block)
+    far = pl.multiple_of((1 - where[0]) * block, block)
+    factor = scale[...]
+    summed = part[...].astype(f32) + arrived[...].astype(f32)
+    start[...] = soft(step_rate * (factor * summed), step_rate * threshold[...]).astype(bf16)
+    rebuilt = sum(
+        lax.dot_general(start[:, i * atoms : (i + 1) * atoms], d[...], contract_last, preferred_element_type=f32)
+        for i, d in enumerate((own, other))
+    )
+    misfit = (factor * mine[...].astype(f32) - rebuilt).astype(bf16)
+    for i, d in enumerate((own, other)):
+        columns = slice(i * block, (i + 1) * block)
+        away[:, columns] = jnp.dot(misfit, d[:, pl.ds(far, block)], preferred_element_type=f32).astype(bf16)
+    for i, d in enumerate((own, other)):
+        columns = slice(i * block, (i + 1) * block)
+        second = jnp.dot(misfit, d[:, pl.ds(near, block)], preferred_element_type=f32)
+        base[:, columns] = start[:, pl.ds(pl.multiple_of(i * atoms + near, block), block)].astype(f32) + (
+            step_rate * second
+        )
+
+
+def sums_body(n, where, *refs):
+    pieces, (gram, cross, send, lhs, sides, right) = refs[:-6], refs[-6:]
+    block = right.shape[1]
+    width = block // 2
+    place = pl.multiple_of(where[0] * block, block)
+    here = where[1] == 1
+    rows = lhs.shape[0] // n
+    for k in range(n):
+        chunks, (there, raw, scale) = pieces[k * 5 : k * 5 + 2], pieces[k * 5 + 2 : k * 5 + 5]
+        step = rows // 2
+        for c, x in enumerate(chunks):
+            window = slice(k * rows + c * step, k * rows + (c + 1) * step)
+            lhs[window, :] = x[...]
+            spot = pl.multiple_of(where[3 + k] * block, block)
+            right[window, :] = jnp.where(
+                here, x[:, pl.ds(place, block)], there[c * step : (c + 1) * step, pl.ds(spot, block)]
+            )
+        sides[k * rows : (k + 1) * rows, :] = (scale[...] * raw[...].astype(f32)).astype(bf16)
+    mine = pl.multiple_of(where[2] * width, width)
+    theirs = pl.multiple_of((1 - where[2]) * width, width)
+
+    def product(a, b):
+        return lax.dot_general(a, b, contract_first, preferred_element_type=f32)
+
+    send[:block, :] = product(lhs[:, block:], right[...]).astype(bf16)
+    part = product(sides[...], right[:, pl.ds(theirs, width)]).astype(bf16)
+    tall = part.shape[0] // 2
+    send[block:, :width] = part[:tall]
+    send[block:, width:] = part[tall:]
+    gram[...] = product(lhs[:, :block], right[...])
+    cross[...] = product(sides[...], right[:, pl.ds(mine, width)])
+
+
+def last_body(count, where, *refs):
+    gram_in, cross_in, sent = refs[:3]
+    halves = (refs[3:8], refs[8:13])
+    gram, cross, lhs, sides, right = refs[13:]
+    block = right.shape[1]
+    width = block // 2
+    rows = lhs.shape[0] // 2
+    step = rows // 2
+    here = where[1] == 1
+    for h, (a, b, there, raw, scale) in enumerate(halves):
+        place = pl.multiple_of((where[0] if h == 0 else 1 - where[0]) * block, block)
+        for c, x in enumerate((a, b)):
+            window = slice(h * rows + c * step, h * rows + (c + 1) * step)
+            lhs[window, :] = x[:, h * block : (h + 1) * block]
+            right[window, :] = jnp.where(here, x[:, pl.ds(place, block)], there[c * step : (c + 1) * step, :])
+        sides[h * rows : (h + 1) * rows, :] = (scale[...] * raw[...].astype(f32)).astype(bf16)
+    mine = pl.multiple_of(where[2] * width, width)
+
+    def product(a, b):
+        return lax.dot_general(a, b, contract_first, preferred_element_type=f32)
+
+    part = gram_in[...] + sent[:block, :].astype(f32)
+    gram[...] = (part + product(lhs[...], right[...])) * (1.0 / count)
+    tall = cross.shape[0] // 2
+    part = product(sides[...], right[:, pl.ds(mine, width)])
+    for i in range(2):
+        window = slice(i * tall, (i + 1) * tall)
+        total = part[window] + cross_in[window, :] + sent[block:, i * width : (i + 1) * width].astype(f32)
+        cross[window, :] = total * (1.0 / count)
+
+
+def group_near(level, half, block):
+    atoms = 2 * block
+    parts = [lax.dynamic_slice_in_dim(level, i * atoms + half * block, block, 1) for i in range(2)]
+    return jnp.concatenate(parts, 1)
+
+
+def paired(patches, dictionary, threshold):
+    n_patch = lax.axis_size("patch")
+    plane = lax.axis_index("patch")
+    core = lax.axis_index("atom")
+    half = lax.axis_index("feat")
+    count = patches.shape[0] * n_patch
+    length = patches.shape[1]
+    rows = patches.shape[0] // 2
+    atoms = dictionary.shape[1]
+    block = atoms // 2
+    width = block // 2
+    step = rows // 2
+
+    def blocks(array, which):
+        return lax.dynamic_slice_in_dim(array, which * block, block, 1)
+
+    mine = lax.dynamic_slice_in_dim(patches, core * rows, rows, 0)
+    dictionary2 = swap(dictionary, "atom")
+    raw_of = [mine]
+    for k in range(1, n_patch):
+        raw_of.append(shift(raw_of[-1]))
+    windows = [slice(c * step, (c + 1) * step) for c in range(2)]
+    parts, others = [], []
+    done = ()
+    for w in windows:
+        piece = after(mine[w], done)
+        part = run(
+            first_body, jax.ShapeDtypeStruct((step, 2 * atoms), bf16), (half,), (piece, dictionary, dictionary2)
+        )
+        parts.append(part)
+        others.append(swap(part, "feat"))
+        done = part
+    values = after(mine, parts[0]).astype(f32)
+    local_sq = jnp.sum(values * values, axis=1)
+    energy = local_sq + swap(local_sq, "feat")
+    scale = lax.rsqrt(energy / (BINS * VOXELS) + 1e-05)
+    scale_of = [scale[:, None]]
+    for k in range(1, n_patch):
+        scale_of.append(shift(scale_of[-1][:, 0])[:, None])
+    level = threshold[None, :]
+    level = jnp.concatenate([level, swap(after(level, parts[1]), "atom")], 1)
+
+    base, backs = [], []
+    for c, w in enumerate(windows):
+        away, so_far = run(
+            second_body,
+            (jax.ShapeDtypeStruct((step, atoms), bf16), jax.ShapeDtypeStruct((step, atoms), f32)),
+            (half,),
+            (parts[c], after(others[c], raw_of[c + 1]), mine[w], scale_of[0][w], level, dictionary, dictionary2),
+            [pltpu.VMEM((step, 2 * atoms), bf16)],
+        )
+        backs.append(swap(away, "feat"))
+        base.append(so_far)
+
+    codes_of = []
+    done = ()
+    for c in range(2):
+        back = after(backs[c], done).astype(f32)
+        codes_of.append(soft(base[c] + step_rate * back, step_rate * group_near(level, half, block)).astype(bf16))
+        done = (codes_of[c], raw_of[-1])
+
+    rings = [codes_of]
+    for k in range(1, n_patch):
+        rings.append([shift(x) for x in rings[-1]])
+    inside = jnp.concatenate(codes_of, 0)
+    outside = swap(inside, "feat")
+
+    home_half = plane % 2
+    place = jnp.where(core == plane // 2, 0, 1)
+    over = [(q * 2 + q % 2, q * 2 + 1 - q % 2) for q in range(n_patch)]
+    below = (plane + n_patch - 1) % n_patch
+    place_below = jnp.where(core == below // 2, 0, 1)
+    down = [
+        (q * 2 + 1 - (q - 1) % n_patch % 2, (q - 1) % n_patch * 2 + 1 - (q - 1) % n_patch % 2) for q in range(n_patch)
+    ]
+    there = [outside]
+    for k in range(1, n_patch - 1):
+        there.append(
+            lax.ppermute(jnp.concatenate([blocks(x, place) for x in rings[k]], 0), ("patch", "feat"), over)
+        )
+    final = lax.ppermute(blocks(outside, place_below), ("patch", "feat"), down)
+    final2 = swap(final, "atom")
+
+    both = [jnp.where(half == 0, inside, outside), jnp.where(half == 0, outside, inside)]
+    upper = jnp.concatenate([x[:, :block] for x in both], 1)
+    lower = swap(jnp.concatenate([x[:, block:] for x in both], 1), "atom")
+    lower = after(lower, rings[1])
+    codes = jnp.where(
+        core == 0, jnp.concatenate([upper, lower], 0), jnp.concatenate([lower, upper], 0)
+    )
+
+    n = n_patch - 1
+    at_home = half == home_half
+    zero = jnp.zeros_like(place)
+    pieces = []
+    for k in range(n):
+        pieces += [*rings[k], there[k], raw_of[k], scale_of[k]]
+    gram, cross, send = run(
+        functools.partial(sums_body, n),
+        (
+            jax.ShapeDtypeStruct((block, block), f32),
+            jax.ShapeDtypeStruct((length, width), f32),
+            jax.ShapeDtypeStruct((block + length // 2, block), bf16),
+        ),
+        (place, at_home, core, place) + (zero,) * (n - 1),
+        pieces,
+        [pltpu.VMEM((n * rows, size), bf16) for size in (atoms, length, block)],
+    )
+    sent = swap(send, "atom")
+    raw2, scale2 = swap(after(raw_of[-1], rings[1]), "atom"), swap(after(scale_of[-1][:, 0], rings[1]), "atom")
+    early, late = [swap(x, "atom") for x in rings[-1]]
+    early, codes = lax.optimization_barrier((early, codes))
+    gram, cross = run(
+        functools.partial(last_body, count),
+        (jax.ShapeDtypeStruct((block, block), f32), jax.ShapeDtypeStruct((length, width), f32)),
+        (place, at_home, core),
+        (gram, cross, sent, *rings[-1], final, raw_of[-1], scale_of[-1], early, late, final2, raw2, scale2[:, None]),
+        [pltpu.VMEM((2 * rows, size), bf16) for size in (block, length, block)],
+    )
+    return (codes, gram, cross)
+
+
 def solution(mesh):
     in_specs = (P(("slab", "patch"), "feat"), P("feat", "atom"), P("atom"))
     out_specs = (
@@ -71,6 +333,8 @@
         P(("slab", "atom", "feat"), "patch"),
         P(("slab", "feat"), ("patch", "atom")),
     )
+    sizes = mesh.shape
+    small = sizes["feat"] == 2 and sizes["atom"] == 2 and sizes["patch"] == 4
     return jax.shard_map(
-        on_device, mesh=mesh, in_specs=in_specs, out_specs=out_specs, check_vma=False
-    )
+        paired if small else general, mesh=mesh, in_specs=in_specs, out_specs=out_specs, check_vma=False
+    )

time: 268 us -> 124 us (0.46)
  waiting for transfers between devices: 209 us -> 64.8 us
  starting transfers between devices: 0.25 us -> 28.3 us
  Pallas kernels: 0 us -> 19.2 us
  matrix products: 17 us -> 0 us
  between operations: 14.1 us -> 1 us
  local copies, waits for them, and re-layouts: 13.4 us -> 5.63 us
  blocking collectives: 5.83 us -> 0 us
  other arithmetic: 8.07 us -> 4.17 us
    psum x3 -> x0, waiting for transfers between devices: 120 us -> none  [the longest x1 52.8 us: on_device(): second = lax.psum(local_second, 'feat')]
    reduce_scatter x2 -> x0, waiting for transfers between devices: 78.8 us -> none  [the longest x1 43.1 us: on_device(): lax.psum_scatter(gram_part.astype(jnp.bfloat16), 'patch', scatter_dimensi...]
    ppermute x0 -> x30, waiting for transfers between devices: none -> 64.8 us  [the longest x12 49.1 us: shift(): return lax.ppermute(value, 'patch', [(i, (i + 1) % n) for i in range(n)])]
    ppermute x0 -> x30, starting transfers between devices: none -> 28.3 us  [the longest x12 10.5 us: shift(): return lax.ppermute(value, 'patch', [(i, (i + 1) % n) for i in range(n)])]
    pallas_call x0 -> x6, Pallas kernels: none -> 19.2 us  [run(): pl.pallas_call(body, out_shape=outs, in_specs=[slow] + [fast] * len(array...]
    dot_general x5 -> x0, matrix products: 17 us -> none  [the longest x1 3.99 us: on_device(): lax.dot_general(start, dictionary, contract_last, preferred_element_type=...]
    all_gather x1 -> x0, waiting for transfers between devices: 9.91 us -> none  [on_device(): codes_whole = lax.all_gather(codes, 'atom', axis=1, tiled=True)]
    psum x1 -> x0, blocking collectives: 5.83 us -> none  [on_device(): summed, energy = lax.psum((local_first, local_sq), 'feat')]
  transfers between devices with their start and end apart: 6 -> 30, of which waited for: 6 -> 13; matrix products, arithmetic and copies ran while one was open for 2% -> 7% of each run, Pallas kernels for 0% -> 10%
where the time goes in v5:
time: 124 us; the launch traced here: 123 us
  waiting for transfers between devices  64.8 us (52%)
  starting transfers between devices  28.3 us (23%)
  Pallas kernels  19.2 us (15%)
  local copies, waits for them, and re-layouts  5.63 us (5%)
  other arithmetic  4.17 us (3%)
    ppermute x12, waiting for transfers between devices, shift(): return lax.ppermute(value, 'patch', [(i, (i + 1) % n) for i in range(n)])  49.1 us
    pallas_call x6, Pallas kernels, run(): pl.pallas_call(body, out_shape=outs, in_specs=[slow] + [fast] * len(array...  19.2 us
    ppermute x15, waiting for transfers between devices, swap(): return lax.ppermute(value, axis, [(0, 1), (1, 0)])  12.8 us
    ppermute x12, starting transfers between devices, shift(): return lax.ppermute(value, 'patch', [(i, (i + 1) % n) for i in range(n)])  10.5 us
    ppermute x15, starting transfers between devices, swap(): return lax.ppermute(value, axis, [(0, 1), (1, 0)])  8.58 us
    ppermute x2, starting transfers between devices, paired(): lax.ppermute(jnp.concatenate([blocks(x, place) for x in rings[k]], 0), ('...  5.82 us
    ppermute x1, starting transfers between devices, paired(): final = lax.ppermute(blocks(outside, place_below), ('patch', 'feat'), down)  3.34 us
    ppermute x2, waiting for transfers between devices, paired(): lax.ppermute(jnp.concatenate([blocks(x, place) for x in rings[k]], 0), ('...  2.94 us
  transfers between devices with their start and end apart: 30, of which 13 were waited for; matrix products, arithmetic and copies ran while one was open for 7% of the time, Pallas kernels for 10%

profile of v5, /device:TPU:0, one launch (start us, length us, event | category | flops | bytes accessed | tf_op | source)
XLA Modules:
  0.0 123.1 jit_solution(218800865715427133)
XLA Ops:
  0.6 0.0 copy-start
  0.7 0.5 collective-permute-start
  1.2 0.6 copy-done
  1.7 0.2 constant_dynamic-slice_fusion.5
  1.9 0.2 copy.17.refs_3_
  2.1 3.1 %collective-permute-start.2 = (bf16[192,864]{1,0:T(8,128)(2,1)S(1)}, bf16[192,864]{1,0:T(8,128)(2,1)S(1)}, u32[]{:S(2)}, u32[]{:S(2)}) collective-permute-start(bf16[192,864]{1,0:T(8,128)(2,1)S(1)} %copy.17.refs_3_), channel_id=1, source_target_pairs={{0,4},{4,8},{8,12},{12,0},{1,5},{5,9},{9,13},{13,1},{2,6},{6,10},{... | collective-permute-start | bytes 995336 | tf_op jit(solution)/shard_map/ppermute | solution.py:77
  5.2 10.1 %collective-permute-done.2.refs_8_ = bf16[192,864]{1,0:T(8,128)(2,1)S(1)} collective-permute-done((bf16[192,864]{1,0:T(8,128)(2,1)S(1)}, bf16[192,864]{1,0:T(8,128)(2,1)S(1)}, u32[]{:S(2)}, u32[]{:S(2)}) %collective-permute-start.2) | collective-permute-done | bytes 331808 | tf_op jit(solution)/shard_map/ppermute | solution.py:77
  15.4 3.1 %shard_map.58.part = bf16[96,2048]{1,0:T(8,128)(2,1)} custom-call(s32[1]{0:T(128)} %bitcast._.where, bf16[96,864]{1,0:T(8,128)(2,1)S(1)} %get-tuple-element.50.mine, bf16[864,1024]{1,0:T(8,128)(2,1)S(1)} %copy-done.1, bf16[864,1024]{1,0:T(8,128)(2,1)} %collective-permute-done.other), custom_call_target="tpu_custom_call" | custom-call | flops 1000 | bytes 1000 | tf_op jit(solution)/shard_map/pallas_call | solution.py:96
  18.4 0.2 multiply_reduce_fusion
  18.6 1.5 %collective-permute-start.3 = (f32[192]{0:T(256)S(1)}, f32[192]{0:T(256)S(1)}, u32[]{:S(2)}, u32[]{:S(2)}) collective-permute-start(f32[192]{0:T(256)S(1)} %multiply_reduce_fusion), channel_id=1, source_target_pairs={{0,1},{1,0},{2,3},{3,2},{4,5},{5,4},{6,7},{7,6},{8,9},{9,8},{10,11... | collective-permute-start | bytes 2312 | tf_op jit(solution)/shard_map/ppermute | solution.py:72
  20.1 6.3 %collective-permute-done.11.refs_13_ = bf16[192,864]{1,0:T(8,128)(2,1)} collective-permute-done((bf16[192,864]{1,0:T(8,128)(2,1)S(1)}, bf16[192,864]{1,0:T(8,128)(2,1)}, u32[]{:S(2)}, u32[]{:S(2)}) %collective-permute-start.11) | collective-permute-done | bytes 331808 | tf_op jit(solution)/shard_map/ppermute | solution.py:77
  26.5 1.2 %collective-permute-start.1 = (bf16[96,2048]{1,0:T(8,128)(2,1)}, bf16[96,2048]{1,0:T(8,128)(2,1)}, u32[]{:S(2)}, u32[]{:S(2)}) collective-permute-start(bf16[96,2048]{1,0:T(8,128)(2,1)} %shard_map.58.part), channel_id=1, source_target_pairs={{0,1},{1,0},{2,3},{3,2},{4,5},{5,4},{6,7},{7,6},{8,9},{9,8},{10,11... | collective-permute-start | bytes 1179656 | tf_op jit(solution)/shard_map/ppermute | solution.py:72
  27.7 2.3 %shard_map.59.part = bf16[96,2048]{1,0:T(8,128)(2,1)S(1)} custom-call(s32[1]{0:T(128)} %bitcast._.where, bf16[96,864]{1,0:T(8,128)(2,1)S(1)} %get-tuple-element.25.mine, bf16[864,1024]{1,0:T(8,128)(2,1)S(1)} %copy-done.1, bf16[864,1024]{1,0:T(8,128)(2,1)} %collective-permute-done.other), custom_call_target="tpu_custom_call" | custom-call | flops 1000 | bytes 1000 | tf_op jit(solution)/shard_map/pallas_call | solution.py:96
  30.0 0.8 collective-permute-start.10
  30.8 0.1 slice_bitcast_fusion
  30.9 0.7 copy.11.scale
  31.6 0.7 copy.10.scale
  32.4 0.0 copy-start.7
  32.4 6.4 %collective-permute-done.1.arrived = bf16[96,2048]{1,0:T(8,128)(2,1)} collective-permute-done((bf16[96,2048]{1,0:T(8,128)(2,1)}, bf16[96,2048]{1,0:T(8,128)(2,1)}, u32[]{:S(2)}, u32[]{:S(2)}) %collective-permute-start.1) | collective-permute-done | bytes 393248 | tf_op jit(solution)/shard_map/ppermute | solution.py:72
  38.8 0.8 copy-done.8
  39.6 3.8 %shard_map.60 = (bf16[96,1024]{1,0:T(8,128)(2,1)S(1)}, f32[96,1024]{1,0:T(8,128)S(1)}) custom-call(s32[1]{0:T(128)} %bitcast._.where, bf16[96,2048]{1,0:T(8,128)(2,1)} %shard_map.58.part, bf16[96,2048]{1,0:T(8,128)(2,1)} %collective-permute-done.1.arrived, bf16[96,864]{1,0:T(8,128)(2,1)S(1)} %get-tuple-element.50.mine, f32[96,1]{1,0:T(8,128)S(1)} %copy-done.8, ...), custom_call_target="tpu_custom_call" | custom-call | flops 1000 | bytes 1000 | tf_op jit(solution)/shard_map/pallas_call | solution.py:96
  43.5 1.3 %collective-permute-start.5 = (bf16[96,1024]{1,0:T(8,128)(2,1)S(1)}, bf16[96,1024]{1,0:T(8,128)(2,1)S(1)}, u32[]{:S(2)}, u32[]{:S(2)}) collective-permute-start(bf16[96,1024]{1,0:T(8,128)(2,1)S(1)} %get-tuple-element.28), channel_id=1, source_target_pairs={{0,1},{1,0},{2,3},{3,2},{4,5},{5,4},{6,7},{7,6},{8,9},{9,8},{10,11... | collective-permute-start | bytes 589832 | tf_op jit(solution)/shard_map/ppermute | solution.py:72
  44.8 1.8 %collective-permute-done.10.arrived = bf16[96,2048]{1,0:T(8,128)(2,1)} collective-permute-done((bf16[96,2048]{1,0:T(8,128)(2,1)S(1)}, bf16[96,2048]{1,0:T(8,128)(2,1)}, u32[]{:S(2)}, u32[]{:S(2)}) %collective-permute-start.10) | collective-permute-done | bytes 393248 | tf_op jit(solution)/shard_map/ppermute | solution.py:72
  46.7 3.7 %shard_map.61 = (bf16[96,1024]{1,0:T(8,128)(2,1)S(1)}, f32[96,1024]{1,0:T(8,128)S(1)}) custom-call(s32[1]{0:T(128)} %bitcast._.where, bf16[96,2048]{1,0:T(8,128)(2,1)S(1)} %shard_map.59.part, bf16[96,2048]{1,0:T(8,128)(2,1)} %collective-permute-done.10.arrived, bf16[96,864]{1,0:T(8,128)(2,1)S(1)} %get-tuple-element.25.mine, f32[96,1]{1,0:T(8,128)S(1)} %copy-done.7, ...), custom_call_target="tpu_custom_call" | custom-call | flops 1000 | bytes 1000 | tf_op jit(solution)/shard_map/pallas_call | solution.py:96
  50.4 1.1 collective-permute-start.12
  51.5 0.1 select_convert_fusion.1.refs_0_
  51.6 4.5 %collective-permute-done.12 = bf16[96,1024]{1,0:T(8,128)(2,1)S(1)} collective-permute-done((bf16[96,1024]{1,0:T(8,128)(2,1)S(1)}, bf16[96,1024]{1,0:T(8,128)(2,1)S(1)}, u32[]{:S(2)}, u32[]{:S(2)}) %collective-permute-start.12) | collective-permute-done | bytes 196640 | tf_op jit(solution)/shard_map/ppermute | solution.py:72
  56.2 0.1 select_convert_fusion.refs_1_
  56.3 0.1 collective-permute-start.16
  56.4 0.3 collective-permute-start.6
  56.6 4.4 %collective-permute-start.18 = (f32[192]{0:T(256)S(1)}, f32[192]{0:T(256)S(1)}, u32[]{:S(2)}, u32[]{:S(2)}) collective-permute-start(f32[192]{0:T(256)S(1)} %add_rsqrt_fusion), channel_id=1, source_target_pairs={{0,4},{4,8},{8,12},{12,0},{1,5},{5,9},{9,13},{13,1},{2,6},{6,10},{... | collective-permute-start | bytes 2312 | tf_op jit(solution)/shard_map/ppermute | solution.py:77
  61.0 5.0 %collective-permute-done.18 = f32[192]{0:T(256)S(1)} collective-permute-done((f32[192]{0:T(256)S(1)}, f32[192]{0:T(256)S(1)}, u32[]{:S(2)}, u32[]{:S(2)}) %collective-permute-start.18) | collective-permute-done | bytes 800 | tf_op jit(solution)/shard_map/ppermute | solution.py:77
  66.0 0.1 stack.34.where
  66.1 0.1 copy.12.refs_4_
  66.2 0.1 copy.13.refs_9_
  66.3 5.0 %collective-permute-done.21 = f32[192]{0:T(256)S(1)} collective-permute-done((f32[192]{0:T(256)S(1)}, f32[192]{0:T(256)S(1)}, u32[]{:S(2)}, u32[]{:S(2)}) %collective-permute-start.21) | collective-permute-done | bytes 800 | tf_op jit(solution)/shard_map/ppermute | solution.py:77
  71.4 0.8 copy.14.refs_14_
  72.1 0.0 copy-start.4
  72.2 0.0 copy-start.6
  72.2 1.1 collective-permute-start.14
  73.3 0.1 collective-permute-start.7
  73.4 2.9 %collective-permute-start.17 = (bf16[192,512]{1,0:T(8,128)(2,1)S(1)}, bf16[192,512]{1,0:T(8,128)(2,1)S(1)}, u32[]{:S(2)}, u32[]{:S(2)}) collective-permute-start(bf16[192,512]{1,0:T(8,128)(2,1)S(1)} %pad_maximum_fusion.2), channel_id=1, source_target_pairs={{0,1},{5,4},{8,9},{13,12},{2,3},{7,6},{10,11},{15,14},{16,17},{21,... | collective-permute-start | bytes 589832 | tf_op jit(solution)/shard_map/ppermute | solution.py:285
  76.3 4.4 %collective-permute-done.19.refs_11_ = bf16[96,1024]{1,0:T(8,128)(2,1)S(1)} collective-permute-done((bf16[96,1024]{1,0:T(8,128)(2,1)S(1)}, bf16[96,1024]{1,0:T(8,128)(2,1)S(1)}, u32[]{:S(2)}, u32[]{:S(2)}) %collective-permute-start.19) | collective-permute-done | bytes 196640 | tf_op jit(solution)/shard_map/ppermute | solution.py:77
  80.8 2.1 %collective-permute-done.7.refs_10_ = bf16[96,1024]{1,0:T(8,128)(2,1)S(1)} collective-permute-done((bf16[96,1024]{1,0:T(8,128)(2,1)S(1)}, bf16[96,1024]{1,0:T(8,128)(2,1)S(1)}, u32[]{:S(2)}, u32[]{:S(2)}) %collective-permute-start.7) | collective-permute-done | bytes 196640 | tf_op jit(solution)/shard_map/ppermute | solution.py:77
  82.9 2.9 %collective-permute-start.20 = (bf16[192,512]{1,0:T(8,128)(2,1)S(1)}, bf16[192,512]{1,0:T(8,128)(2,1)S(1)}, u32[]{:S(2)}, u32[]{:S(2)}) collective-permute-start(bf16[192,512]{1,0:T(8,128)(2,1)S(1)} %pad_maximum_fusion.3), channel_id=1, source_target_pairs={{0,1},{5,4},{8,9},{13,12},{2,3},{7,6},{10,11},{15,14},{16,17},{21,... | collective-permute-start | bytes 589832 | tf_op jit(solution)/shard_map/ppermute | solution.py:285
  85.8 0.2 broadcast_select_fusion.1
  86.0 2.9 %collective-permute-done.20.refs_12_ = bf16[192,512]{1,0:T(8,128)(2,1)S(1)} collective-permute-done((bf16[192,512]{1,0:T(8,128)(2,1)S(1)}, bf16[192,512]{1,0:T(8,128)(2,1)S(1)}, u32[]{:S(2)}, u32[]{:S(2)}) %collective-permute-start.20) | collective-permute-done | bytes 196640 | tf_op jit(solution)/shard_map/ppermute | solution.py:285
  89.0 3.1 %shard_map.62 = (f32[512,512]{1,0:T(8,128)S(1)}, f32[864,256]{1,0:T(8,128)S(1)}, bf16[944,512]{1,0:T(8,128)(2,1)}) custom-call(s32[6]{0:T(128)S(1)} %stack.34.where, bf16[96,1024]{1,0:T(8,128)(2,1)S(1)} %select_convert_fusion.1.refs_0_, bf16[96,1024]{1,0:T(8,128)(2,1)S(1)} %select_convert_fusion.refs_1_, ...), custom_call_target="tpu_custom_call" | custom-call | flops 1000 | bytes 1000 | tf_op jit(solution)/shard_map/pallas_call | solution.py:96
  92.1 0.9 fusion.3
  93.0 0.8 pad_maximum_fusion.1
  93.8 0.4 collective-permute-start.15
  94.2 3.3 %collective-permute-start.24 = (bf16[192,512]{1,0:T(8,128)(2,1)S(1)}, bf16[192,512]{1,0:T(8,128)(2,1)S(1)}, u32[]{:S(2)}, u32[]{:S(2)}) collective-permute-start(bf16[192,512]{1,0:T(8,128)(2,1)S(1)} %constant_dynamic-slice_fusion), channel_id=1, source_target_pairs={{0,12},{5,1},{8,4},{13,9},{2,14},{7,3},{10,6},{15,11},{16,28},{21,... | collective-permute-start | bytes 589832 | tf_op jit(solution)/shard_map/ppermute | solution.py:287
  97.6 0.1 collective-permute-start.25
  97.6 5.4 %collective-permute-done.25 = f32[192]{0:T(256)S(1)} collective-permute-done((f32[192]{0:T(256)S(1)}, f32[192]{0:T(256)S(1)}, u32[]{:S(2)}, u32[]{:S(2)}) %collective-permute-start.25) | collective-permute-done | bytes 800 | tf_op jit(solution)/shard_map/ppermute | solution.py:77
  103.0 1.5 %collective-permute-start.8 = (bf16[96,1024]{1,0:T(8,128)(2,1)S(1)}, bf16[96,1024]{1,0:T(8,128)(2,1)}, u32[]{:S(2)}, u32[]{:S(2)}) collective-permute-start(bf16[96,1024]{1,0:T(8,128)(2,1)S(1)} %collective-permute-done.7.refs_10_), channel_id=1, source_target_pairs={{0,4},{4,8},{8,12},{12,0},{1,5},{5,9},{9,13},{13,1},{2,6},{6,10},{... | collective-permute-start | bytes 589832 | tf_op jit(solution)/shard_map/ppermute | solution.py:77
  104.4 1.1 collective-permute-start.23
  105.6 7.0 %collective-permute-done.8.refs_3_ = bf16[96,1024]{1,0:T(8,128)(2,1)} collective-permute-done((bf16[96,1024]{1,0:T(8,128)(2,1)S(1)}, bf16[96,1024]{1,0:T(8,128)(2,1)}, u32[]{:S(2)}, u32[]{:S(2)}) %collective-permute-start.8) | collective-permute-done | bytes 196640 | tf_op jit(solution)/shard_map/ppermute | solution.py:77
  112.6 3.8 %collective-permute-done.23.refs_4_ = bf16[96,1024]{1,0:T(8,128)(2,1)} collective-permute-done((bf16[96,1024]{1,0:T(8,128)(2,1)S(1)}, bf16[96,1024]{1,0:T(8,128)(2,1)}, u32[]{:S(2)}, u32[]{:S(2)}) %collective-permute-start.23) | collective-permute-done | bytes 196640 | tf_op jit(solution)/shard_map/ppermute | solution.py:77
  116.4 0.5 collective-permute-start.26
  116.9 0.1 pad_add_fusion.where
  117.0 0.1 copy.15.refs_7_
  117.1 0.1 copy.16.refs_12_
  117.3 2.6 %maximum_select_fusion = bf16[384,1024]{1,0:T(8,128)(2,1)} fusion(bf16[192,1024]{1,0:T(8,128)(2,1)} %collective-permute-done.15, bf16[192,512]{1,0:T(8,128)(2,1)} %get-tuple-element.58, bf16[192,512]{1,0:T(8,128)(2,1)} %get-tuple-element.45, pred[]{:T(512)S(6)} %eq.19), kind=kLoop, calls=%fused_computation | loop fusion | flops 5111808 | bytes 1572865 | tf_op jit(solution)/shard_map/jit(_where)/select_n | solution.py:294
  119.9 3.2 %shard_map.63 = (f32[512,512]{1,0:T(8,128)}, f32[864,256]{1,0:T(8,128)}) custom-call(s32[3]{0:T(128)S(1)} %pad_add_fusion.where, f32[512,512]{1,0:T(8,128)S(1)} %get-tuple-element.35.refs_0_, f32[864,256]{1,0:T(8,128)S(1)} %copy-done.3, bf16[944,512]{1,0:T(8,128)(2,1)S(1)} %collective-permute-done.22.refs_2_, ...), custom_call_target="tpu_custom_call" | custom-call | flops 1000 | bytes 1000 | tf_op jit(solution)/shard_map/pallas_call | solution.py:96
  (55 shorter events, 0.3 us)
Async XLA Ops:
  0.6 1.1 copy-start
  0.6 14.7 %copy-start.1 = (bf16[864,1024]{1,0:T(8,128)(2,1)S(1)}, bf16[864,1024]{1,0:T(8,128)(2,1)}, u32[]{:S(2)}) copy-start(bf16[864,1024]{1,0:T(8,128)(2,1)} %own.7) | copy-start | bytes 5308420
  0.7 14.7 %collective-permute-start = (bf16[864,1024]{1,0:T(8,128)(2,1)}, bf16[864,1024]{1,0:T(8,128)(2,1)}, u32[]{:S(2)}, u32[]{:S(2)}) collective-permute-start(bf16[864,1024]{1,0:T(8,128)(2,1)} %own.7), channel_id=1, source_target_pairs={{0,2},{2,0},{1,3},{3,1},{4,6},{6,4},{5,7},{7,5},{8,10},{10,8},{9,1... | collective-permute-start | bytes 5308424 | tf_op jit(solution)/shard_map/ppermute | solution.py:72
  2.1 13.2 %collective-permute-start.2 = (bf16[192,864]{1,0:T(8,128)(2,1)S(1)}, bf16[192,864]{1,0:T(8,128)(2,1)S(1)}, u32[]{:S(2)}, u32[]{:S(2)}) collective-permute-start(bf16[192,864]{1,0:T(8,128)(2,1)S(1)} %copy.17.refs_3_), channel_id=1, source_target_pairs={{0,4},{4,8},{8,12},{12,0},{1,5},{5,9},{9,13},{13,1},{2,6},{6,10},{... | collective-permute-start | bytes 995336 | tf_op jit(solution)/shard_map/ppermute | solution.py:77
  15.3 3.1 %copy-start.5 = (bf16[192,864]{1,0:T(8,128)(2,1)}, bf16[192,864]{1,0:T(8,128)(2,1)S(1)}, u32[]{:S(2)}) copy-start(bf16[192,864]{1,0:T(8,128)(2,1)S(1)} %collective-permute-done.2.refs_8_) | copy-start | bytes 995332
  15.3 11.2 %collective-permute-start.11 = (bf16[192,864]{1,0:T(8,128)(2,1)S(1)}, bf16[192,864]{1,0:T(8,128)(2,1)}, u32[]{:S(2)}, u32[]{:S(2)}) collective-permute-start(bf16[192,864]{1,0:T(8,128)(2,1)S(1)} %collective-permute-done.2.refs_8_), channel_id=1, source_target_pairs={{0,4},{4,8},{8,12},{12,0},{1,5},{5,9},{9,13},{13,1},{2,6},{6,10},{... | collective-permute-start | bytes 995336 | tf_op jit(solution)/shard_map/ppermute | solution.py:77
  18.6 12.2 %collective-permute-start.3 = (f32[192]{0:T(256)S(1)}, f32[192]{0:T(256)S(1)}, u32[]{:S(2)}, u32[]{:S(2)}) collective-permute-start(f32[192]{0:T(256)S(1)} %multiply_reduce_fusion), channel_id=1, source_target_pairs={{0,1},{1,0},{2,3},{3,2},{4,5},{5,4},{6,7},{7,6},{8,9},{9,8},{10,11... | collective-permute-start | bytes 2312 | tf_op jit(solution)/shard_map/ppermute | solution.py:72
  26.5 25.2 %collective-permute-start.13 = (bf16[192,864]{1,0:T(8,128)(2,1)}, bf16[192,864]{1,0:T(8,128)(2,1)}, u32[]{:S(2)}, u32[]{:S(2)}) collective-permute-start(bf16[192,864]{1,0:T(8,128)(2,1)} %collective-permute-done.11.refs_13_), channel_id=1, source_target_pairs={{0,4},{4,8},{8,12},{12,0},{1,5},{5,9},{9,13},{13,1},{2,6},{6,10},{... | collective-permute-start | bytes 995336 | tf_op jit(solution)/shard_map/ppermute | solution.py:77
  26.5 12.4 %collective-permute-start.1 = (bf16[96,2048]{1,0:T(8,128)(2,1)}, bf16[96,2048]{1,0:T(8,128)(2,1)}, u32[]{:S(2)}, u32[]{:S(2)}) collective-permute-start(bf16[96,2048]{1,0:T(8,128)(2,1)} %shard_map.58.part), channel_id=1, source_target_pairs={{0,1},{1,0},{2,3},{3,2},{4,5},{5,4},{6,7},{7,6},{8,9},{9,8},{10,11... | collective-permute-start | bytes 1179656 | tf_op jit(solution)/shard_map/ppermute | solution.py:72
  27.7 3.1 %copy-start.9 = (f32[1024]{0:T(1024)S(1)}, f32[1024]{0:T(1024)}, u32[]{:S(2)}) copy-start(f32[1024]{0:T(1024)} %param.5) | copy-start | bytes 12292
  30.0 16.7 %collective-permute-start.10 = (bf16[96,2048]{1,0:T(8,128)(2,1)S(1)}, bf16[96,2048]{1,0:T(8,128)(2,1)}, u32[]{:S(2)}, u32[]{:S(2)}) collective-permute-start(bf16[96,2048]{1,0:T(8,128)(2,1)S(1)} %shard_map.59.part), channel_id=1, source_target_pairs={{0,1},{1,0},{2,3},{3,2},{4,5},{5,4},{6,7},{7,6},{8,9},{9,8},{10,11... | collective-permute-start | bytes 1179656 | tf_op jit(solution)/shard_map/ppermute | solution.py:72
  30.8 1.5 %collective-permute-start.4 = (f32[1,1024]{1,0:T(1,128)S(1)}, f32[1,1024]{1,0:T(1,128)S(1)}, u32[]{:S(2)}, u32[]{:S(2)}) collective-permute-start(f32[1,1024]{1,0:T(1,128)S(1)} %bitcast.16), channel_id=1, source_target_pairs={{0,2},{2,0},{1,3},{3,1},{4,6},{6,4},{5,7},{7,5},{8,10},{10,8},{9,1... | collective-permute-start | bytes 12296 | tf_op jit(solution)/shard_map/ppermute | solution.py:72
  32.4 14.3 %copy-start.7 = (f32[96,1]{1,0:T(8,128)S(1)}, f32[96,1]{1,0:T(8,128)}, u32[]{:S(2)}) copy-start(f32[96,1]{1,0:T(8,128)} %copy.11.scale) | copy-start | bytes 1156
  38.8 0.8 copy-start.8
  43.5 8.0 %collective-permute-start.5 = (bf16[96,1024]{1,0:T(8,128)(2,1)S(1)}, bf16[96,1024]{1,0:T(8,128)(2,1)S(1)}, u32[]{:S(2)}, u32[]{:S(2)}) collective-permute-start(bf16[96,1024]{1,0:T(8,128)(2,1)S(1)} %get-tuple-element.28), channel_id=1, source_target_pairs={{0,1},{1,0},{2,3},{3,2},{4,5},{5,4},{6,7},{7,6},{8,9},{9,8},{10,11... | collective-permute-start | bytes 589832 | tf_op jit(solution)/shard_map/ppermute | solution.py:72
  50.4 5.7 %collective-permute-start.12 = (bf16[96,1024]{1,0:T(8,128)(2,1)S(1)}, bf16[96,1024]{1,0:T(8,128)(2,1)S(1)}, u32[]{:S(2)}, u32[]{:S(2)}) collective-permute-start(bf16[96,1024]{1,0:T(8,128)(2,1)S(1)} %get-tuple-element.31), channel_id=1, source_target_pairs={{0,1},{1,0},{2,3},{3,2},{4,5},{5,4},{6,7},{7,6},{8,9},{9,8},{10,11... | collective-permute-start | bytes 589832 | tf_op jit(solution)/shard_map/ppermute | solution.py:72
  56.3 17.0 %collective-permute-start.16 = (bf16[96,1024]{1,0:T(8,128)(2,1)S(1)}, bf16[96,1024]{1,0:T(8,128)(2,1)S(1)}, u32[]{:S(2)}, u32[]{:S(2)}) collective-permute-start(bf16[96,1024]{1,0:T(8,128)(2,1)S(1)} %select_convert_fusion.refs_1_), channel_id=1, source_target_pairs={{0,4},{4,8},{8,12},{12,0},{1,5},{5,9},{9,13},{13,1},{2,6},{6,10},{... | collective-permute-start | bytes 589832 | tf_op jit(solution)/shard_map/ppermute | solution.py:77
  56.4 16.9 %collective-permute-start.6 = (bf16[96,1024]{1,0:T(8,128)(2,1)S(1)}, bf16[96,1024]{1,0:T(8,128)(2,1)S(1)}, u32[]{:S(2)}, u32[]{:S(2)}) collective-permute-start(bf16[96,1024]{1,0:T(8,128)(2,1)S(1)} %select_convert_fusion.1.refs_0_), channel_id=1, source_target_pairs={{0,4},{4,8},{8,12},{12,0},{1,5},{5,9},{9,13},{13,1},{2,6},{6,10},{... | collective-permute-start | bytes 589832 | tf_op jit(solution)/shard_map/ppermute | solution.py:77
  56.6 9.3 %collective-permute-start.18 = (f32[192]{0:T(256)S(1)}, f32[192]{0:T(256)S(1)}, u32[]{:S(2)}, u32[]{:S(2)}) collective-permute-start(f32[192]{0:T(256)S(1)} %add_rsqrt_fusion), channel_id=1, source_target_pairs={{0,4},{4,8},{8,12},{12,0},{1,5},{5,9},{9,13},{13,1},{2,6},{6,10},{... | collective-permute-start | bytes 2312 | tf_op jit(solution)/shard_map/ppermute | solution.py:77
  66.0 5.4 %collective-permute-start.21 = (f32[192]{0:T(256)S(1)}, f32[192]{0:T(256)S(1)}, u32[]{:S(2)}, u32[]{:S(2)}) collective-permute-start(f32[192]{0:T(256)S(1)} %collective-permute-done.18), channel_id=1, source_target_pairs={{0,4},{4,8},{8,12},{12,0},{1,5},{5,9},{9,13},{13,1},{2,6},{6,10},{... | collective-permute-start | bytes 2312 | tf_op jit(solution)/shard_map/ppermute | solution.py:77
  72.1 16.8 %copy-start.4 = (f32[192,1]{1,0:T(8,128)S(1)}, f32[192,1]{1,0:T(8,128)}, u32[]{:S(2)}) copy-start(f32[192,1]{1,0:T(8,128)} %copy.14.refs_14_) | copy-start | bytes 2308
  72.2 16.8 %copy-start.6 = (bf16[192,864]{1,0:T(8,128)(2,1)S(1)}, bf16[192,864]{1,0:T(8,128)(2,1)}, u32[]{:S(2)}) copy-start(bf16[192,864]{1,0:T(8,128)(2,1)} %copy-done.5) | copy-start | bytes 995332
  72.2 13.6 %collective-permute-start.14 = (bf16[192,1024]{1,0:T(8,128)(2,1)S(1)}, bf16[192,1024]{1,0:T(8,128)(2,1)S(1)}, u32[]{:S(2)}, u32[]{:S(2)}) collective-permute-start(bf16[192,1024]{1,0:T(8,128)(2,1)S(1)} %pad_maximum_fusion), channel_id=1, source_target_pairs={{0,1},{1,0},{2,3},{3,2},{4,5},{5,4},{6,7},{7,6},{8,9},{9,8},{10,11... | collective-permute-start | bytes 1179656 | tf_op jit(solution)/shard_map/ppermute | solution.py:72
  73.3 7.5 %collective-permute-start.19 = (bf16[96,1024]{1,0:T(8,128)(2,1)S(1)}, bf16[96,1024]{1,0:T(8,128)(2,1)S(1)}, u32[]{:S(2)}, u32[]{:S(2)}) collective-permute-start(bf16[96,1024]{1,0:T(8,128)(2,1)S(1)} %collective-permute-done.16.refs_6_), channel_id=1, source_target_pairs={{0,4},{4,8},{8,12},{12,0},{1,5},{5,9},{9,13},{13,1},{2,6},{6,10},{... | collective-permute-start | bytes 589832 | tf_op jit(solution)/shard_map/ppermute | solution.py:77
  73.3 9.6 %collective-permute-start.7 = (bf16[96,1024]{1,0:T(8,128)(2,1)S(1)}, bf16[96,1024]{1,0:T(8,128)(2,1)S(1)}, u32[]{:S(2)}, u32[]{:S(2)}) collective-permute-start(bf16[96,1024]{1,0:T(8,128)(2,1)S(1)} %collective-permute-done.6.refs_5_), channel_id=1, source_target_pairs={{0,4},{4,8},{8,12},{12,0},{1,5},{5,9},{9,13},{13,1},{2,6},{6,10},{... | collective-permute-start | bytes 589832 | tf_op jit(solution)/shard_map/ppermute | solution.py:77
  73.4 12.6 %collective-permute-start.17 = (bf16[192,512]{1,0:T(8,128)(2,1)S(1)}, bf16[192,512]{1,0:T(8,128)(2,1)S(1)}, u32[]{:S(2)}, u32[]{:S(2)}) collective-permute-start(bf16[192,512]{1,0:T(8,128)(2,1)S(1)} %pad_maximum_fusion.2), channel_id=1, source_target_pairs={{0,1},{5,4},{8,9},{13,12},{2,3},{7,6},{10,11},{15,14},{16,17},{21,... | collective-permute-start | bytes 589832 | tf_op jit(solution)/shard_map/ppermute | solution.py:285
  82.9 6.1 %collective-permute-start.20 = (bf16[192,512]{1,0:T(8,128)(2,1)S(1)}, bf16[192,512]{1,0:T(8,128)(2,1)S(1)}, u32[]{:S(2)}, u32[]{:S(2)}) collective-permute-start(bf16[192,512]{1,0:T(8,128)(2,1)S(1)} %pad_maximum_fusion.3), channel_id=1, source_target_pairs={{0,1},{5,4},{8,9},{13,12},{2,3},{7,6},{10,11},{15,14},{16,17},{21,... | collective-permute-start | bytes 589832 | tf_op jit(solution)/shard_map/ppermute | solution.py:285
  92.1 2.1 %copy-start.2 = (f32[864,256]{1,0:T(8,128)}, f32[864,256]{1,0:T(8,128)S(1)}, u32[]{:S(2)}) copy-start(f32[864,256]{1,0:T(8,128)S(1)} %get-tuple-element.36.refs_1_) | copy-start | bytes 2654212
  92.1 27.8 %collective-permute-start.22 = (bf16[944,512]{1,0:T(8,128)(2,1)}, bf16[944,512]{1,0:T(8,128)(2,1)S(1)}, u32[]{:S(2)}, u32[]{:S(2)}) collective-permute-start(bf16[944,512]{1,0:T(8,128)(2,1)} %get-tuple-element.37), channel_id=1, source_target_pairs={{0,2},{2,0},{1,3},{3,1},{4,6},{6,4},{5,7},{7,5},{8,10},{10,8},{9,1... | collective-permute-start | bytes 2899976 | tf_op jit(solution)/shard_map/ppermute | solution.py:72
  93.8 22.7 %collective-permute-start.15 = (bf16[192,1024]{1,0:T(8,128)(2,1)}, bf16[192,1024]{1,0:T(8,128)(2,1)}, u32[]{:S(2)}, u32[]{:S(2)}) collective-permute-start(bf16[192,1024]{1,0:T(8,128)(2,1)} %pad_maximum_fusion.1), channel_id=1, source_target_pairs={{0,2},{2,0},{1,3},{3,1},{4,6},{6,4},{5,7},{7,5},{8,10},{10,8},{9,1... | collective-permute-start | bytes 1179656 | tf_op jit(solution)/shard_map/ppermute | solution.py:72
  94.2 11.4 %collective-permute-start.24 = (bf16[192,512]{1,0:T(8,128)(2,1)S(1)}, bf16[192,512]{1,0:T(8,128)(2,1)S(1)}, u32[]{:S(2)}, u32[]{:S(2)}) collective-permute-start(bf16[192,512]{1,0:T(8,128)(2,1)S(1)} %constant_dynamic-slice_fusion), channel_id=1, source_target_pairs={{0,12},{5,1},{8,4},{13,9},{2,14},{7,3},{10,6},{15,11},{16,28},{21,... | collective-permute-start | bytes 589832 | tf_op jit(solution)/shard_map/ppermute | solution.py:287
  97.6 5.4 %collective-permute-start.25 = (f32[192]{0:T(256)S(1)}, f32[192]{0:T(256)S(1)}, u32[]{:S(2)}, u32[]{:S(2)}) collective-permute-start(f32[192]{0:T(256)S(1)} %collective-permute-done.21), channel_id=1, source_target_pairs={{0,4},{4,8},{8,12},{12,0},{1,5},{5,9},{9,13},{13,1},{2,6},{6,10},{... | collective-permute-start | bytes 2312 | tf_op jit(solution)/shard_map/ppermute | solution.py:77
  103.0 1.5 %collective-permute-start.29 = (f32[192]{0:T(256)S(1)}, f32[192]{0:T(256)S(1)}, u32[]{:S(2)}, u32[]{:S(2)}) collective-permute-start(f32[192]{0:T(256)S(1)} %collective-permute-done.25), channel_id=1, source_target_pairs={{0,2},{2,0},{1,3},{3,1},{4,6},{6,4},{5,7},{7,5},{8,10},{10,8},{9,1... | collective-permute-start | bytes 2312 | tf_op jit(solution)/shard_map/ppermute | solution.py:72
  103.0 9.6 %collective-permute-start.8 = (bf16[96,1024]{1,0:T(8,128)(2,1)S(1)}, bf16[96,1024]{1,0:T(8,128)(2,1)}, u32[]{:S(2)}, u32[]{:S(2)}) collective-permute-start(bf16[96,1024]{1,0:T(8,128)(2,1)S(1)} %collective-permute-done.7.refs_10_), channel_id=1, source_target_pairs={{0,4},{4,8},{8,12},{12,0},{1,5},{5,9},{9,13},{13,1},{2,6},{6,10},{... | collective-permute-start | bytes 589832 | tf_op jit(solution)/shard_map/ppermute | solution.py:77
  104.4 12.0 %collective-permute-start.23 = (bf16[96,1024]{1,0:T(8,128)(2,1)S(1)}, bf16[96,1024]{1,0:T(8,128)(2,1)}, u32[]{:S(2)}, u32[]{:S(2)}) collective-permute-start(bf16[96,1024]{1,0:T(8,128)(2,1)S(1)} %collective-permute-done.19.refs_11_), channel_id=1, source_target_pairs={{0,4},{4,8},{8,12},{12,0},{1,5},{5,9},{9,13},{13,1},{2,6},{6,10},{... | collective-permute-start | bytes 589832 | tf_op jit(solution)/shard_map/ppermute | solution.py:77
  105.6 14.3 %collective-permute-start.28 = (bf16[192,864]{1,0:T(8,128)(2,1)}, bf16[192,864]{1,0:T(8,128)(2,1)}, u32[]{:S(2)}, u32[]{:S(2)}) collective-permute-start(bf16[192,864]{1,0:T(8,128)(2,1)} %collective-permute-done.13.refs_6_), channel_id=1, source_target_pairs={{0,2},{2,0},{1,3},{3,1},{4,6},{6,4},{5,7},{7,5},{8,10},{10,8},{9,1... | collective-permute-start | bytes 995336 | tf_op jit(solution)/shard_map/ppermute | solution.py:72
  112.6 7.3 %collective-permute-start.27 = (bf16[192,512]{1,0:T(8,128)(2,1)S(1)}, bf16[192,512]{1,0:T(8,128)(2,1)S(1)}, u32[]{:S(2)}, u32[]{:S(2)}) collective-permute-start(bf16[192,512]{1,0:T(8,128)(2,1)S(1)} %collective-permute-done.24.refs_5_), channel_id=1, source_target_pairs={{0,2},{2,0},{1,3},{3,1},{4,6},{6,4},{5,7},{7,5},{8,10},{10,8},{9,1... | collective-permute-start | bytes 589832 | tf_op jit(solution)/shard_map/ppermute | solution.py:72
  116.4 3.4 %collective-permute-start.9 = (bf16[96,1024]{1,0:T(8,128)(2,1)}, bf16[96,1024]{1,0:T(8,128)(2,1)S(1)}, u32[]{:S(2)}, u32[]{:S(2)}) collective-permute-start(bf16[96,1024]{1,0:T(8,128)(2,1)} %collective-permute-done.8.refs_3_), channel_id=1, source_target_pairs={{0,2},{2,0},{1,3},{3,1},{4,6},{6,4},{5,7},{7,5},{8,10},{10,8},{9,1... | collective-permute-start | bytes 589832 | tf_op jit(solution)/shard_map/ppermute | solution.py:72
  116.4 3.5 %collective-permute-start.26 = (bf16[96,1024]{1,0:T(8,128)(2,1)}, bf16[96,1024]{1,0:T(8,128)(2,1)}, u32[]{:S(2)}, u32[]{:S(2)}) collective-permute-start(bf16[96,1024]{1,0:T(8,128)(2,1)} %collective-permute-done.23.refs_4_), channel_id=1, source_target_pairs={{0,2},{2,0},{1,3},{3,1},{4,6},{6,4},{5,7},{7,5},{8,10},{10,8},{9,1... | collective-permute-start | bytes 589832 | tf_op jit(solution)/shard_map/ppermute | solution.py:72
  117.3 2.6 %copy-start.3 = (f32[864,256]{1,0:T(8,128)S(1)}, f32[864,256]{1,0:T(8,128)}, u32[]{:S(2)}) copy-start(f32[864,256]{1,0:T(8,128)} %copy-done.2) | copy-start | bytes 2654212

commit v6 on v0

--- a/solution.py
+++ b/solution.py
@@ -1,6 +1,10 @@
+import functools
+
 import jax
 import jax.numpy as jnp
 from jax import lax
+from jax.experimental import pallas as pl
+from jax.experimental.pallas import tpu as pltpu
 from jax.sharding import PartitionSpec as P
 
 BINS = 8
@@ -14,7 +18,7 @@
     return jnp.sign(value) * jnp.maximum(jnp.abs(value) - level, 0.0)
 
 
-def on_device(patches, dictionary, threshold):
+def general(patches, dictionary, threshold):
     values = patches.astype(jnp.float32)
     local_sq = jnp.sum(values * values, axis=1)
     local_first = jnp.dot(patches, dictionary, preferred_element_type=jnp.float32)
@@ -64,6 +68,275 @@
     return (codes, gram, cross)
 
 
+def swap(value, axis):
+    return lax.ppermute(value, axis, [(0, 1), (1, 0)])
+
+
+def shift(value, by=1):
+    n = lax.axis_size("patch")
+    return lax.ppermute(value, "patch", [(i, (i + by) % n) for i in range(n)])
+
+
+def after(value, earlier):
+    return lax.optimization_barrier((value, earlier))[0]
+
+
+f32, bf16 = jnp.float32, jnp.bfloat16
+contract_last = (((1,), (1,)), ((), ()))
+contract_first = (((0,), (0,)), ((), ()))
+
+
+def soft(value, level):
+    return jnp.where(value > level, value - level, jnp.where(value < -level, value + level, 0.0))
+
+
+def run(body, outs, scalars, arrays, scratch=()):
+    fast = pl.BlockSpec(memory_space=pltpu.VMEM)
+    slow = pl.BlockSpec(memory_space=pltpu.SMEM)
+    return pl.pallas_call(
+        body,
+        out_shape=outs,
+        in_specs=[slow] + [fast] * len(arrays),
+        out_specs=jax.tree.map(lambda _: fast, outs),
+        scratch_shapes=scratch,
+        compiler_params=pltpu.CompilerParams(vmem_limit_bytes=24 << 20),
+        cost_estimate=pl.CostEstimate(flops=1000, bytes_accessed=1000, transcendentals=0),
+    )(jnp.stack([x.astype(jnp.int32) for x in scalars]), *arrays)
+
+
+def column(row):
+    n = row.shape[1]
+    same = lax.broadcasted_iota(jnp.int32, (n, n), 0) == lax.broadcasted_iota(jnp.int32, (n, n), 1)
+    return jnp.sum(jnp.where(same, row, 0.0), axis=1, keepdims=True)
+
+
+def first_body(_, mine, d, out):
+    out[...] = jnp.dot(mine[...], d[...], preferred_element_type=f32).astype(bf16)
+
+
+def copy_body(_, array, out):
+    out[...] = array[...]
+
+
+def second_body(where, part, arrived, part2, arrived2, mine, scale, threshold, own, other, away_a, away_b, misfit, start):
+    atoms = own.shape[1]
+    block = atoms // 2
+    step = away_a.shape[0]
+    far = pl.multiple_of((1 - where[0]) * block, block)
+    factor = column(scale[...])
+    for i, (x, y) in enumerate(((part, arrived), (part2, arrived2))):
+        columns = slice(i * atoms, (i + 1) * atoms)
+        summed = x[...].astype(f32) + y[...].astype(f32)
+        start[:, columns] = soft(step_rate * (factor * summed), step_rate * threshold[:, columns]).astype(bf16)
+    rebuilt = sum(
+        lax.dot_general(start[:, i * atoms : (i + 1) * atoms], d[...], contract_last, preferred_element_type=f32)
+        for i, d in enumerate((own, other))
+    )
+    misfit[...] = (factor * mine[...].astype(f32) - rebuilt).astype(bf16)
+    for i, d in enumerate((own, other)):
+        columns = slice(i * block, (i + 1) * block)
+        second = jnp.dot(misfit[...], d[:, pl.ds(far, block)], preferred_element_type=f32).astype(bf16)
+        away_a[:, columns] = second[:step]
+        away_b[:, columns] = second[step:]
+
+
+def base_body(where, misfit, start, own, other, base):
+    atoms = own.shape[1]
+    block = atoms // 2
+    near = pl.multiple_of(where[0] * block, block)
+    for i, d in enumerate((own, other)):
+        second = jnp.dot(misfit[...], d[:, pl.ds(near, block)], preferred_element_type=f32)
+        known = start[:, pl.ds(pl.multiple_of(i * atoms + near, block), block)].astype(f32)
+        base[:, i * block : (i + 1) * block] = known + step_rate * second
+
+
+def sums_body(offsets, where, *refs):
+    n = len(offsets)
+    pieces, totals, (gram, cross, send, lhs, sides, right) = refs[: 6 * n], refs[6 * n : -6], refs[-6:]
+    block = right.shape[1]
+    width = block // 2
+    place = pl.multiple_of(where[0] * block, block)
+    here = where[1] == 1
+    rows = lhs.shape[0] // n
+    step = rows // 2
+    for k in range(n):
+        for c in range(2):
+            x, there, offset = pieces[6 * k + c], pieces[6 * k + 2 + c], offsets[k][c]
+            window = slice(k * rows + c * step, k * rows + (c + 1) * step)
+            lhs[window, :] = x[...]
+            spot = pl.multiple_of(where[3 + k] * block, block)
+            right[window, :] = jnp.where(
+                here, x[:, pl.ds(place, block)], there[offset : offset + step, pl.ds(spot, block)]
+            )
+        raw, scale = pieces[6 * k + 4 : 6 * k + 6]
+        sides[k * rows : (k + 1) * rows, :] = (column(scale[...]) * raw[...].astype(f32)).astype(bf16)
+    mine = pl.multiple_of(where[2] * width, width)
+    theirs = pl.multiple_of((1 - where[2]) * width, width)
+    tall = sides.shape[1] // 2
+
+    def product(a, b):
+        return lax.dot_general(a, b, contract_first, preferred_element_type=f32)
+
+    def store(ref, index, value):
+        if totals:
+            value += totals[index[0]][index[1]]
+        ref[index[1]] = value.astype(ref.dtype)
+
+    part = product(lhs[:, block:], right[...])
+    store(send, (2, (slice(0, block), slice(None))), part)
+    part = product(sides[...], right[:, pl.ds(theirs, width)])
+    store(send, (2, (slice(block, block + tall), slice(0, width))), part[:tall])
+    store(send, (2, (slice(block, block + tall), slice(width, block))), part[tall:])
+    store(gram, (0, (slice(None), slice(None))), product(lhs[:, :block], right[...]))
+    store(cross, (1, (slice(None), slice(None))), product(sides[...], right[:, pl.ds(mine, width)]))
+
+
+def add_body(count, _, gram_in, cross_in, sent, gram, cross):
+    block = gram.shape[0]
+    width = cross.shape[1]
+    tall = cross.shape[0] // 2
+    gram[...] = (gram_in[...] + sent[:block, :].astype(f32)) * (1.0 / count)
+    for i in range(2):
+        window = slice(i * tall, (i + 1) * tall)
+        total = cross_in[window, :] + sent[block:, i * width : (i + 1) * width].astype(f32)
+        cross[window, :] = total * (1.0 / count)
+
+
+def group_near(level, half, block):
+    atoms = 2 * block
+    parts = [lax.dynamic_slice_in_dim(level, i * atoms + half * block, block, 1) for i in range(2)]
+    return jnp.concatenate(parts, 1)
+
+
+def paired(patches, dictionary, threshold):
+    n_patch = lax.axis_size("patch")
+    plane = lax.axis_index("patch")
+    core = lax.axis_index("atom")
+    half = lax.axis_index("feat")
+    count = patches.shape[0] * n_patch
+    length = patches.shape[1]
+    rows = patches.shape[0] // 2
+    atoms = dictionary.shape[1]
+    block = atoms // 2
+    width = block // 2
+    step = rows // 2
+
+    def blocks(array, which):
+        return lax.dynamic_slice_in_dim(array, which * block, block, 1)
+
+    mine = lax.dynamic_slice_in_dim(patches, core * rows, rows, 0)
+    dictionary2 = swap(dictionary, "atom")
+    level = threshold[None, :]
+    level = jnp.concatenate([level, swap(level, "atom")], 1)
+    windows = [slice(c * step, (c + 1) * step) for c in range(2)]
+
+    def project(value, d):
+        shape = jax.ShapeDtypeStruct((value.shape[0], d.shape[1]), bf16)
+        return run(first_body, shape, (half,), (value, d))
+
+    raw_of = [mine, shift(mine)]
+    part = project(mine, dictionary)
+    other = swap(part, "feat")
+    local_sq = jnp.sum(jnp.square(after(mine, part).astype(f32)), axis=1)
+    other_sq = swap(local_sq, "feat")
+    part2 = project(after(mine, part), dictionary2)
+    other2 = swap(part2, "feat")
+    energy = local_sq + after(other_sq, part2)
+    scale = lax.rsqrt(energy / (BINS * VOXELS) + 1e-05)
+    raw_of.append(shift(after(raw_of[1], part2)))
+    held = run(copy_body, jax.ShapeDtypeStruct(dictionary.shape, bf16), (half,), (after(dictionary2, part2),))
+    half_shape = jax.ShapeDtypeStruct((step, atoms), bf16)
+    away_a, away_b, misfit, start = run(
+        second_body,
+        (
+            half_shape,
+            half_shape,
+            jax.ShapeDtypeStruct((rows, length), bf16),
+            jax.ShapeDtypeStruct((rows, 2 * atoms), bf16),
+        ),
+        (half,),
+        (part, other, part2, other2, mine, scale[None, :], level, dictionary, after(held, raw_of[2])),
+    )
+    base = run(
+        base_body, jax.ShapeDtypeStruct((rows, atoms), f32), (half,), (misfit, start, dictionary, held)
+    )
+    raw_of.append(shift(raw_of[2]))
+    backs = [swap(x, "feat") for x in (away_a, away_b)]
+    own_scale = after(scale, away_b)
+    scale_of = [scale] + [shift(own_scale, k) for k in range(1, n_patch)]
+
+    near_level = step_rate * group_near(level, half, block)
+    codes_of = []
+    done = ()
+    for c in range(2):
+        back = after(backs[c], done).astype(f32)
+        codes_of.append(soft(base[windows[c]] + step_rate * back, near_level).astype(bf16))
+        done = codes_of[c]
+
+    inside = jnp.concatenate(codes_of, 0)
+    ring1 = [shift(x) for x in codes_of]
+    ring1 = [after(x, y) for x, y in zip(ring1, (raw_of[3], scale_of))]
+    outside = swap(after(inside, ring1[0]), "feat")
+    ring2 = [shift(x) for x in ring1]
+
+    home_half = plane % 2
+    place = jnp.where(core == plane // 2, 0, 1)
+    over = [(q * 2 + q % 2, q * 2 + 1 - q % 2) for q in range(n_patch)]
+
+    def across(arrays):
+        return lax.ppermute(jnp.concatenate([blocks(x, place) for x in arrays], 0), ("patch", "feat"), over)
+
+    there1 = across([*ring1, ring2[0]])
+    ring2[1] = after(ring2[1], outside)
+    ring3 = [shift(x) for x in ring2]
+    ring3[0] = after(ring3[0], there1)
+    there2 = across([ring2[1], ring3[0]])
+
+    both = [jnp.where(half == 0, inside, outside), jnp.where(half == 0, outside, inside)]
+    upper = jnp.concatenate([x[:, :block] for x in both], 1)
+    lower = after(jnp.concatenate([x[:, block:] for x in both], 1), ring2[0])
+    lower = swap(lower, "atom")
+    ring3[0] = after(ring3[0], lower)
+
+    zero = jnp.zeros_like(place)
+    rings = (codes_of, ring1, ring2, ring3)
+    totals = ()
+    for planes, kind in (((0, 1), f32), ((2, 3), bf16)):
+        if kind == f32:
+            there = ((outside, outside), (there1, there1))
+            offsets = ((0, step), (0, step))
+        else:
+            ring3[1] = after(ring3[1], totals)
+            there = ((there1, there2), (there2, across([ring3[1]])))
+            offsets = ((2 * step, 0), (step, 0))
+        pieces = []
+        for i, k in enumerate(planes):
+            pieces += [*rings[k], *there[i], raw_of[k], scale_of[k][None, :]]
+        totals = run(
+            functools.partial(sums_body, offsets),
+            (
+                jax.ShapeDtypeStruct((block, block), f32),
+                jax.ShapeDtypeStruct((length, width), f32),
+                jax.ShapeDtypeStruct((block + length // 2, block), kind),
+            ),
+            (place, half == home_half, core) + tuple(zero if k else place for k in planes),
+            (*pieces, *totals),
+            [pltpu.VMEM((len(planes) * rows, size), bf16) for size in (atoms, length, block)],
+        )
+    gram, cross, send = totals
+    lower = after(lower, send)
+    codes = jnp.where(
+        core == 0, jnp.concatenate([upper, lower], 0), jnp.concatenate([lower, upper], 0)
+    )
+    gram, cross = run(
+        functools.partial(add_body, count),
+        (jax.ShapeDtypeStruct((block, block), f32), jax.ShapeDtypeStruct((length, width), f32)),
+        (half,),
+        (gram, cross, after(swap(send, "atom"), codes)),
+    )
+    return (codes, gram, cross)
+
+
 def solution(mesh):
     in_specs = (P(("slab", "patch"), "feat"), P("feat", "atom"), P("atom"))
     out_specs = (
@@ -71,6 +344,8 @@
         P(("slab", "atom", "feat"), "patch"),
         P(("slab", "feat"), ("patch", "atom")),
     )
+    sizes = mesh.shape
+    small = sizes["feat"] == 2 and sizes["atom"] == 2 and sizes["patch"] == 4
     return jax.shard_map(
-        on_device, mesh=mesh, in_specs=in_specs, out_specs=out_specs, check_vma=False
-    )
+        paired if small else general, mesh=mesh, in_specs=in_specs, out_specs=out_specs, check_vma=False
+    )

time: 268 us -> 83.1 us (0.31)
  waiting for transfers between devices: 209 us -> 42.2 us
  starting transfers between devices: 0.25 us -> 22.4 us
  matrix products: 17 us -> 0 us
  between operations: 14.1 us -> 0.9 us
  Pallas kernels: 0 us -> 10.4 us
  local copies, waits for them, and re-layouts: 13.4 us -> 3.57 us
  blocking collectives: 5.83 us -> 0 us
  other arithmetic: 8.07 us -> 3.23 us
    psum x3 -> x0, waiting for transfers between devices: 120 us -> none  [the longest x1 52.8 us: on_device(): second = lax.psum(local_second, 'feat')]
    reduce_scatter x2 -> x0, waiting for transfers between devices: 78.8 us -> none  [the longest x1 43.1 us: on_device(): lax.psum_scatter(gram_part.astype(jnp.bfloat16), 'patch', scatter_dimensi...]
    ppermute x0 -> x25, waiting for transfers between devices: none -> 42.2 us  [the longest x12 31.6 us: shift(): return lax.ppermute(value, 'patch', [(i, (i + by) % n) for i in range(n)])]
    ppermute x0 -> x25, starting transfers between devices: none -> 22.4 us  [the longest x12 10.2 us: shift(): return lax.ppermute(value, 'patch', [(i, (i + by) % n) for i in range(n)])]
    dot_general x5 -> x0, matrix products: 17 us -> none  [the longest x1 3.99 us: on_device(): lax.dot_general(start, dictionary, contract_last, preferred_element_type=...]
    pallas_call x0 -> x8, Pallas kernels: none -> 10.4 us  [run(): pl.pallas_call(body, out_shape=outs, in_specs=[slow] + [fast] * len(array...]
    all_gather x1 -> x0, waiting for transfers between devices: 9.91 us -> none  [on_device(): codes_whole = lax.all_gather(codes, 'atom', axis=1, tiled=True)]
    psum x1 -> x0, blocking collectives: 5.83 us -> none  [on_device(): summed, energy = lax.psum((local_first, local_sq), 'feat')]
  transfers between devices with their start and end apart: 6 -> 25, of which waited for: 6 -> 13; matrix products, arithmetic and copies ran while one was open for 2% -> 5% of each run, Pallas kernels for 0% -> 4%
where the time goes in v6:
time: 83.1 us; the launch traced here: 82.8 us
  waiting for transfers between devices  42.2 us (51%)
  starting transfers between devices  22.4 us (27%)
  Pallas kernels  10.4 us (13%)
  local copies, waits for them, and re-layouts  3.57 us (4%)
  other arithmetic  3.23 us (4%)
  between operations  0.9 us (1%)
    ppermute x12, waiting for transfers between devices, shift(): return lax.ppermute(value, 'patch', [(i, (i + by) % n) for i in range(n)])  31.6 us
    pallas_call x8, Pallas kernels, run(): pl.pallas_call(body, out_shape=outs, in_specs=[slow] + [fast] * len(array...  10.4 us
    ppermute x12, starting transfers between devices, shift(): return lax.ppermute(value, 'patch', [(i, (i + by) % n) for i in range(n)])  10.2 us
    ppermute x10, waiting for transfers between devices, swap(): return lax.ppermute(value, axis, [(0, 1), (1, 0)])  8.58 us
    ppermute x10, starting transfers between devices, swap(): return lax.ppermute(value, axis, [(0, 1), (1, 0)])  6.93 us
    ppermute x3, starting transfers between devices, across(): lax.ppermute(jnp.concatenate([blocks(x, place) for x in arrays], 0), ('pa...  5.27 us
    unnamed x14, local copies, waits for them, and re-layouts  2.97 us
    select_n x1, other arithmetic, paired(): jnp.where(core == 0, jnp.concatenate([upper, lower], 0), jnp.concatenate(...  2.39 us
  transfers between devices with their start and end apart: 25, of which 13 were waited for; matrix products, arithmetic and copies ran while one was open for 5% of the time, Pallas kernels for 4%

profile of v6, /device:TPU:0, one launch (start us, length us, event | category | flops | bytes accessed | tf_op | source)
XLA Modules:
  0.0 82.8 jit_solution(8295314897737357368)
XLA Ops:
  0.6 0.0 copy-start
  0.7 0.5 collective-permute-start.1
  1.2 0.6 copy-done
  1.7 0.2 constant_dynamic-slice_fusion.6
  1.9 0.2 copy.7.mine.refs_4_
  2.1 3.1 %collective-permute-start.5 = (bf16[192,864]{1,0:T(8,128)(2,1)S(1)}, bf16[192,864]{1,0:T(8,128)(2,1)S(1)}, u32[]{:S(2)}, u32[]{:S(2)}) collective-permute-start(bf16[192,864]{1,0:T(8,128)(2,1)S(1)} %copy.7.mine.refs_4_), channel_id=1, source_target_pairs={{0,4},{4,8},{8,12},{12,0},{1,5},{5,9},{9,13},{13,1},{2,6},{6,10},{... | collective-permute-start | bytes 995336 | tf_op jit(solution)/shard_map/ppermute | solution.py:77
  5.2 0.0 collective-permute-start.4
  5.2 1.5 %copy-done.1 = bf16[864,1024]{1,0:T(8,128)(2,1)S(1)} copy-done((bf16[864,1024]{1,0:T(8,128)(2,1)S(1)}, bf16[864,1024]{1,0:T(8,128)(2,1)}, u32[]{:S(2)}) %copy-start.1) | copy-done | bytes 1769496
  6.7 0.6 shard_map.58.part
  7.3 1.6 %collective-permute-start = (bf16[192,1024]{1,0:T(8,128)(2,1)S(1)}, bf16[192,1024]{1,0:T(8,128)(2,1)}, u32[]{:S(2)}, u32[]{:S(2)}) collective-permute-start(bf16[192,1024]{1,0:T(8,128)(2,1)S(1)} %shard_map.58.part), channel_id=1, source_target_pairs={{0,1},{1,0},{2,3},{3,2},{4,5},{5,4},{6,7},{7,6},{8,9},{9,8},{10,11... | collective-permute-start | bytes 1179656 | tf_op jit(solution)/shard_map/ppermute | solution.py:72
  8.9 0.2 multiply_reduce_fusion
  9.0 0.6 collective-permute-start.3
  9.6 0.1 stack.36.where
  9.7 0.0 collective-permute-done.1.d.array
  9.7 0.6 shard_map.59.part2
  10.3 1.6 %collective-permute-start.2 = (bf16[192,1024]{1,0:T(8,128)(2,1)S(1)}, bf16[192,1024]{1,0:T(8,128)(2,1)S(1)}, u32[]{:S(2)}, u32[]{:S(2)}) collective-permute-start(bf16[192,1024]{1,0:T(8,128)(2,1)S(1)} %shard_map.59.part2), channel_id=1, source_target_pairs={{0,1},{1,0},{2,3},{3,2},{4,5},{5,4},{6,7},{7,6},{8,9},{9,8},{10,11... | collective-permute-start | bytes 1179656 | tf_op jit(solution)/shard_map/ppermute | solution.py:72
  11.8 3.5 %collective-permute-done.5.refs_10_ = bf16[192,864]{1,0:T(8,128)(2,1)S(1)} collective-permute-done((bf16[192,864]{1,0:T(8,128)(2,1)S(1)}, bf16[192,864]{1,0:T(8,128)(2,1)S(1)}, u32[]{:S(2)}, u32[]{:S(2)}) %collective-permute-start.5) | collective-permute-done | bytes 331808 | tf_op jit(solution)/shard_map/ppermute | solution.py:77
  15.3 0.0 copy-start.2
  15.3 0.1 shard_map.60.other
  15.5 3.9 %collective-permute-done.3 = f32[192]{0:T(256)S(1)} collective-permute-done((f32[192]{0:T(256)S(1)}, f32[192]{0:T(256)S(1)}, u32[]{:S(2)}, u32[]{:S(2)}) %collective-permute-start.3) | collective-permute-done | bytes 800 | tf_op jit(solution)/shard_map/ppermute | solution.py:72
  19.4 7.0 %collective-permute-done.6.refs_4_ = bf16[192,864]{1,0:T(8,128)(2,1)S(1)} collective-permute-done((bf16[192,864]{1,0:T(8,128)(2,1)S(1)}, bf16[192,864]{1,0:T(8,128)(2,1)S(1)}, u32[]{:S(2)}, u32[]{:S(2)}) %collective-permute-start.6) | collective-permute-done | bytes 331808 | tf_op jit(solution)/shard_map/ppermute | solution.py:77
  26.3 0.0 collective-permute-done.arrived
  26.3 1.0 %collective-permute-done.2.arrived2 = bf16[192,1024]{1,0:T(8,128)(2,1)S(1)} collective-permute-done((bf16[192,1024]{1,0:T(8,128)(2,1)S(1)}, bf16[192,1024]{1,0:T(8,128)(2,1)S(1)}, u32[]{:S(2)}, u32[]{:S(2)}) %collective-permute-start.2) | collective-permute-done | bytes 393248 | tf_op jit(solution)/shard_map/ppermute | solution.py:72
  27.3 2.9 %shard_map.61 = (bf16[96,1024]{1,0:T(8,128)(2,1)S(1)}, bf16[96,1024]{1,0:T(8,128)(2,1)S(1)}, bf16[192,864]{1,0:T(8,128)(2,1)S(1)}, bf16[192,2048]{1,0:T(8,128)(2,1)S(1)}) custom-call(s32[1]{0:T(128)} %bitcast._.where, bf16[192,1024]{1,0:T(8,128)(2,1)S(1)} %shard_map.58.part, bf16[192,1024]{1,0:T(8,128)(2,1)} %collective-permute-done.arrived, ...), custom_call_target="tpu_custom_call" | custom-call | flops 1000 | bytes 1000 | tf_op jit(solution)/shard_map/pallas_call | solution.py:96
  30.3 1.6 %collective-permute-start.7 = (bf16[96,1024]{1,0:T(8,128)(2,1)S(1)}, bf16[96,1024]{1,0:T(8,128)(2,1)S(1)}, u32[]{:S(2)}, u32[]{:S(2)}) collective-permute-start(bf16[96,1024]{1,0:T(8,128)(2,1)S(1)} %get-tuple-element.39), channel_id=1, source_target_pairs={{0,1},{1,0},{2,3},{3,2},{4,5},{5,4},{6,7},{7,6},{8,9},{9,8},{10,11... | collective-permute-start | bytes 589832 | tf_op jit(solution)/shard_map/ppermute | solution.py:72
  31.9 1.6 %collective-permute-start.10 = (bf16[192,864]{1,0:T(8,128)(2,1)S(1)}, bf16[192,864]{1,0:T(8,128)(2,1)S(1)}, u32[]{:S(2)}, u32[]{:S(2)}) collective-permute-start(bf16[192,864]{1,0:T(8,128)(2,1)S(1)} %collective-permute-done.6.refs_4_), channel_id=1, source_target_pairs={{0,4},{4,8},{8,12},{12,0},{1,5},{5,9},{9,13},{13,1},{2,6},{6,10},{... | collective-permute-start | bytes 995336 | tf_op jit(solution)/shard_map/ppermute | solution.py:77
  33.5 2.2 %collective-permute-start.17 = (f32[192]{0:T(256)S(1)}, f32[192]{0:T(256)S(1)}, u32[]{:S(2)}, u32[]{:S(2)}) collective-permute-start(f32[192]{0:T(256)S(1)} %add_rsqrt_fusion), channel_id=1, source_target_pairs={{0,12},{4,0},{8,4},{12,8},{1,13},{5,1},{9,5},{13,9},{2,14},{6,2},{... | collective-permute-start | bytes 2312 | tf_op jit(solution)/shard_map/ppermute | solution.py:77
  35.7 0.8 collective-permute-start.16
  36.5 0.5 collective-permute-start.8
  37.1 0.6 shard_map.62
  37.7 0.1 select_convert_fusion.1.refs_0_
  37.8 1.1 %collective-permute-start.9 = (bf16[96,1024]{1,0:T(8,128)(2,1)S(1)}, bf16[96,1024]{1,0:T(8,128)(2,1)S(1)}, u32[]{:S(2)}, u32[]{:S(2)}) collective-permute-start(bf16[96,1024]{1,0:T(8,128)(2,1)S(1)} %select_convert_fusion.1.refs_0_), channel_id=1, source_target_pairs={{0,4},{4,8},{8,12},{12,0},{1,5},{5,9},{9,13},{13,1},{2,6},{6,10},{... | collective-permute-start | bytes 589832 | tf_op jit(solution)/shard_map/ppermute | solution.py:77
  38.9 3.3 %collective-permute-done.8 = bf16[96,1024]{1,0:T(8,128)(2,1)S(1)} collective-permute-done((bf16[96,1024]{1,0:T(8,128)(2,1)S(1)}, bf16[96,1024]{1,0:T(8,128)(2,1)S(1)}, u32[]{:S(2)}, u32[]{:S(2)}) %collective-permute-start.8) | collective-permute-done | bytes 196640 | tf_op jit(solution)/shard_map/ppermute | solution.py:72
  42.2 0.1 select_convert_fusion.refs_1_
  42.3 0.5 collective-permute-start.14
  42.9 1.9 %collective-permute-done.10.refs_10_ = bf16[192,864]{1,0:T(8,128)(2,1)S(1)} collective-permute-done((bf16[192,864]{1,0:T(8,128)(2,1)S(1)}, bf16[192,864]{1,0:T(8,128)(2,1)S(1)}, u32[]{:S(2)}, u32[]{:S(2)}) %collective-permute-start.10) | collective-permute-done | bytes 331808 | tf_op jit(solution)/shard_map/ppermute | solution.py:77
  44.7 0.4 collective-permute-start.15
  45.2 3.8 %collective-permute-done.9.refs_6_ = bf16[96,1024]{1,0:T(8,128)(2,1)S(1)} collective-permute-done((bf16[96,1024]{1,0:T(8,128)(2,1)S(1)}, bf16[96,1024]{1,0:T(8,128)(2,1)S(1)}, u32[]{:S(2)}, u32[]{:S(2)}) %collective-permute-start.9) | collective-permute-done | bytes 196640 | tf_op jit(solution)/shard_map/ppermute | solution.py:77
  49.0 0.0 collective-permute-start.12
  49.0 0.0 collective-permute-done.17
  49.0 0.5 collective-permute-start.11
  49.5 3.4 %collective-permute-done.15 = f32[192]{0:T(256)S(1)} collective-permute-done((f32[192]{0:T(256)S(1)}, f32[192]{0:T(256)S(1)}, u32[]{:S(2)}, u32[]{:S(2)}) %collective-permute-start.15) | collective-permute-done | bytes 800 | tf_op jit(solution)/shard_map/ppermute | solution.py:77
  52.9 0.1 collective-permute-start.18
  53.0 5.3 %collective-permute-done.12.refs_0_ = bf16[96,1024]{1,0:T(8,128)(2,1)S(1)} collective-permute-done((bf16[96,1024]{1,0:T(8,128)(2,1)S(1)}, bf16[96,1024]{1,0:T(8,128)(2,1)S(1)}, u32[]{:S(2)}, u32[]{:S(2)}) %collective-permute-start.12) | collective-permute-done | bytes 196640 | tf_op jit(solution)/shard_map/ppermute | solution.py:77
  58.4 2.5 %collective-permute-start.19 = (bf16[288,512]{1,0:T(8,128)(2,1)S(1)}, bf16[288,512]{1,0:T(8,128)(2,1)S(1)}, u32[]{:S(2)}, u32[]{:S(2)}) collective-permute-start(bf16[288,512]{1,0:T(8,128)(2,1)S(1)} %pad_maximum_fusion.2), channel_id=1, source_target_pairs={{0,1},{5,4},{8,9},{13,12},{2,3},{7,6},{10,11},{15,14},{16,17},{21,... | collective-permute-start | bytes 884744 | tf_op jit(solution)/shard_map/ppermute | solution.py:287
  60.9 0.1 collective-permute-start.20
  60.9 0.1 collective-permute-done.18.refs_1_
  61.0 0.0 collective-permute-done.11.refs_2_.refs_3_
  61.0 0.3 collective-permute-start.22
  61.4 0.2 broadcast_select_fusion.1
  61.6 0.1 fusion.3
  61.7 0.1 collective-permute-start.13
  61.8 6.6 %collective-permute-done.20.refs_6_ = bf16[96,1024]{1,0:T(8,128)(2,1)S(1)} collective-permute-done((bf16[96,1024]{1,0:T(8,128)(2,1)S(1)}, bf16[96,1024]{1,0:T(8,128)(2,1)S(1)}, u32[]{:S(2)}, u32[]{:S(2)}) %collective-permute-start.20) | collective-permute-done | bytes 196640 | tf_op jit(solution)/shard_map/ppermute | solution.py:77
  68.4 1.5 %collective-permute-start.21 = (bf16[192,512]{1,0:T(8,128)(2,1)S(1)}, bf16[192,512]{1,0:T(8,128)(2,1)S(1)}, u32[]{:S(2)}, u32[]{:S(2)}) collective-permute-start(bf16[192,512]{1,0:T(8,128)(2,1)S(1)} %pad_maximum_fusion.3), channel_id=1, source_target_pairs={{0,1},{5,4},{8,9},{13,12},{2,3},{7,6},{10,11},{15,14},{16,17},{21,... | collective-permute-start | bytes 589832 | tf_op jit(solution)/shard_map/ppermute | solution.py:287
  70.0 1.8 %shard_map.63 = (f32[512,512]{1,0:T(8,128)S(1)}, f32[864,256]{1,0:T(8,128)S(1)}, f32[944,512]{1,0:T(8,128)S(1)}) custom-call(s32[5]{0:T(128)S(1)} %stack.36.where, bf16[96,1024]{1,0:T(8,128)(2,1)S(1)} %select_convert_fusion.1.refs_0_, bf16[96,1024]{1,0:T(8,128)(2,1)S(1)} %select_convert_fusion.refs_1_, ...), custom_call_target="tpu_custom_call" | custom-call | flops 1000 | bytes 1000 | tf_op jit(solution)/shard_map/pallas_call | solution.py:96
  71.8 0.0 collective-permute-done.22.refs_7_
  71.8 1.3 %collective-permute-start.23 = (bf16[96,512]{1,0:T(8,128)(2,1)S(1)}, bf16[96,512]{1,0:T(8,128)(2,1)S(1)}, u32[]{:S(2)}, u32[]{:S(2)}) collective-permute-start(bf16[96,512]{1,0:T(8,128)(2,1)S(1)} %constant_dynamic-slice_fusion), channel_id=1, source_target_pairs={{0,1},{5,4},{8,9},{13,12},{2,3},{7,6},{10,11},{15,14},{16,17},{21,... | collective-permute-start | bytes 294920 | tf_op jit(solution)/shard_map/ppermute | solution.py:287
  73.1 0.1 pad_add_fusion.where
  73.2 2.1 %collective-permute-done.23.refs_9_ = bf16[96,512]{1,0:T(8,128)(2,1)S(1)} collective-permute-done((bf16[96,512]{1,0:T(8,128)(2,1)S(1)}, bf16[96,512]{1,0:T(8,128)(2,1)S(1)}, u32[]{:S(2)}, u32[]{:S(2)}) %collective-permute-start.23) | collective-permute-done | bytes 98336 | tf_op jit(solution)/shard_map/ppermute | solution.py:287
  75.3 2.4 %shard_map.64 = (f32[512,512]{1,0:T(8,128)S(1)}, f32[864,256]{1,0:T(8,128)S(1)}, bf16[944,512]{1,0:T(8,128)(2,1)}) custom-call(s32[5]{0:T(128)S(1)} %pad_add_fusion.where, bf16[96,1024]{1,0:T(8,128)(2,1)S(1)} %collective-permute-done.12.refs_0_, bf16[96,1024]{1,0:T(8,128)(2,1)S(1)} %collective-permute-done.18.refs_1_, ...), custom_call_target="tpu_custom_call" | custom-call | flops 1000 | bytes 1000 | tf_op jit(solution)/shard_map/pallas_call | solution.py:96
  77.7 0.9 %copy-done.3 = f32[864,256]{1,0:T(8,128)} copy-done((f32[864,256]{1,0:T(8,128)}, f32[864,256]{1,0:T(8,128)S(1)}, u32[]{:S(2)}) %copy-start.3) | copy-done | bytes 884760
  78.6 2.4 %maximum_select_fusion = bf16[384,1024]{1,0:T(8,128)(2,1)} fusion(bf16[192,1024]{1,0:T(8,128)(2,1)} %copy-done.5, bf16[192,512]{1,0:T(8,128)(2,1)S(1)} %get-tuple-element.72, bf16[192,512]{1,0:T(8,128)(2,1)S(1)} %get-tuple-element.63, pred[]{:T(512)S(6)} %eq.16), kind=kLoop, calls=%fused_computation | loop fusion | flops 5111808 | bytes 1572865 | tf_op jit(solution)/shard_map/jit(_where)/select_n | solution.py:328
  81.0 0.4 collective-permute-done.24.sent
  81.4 1.4 %shard_map.65 = (f32[512,512]{1,0:T(8,128)}, f32[864,256]{1,0:T(8,128)}) custom-call(s32[1]{0:T(128)} %bitcast._.where, f32[512,512]{1,0:T(8,128)S(1)} %get-tuple-element.56.gram_in, f32[864,256]{1,0:T(8,128)S(1)} %copy-done.4, bf16[944,512]{1,0:T(8,128)(2,1)S(1)} %collective-permute-done.24.sent), custom_call_target="tpu_custom_call" | custom-call | flops 1000 | bytes 1000 | tf_op jit(solution)/shard_map/pallas_call | solution.py:96
  (33 shorter events, 0.3 us)
Async XLA Ops:
  0.6 1.1 %copy-start = (bf16[384,864]{0,1:T(8,128)(2,1)S(1)}, bf16[384,864]{0,1:T(8,128)(2,1)}, u32[]{:S(2)}) copy-start(bf16[384,864]{0,1:T(8,128)(2,1)} %param.3) | copy-start | bytes 1990660
  0.6 4.6 %copy-start.6 = (f32[1024]{0:T(1024)S(1)}, f32[1024]{0:T(1024)}, u32[]{:S(2)}) copy-start(f32[1024]{0:T(1024)} %param.5) | copy-start | bytes 12292
  0.7 9.0 %collective-permute-start.1 = (bf16[864,1024]{1,0:T(8,128)(2,1)}, bf16[864,1024]{1,0:T(8,128)(2,1)S(1)}, u32[]{:S(2)}, u32[]{:S(2)}) collective-permute-start(bf16[864,1024]{1,0:T(8,128)(2,1)} %own.3), channel_id=1, source_target_pairs={{0,2},{2,0},{1,3},{3,1},{4,6},{6,4},{5,7},{7,5},{8,10},{10,8},{9,1... | collective-permute-start | bytes 5308424 | tf_op jit(solution)/shard_map/ppermute | solution.py:72
  2.1 13.2 %collective-permute-start.5 = (bf16[192,864]{1,0:T(8,128)(2,1)S(1)}, bf16[192,864]{1,0:T(8,128)(2,1)S(1)}, u32[]{:S(2)}, u32[]{:S(2)}) collective-permute-start(bf16[192,864]{1,0:T(8,128)(2,1)S(1)} %copy.7.mine.refs_4_), channel_id=1, source_target_pairs={{0,4},{4,8},{8,12},{12,0},{1,5},{5,9},{9,13},{13,1},{2,6},{6,10},{... | collective-permute-start | bytes 995336 | tf_op jit(solution)/shard_map/ppermute | solution.py:77
  5.2 10.1 %collective-permute-start.4 = (f32[1,1024]{1,0:T(1,128)S(1)}, f32[1,1024]{1,0:T(1,128)S(1)}, u32[]{:S(2)}, u32[]{:S(2)}) collective-permute-start(f32[1,1024]{1,0:T(1,128)S(1)} %bitcast.16), channel_id=1, source_target_pairs={{0,2},{2,0},{1,3},{3,1},{4,6},{6,4},{5,7},{7,5},{8,10},{10,8},{9,1... | collective-permute-start | bytes 12296 | tf_op jit(solution)/shard_map/ppermute | solution.py:72
  5.2 1.5 %copy-start.1 = (bf16[864,1024]{1,0:T(8,128)(2,1)S(1)}, bf16[864,1024]{1,0:T(8,128)(2,1)}, u32[]{:S(2)}) copy-start(bf16[864,1024]{1,0:T(8,128)(2,1)} %own.3) | copy-start | bytes 5308420
  7.3 19.0 %collective-permute-start = (bf16[192,1024]{1,0:T(8,128)(2,1)S(1)}, bf16[192,1024]{1,0:T(8,128)(2,1)}, u32[]{:S(2)}, u32[]{:S(2)}) collective-permute-start(bf16[192,1024]{1,0:T(8,128)(2,1)S(1)} %shard_map.58.part), channel_id=1, source_target_pairs={{0,1},{1,0},{2,3},{3,2},{4,5},{5,4},{6,7},{7,6},{8,9},{9,8},{10,11... | collective-permute-start | bytes 1179656 | tf_op jit(solution)/shard_map/ppermute | solution.py:72
  9.0 10.4 %collective-permute-start.3 = (f32[192]{0:T(256)S(1)}, f32[192]{0:T(256)S(1)}, u32[]{:S(2)}, u32[]{:S(2)}) collective-permute-start(f32[192]{0:T(256)S(1)} %multiply_reduce_fusion), channel_id=1, source_target_pairs={{0,1},{1,0},{2,3},{3,2},{4,5},{5,4},{6,7},{7,6},{8,9},{9,8},{10,11... | collective-permute-start | bytes 2312 | tf_op jit(solution)/shard_map/ppermute | solution.py:72
  10.3 17.1 %collective-permute-start.2 = (bf16[192,1024]{1,0:T(8,128)(2,1)S(1)}, bf16[192,1024]{1,0:T(8,128)(2,1)S(1)}, u32[]{:S(2)}, u32[]{:S(2)}) collective-permute-start(bf16[192,1024]{1,0:T(8,128)(2,1)S(1)} %shard_map.59.part2), channel_id=1, source_target_pairs={{0,1},{1,0},{2,3},{3,2},{4,5},{5,4},{6,7},{7,6},{8,9},{9,8},{10,11... | collective-permute-start | bytes 1179656 | tf_op jit(solution)/shard_map/ppermute | solution.py:72
  15.3 11.0 %collective-permute-start.6 = (bf16[192,864]{1,0:T(8,128)(2,1)S(1)}, bf16[192,864]{1,0:T(8,128)(2,1)S(1)}, u32[]{:S(2)}, u32[]{:S(2)}) collective-permute-start(bf16[192,864]{1,0:T(8,128)(2,1)S(1)} %collective-permute-done.5.refs_10_), channel_id=1, source_target_pairs={{0,4},{4,8},{8,12},{12,0},{1,5},{5,9},{9,13},{13,1},{2,6},{6,10},{... | collective-permute-start | bytes 995336 | tf_op jit(solution)/shard_map/ppermute | solution.py:77
  15.3 12.0 %copy-start.2 = (bf16[864,1024]{1,0:T(8,128)(2,1)S(1)}, bf16[864,1024]{1,0:T(8,128)(2,1)}, u32[]{:S(2)}) copy-start(bf16[864,1024]{1,0:T(8,128)(2,1)} %own.3) | copy-start | bytes 5308420
  30.3 7.4 %collective-permute-start.7 = (bf16[96,1024]{1,0:T(8,128)(2,1)S(1)}, bf16[96,1024]{1,0:T(8,128)(2,1)S(1)}, u32[]{:S(2)}, u32[]{:S(2)}) collective-permute-start(bf16[96,1024]{1,0:T(8,128)(2,1)S(1)} %get-tuple-element.39), channel_id=1, source_target_pairs={{0,1},{1,0},{2,3},{3,2},{4,5},{5,4},{6,7},{7,6},{8,9},{9,8},{10,11... | collective-permute-start | bytes 589832 | tf_op jit(solution)/shard_map/ppermute | solution.py:72
  31.9 12.9 %collective-permute-start.10 = (bf16[192,864]{1,0:T(8,128)(2,1)S(1)}, bf16[192,864]{1,0:T(8,128)(2,1)S(1)}, u32[]{:S(2)}, u32[]{:S(2)}) collective-permute-start(bf16[192,864]{1,0:T(8,128)(2,1)S(1)} %collective-permute-done.6.refs_4_), channel_id=1, source_target_pairs={{0,4},{4,8},{8,12},{12,0},{1,5},{5,9},{9,13},{13,1},{2,6},{6,10},{... | collective-permute-start | bytes 995336 | tf_op jit(solution)/shard_map/ppermute | solution.py:77
  33.5 15.5 %collective-permute-start.17 = (f32[192]{0:T(256)S(1)}, f32[192]{0:T(256)S(1)}, u32[]{:S(2)}, u32[]{:S(2)}) collective-permute-start(f32[192]{0:T(256)S(1)} %add_rsqrt_fusion), channel_id=1, source_target_pairs={{0,12},{4,0},{8,4},{12,8},{1,13},{5,1},{9,5},{13,9},{2,14},{6,2},{... | collective-permute-start | bytes 2312 | tf_op jit(solution)/shard_map/ppermute | solution.py:77
  35.7 13.8 %collective-permute-start.16 = (f32[192]{0:T(256)S(1)}, f32[192]{0:T(256)S(1)}, u32[]{:S(2)}, u32[]{:S(2)}) collective-permute-start(f32[192]{0:T(256)S(1)} %add_rsqrt_fusion), channel_id=1, source_target_pairs={{0,8},{4,12},{8,0},{12,4},{1,9},{5,13},{9,1},{13,5},{2,10},{6,14},... | collective-permute-start | bytes 2312 | tf_op jit(solution)/shard_map/ppermute | solution.py:77
  36.5 5.7 %collective-permute-start.8 = (bf16[96,1024]{1,0:T(8,128)(2,1)S(1)}, bf16[96,1024]{1,0:T(8,128)(2,1)S(1)}, u32[]{:S(2)}, u32[]{:S(2)}) collective-permute-start(bf16[96,1024]{1,0:T(8,128)(2,1)S(1)} %get-tuple-element.40), channel_id=1, source_target_pairs={{0,1},{1,0},{2,3},{3,2},{4,5},{5,4},{6,7},{7,6},{8,9},{9,8},{10,11... | collective-permute-start | bytes 589832 | tf_op jit(solution)/shard_map/ppermute | solution.py:72
  37.8 11.2 %collective-permute-start.9 = (bf16[96,1024]{1,0:T(8,128)(2,1)S(1)}, bf16[96,1024]{1,0:T(8,128)(2,1)S(1)}, u32[]{:S(2)}, u32[]{:S(2)}) collective-permute-start(bf16[96,1024]{1,0:T(8,128)(2,1)S(1)} %select_convert_fusion.1.refs_0_), channel_id=1, source_target_pairs={{0,4},{4,8},{8,12},{12,0},{1,5},{5,9},{9,13},{13,1},{2,6},{6,10},{... | collective-permute-start | bytes 589832 | tf_op jit(solution)/shard_map/ppermute | solution.py:77
  42.3 10.6 %collective-permute-start.14 = (bf16[96,1024]{1,0:T(8,128)(2,1)S(1)}, bf16[96,1024]{1,0:T(8,128)(2,1)S(1)}, u32[]{:S(2)}, u32[]{:S(2)}) collective-permute-start(bf16[96,1024]{1,0:T(8,128)(2,1)S(1)} %select_convert_fusion.refs_1_), channel_id=1, source_target_pairs={{0,4},{4,8},{8,12},{12,0},{1,5},{5,9},{9,13},{13,1},{2,6},{6,10},{... | collective-permute-start | bytes 589832 | tf_op jit(solution)/shard_map/ppermute | solution.py:77
  44.7 8.2 %collective-permute-start.15 = (f32[192]{0:T(256)S(1)}, f32[192]{0:T(256)S(1)}, u32[]{:S(2)}, u32[]{:S(2)}) collective-permute-start(f32[192]{0:T(256)S(1)} %add_rsqrt_fusion), channel_id=1, source_target_pairs={{0,4},{4,8},{8,12},{12,0},{1,5},{5,9},{9,13},{13,1},{2,6},{6,10},{... | collective-permute-start | bytes 2312 | tf_op jit(solution)/shard_map/ppermute | solution.py:77
  49.0 9.4 %collective-permute-start.12 = (bf16[96,1024]{1,0:T(8,128)(2,1)S(1)}, bf16[96,1024]{1,0:T(8,128)(2,1)S(1)}, u32[]{:S(2)}, u32[]{:S(2)}) collective-permute-start(bf16[96,1024]{1,0:T(8,128)(2,1)S(1)} %collective-permute-done.9.refs_6_), channel_id=1, source_target_pairs={{0,4},{4,8},{8,12},{12,0},{1,5},{5,9},{9,13},{13,1},{2,6},{6,10},{... | collective-permute-start | bytes 589832 | tf_op jit(solution)/shard_map/ppermute | solution.py:77
  49.0 12.0 %collective-permute-start.11 = (bf16[192,1024]{1,0:T(8,128)(2,1)S(1)}, bf16[192,1024]{1,0:T(8,128)(2,1)S(1)}, u32[]{:S(2)}, u32[]{:S(2)}) collective-permute-start(bf16[192,1024]{1,0:T(8,128)(2,1)S(1)} %pad_maximum_fusion), channel_id=1, source_target_pairs={{0,1},{1,0},{2,3},{3,2},{4,5},{5,4},{6,7},{7,6},{8,9},{9,8},{10,11... | collective-permute-start | bytes 1179656 | tf_op jit(solution)/shard_map/ppermute | solution.py:72
  52.9 8.1 %collective-permute-start.18 = (bf16[96,1024]{1,0:T(8,128)(2,1)S(1)}, bf16[96,1024]{1,0:T(8,128)(2,1)S(1)}, u32[]{:S(2)}, u32[]{:S(2)}) collective-permute-start(bf16[96,1024]{1,0:T(8,128)(2,1)S(1)} %collective-permute-done.14.refs_7_), channel_id=1, source_target_pairs={{0,4},{4,8},{8,12},{12,0},{1,5},{5,9},{9,13},{13,1},{2,6},{6,10},{... | collective-permute-start | bytes 589832 | tf_op jit(solution)/shard_map/ppermute | solution.py:77
  58.4 10.0 %collective-permute-start.19 = (bf16[288,512]{1,0:T(8,128)(2,1)S(1)}, bf16[288,512]{1,0:T(8,128)(2,1)S(1)}, u32[]{:S(2)}, u32[]{:S(2)}) collective-permute-start(bf16[288,512]{1,0:T(8,128)(2,1)S(1)} %pad_maximum_fusion.2), channel_id=1, source_target_pairs={{0,1},{5,4},{8,9},{13,12},{2,3},{7,6},{10,11},{15,14},{16,17},{21,... | collective-permute-start | bytes 884744 | tf_op jit(solution)/shard_map/ppermute | solution.py:287
  60.9 7.5 %collective-permute-start.20 = (bf16[96,1024]{1,0:T(8,128)(2,1)S(1)}, bf16[96,1024]{1,0:T(8,128)(2,1)S(1)}, u32[]{:S(2)}, u32[]{:S(2)}) collective-permute-start(bf16[96,1024]{1,0:T(8,128)(2,1)S(1)} %collective-permute-done.12.refs_0_), channel_id=1, source_target_pairs={{0,4},{4,8},{8,12},{12,0},{1,5},{5,9},{9,13},{13,1},{2,6},{6,10},{... | collective-permute-start | bytes 589832 | tf_op jit(solution)/shard_map/ppermute | solution.py:77
  61.0 10.8 %collective-permute-start.22 = (bf16[96,1024]{1,0:T(8,128)(2,1)S(1)}, bf16[96,1024]{1,0:T(8,128)(2,1)S(1)}, u32[]{:S(2)}, u32[]{:S(2)}) collective-permute-start(bf16[96,1024]{1,0:T(8,128)(2,1)S(1)} %collective-permute-done.18.refs_1_), channel_id=1, source_target_pairs={{0,4},{4,8},{8,12},{12,0},{1,5},{5,9},{9,13},{13,1},{2,6},{6,10},{... | collective-permute-start | bytes 589832 | tf_op jit(solution)/shard_map/ppermute | solution.py:77
  61.7 11.6 %collective-permute-start.13 = (bf16[192,1024]{1,0:T(8,128)(2,1)S(1)}, bf16[192,1024]{1,0:T(8,128)(2,1)S(1)}, u32[]{:S(2)}, u32[]{:S(2)}) collective-permute-start(bf16[192,1024]{1,0:T(8,128)(2,1)S(1)} %pad_maximum_fusion.1), channel_id=1, source_target_pairs={{0,2},{2,0},{1,3},{3,1},{4,6},{6,4},{5,7},{7,5},{8,10},{10,8},{9,1... | collective-permute-start | bytes 1179656 | tf_op jit(solution)/shard_map/ppermute | solution.py:72
  68.4 4.8 %collective-permute-start.21 = (bf16[192,512]{1,0:T(8,128)(2,1)S(1)}, bf16[192,512]{1,0:T(8,128)(2,1)S(1)}, u32[]{:S(2)}, u32[]{:S(2)}) collective-permute-start(bf16[192,512]{1,0:T(8,128)(2,1)S(1)} %pad_maximum_fusion.3), channel_id=1, source_target_pairs={{0,1},{5,4},{8,9},{13,12},{2,3},{7,6},{10,11},{15,14},{16,17},{21,... | collective-permute-start | bytes 589832 | tf_op jit(solution)/shard_map/ppermute | solution.py:287
  71.8 3.5 %collective-permute-start.23 = (bf16[96,512]{1,0:T(8,128)(2,1)S(1)}, bf16[96,512]{1,0:T(8,128)(2,1)S(1)}, u32[]{:S(2)}, u32[]{:S(2)}) collective-permute-start(bf16[96,512]{1,0:T(8,128)(2,1)S(1)} %constant_dynamic-slice_fusion), channel_id=1, source_target_pairs={{0,1},{5,4},{8,9},{13,12},{2,3},{7,6},{10,11},{15,14},{16,17},{21,... | collective-permute-start | bytes 294920 | tf_op jit(solution)/shard_map/ppermute | solution.py:287
  73.2 4.5 %copy-start.5 = (bf16[192,1024]{1,0:T(8,128)(2,1)}, bf16[192,1024]{1,0:T(8,128)(2,1)S(1)}, u32[]{:S(2)}) copy-start(bf16[192,1024]{1,0:T(8,128)(2,1)S(1)} %collective-permute-done.13) | copy-start | bytes 1179652
  77.7 0.9 %copy-start.3 = (f32[864,256]{1,0:T(8,128)}, f32[864,256]{1,0:T(8,128)S(1)}, u32[]{:S(2)}) copy-start(f32[864,256]{1,0:T(8,128)S(1)} %get-tuple-element.57.cross_in) | copy-start | bytes 2654212
  78.6 2.8 %collective-permute-start.24 = (bf16[944,512]{1,0:T(8,128)(2,1)}, bf16[944,512]{1,0:T(8,128)(2,1)S(1)}, u32[]{:S(2)}, u32[]{:S(2)}) collective-permute-start(bf16[944,512]{1,0:T(8,128)(2,1)} %get-tuple-element.54), channel_id=1, source_target_pairs={{0,2},{2,0},{1,3},{3,1},{4,6},{6,4},{5,7},{7,5},{8,10},{10,8},{9,1... | collective-permute-start | bytes 2899976 | tf_op jit(solution)/shard_map/ppermute | solution.py:72
  78.6 2.8 %copy-start.4 = (f32[864,256]{1,0:T(8,128)S(1)}, f32[864,256]{1,0:T(8,128)}, u32[]{:S(2)}) copy-start(f32[864,256]{1,0:T(8,128)} %copy-done.3) | copy-start | bytes 2654212

commit v7 on v6

--- a/solution.py
+++ b/solution.py
@@ -12,6 +12,26 @@
 
 
 step_rate = 0.2
+ORDER = {
+    "square": ("part",),
+    "n1 out": ("part",),
+    "part2": ("part",),
+    "e in": ("part2",),
+    "n2 out": ("part2",),
+    "held in": ("part2",),
+    "second": ("n1 in",),
+    "sb out": ("n2 in",),
+    "z1a in": ("n3 in",),
+    "x out": ("codes b",),
+    "e2 out": ("z1a in",),
+    "z2b in": ("x in", "e2 in",),
+    "c out": ("x in",),
+    "qd in": ("codes",),
+    "z3b in": ("sums1",),
+    "z3a in": ("qb in",),
+    "qb out": ("z2b in",),
+    "sb in": ("z1a out",),
+}
 
 
 def soften(value, level):
@@ -99,7 +119,7 @@
         in_specs=[slow] + [fast] * len(arrays),
         out_specs=jax.tree.map(lambda _: fast, outs),
         scratch_shapes=scratch,
-        compiler_params=pltpu.CompilerParams(vmem_limit_bytes=24 << 20),
+        compiler_params=pltpu.CompilerParams(vmem_limit_bytes=8 << 20),
         cost_estimate=pl.CostEstimate(flops=1000, bytes_accessed=1000, transcendentals=0),
     )(jnp.stack([x.astype(jnp.int32) for x in scalars]), *arrays)
 
@@ -150,26 +170,26 @@
         base[:, i * block : (i + 1) * block] = known + step_rate * second
 
 
-def sums_body(offsets, where, *refs):
-    n = len(offsets)
-    pieces, totals, (gram, cross, send, lhs, sides, right) = refs[: 6 * n], refs[6 * n : -6], refs[-6:]
+def sums_body(segments, sides_of, where, *refs):
+    n = len(segments)
+    m = len(sides_of)
+    pieces, totals = refs[: 4 * n], refs[4 * n : -3 - m]
+    outs, (lhs, sides, right) = refs[-3 - m : -3], refs[-3:]
     block = right.shape[1]
     width = block // 2
     place = pl.multiple_of(where[0] * block, block)
     here = where[1] == 1
-    rows = lhs.shape[0] // n
-    step = rows // 2
-    for k in range(n):
-        for c in range(2):
-            x, there, offset = pieces[6 * k + c], pieces[6 * k + 2 + c], offsets[k][c]
-            window = slice(k * rows + c * step, k * rows + (c + 1) * step)
-            lhs[window, :] = x[...]
-            spot = pl.multiple_of(where[3 + k] * block, block)
-            right[window, :] = jnp.where(
-                here, x[:, pl.ds(place, block)], there[offset : offset + step, pl.ds(spot, block)]
-            )
-        raw, scale = pieces[6 * k + 4 : 6 * k + 6]
-        sides[k * rows : (k + 1) * rows, :] = (column(scale[...]) * raw[...].astype(f32)).astype(bf16)
+    step = lhs.shape[0] // n
+    for k, (offset, base, entry) in enumerate(segments):
+        x, there, raw, scale = pieces[4 * k : 4 * k + 4]
+        window = slice(k * step, (k + 1) * step)
+        lhs[window, :] = x[...]
+        spot = pl.multiple_of(where[entry] * block, block)
+        right[window, :] = jnp.where(
+            here, x[:, pl.ds(place, block)], there[offset : offset + step, pl.ds(spot, block)]
+        )
+        factor = column(scale[...])[base : base + step]
+        sides[window, :] = (factor * raw[base : base + step, :].astype(f32)).astype(bf16)
     mine = pl.multiple_of(where[2] * width, width)
     theirs = pl.multiple_of((1 - where[2]) * width, width)
     tall = sides.shape[1] // 2
@@ -177,29 +197,27 @@
     def product(a, b):
         return lax.dot_general(a, b, contract_first, preferred_element_type=f32)
 
-    def store(ref, index, value):
-        if totals:
-            value += totals[index[0]][index[1]]
-        ref[index[1]] = value.astype(ref.dtype)
-
-    part = product(lhs[:, block:], right[...])
-    store(send, (2, (slice(0, block), slice(None))), part)
-    part = product(sides[...], right[:, pl.ds(theirs, width)])
-    store(send, (2, (slice(block, block + tall), slice(0, width))), part[:tall])
-    store(send, (2, (slice(block, block + tall), slice(width, block))), part[tall:])
-    store(gram, (0, (slice(None), slice(None))), product(lhs[:, :block], right[...]))
-    store(cross, (1, (slice(None), slice(None))), product(sides[...], right[:, pl.ds(mine, width)]))
-
-
-def add_body(count, _, gram_in, cross_in, sent, gram, cross):
+    for i, ours in enumerate(sides_of):
+        left, columns = (slice(0, block), mine) if ours else (slice(block, 2 * block), theirs)
+        for window, value in (
+            ((slice(0, block), slice(0, block)), product(lhs[:, left], right[...])),
+            ((slice(block, block + tall), slice(0, width)), product(sides[:, :tall], right[:, pl.ds(columns, width)])),
+            ((slice(block, block + tall), slice(width, block)), product(sides[:, tall:], right[:, pl.ds(columns, width)])),
+        ):
+            if totals:
+                value += totals[i][window]
+            outs[i][window] = value.astype(outs[i].dtype)
+
+
+def add_body(count, _, kept, sent, gram, cross):
     block = gram.shape[0]
     width = cross.shape[1]
     tall = cross.shape[0] // 2
-    gram[...] = (gram_in[...] + sent[:block, :].astype(f32)) * (1.0 / count)
+    gram[...] = (kept[:block, :] + sent[:block, :].astype(f32)) * (1.0 / count)
     for i in range(2):
-        window = slice(i * tall, (i + 1) * tall)
-        total = cross_in[window, :] + sent[block:, i * width : (i + 1) * width].astype(f32)
-        cross[window, :] = total * (1.0 / count)
+        window = slice(i * width, (i + 1) * width)
+        total = kept[block:, window] + sent[block:, window].astype(f32)
+        cross[i * tall : (i + 1) * tall, :] = total * (1.0 / count)
 
 
 def group_near(level, half, block):
@@ -220,31 +238,54 @@
     block = atoms // 2
     width = block // 2
     step = rows // 2
+    there_is = {}
+
+    def tie(name, value):
+        earlier = [there_is[x] for x in ORDER.get(name, ())]
+        there_is[name] = after(value, earlier) if earlier else value
+        return there_is[name]
+
+    def send(name, value, how):
+        return how(tie(name + " out", value))
+
+    def over_feat(value):
+        return swap(value, "feat")
+
+    def over_cores(value):
+        return swap(value, "atom")
 
     def blocks(array, which):
         return lax.dynamic_slice_in_dim(array, which * block, block, 1)
-
-    mine = lax.dynamic_slice_in_dim(patches, core * rows, rows, 0)
-    dictionary2 = swap(dictionary, "atom")
-    level = threshold[None, :]
-    level = jnp.concatenate([level, swap(level, "atom")], 1)
-    windows = [slice(c * step, (c + 1) * step) for c in range(2)]
 
     def project(value, d):
         shape = jax.ShapeDtypeStruct((value.shape[0], d.shape[1]), bf16)
         return run(first_body, shape, (half,), (value, d))
 
-    raw_of = [mine, shift(mine)]
-    part = project(mine, dictionary)
-    other = swap(part, "feat")
-    local_sq = jnp.sum(jnp.square(after(mine, part).astype(f32)), axis=1)
-    other_sq = swap(local_sq, "feat")
-    part2 = project(after(mine, part), dictionary2)
-    other2 = swap(part2, "feat")
-    energy = local_sq + after(other_sq, part2)
-    scale = lax.rsqrt(energy / (BINS * VOXELS) + 1e-05)
-    raw_of.append(shift(after(raw_of[1], part2)))
-    held = run(copy_body, jax.ShapeDtypeStruct(dictionary.shape, bf16), (half,), (after(dictionary2, part2),))
+    def scale_from(energy):
+        return lax.rsqrt(energy / (BINS * VOXELS) + 1e-05)
+
+    mine = lax.dynamic_slice_in_dim(patches, core * rows, rows, 0)
+    dictionary2 = tie("d in", send("d", dictionary, over_cores))
+    level = threshold[None, :]
+    level2 = send("level", level, over_cores)
+    part = project(tie("part", mine), dictionary)
+    there_is["part"] = part
+    other = send("f1", part, over_feat)
+    raw_of = [mine, send("n1", mine, shift)]
+    local_sq = jnp.sum(jnp.square(tie("square", mine).astype(f32)), axis=1)
+    other_sq = send("e", local_sq, over_feat)
+    part2 = project(tie("part2", mine), dictionary2)
+    there_is["part2"] = part2
+    other2 = send("f2", part2, over_feat)
+    raw_of[1] = tie("n1 in", raw_of[1])
+    raw_of.append(send("n2", raw_of[1], shift))
+    level = jnp.concatenate([level, tie("level in", level2)], 1)
+    scale = scale_from(local_sq + tie("e in", other_sq))
+    held = tie("held in", dictionary2)
+    held = run(copy_body, jax.ShapeDtypeStruct(dictionary.shape, bf16), (half,), (held,))
+    there_is["held"] = held
+    other, other2 = tie("f1 in", other), tie("f2 in", other2)
+
     half_shape = jax.ShapeDtypeStruct((step, atoms), bf16)
     away_a, away_b, misfit, start = run(
         second_body,
@@ -255,84 +296,104 @@
             jax.ShapeDtypeStruct((rows, 2 * atoms), bf16),
         ),
         (half,),
-        (part, other, part2, other2, mine, scale[None, :], level, dictionary, after(held, raw_of[2])),
-    )
+        (part, other, part2, other2, mine, scale[None, :], level, dictionary, tie("second", held)),
+    )
+    there_is["second"] = away_a
+    raw_of[2] = tie("n2 in", raw_of[2])
+    raw_of.append(send("n3", raw_of[2], shift))
+    back_a = send("sa", away_a, over_feat)
+    back_b = send("sb", away_b, over_feat)
     base = run(
-        base_body, jax.ShapeDtypeStruct((rows, atoms), f32), (half,), (misfit, start, dictionary, held)
-    )
-    raw_of.append(shift(raw_of[2]))
-    backs = [swap(x, "feat") for x in (away_a, away_b)]
-    own_scale = after(scale, away_b)
-    scale_of = [scale] + [shift(own_scale, k) for k in range(1, n_patch)]
+        base_body, jax.ShapeDtypeStruct((rows, atoms), f32), (half,), (tie("base", misfit), start, dictionary, held)
+    )
+    there_is["base"] = base
 
     near_level = step_rate * group_near(level, half, block)
-    codes_of = []
-    done = ()
-    for c in range(2):
-        back = after(backs[c], done).astype(f32)
-        codes_of.append(soft(base[windows[c]] + step_rate * back, near_level).astype(bf16))
-        done = codes_of[c]
-
+
+    def codes_from(back, window):
+        return soft(base[window] + step_rate * back.astype(f32), near_level).astype(bf16)
+
+    codes_of = [codes_from(tie("sa in", back_a), slice(0, step))]
+    there_is["codes a"] = codes_of[0]
+    ring1 = [send("z1a", codes_of[0], shift)]
+    codes_of.append(codes_from(tie("sb in", back_b), slice(step, rows)))
+    there_is["codes b"] = codes_of[1]
+    ring1.append(send("z1b", codes_of[1], shift))
+    raw_of[3] = tie("n3 in", raw_of[3])
+    ring1[0] = tie("z1a in", ring1[0])
+    ring2 = [send("z2a", ring1[0], shift)]
     inside = jnp.concatenate(codes_of, 0)
-    ring1 = [shift(x) for x in codes_of]
-    ring1 = [after(x, y) for x, y in zip(ring1, (raw_of[3], scale_of))]
-    outside = swap(after(inside, ring1[0]), "feat")
-    ring2 = [shift(x) for x in ring1]
+    outside = send("x", inside, over_feat)
+    sums = jnp.concatenate([jnp.sum(jnp.square(x.astype(f32)), axis=1) for x in raw_of[1:]])
+    sums += tie("e2 in", send("e2", sums, over_feat))
+    scales = scale_from(sums)
+    scale_of = [scale] + [scales[k * rows : (k + 1) * rows] for k in range(n_patch - 1)]
 
     home_half = plane % 2
     place = jnp.where(core == plane // 2, 0, 1)
-    over = [(q * 2 + q % 2, q * 2 + 1 - q % 2) for q in range(n_patch)]
-
-    def across(arrays):
-        return lax.ppermute(jnp.concatenate([blocks(x, place) for x in arrays], 0), ("patch", "feat"), over)
-
-    there1 = across([*ring1, ring2[0]])
-    ring2[1] = after(ring2[1], outside)
-    ring3 = [shift(x) for x in ring2]
-    ring3[0] = after(ring3[0], there1)
-    there2 = across([ring2[1], ring3[0]])
-
-    both = [jnp.where(half == 0, inside, outside), jnp.where(half == 0, outside, inside)]
-    upper = jnp.concatenate([x[:, :block] for x in both], 1)
-    lower = after(jnp.concatenate([x[:, block:] for x in both], 1), ring2[0])
-    lower = swap(lower, "atom")
-    ring3[0] = after(ring3[0], lower)
-
-    zero = jnp.zeros_like(place)
+    def own_block(arrays):
+        return jnp.concatenate([blocks(x, place) for x in arrays], 0)
+
+    outside = tie("x in", outside)
+    ring1[1] = tie("z1b in", ring1[1])
+    ring2.append(send("z2b", ring1[1], shift))
+    def whole_codes():
+        both = [jnp.where(half == 0, inside, outside), jnp.where(half == 0, outside, inside)]
+        upper = jnp.concatenate([x[:, :block] for x in both], 1)
+        lower = send("c", jnp.concatenate([x[:, block:] for x in both], 1), over_cores)
+        lower = tie("c in", lower)
+        there_is["codes"] = jnp.where(
+            core == 0, jnp.concatenate([upper, lower], 0), jnp.concatenate([lower, upper], 0)
+        )
+        return there_is["codes"]
+
+    ring2[0] = tie("z2a in", ring2[0])
+    ring3 = [send("z3a", ring2[0], shift)]
+    codes = whole_codes()
+    ring2[1] = tie("z2b in", ring2[1])
+    ring3.append(send("z3b", ring2[1], shift))
+    there1 = send("qa", own_block(ring1), over_feat)
+    there2 = send("qb", own_block(ring2), over_feat)
+    there1 = tie("qa in", there1)
     rings = (codes_of, ring1, ring2, ring3)
-    totals = ()
-    for planes, kind in (((0, 1), f32), ((2, 3), bf16)):
-        if kind == f32:
-            there = ((outside, outside), (there1, there1))
-            offsets = ((0, step), (0, step))
-        else:
-            ring3[1] = after(ring3[1], totals)
-            there = ((there1, there2), (there2, across([ring3[1]])))
-            offsets = ((2 * step, 0), (step, 0))
+
+    def add_products(name, segments, kinds, totals=()):
         pieces = []
-        for i, k in enumerate(planes):
-            pieces += [*rings[k], *there[i], raw_of[k], scale_of[k][None, :]]
+        for i, (k, c, there, _) in enumerate(segments):
+            pieces += [rings[k][c], there if i else tie(name, there), raw_of[k], scale_of[k][None, :]]
         totals = run(
-            functools.partial(sums_body, offsets),
-            (
-                jax.ShapeDtypeStruct((block, block), f32),
-                jax.ShapeDtypeStruct((length, width), f32),
-                jax.ShapeDtypeStruct((block + length // 2, block), kind),
+            functools.partial(
+                sums_body, [(offset, c * step, 4 if k else 3) for k, c, _, offset in segments], tuple(kinds)
             ),
-            (place, half == home_half, core) + tuple(zero if k else place for k in planes),
+            [jax.ShapeDtypeStruct((block + length // 2, block), x) for x in kinds.values()],
+            (place, half == home_half, core, place, jnp.zeros_like(place)),
             (*pieces, *totals),
-            [pltpu.VMEM((len(planes) * rows, size), bf16) for size in (atoms, length, block)],
+            [pltpu.VMEM((len(segments) * step, size), bf16) for size in (atoms, length, block)],
         )
-    gram, cross, send = totals
-    lower = after(lower, send)
-    codes = jnp.where(
-        core == 0, jnp.concatenate([upper, lower], 0), jnp.concatenate([lower, upper], 0)
-    )
+        there_is[name] = totals[0]
+        return totals
+
+    first = [(0, 0, outside, 0), (0, 1, outside, step), (1, 0, there1, 0), (1, 1, there1, step)]
+    totals = add_products("sums1", first, {False: f32, True: f32})
+    there2 = tie("qb in", there2)
+    ring3[0] = tie("z3a in", ring3[0])
+    there3 = [send("qc", own_block(ring3[:1]), over_feat)]
+    second = [(2, 0, there2, 0), (2, 1, there2, step)]
+    totals = add_products("sums2", second, {False: f32, True: f32}, totals)
+    ring3[1] = tie("z3b in", ring3[1])
+    there3.append(send("qd", own_block(ring3[1:]), over_feat))
+    there3[0] = tie("qc in", there3[0])
+    there3[1] = tie("qd in", there3[1])
+    third = [(3, 0, there3[0], 0), (3, 1, there3[1], 0)]
+    (total,) = add_products("sums3", third, {False: bf16}, totals[:1])
+    sent = tie("sent in", send("sent", total, over_cores))
+    third = [(3, 0, after(there3[0], total), 0), (3, 1, there3[1], 0)]
+    (kept,) = add_products("sums4", third, {True: f32}, totals[1:])
     gram, cross = run(
         functools.partial(add_body, count),
         (jax.ShapeDtypeStruct((block, block), f32), jax.ShapeDtypeStruct((length, width), f32)),
         (half,),
-        (gram, cross, after(swap(send, "atom"), codes)),
+        (kept, sent),
     )
     return (codes, gram, cross)
 

time: 83.1 us -> 78.4 us (0.943)
  waiting for transfers between devices: 42.2 us -> 36.4 us
  Pallas kernels: 10.4 us -> 12.7 us
  local copies, waits for them, and re-layouts: 3.57 us -> 2.72 us
    ppermute x12 -> x9, waiting for transfers between devices: 31.6 us -> 20.2 us  [shift(): return lax.ppermute(value, 'patch', [(i, (i + by) % n) for i in range(n)])]
    ppermute x10 -> x15, starting transfers between devices: 6.93 us -> 15.5 us  [swap(): return lax.ppermute(value, axis, [(0, 1), (1, 0)])]
    ppermute x10 -> x15, waiting for transfers between devices: 8.58 us -> 16.2 us  [swap(): return lax.ppermute(value, axis, [(0, 1), (1, 0)])]
    ppermute x3 -> x0, starting transfers between devices: 5.27 us -> none  [across(): lax.ppermute(jnp.concatenate([blocks(x, place) for x in arrays], 0), ('pa...]
    ppermute x12 -> x9, starting transfers between devices: 10.2 us -> 7.46 us  [shift(): return lax.ppermute(value, 'patch', [(i, (i + by) % n) for i in range(n)])]
    pallas_call x8 -> x10, Pallas kernels: 10.4 us -> 12.7 us  [run(): pl.pallas_call(body, out_shape=outs, in_specs=[slow] + [fast] * len(array...]
    ppermute x3 -> x0, waiting for transfers between devices: 2.09 us -> none  [across(): lax.ppermute(jnp.concatenate([blocks(x, place) for x in arrays], 0), ('pa...]
    select_n x2, other arithmetic: 2.59 us -> 1.36 us  [the longest x1 1.16 us: whole_codes(): jnp.where(core == 0, jnp.concatenate([upper, lower], 0), jnp.concatenate(...]
  transfers between devices with their start and end apart: 25 -> 24, of which waited for: 13 -> 14; matrix products, arithmetic and copies ran while one was open for 5% -> 4% of each run, Pallas kernels for 4% -> 13%
where the time goes in v7:
time: 78.4 us; the launch traced here: 78.2 us
  waiting for transfers between devices  36.4 us (46%)
  starting transfers between devices  23 us (29%)
  Pallas kernels  12.7 us (16%)
  local copies, waits for them, and re-layouts  2.72 us (3%)
  other arithmetic  2.53 us (3%)
  between operations  0.89 us (1%)
    ppermute x9, waiting for transfers between devices, shift(): return lax.ppermute(value, 'patch', [(i, (i + by) % n) for i in range(n)])  20.2 us
    ppermute x15, waiting for transfers between devices, swap(): return lax.ppermute(value, axis, [(0, 1), (1, 0)])  16.2 us
    ppermute x15, starting transfers between devices, swap(): return lax.ppermute(value, axis, [(0, 1), (1, 0)])  15.5 us
    pallas_call x10, Pallas kernels, run(): pl.pallas_call(body, out_shape=outs, in_specs=[slow] + [fast] * len(array...  12.7 us
    ppermute x9, starting transfers between devices, shift(): return lax.ppermute(value, 'patch', [(i, (i + by) % n) for i in range(n)])  7.46 us
    unnamed x8, local copies, waits for them, and re-layouts  2.05 us
  transfers between devices with their start and end apart: 24, of which 14 were waited for; matrix products, arithmetic and copies ran while one was open for 4% of the time, Pallas kernels for 13%

profile of v7, /device:TPU:0, one launch (start us, length us, event | category | flops | bytes accessed | tf_op | source)
XLA Modules:
  0.0 78.2 jit_solution(9164580996468415475)
XLA Ops:
  0.6 0.0 copy-start
  0.6 0.5 collective-permute-start.1
  1.2 0.6 copy-done
  1.7 0.2 constant_dynamic-slice_fusion.6
  1.9 0.0 copy-start.3
  1.9 0.2 copy.7.mine.refs_2_.refs_6_
  2.2 1.5 %copy-done.1 = bf16[864,1024]{1,0:T(8,128)(2,1)S(1)} copy-done((bf16[864,1024]{1,0:T(8,128)(2,1)S(1)}, bf16[864,1024]{1,0:T(8,128)(2,1)}, u32[]{:S(2)}) %copy-start.1) | copy-done | bytes 1769496
  3.6 0.6 shard_map.58.part
  4.2 3.0 %collective-permute-start = (bf16[192,1024]{1,0:T(8,128)(2,1)S(1)}, bf16[192,1024]{1,0:T(8,128)(2,1)}, u32[]{:S(2)}, u32[]{:S(2)}) collective-permute-start(bf16[192,1024]{1,0:T(8,128)(2,1)S(1)} %shard_map.58.part), channel_id=1, source_target_pairs={{0,1},{1,0},{2,3},{3,2},{4,5},{5,4},{6,7},{7,6},{8,9},{9,8},{10,11... | collective-permute-start | bytes 1179656 | tf_op jit(solution)/shard_map/ppermute | solution.py:92
  7.2 1.6 %collective-permute-start.5 = (bf16[192,864]{1,0:T(8,128)(2,1)S(1)}, bf16[192,864]{1,0:T(8,128)(2,1)S(1)}, u32[]{:S(2)}, u32[]{:S(2)}) collective-permute-start(bf16[192,864]{1,0:T(8,128)(2,1)S(1)} %copy.7.mine.refs_2_.refs_6_), channel_id=1, source_target_pairs={{0,4},{4,8},{8,12},{12,0},{1,5},{5,9},{9,13},{13,1},{2,6},{6,10},{... | collective-permute-start | bytes 995336 | tf_op jit(solution)/shard_map/ppermute | solution.py:97
  8.8 0.2 multiply_reduce_fusion.3
  9.0 0.6 collective-permute-start.3
  9.6 0.1 stack.18.where
  9.6 0.3 collective-permute-done.4
  10.0 0.6 shard_map.59.part2
  10.6 1.2 %collective-permute-start.2 = (bf16[192,1024]{1,0:T(8,128)(2,1)S(1)}, bf16[192,1024]{1,0:T(8,128)(2,1)S(1)}, u32[]{:S(2)}, u32[]{:S(2)}) collective-permute-start(bf16[192,1024]{1,0:T(8,128)(2,1)S(1)} %shard_map.59.part2), channel_id=1, source_target_pairs={{0,1},{1,0},{2,3},{3,2},{4,5},{5,4},{6,7},{7,6},{8,9},{9,8},{10,11... | collective-permute-start | bytes 1179656 | tf_op jit(solution)/shard_map/ppermute | solution.py:92
  11.9 0.1 shard_map.60.other
  12.0 5.3 %collective-permute-done.3 = f32[192]{0:T(256)S(1)} collective-permute-done((f32[192]{0:T(256)S(1)}, f32[192]{0:T(256)S(1)}, u32[]{:S(2)}, u32[]{:S(2)}) %collective-permute-start.3) | collective-permute-done | bytes 800 | tf_op jit(solution)/shard_map/ppermute | solution.py:92
  17.3 1.3 %collective-permute-done.5.refs_10_.refs_14_ = bf16[192,864]{1,0:T(8,128)(2,1)S(1)} collective-permute-done((bf16[192,864]{1,0:T(8,128)(2,1)S(1)}, bf16[192,864]{1,0:T(8,128)(2,1)S(1)}, u32[]{:S(2)}, u32[]{:S(2)}) %collective-permute-start.5) | collective-permute-done | bytes 331808 | tf_op jit(solution)/shard_map/ppermute | solution.py:97
  18.6 0.8 %collective-permute-start.7 = (bf16[192,864]{1,0:T(8,128)(2,1)S(1)}, bf16[192,864]{1,0:T(8,128)(2,1)S(1)}, u32[]{:S(2)}, u32[]{:S(2)}) collective-permute-start(bf16[192,864]{1,0:T(8,128)(2,1)S(1)} %collective-permute-done.5.refs_10_.refs_14_), channel_id=1, source_target_pairs={{0,4},{4,8},{8,12},{12,0},{1,5},{5,9},{9,13},{13,1},{2,6},{6,10},{... | collective-permute-start | bytes 995336 | tf_op jit(solution)/shard_map/ppermute | solution.py:97
  19.4 5.4 %collective-permute-done.2.arrived2 = bf16[192,1024]{1,0:T(8,128)(2,1)S(1)} collective-permute-done((bf16[192,1024]{1,0:T(8,128)(2,1)S(1)}, bf16[192,1024]{1,0:T(8,128)(2,1)S(1)}, u32[]{:S(2)}, u32[]{:S(2)}) %collective-permute-start.2) | collective-permute-done | bytes 393248 | tf_op jit(solution)/shard_map/ppermute | solution.py:92
  24.8 2.9 %shard_map.61 = (bf16[96,1024]{1,0:T(8,128)(2,1)S(1)}, bf16[96,1024]{1,0:T(8,128)(2,1)S(1)}, bf16[192,864]{1,0:T(8,128)(2,1)S(1)}, bf16[192,2048]{1,0:T(8,128)(2,1)S(1)}) custom-call(s32[1]{0:T(128)} %bitcast._.where, bf16[192,1024]{1,0:T(8,128)(2,1)S(1)} %shard_map.58.part, bf16[192,1024]{1,0:T(8,128)(2,1)} %collective-permute-done.arrived, ...), custom_call_target="tpu_custom_call" | custom-call | flops 1000 | bytes 1000 | tf_op jit(solution)/shard_map/pallas_call | solution.py:116
  27.7 1.8 %collective-permute-start.6 = (bf16[96,1024]{1,0:T(8,128)(2,1)S(1)}, bf16[96,1024]{1,0:T(8,128)(2,1)S(1)}, u32[]{:S(2)}, u32[]{:S(2)}) collective-permute-start(bf16[96,1024]{1,0:T(8,128)(2,1)S(1)} %get-tuple-element.36), channel_id=1, source_target_pairs={{0,1},{1,0},{2,3},{3,2},{4,5},{5,4},{6,7},{7,6},{8,9},{9,8},{10,11... | collective-permute-start | bytes 589832 | tf_op jit(solution)/shard_map/ppermute | solution.py:92
  29.5 0.2 multiply_reduce_fusion.2
  29.7 1.6 %collective-permute-start.12 = (bf16[192,864]{1,0:T(8,128)(2,1)S(1)}, bf16[192,864]{1,0:T(8,128)(2,1)S(1)}, u32[]{:S(2)}, u32[]{:S(2)}) collective-permute-start(bf16[192,864]{1,0:T(8,128)(2,1)S(1)} %collective-permute-done.7.refs_2_.refs_6_), channel_id=1, source_target_pairs={{0,4},{4,8},{8,12},{12,0},{1,5},{5,9},{9,13},{13,1},{2,6},{6,10},{... | collective-permute-start | bytes 995336 | tf_op jit(solution)/shard_map/ppermute | solution.py:97
  31.3 0.2 multiply_reduce_fusion.1
  31.4 0.6 collective-permute-start.8
  32.1 0.6 shard_map.62
  32.7 2.6 %collective-permute-done.6 = bf16[96,1024]{1,0:T(8,128)(2,1)S(1)} collective-permute-done((bf16[96,1024]{1,0:T(8,128)(2,1)S(1)}, bf16[96,1024]{1,0:T(8,128)(2,1)S(1)}, u32[]{:S(2)}, u32[]{:S(2)}) %collective-permute-start.6) | collective-permute-done | bytes 196640 | tf_op jit(solution)/shard_map/ppermute | solution.py:92
  35.2 0.1 select_convert_fusion.1.refs_0_
  35.3 1.5 %collective-permute-start.11 = (bf16[96,1024]{1,0:T(8,128)(2,1)S(1)}, bf16[96,1024]{1,0:T(8,128)(2,1)S(1)}, u32[]{:S(2)}, u32[]{:S(2)}) collective-permute-start(bf16[96,1024]{1,0:T(8,128)(2,1)S(1)} %select_convert_fusion.1.refs_0_), channel_id=1, source_target_pairs={{0,4},{4,8},{8,12},{12,0},{1,5},{5,9},{9,13},{13,1},{2,6},{6,10},{... | collective-permute-start | bytes 589832 | tf_op jit(solution)/shard_map/ppermute | solution.py:97
  36.9 1.2 %collective-permute-done.8 = bf16[96,1024]{1,0:T(8,128)(2,1)S(1)} collective-permute-done((bf16[96,1024]{1,0:T(8,128)(2,1)S(1)}, bf16[96,1024]{1,0:T(8,128)(2,1)S(1)}, u32[]{:S(2)}, u32[]{:S(2)}) %collective-permute-start.8) | collective-permute-done | bytes 196640 | tf_op jit(solution)/shard_map/ppermute | solution.py:92
  38.1 0.1 select_convert_fusion.refs_4_
  38.2 1.6 %collective-permute-start.15 = (bf16[96,1024]{1,0:T(8,128)(2,1)S(1)}, bf16[96,1024]{1,0:T(8,128)(2,1)S(1)}, u32[]{:S(2)}, u32[]{:S(2)}) collective-permute-start(bf16[96,1024]{1,0:T(8,128)(2,1)S(1)} %select_convert_fusion.refs_4_), channel_id=1, source_target_pairs={{0,4},{4,8},{8,12},{12,0},{1,5},{5,9},{9,13},{13,1},{2,6},{6,10},{... | collective-permute-start | bytes 589832 | tf_op jit(solution)/shard_map/ppermute | solution.py:97
  39.8 1.5 %collective-permute-start.9 = (bf16[192,1024]{1,0:T(8,128)(2,1)S(1)}, bf16[192,1024]{1,0:T(8,128)(2,1)S(1)}, u32[]{:S(2)}, u32[]{:S(2)}) collective-permute-start(bf16[192,1024]{1,0:T(8,128)(2,1)S(1)} %pad_maximum_fusion), channel_id=1, source_target_pairs={{0,1},{1,0},{2,3},{3,2},{4,5},{5,4},{6,7},{7,6},{8,9},{9,8},{10,11... | collective-permute-start | bytes 1179656 | tf_op jit(solution)/shard_map/ppermute | solution.py:92
  41.3 1.2 %collective-permute-done.12.refs_2_.refs_6_ = bf16[192,864]{1,0:T(8,128)(2,1)S(1)} collective-permute-done((bf16[192,864]{1,0:T(8,128)(2,1)S(1)}, bf16[192,864]{1,0:T(8,128)(2,1)S(1)}, u32[]{:S(2)}, u32[]{:S(2)}) %collective-permute-start.12) | collective-permute-done | bytes 331808 | tf_op jit(solution)/shard_map/ppermute | solution.py:97
  42.5 0.2 multiply_reduce_fusion
  42.7 0.1 pad_maximum_fusion.5
  42.7 3.8 %collective-permute-done.11.refs_8_ = bf16[96,1024]{1,0:T(8,128)(2,1)S(1)} collective-permute-done((bf16[96,1024]{1,0:T(8,128)(2,1)S(1)}, bf16[96,1024]{1,0:T(8,128)(2,1)S(1)}, u32[]{:S(2)}, u32[]{:S(2)}) %collective-permute-start.11) | collective-permute-done | bytes 196640 | tf_op jit(solution)/shard_map/ppermute | solution.py:97
  46.6 0.6 collective-permute-start.17
  47.1 3.5 %collective-permute-done.15.refs_12_ = bf16[96,1024]{1,0:T(8,128)(2,1)S(1)} collective-permute-done((bf16[96,1024]{1,0:T(8,128)(2,1)S(1)}, bf16[96,1024]{1,0:T(8,128)(2,1)S(1)}, u32[]{:S(2)}, u32[]{:S(2)}) %collective-permute-start.15) | collective-permute-done | bytes 196640 | tf_op jit(solution)/shard_map/ppermute | solution.py:97
  50.6 0.5 collective-permute-start.21
  51.1 0.0 collective-permute-start.16
  51.1 0.1 add_rsqrt_fusion
  51.2 0.2 broadcast_select_fusion.1
  51.4 0.1 fusion.3
  51.5 0.1 collective-permute-start.10
  51.6 7.0 %collective-permute-done.16.refs_4_ = bf16[96,1024]{1,0:T(8,128)(2,1)S(1)} collective-permute-done((bf16[96,1024]{1,0:T(8,128)(2,1)S(1)}, bf16[96,1024]{1,0:T(8,128)(2,1)S(1)}, u32[]{:S(2)}, u32[]{:S(2)}) %collective-permute-start.16) | collective-permute-done | bytes 196640 | tf_op jit(solution)/shard_map/ppermute | solution.py:97
  58.6 1.7 %collective-permute-start.18 = (bf16[192,512]{1,0:T(8,128)(2,1)S(1)}, bf16[192,512]{1,0:T(8,128)(2,1)S(1)}, u32[]{:S(2)}, u32[]{:S(2)}) collective-permute-start(bf16[192,512]{1,0:T(8,128)(2,1)S(1)} %pad_maximum_fusion.2), channel_id=1, source_target_pairs={{0,1},{1,0},{2,3},{3,2},{4,5},{5,4},{6,7},{7,6},{8,9},{9,8},{10,11... | collective-permute-start | bytes 589832 | tf_op jit(solution)/shard_map/ppermute | solution.py:92
  60.3 0.3 collective-permute-start.14
  60.7 0.1 fusion.5
  60.7 2.3 %shard_map.63 = (f32[944,512]{1,0:T(8,128)S(1)}, f32[944,512]{1,0:T(8,128)S(1)}) custom-call(s32[5]{0:T(128)S(1)} %stack.18.where, bf16[96,1024]{1,0:T(8,128)(2,1)S(1)} %select_convert_fusion.1.refs_0_, bf16[192,1024]{1,0:T(8,128)(2,1)S(1)} %collective-permute-done.9.refs_1_.refs_5_, bf16[192,864]{1,0:T(8,128)(2,1)S(1)} %copy.7.mine.refs_2_.refs_6_, ...), custom_call_target="tpu_custom_call" | custom-call | flops 1000 | bytes 1000 | tf_op jit(solution)/shard_map/pallas_call | solution.py:116
  63.0 3.0 %collective-permute-done.20.refs_4_ = bf16[96,1024]{1,0:T(8,128)(2,1)S(1)} collective-permute-done((bf16[96,1024]{1,0:T(8,128)(2,1)S(1)}, bf16[96,1024]{1,0:T(8,128)(2,1)S(1)}, u32[]{:S(2)}, u32[]{:S(2)}) %collective-permute-start.20) | collective-permute-done | bytes 196640 | tf_op jit(solution)/shard_map/ppermute | solution.py:97
  66.1 1.7 %collective-permute-start.22 = (bf16[96,512]{1,0:T(8,128)(2,1)S(1)}, bf16[96,512]{1,0:T(8,128)(2,1)S(1)}, u32[]{:S(2)}, u32[]{:S(2)}) collective-permute-start(bf16[96,512]{1,0:T(8,128)(2,1)S(1)} %constant_dynamic-slice_fusion), channel_id=1, source_target_pairs={{0,1},{1,0},{2,3},{3,2},{4,5},{5,4},{6,7},{7,6},{8,9},{9,8},{10,11... | collective-permute-start | bytes 294920 | tf_op jit(solution)/shard_map/ppermute | solution.py:92
  67.7 0.4 collective-permute-done.14.refs_0_
  68.2 1.7 %collective-permute-start.19 = (bf16[96,512]{1,0:T(8,128)(2,1)S(1)}, bf16[96,512]{1,0:T(8,128)(2,1)S(1)}, u32[]{:S(2)}, u32[]{:S(2)}) collective-permute-start(bf16[96,512]{1,0:T(8,128)(2,1)S(1)} %constant_dynamic-slice_fusion.3), channel_id=1, source_target_pairs={{0,1},{1,0},{2,3},{3,2},{4,5},{5,4},{6,7},{7,6},{8,9},{9,8},{10,11... | collective-permute-start | bytes 294920 | tf_op jit(solution)/shard_map/ppermute | solution.py:92
  69.8 1.6 %shard_map.64 = (f32[944,512]{1,0:T(8,128)S(1)}, f32[944,512]{1,0:T(8,128)S(1)}) custom-call(s32[5]{0:T(128)S(1)} %stack.18.where, bf16[96,1024]{1,0:T(8,128)(2,1)S(1)} %collective-permute-done.13.refs_0_, bf16[192,512]{1,0:T(8,128)(2,1)S(1)} %collective-permute-done.18.refs_1_.refs_5_, bf16[192,864]{1,0:T(8,128)(2,1)S(1)} %collective-permute-done.7.refs_2_.refs_6_, ...), custom_call_target="tpu_custom_call" | custom-call | flops 1000 | bytes 1000 | tf_op jit(solution)/shard_map/pallas_call | solution.py:116
  71.5 1.2 %maximum_select_fusion = bf16[384,1024]{1,0:T(8,128)(2,1)} fusion(bf16[192,1024]{1,0:T(8,128)(2,1)S(1)} %collective-permute-done.10, bf16[192,512]{1,0:T(8,128)(2,1)S(1)} %get-tuple-element.71, bf16[192,512]{1,0:T(8,128)(2,1)S(1)} %get-tuple-element.59, pred[]{:T(512)S(6)} %eq.18), kind=kLoop, calls=%fused_computation | loop fusion | flops 5111808 | bytes 1572865 | tf_op jit(solution)/shard_map/jit(_where)/select_n | solution.py:345
  72.6 0.2 collective-permute-done.19.refs_1_
  72.8 1.3 %shard_map.65 = bf16[944,512]{1,0:T(8,128)(2,1)S(1)} custom-call(s32[5]{0:T(128)S(1)} %stack.18.where, bf16[96,1024]{1,0:T(8,128)(2,1)S(1)} %collective-permute-done.14.refs_0_, bf16[96,512]{1,0:T(8,128)(2,1)S(1)} %collective-permute-done.19.refs_1_, bf16[192,864]{1,0:T(8,128)(2,1)S(1)} %collective-permute-done.12.refs_2_.refs_6_, f32[1,192]{1,0:T(1,128)S(1)} %bitcast.11, ...), custom_call_target="tpu_custom_call" | custom-call | flops 1000 | bytes 1000 | tf_op jit(solution)/shard_map/pallas_call | solution.py:116
  74.1 0.1 collective-permute-start.23
  74.2 1.3 %shard_map.66.kept = f32[944,512]{1,0:T(8,128)S(1)} custom-call(s32[5]{0:T(128)S(1)} %stack.18.where, bf16[96,1024]{1,0:T(8,128)(2,1)S(1)} %collective-permute-done.14.refs_0_, bf16[96,512]{1,0:T(8,128)(2,1)S(1)} %collective-permute-done.19.refs_1_, bf16[192,864]{1,0:T(8,128)(2,1)S(1)} %collective-permute-done.12.refs_2_.refs_6_, f32[1,192]{1,0:T(1,128)S(1)} %bitcast.13, ...), custom_call_target="tpu_custom_call" | custom-call | flops 1000 | bytes 1000 | tf_op jit(solution)/shard_map/pallas_call | solution.py:116
  75.5 1.2 %collective-permute-done.23.sent = bf16[944,512]{1,0:T(8,128)(2,1)S(1)} collective-permute-done((bf16[944,512]{1,0:T(8,128)(2,1)S(1)}, bf16[944,512]{1,0:T(8,128)(2,1)S(1)}, u32[]{:S(2)}, u32[]{:S(2)}) %collective-permute-start.23) | collective-permute-done | bytes 966688 | tf_op jit(solution)/shard_map/ppermute | solution.py:92
  76.7 1.4 %shard_map.67 = (f32[512,512]{1,0:T(8,128)}, f32[864,256]{1,0:T(8,128)}) custom-call(s32[1]{0:T(128)} %bitcast._.where, f32[944,512]{1,0:T(8,128)S(1)} %shard_map.66.kept, bf16[944,512]{1,0:T(8,128)(2,1)S(1)} %collective-permute-done.23.sent), custom_call_target="tpu_custom_call" | custom-call | flops 1000 | bytes 1000 | tf_op jit(solution)/shard_map/pallas_call | solution.py:116
  (31 shorter events, 0.2 us)
Async XLA Ops:
  0.6 1.1 %copy-start = (bf16[384,864]{0,1:T(8,128)(2,1)S(1)}, bf16[384,864]{0,1:T(8,128)(2,1)}, u32[]{:S(2)}) copy-start(bf16[384,864]{0,1:T(8,128)(2,1)} %param.3) | copy-start | bytes 1990660
  0.6 9.4 %collective-permute-start.1 = (bf16[864,1024]{1,0:T(8,128)(2,1)}, bf16[864,1024]{1,0:T(8,128)(2,1)S(1)}, u32[]{:S(2)}, u32[]{:S(2)}) collective-permute-start(bf16[864,1024]{1,0:T(8,128)(2,1)} %own.3), channel_id=1, source_target_pairs={{0,2},{2,0},{1,3},{3,1},{4,6},{6,4},{5,7},{7,5},{8,10},{10,8},{9,1... | collective-permute-start | bytes 5308424 | tf_op jit(solution)/shard_map/ppermute | solution.py:92
  1.9 6.9 %copy-start.3 = (f32[1024]{0:T(1024)S(1)}, f32[1024]{0:T(1024)}, u32[]{:S(2)}) copy-start(f32[1024]{0:T(1024)} %param.5) | copy-start | bytes 12292
  2.1 1.5 %copy-start.1 = (bf16[864,1024]{1,0:T(8,128)(2,1)S(1)}, bf16[864,1024]{1,0:T(8,128)(2,1)}, u32[]{:S(2)}) copy-start(bf16[864,1024]{1,0:T(8,128)(2,1)} %own.3) | copy-start | bytes 5308420
  4.2 15.2 %collective-permute-start = (bf16[192,1024]{1,0:T(8,128)(2,1)S(1)}, bf16[192,1024]{1,0:T(8,128)(2,1)}, u32[]{:S(2)}, u32[]{:S(2)}) collective-permute-start(bf16[192,1024]{1,0:T(8,128)(2,1)S(1)} %shard_map.58.part), channel_id=1, source_target_pairs={{0,1},{1,0},{2,3},{3,2},{4,5},{5,4},{6,7},{7,6},{8,9},{9,8},{10,11... | collective-permute-start | bytes 1179656 | tf_op jit(solution)/shard_map/ppermute | solution.py:92
  7.2 11.4 %collective-permute-start.5 = (bf16[192,864]{1,0:T(8,128)(2,1)S(1)}, bf16[192,864]{1,0:T(8,128)(2,1)S(1)}, u32[]{:S(2)}, u32[]{:S(2)}) collective-permute-start(bf16[192,864]{1,0:T(8,128)(2,1)S(1)} %copy.7.mine.refs_2_.refs_6_), channel_id=1, source_target_pairs={{0,4},{4,8},{8,12},{12,0},{1,5},{5,9},{9,13},{13,1},{2,6},{6,10},{... | collective-permute-start | bytes 995336 | tf_op jit(solution)/shard_map/ppermute | solution.py:97
  8.8 1.2 %collective-permute-start.4 = (f32[1,1024]{1,0:T(1,128)S(1)}, f32[1,1024]{1,0:T(1,128)S(1)}, u32[]{:S(2)}, u32[]{:S(2)}) collective-permute-start(f32[1,1024]{1,0:T(1,128)S(1)} %bitcast.22), channel_id=1, source_target_pairs={{0,2},{2,0},{1,3},{3,1},{4,6},{6,4},{5,7},{7,5},{8,10},{10,8},{9,1... | collective-permute-start | bytes 12296 | tf_op jit(solution)/shard_map/ppermute | solution.py:92
  9.0 8.3 %collective-permute-start.3 = (f32[192]{0:T(256)S(1)}, f32[192]{0:T(256)S(1)}, u32[]{:S(2)}, u32[]{:S(2)}) collective-permute-start(f32[192]{0:T(256)S(1)} %multiply_reduce_fusion.3), channel_id=1, source_target_pairs={{0,1},{1,0},{2,3},{3,2},{4,5},{5,4},{6,7},{7,6},{8,9},{9,8},{10,11... | collective-permute-start | bytes 2312 | tf_op jit(solution)/shard_map/ppermute | solution.py:92
  10.6 14.2 %collective-permute-start.2 = (bf16[192,1024]{1,0:T(8,128)(2,1)S(1)}, bf16[192,1024]{1,0:T(8,128)(2,1)S(1)}, u32[]{:S(2)}, u32[]{:S(2)}) collective-permute-start(bf16[192,1024]{1,0:T(8,128)(2,1)S(1)} %shard_map.59.part2), channel_id=1, source_target_pairs={{0,1},{1,0},{2,3},{3,2},{4,5},{5,4},{6,7},{7,6},{8,9},{9,8},{10,11... | collective-permute-start | bytes 1179656 | tf_op jit(solution)/shard_map/ppermute | solution.py:92
  11.9 12.9 %copy-start.2 = (bf16[864,1024]{1,0:T(8,128)(2,1)S(1)}, bf16[864,1024]{1,0:T(8,128)(2,1)}, u32[]{:S(2)}) copy-start(bf16[864,1024]{1,0:T(8,128)(2,1)} %own.3) | copy-start | bytes 5308420
  18.6 11.1 %collective-permute-start.7 = (bf16[192,864]{1,0:T(8,128)(2,1)S(1)}, bf16[192,864]{1,0:T(8,128)(2,1)S(1)}, u32[]{:S(2)}, u32[]{:S(2)}) collective-permute-start(bf16[192,864]{1,0:T(8,128)(2,1)S(1)} %collective-permute-done.5.refs_10_.refs_14_), channel_id=1, source_target_pairs={{0,4},{4,8},{8,12},{12,0},{1,5},{5,9},{9,13},{13,1},{2,6},{6,10},{... | collective-permute-start | bytes 995336 | tf_op jit(solution)/shard_map/ppermute | solution.py:97
  27.7 7.5 %collective-permute-start.6 = (bf16[96,1024]{1,0:T(8,128)(2,1)S(1)}, bf16[96,1024]{1,0:T(8,128)(2,1)S(1)}, u32[]{:S(2)}, u32[]{:S(2)}) collective-permute-start(bf16[96,1024]{1,0:T(8,128)(2,1)S(1)} %get-tuple-element.36), channel_id=1, source_target_pairs={{0,1},{1,0},{2,3},{3,2},{4,5},{5,4},{6,7},{7,6},{8,9},{9,8},{10,11... | collective-permute-start | bytes 589832 | tf_op jit(solution)/shard_map/ppermute | solution.py:92
  29.7 12.8 %collective-permute-start.12 = (bf16[192,864]{1,0:T(8,128)(2,1)S(1)}, bf16[192,864]{1,0:T(8,128)(2,1)S(1)}, u32[]{:S(2)}, u32[]{:S(2)}) collective-permute-start(bf16[192,864]{1,0:T(8,128)(2,1)S(1)} %collective-permute-done.7.refs_2_.refs_6_), channel_id=1, source_target_pairs={{0,4},{4,8},{8,12},{12,0},{1,5},{5,9},{9,13},{13,1},{2,6},{6,10},{... | collective-permute-start | bytes 995336 | tf_op jit(solution)/shard_map/ppermute | solution.py:97
  31.4 6.6 %collective-permute-start.8 = (bf16[96,1024]{1,0:T(8,128)(2,1)S(1)}, bf16[96,1024]{1,0:T(8,128)(2,1)S(1)}, u32[]{:S(2)}, u32[]{:S(2)}) collective-permute-start(bf16[96,1024]{1,0:T(8,128)(2,1)S(1)} %get-tuple-element.39), channel_id=1, source_target_pairs={{0,1},{1,0},{2,3},{3,2},{4,5},{5,4},{6,7},{7,6},{8,9},{9,8},{10,11... | collective-permute-start | bytes 589832 | tf_op jit(solution)/shard_map/ppermute | solution.py:92
  35.3 11.2 %collective-permute-start.11 = (bf16[96,1024]{1,0:T(8,128)(2,1)S(1)}, bf16[96,1024]{1,0:T(8,128)(2,1)S(1)}, u32[]{:S(2)}, u32[]{:S(2)}) collective-permute-start(bf16[96,1024]{1,0:T(8,128)(2,1)S(1)} %select_convert_fusion.1.refs_0_), channel_id=1, source_target_pairs={{0,4},{4,8},{8,12},{12,0},{1,5},{5,9},{9,13},{13,1},{2,6},{6,10},{... | collective-permute-start | bytes 589832 | tf_op jit(solution)/shard_map/ppermute | solution.py:97
  38.2 12.4 %collective-permute-start.15 = (bf16[96,1024]{1,0:T(8,128)(2,1)S(1)}, bf16[96,1024]{1,0:T(8,128)(2,1)S(1)}, u32[]{:S(2)}, u32[]{:S(2)}) collective-permute-start(bf16[96,1024]{1,0:T(8,128)(2,1)S(1)} %select_convert_fusion.refs_4_), channel_id=1, source_target_pairs={{0,4},{4,8},{8,12},{12,0},{1,5},{5,9},{9,13},{13,1},{2,6},{6,10},{... | collective-permute-start | bytes 589832 | tf_op jit(solution)/shard_map/ppermute | solution.py:97
  39.8 11.4 %collective-permute-start.9 = (bf16[192,1024]{1,0:T(8,128)(2,1)S(1)}, bf16[192,1024]{1,0:T(8,128)(2,1)S(1)}, u32[]{:S(2)}, u32[]{:S(2)}) collective-permute-start(bf16[192,1024]{1,0:T(8,128)(2,1)S(1)} %pad_maximum_fusion), channel_id=1, source_target_pairs={{0,1},{1,0},{2,3},{3,2},{4,5},{5,4},{6,7},{7,6},{8,9},{9,8},{10,11... | collective-permute-start | bytes 1179656 | tf_op jit(solution)/shard_map/ppermute | solution.py:92
  46.5 12.0 %collective-permute-start.13 = (bf16[96,1024]{1,0:T(8,128)(2,1)S(1)}, bf16[96,1024]{1,0:T(8,128)(2,1)S(1)}, u32[]{:S(2)}, u32[]{:S(2)}) collective-permute-start(bf16[96,1024]{1,0:T(8,128)(2,1)S(1)} %collective-permute-done.11.refs_8_), channel_id=1, source_target_pairs={{0,4},{4,8},{8,12},{12,0},{1,5},{5,9},{9,13},{13,1},{2,6},{6,10},{... | collective-permute-start | bytes 589832 | tf_op jit(solution)/shard_map/ppermute | solution.py:97
  46.6 4.6 %collective-permute-start.17 = (f32[576]{0:T(1024)S(1)}, f32[576]{0:T(1024)S(1)}, u32[]{:S(2)}, u32[]{:S(2)}) collective-permute-start(f32[576]{0:T(1024)S(1)} %pad_maximum_fusion.5), channel_id=1, source_target_pairs={{0,1},{1,0},{2,3},{3,2},{4,5},{5,4},{6,7},{7,6},{8,9},{9,8},{10,11... | collective-permute-start | bytes 6920 | tf_op jit(solution)/shard_map/ppermute | solution.py:92
  50.6 10.1 %collective-permute-start.21 = (bf16[192,512]{1,0:T(8,128)(2,1)S(1)}, bf16[192,512]{1,0:T(8,128)(2,1)S(1)}, u32[]{:S(2)}, u32[]{:S(2)}) collective-permute-start(bf16[192,512]{1,0:T(8,128)(2,1)S(1)} %pad_maximum_fusion.3), channel_id=1, source_target_pairs={{0,1},{1,0},{2,3},{3,2},{4,5},{5,4},{6,7},{7,6},{8,9},{9,8},{10,11... | collective-permute-start | bytes 589832 | tf_op jit(solution)/shard_map/ppermute | solution.py:92
  51.1 7.5 %collective-permute-start.16 = (bf16[96,1024]{1,0:T(8,128)(2,1)S(1)}, bf16[96,1024]{1,0:T(8,128)(2,1)S(1)}, u32[]{:S(2)}, u32[]{:S(2)}) collective-permute-start(bf16[96,1024]{1,0:T(8,128)(2,1)S(1)} %collective-permute-done.15.refs_12_), channel_id=1, source_target_pairs={{0,4},{4,8},{8,12},{12,0},{1,5},{5,9},{9,13},{13,1},{2,6},{6,10},{... | collective-permute-start | bytes 589832 | tf_op jit(solution)/shard_map/ppermute | solution.py:97
  51.5 19.9 %collective-permute-start.10 = (bf16[192,1024]{1,0:T(8,128)(2,1)S(1)}, bf16[192,1024]{1,0:T(8,128)(2,1)S(1)}, u32[]{:S(2)}, u32[]{:S(2)}) collective-permute-start(bf16[192,1024]{1,0:T(8,128)(2,1)S(1)} %pad_maximum_fusion.1), channel_id=1, source_target_pairs={{0,2},{2,0},{1,3},{3,1},{4,6},{6,4},{5,7},{7,5},{8,10},{10,8},{9,1... | collective-permute-start | bytes 1179656 | tf_op jit(solution)/shard_map/ppermute | solution.py:92
  58.6 7.5 %collective-permute-start.20 = (bf16[96,1024]{1,0:T(8,128)(2,1)S(1)}, bf16[96,1024]{1,0:T(8,128)(2,1)S(1)}, u32[]{:S(2)}, u32[]{:S(2)}) collective-permute-start(bf16[96,1024]{1,0:T(8,128)(2,1)S(1)} %collective-permute-done.16.refs_4_), channel_id=1, source_target_pairs={{0,4},{4,8},{8,12},{12,0},{1,5},{5,9},{9,13},{13,1},{2,6},{6,10},{... | collective-permute-start | bytes 589832 | tf_op jit(solution)/shard_map/ppermute | solution.py:97
  58.6 9.1 %collective-permute-start.18 = (bf16[192,512]{1,0:T(8,128)(2,1)S(1)}, bf16[192,512]{1,0:T(8,128)(2,1)S(1)}, u32[]{:S(2)}, u32[]{:S(2)}) collective-permute-start(bf16[192,512]{1,0:T(8,128)(2,1)S(1)} %pad_maximum_fusion.2), channel_id=1, source_target_pairs={{0,1},{1,0},{2,3},{3,2},{4,5},{5,4},{6,7},{7,6},{8,9},{9,8},{10,11... | collective-permute-start | bytes 589832 | tf_op jit(solution)/shard_map/ppermute | solution.py:92
  60.3 7.8 %collective-permute-start.14 = (bf16[96,1024]{1,0:T(8,128)(2,1)S(1)}, bf16[96,1024]{1,0:T(8,128)(2,1)S(1)}, u32[]{:S(2)}, u32[]{:S(2)}) collective-permute-start(bf16[96,1024]{1,0:T(8,128)(2,1)S(1)} %collective-permute-done.13.refs_0_), channel_id=1, source_target_pairs={{0,4},{4,8},{8,12},{12,0},{1,5},{5,9},{9,13},{13,1},{2,6},{6,10},{... | collective-permute-start | bytes 589832 | tf_op jit(solution)/shard_map/ppermute | solution.py:97
  66.1 6.6 %collective-permute-start.22 = (bf16[96,512]{1,0:T(8,128)(2,1)S(1)}, bf16[96,512]{1,0:T(8,128)(2,1)S(1)}, u32[]{:S(2)}, u32[]{:S(2)}) collective-permute-start(bf16[96,512]{1,0:T(8,128)(2,1)S(1)} %constant_dynamic-slice_fusion), channel_id=1, source_target_pairs={{0,1},{1,0},{2,3},{3,2},{4,5},{5,4},{6,7},{7,6},{8,9},{9,8},{10,11... | collective-permute-start | bytes 294920 | tf_op jit(solution)/shard_map/ppermute | solution.py:92
  68.2 4.7 %collective-permute-start.19 = (bf16[96,512]{1,0:T(8,128)(2,1)S(1)}, bf16[96,512]{1,0:T(8,128)(2,1)S(1)}, u32[]{:S(2)}, u32[]{:S(2)}) collective-permute-start(bf16[96,512]{1,0:T(8,128)(2,1)S(1)} %constant_dynamic-slice_fusion.3), channel_id=1, source_target_pairs={{0,1},{1,0},{2,3},{3,2},{4,5},{5,4},{6,7},{7,6},{8,9},{9,8},{10,11... | collective-permute-start | bytes 294920 | tf_op jit(solution)/shard_map/ppermute | solution.py:92
  74.1 2.6 %collective-permute-start.23 = (bf16[944,512]{1,0:T(8,128)(2,1)S(1)}, bf16[944,512]{1,0:T(8,128)(2,1)S(1)}, u32[]{:S(2)}, u32[]{:S(2)}) collective-permute-start(bf16[944,512]{1,0:T(8,128)(2,1)S(1)} %shard_map.65), channel_id=1, source_target_pairs={{0,2},{2,0},{1,3},{3,1},{4,6},{6,4},{5,7},{7,5},{8,10},{10,8},{9,1... | collective-permute-start | bytes 2899976 | tf_op jit(solution)/shard_map/ppermute | solution.py:92

commit v8 on v7

--- a/solution.py
+++ b/solution.py
@@ -22,15 +22,14 @@
     "second": ("n1 in",),
     "sb out": ("n2 in",),
     "z1a in": ("n3 in",),
-    "x out": ("codes b",),
     "e2 out": ("z1a in",),
     "z2b in": ("x in", "e2 in",),
-    "c out": ("x in",),
-    "qd in": ("codes",),
+    "c out": ("z1b in",),
     "z3b in": ("sums1",),
-    "z3a in": ("qb in",),
-    "qb out": ("z2b in",),
+    "z3a in": ("qa in",),
     "sb in": ("z1a out",),
+    "z1b in": ("e2 in",),
+    "sums2": ("codes",),
 }
 
 

time: 78.4 us -> 76.7 us (0.978)
  starting transfers between devices: 23 us -> 21.5 us
    ppermute x15, starting transfers between devices: 15.5 us -> 13.2 us  [swap(): return lax.ppermute(value, axis, [(0, 1), (1, 0)])]
    ppermute x9, starting transfers between devices: 7.46 us -> 8.3 us  [shift(): return lax.ppermute(value, 'patch', [(i, (i + by) % n) for i in range(n)])]
  transfers between devices with their start and end apart: 24 -> 24, of which waited for: 14 -> 15; matrix products, arithmetic and copies ran while one was open for 4% -> 4% of each run, Pallas kernels for 13% -> 13%
where the time goes in v8:
time: 76.7 us; the launch traced here: 76.5 us
  waiting for transfers between devices  36.2 us (47%)
  starting transfers between devices  21.5 us (28%)
  Pallas kernels  12.6 us (16%)
  local copies, waits for them, and re-layouts  2.71 us (4%)
  other arithmetic  2.52 us (3%)
  between operations  0.88 us (1%)
    ppermute x9, waiting for transfers between devices, shift(): return lax.ppermute(value, 'patch', [(i, (i + by) % n) for i in range(n)])  19.6 us
    ppermute x15, waiting for transfers between devices, swap(): return lax.ppermute(value, axis, [(0, 1), (1, 0)])  16.6 us
    ppermute x15, starting transfers between devices, swap(): return lax.ppermute(value, axis, [(0, 1), (1, 0)])  13.2 us
    pallas_call x10, Pallas kernels, run(): pl.pallas_call(body, out_shape=outs, in_specs=[slow] + [fast] * len(array...  12.6 us
    ppermute x9, starting transfers between devices, shift(): return lax.ppermute(value, 'patch', [(i, (i + by) % n) for i in range(n)])  8.3 us
    unnamed x8, local copies, waits for them, and re-layouts  2.05 us
  transfers between devices with their start and end apart: 24, of which 15 were waited for; matrix products, arithmetic and copies ran while one was open for 4% of the time, Pallas kernels for 13%

profile of v8, /device:TPU:0, one launch (start us, length us, event | category | flops | bytes accessed | tf_op | source)
XLA Modules:
  0.0 76.5 jit_solution(18408814211455669300)
XLA Ops:
  0.6 0.0 copy-start
  0.6 0.5 collective-permute-start.1
  1.2 0.6 copy-done
  1.7 0.2 constant_dynamic-slice_fusion.6
  1.9 0.2 copy.7.mine.refs_2_.refs_6_
  2.2 1.5 %copy-done.1 = bf16[864,1024]{1,0:T(8,128)(2,1)S(1)} copy-done((bf16[864,1024]{1,0:T(8,128)(2,1)S(1)}, bf16[864,1024]{1,0:T(8,128)(2,1)}, u32[]{:S(2)}) %copy-start.1) | copy-done | bytes 1769496
  3.6 0.6 shard_map.58.part
  4.2 3.0 %collective-permute-start = (bf16[192,1024]{1,0:T(8,128)(2,1)S(1)}, bf16[192,1024]{1,0:T(8,128)(2,1)}, u32[]{:S(2)}, u32[]{:S(2)}) collective-permute-start(bf16[192,1024]{1,0:T(8,128)(2,1)S(1)} %shard_map.58.part), channel_id=1, source_target_pairs={{0,1},{1,0},{2,3},{3,2},{4,5},{5,4},{6,7},{7,6},{8,9},{9,8},{10,11... | collective-permute-start | bytes 1179656 | tf_op jit(solution)/shard_map/ppermute | solution.py:91
  7.2 1.6 %collective-permute-start.5 = (bf16[192,864]{1,0:T(8,128)(2,1)S(1)}, bf16[192,864]{1,0:T(8,128)(2,1)S(1)}, u32[]{:S(2)}, u32[]{:S(2)}) collective-permute-start(bf16[192,864]{1,0:T(8,128)(2,1)S(1)} %copy.7.mine.refs_2_.refs_6_), channel_id=1, source_target_pairs={{0,4},{4,8},{8,12},{12,0},{1,5},{5,9},{9,13},{13,1},{2,6},{6,10},{... | collective-permute-start | bytes 995336 | tf_op jit(solution)/shard_map/ppermute | solution.py:96
  8.8 0.2 multiply_reduce_fusion.3
  9.0 0.6 collective-permute-start.3
  9.6 0.1 stack.18.where
  9.6 0.3 collective-permute-done.4
  10.0 0.6 shard_map.59.part2
  10.6 1.2 %collective-permute-start.2 = (bf16[192,1024]{1,0:T(8,128)(2,1)S(1)}, bf16[192,1024]{1,0:T(8,128)(2,1)S(1)}, u32[]{:S(2)}, u32[]{:S(2)}) collective-permute-start(bf16[192,1024]{1,0:T(8,128)(2,1)S(1)} %shard_map.59.part2), channel_id=1, source_target_pairs={{0,1},{1,0},{2,3},{3,2},{4,5},{5,4},{6,7},{7,6},{8,9},{9,8},{10,11... | collective-permute-start | bytes 1179656 | tf_op jit(solution)/shard_map/ppermute | solution.py:91
  11.9 0.1 shard_map.60.other
  12.0 5.3 %collective-permute-done.3 = f32[192]{0:T(256)S(1)} collective-permute-done((f32[192]{0:T(256)S(1)}, f32[192]{0:T(256)S(1)}, u32[]{:S(2)}, u32[]{:S(2)}) %collective-permute-start.3) | collective-permute-done | bytes 800 | tf_op jit(solution)/shard_map/ppermute | solution.py:91
  17.3 1.3 %collective-permute-done.5.refs_10_.refs_14_ = bf16[192,864]{1,0:T(8,128)(2,1)S(1)} collective-permute-done((bf16[192,864]{1,0:T(8,128)(2,1)S(1)}, bf16[192,864]{1,0:T(8,128)(2,1)S(1)}, u32[]{:S(2)}, u32[]{:S(2)}) %collective-permute-start.5) | collective-permute-done | bytes 331808 | tf_op jit(solution)/shard_map/ppermute | solution.py:96
  18.6 0.8 %collective-permute-start.7 = (bf16[192,864]{1,0:T(8,128)(2,1)S(1)}, bf16[192,864]{1,0:T(8,128)(2,1)S(1)}, u32[]{:S(2)}, u32[]{:S(2)}) collective-permute-start(bf16[192,864]{1,0:T(8,128)(2,1)S(1)} %collective-permute-done.5.refs_10_.refs_14_), channel_id=1, source_target_pairs={{0,4},{4,8},{8,12},{12,0},{1,5},{5,9},{9,13},{13,1},{2,6},{6,10},{... | collective-permute-start | bytes 995336 | tf_op jit(solution)/shard_map/ppermute | solution.py:96
  19.4 5.4 %collective-permute-done.2.arrived2 = bf16[192,1024]{1,0:T(8,128)(2,1)S(1)} collective-permute-done((bf16[192,1024]{1,0:T(8,128)(2,1)S(1)}, bf16[192,1024]{1,0:T(8,128)(2,1)S(1)}, u32[]{:S(2)}, u32[]{:S(2)}) %collective-permute-start.2) | collective-permute-done | bytes 393248 | tf_op jit(solution)/shard_map/ppermute | solution.py:91
  24.8 2.9 %shard_map.61 = (bf16[96,1024]{1,0:T(8,128)(2,1)S(1)}, bf16[96,1024]{1,0:T(8,128)(2,1)S(1)}, bf16[192,864]{1,0:T(8,128)(2,1)S(1)}, bf16[192,2048]{1,0:T(8,128)(2,1)S(1)}) custom-call(s32[1]{0:T(128)} %bitcast._.where, bf16[192,1024]{1,0:T(8,128)(2,1)S(1)} %shard_map.58.part, bf16[192,1024]{1,0:T(8,128)(2,1)} %collective-permute-done.arrived, ...), custom_call_target="tpu_custom_call" | custom-call | flops 1000 | bytes 1000 | tf_op jit(solution)/shard_map/pallas_call | solution.py:115
  27.7 1.8 %collective-permute-start.6 = (bf16[96,1024]{1,0:T(8,128)(2,1)S(1)}, bf16[96,1024]{1,0:T(8,128)(2,1)S(1)}, u32[]{:S(2)}, u32[]{:S(2)}) collective-permute-start(bf16[96,1024]{1,0:T(8,128)(2,1)S(1)} %get-tuple-element.35), channel_id=1, source_target_pairs={{0,1},{1,0},{2,3},{3,2},{4,5},{5,4},{6,7},{7,6},{8,9},{9,8},{10,11... | collective-permute-start | bytes 589832 | tf_op jit(solution)/shard_map/ppermute | solution.py:91
  29.5 0.2 multiply_reduce_fusion.2
  29.7 1.6 %collective-permute-start.11 = (bf16[192,864]{1,0:T(8,128)(2,1)S(1)}, bf16[192,864]{1,0:T(8,128)(2,1)S(1)}, u32[]{:S(2)}, u32[]{:S(2)}) collective-permute-start(bf16[192,864]{1,0:T(8,128)(2,1)S(1)} %collective-permute-done.7.refs_2_.refs_6_), channel_id=1, source_target_pairs={{0,4},{4,8},{8,12},{12,0},{1,5},{5,9},{9,13},{13,1},{2,6},{6,10},{... | collective-permute-start | bytes 995336 | tf_op jit(solution)/shard_map/ppermute | solution.py:96
  31.3 0.2 multiply_reduce_fusion.1
  31.4 0.6 collective-permute-start.8
  32.1 0.6 shard_map.62
  32.7 2.6 %collective-permute-done.6 = bf16[96,1024]{1,0:T(8,128)(2,1)S(1)} collective-permute-done((bf16[96,1024]{1,0:T(8,128)(2,1)S(1)}, bf16[96,1024]{1,0:T(8,128)(2,1)S(1)}, u32[]{:S(2)}, u32[]{:S(2)}) %collective-permute-start.6) | collective-permute-done | bytes 196640 | tf_op jit(solution)/shard_map/ppermute | solution.py:91
  35.2 0.1 select_convert_fusion.1.refs_0_
  35.3 1.5 %collective-permute-start.12 = (bf16[96,1024]{1,0:T(8,128)(2,1)S(1)}, bf16[96,1024]{1,0:T(8,128)(2,1)S(1)}, u32[]{:S(2)}, u32[]{:S(2)}) collective-permute-start(bf16[96,1024]{1,0:T(8,128)(2,1)S(1)} %select_convert_fusion.1.refs_0_), channel_id=1, source_target_pairs={{0,4},{4,8},{8,12},{12,0},{1,5},{5,9},{9,13},{13,1},{2,6},{6,10},{... | collective-permute-start | bytes 589832 | tf_op jit(solution)/shard_map/ppermute | solution.py:96
  36.9 1.2 %collective-permute-done.8 = bf16[96,1024]{1,0:T(8,128)(2,1)S(1)} collective-permute-done((bf16[96,1024]{1,0:T(8,128)(2,1)S(1)}, bf16[96,1024]{1,0:T(8,128)(2,1)S(1)}, u32[]{:S(2)}, u32[]{:S(2)}) %collective-permute-start.8) | collective-permute-done | bytes 196640 | tf_op jit(solution)/shard_map/ppermute | solution.py:91
  38.1 0.1 select_convert_fusion.refs_4_
  38.2 1.6 %collective-permute-start.10 = (bf16[96,1024]{1,0:T(8,128)(2,1)S(1)}, bf16[96,1024]{1,0:T(8,128)(2,1)S(1)}, u32[]{:S(2)}, u32[]{:S(2)}) collective-permute-start(bf16[96,1024]{1,0:T(8,128)(2,1)S(1)} %select_convert_fusion.refs_4_), channel_id=1, source_target_pairs={{0,4},{4,8},{8,12},{12,0},{1,5},{5,9},{9,13},{13,1},{2,6},{6,10},{... | collective-permute-start | bytes 589832 | tf_op jit(solution)/shard_map/ppermute | solution.py:96
  39.8 1.5 %collective-permute-start.9 = (bf16[192,1024]{1,0:T(8,128)(2,1)S(1)}, bf16[192,1024]{1,0:T(8,128)(2,1)S(1)}, u32[]{:S(2)}, u32[]{:S(2)}) collective-permute-start(bf16[192,1024]{1,0:T(8,128)(2,1)S(1)} %pad_maximum_fusion), channel_id=1, source_target_pairs={{0,1},{1,0},{2,3},{3,2},{4,5},{5,4},{6,7},{7,6},{8,9},{9,8},{10,11... | collective-permute-start | bytes 1179656 | tf_op jit(solution)/shard_map/ppermute | solution.py:91
  41.3 1.2 %collective-permute-done.11.refs_2_.refs_6_ = bf16[192,864]{1,0:T(8,128)(2,1)S(1)} collective-permute-done((bf16[192,864]{1,0:T(8,128)(2,1)S(1)}, bf16[192,864]{1,0:T(8,128)(2,1)S(1)}, u32[]{:S(2)}, u32[]{:S(2)}) %collective-permute-start.11) | collective-permute-done | bytes 331808 | tf_op jit(solution)/shard_map/ppermute | solution.py:96
  42.5 0.2 multiply_reduce_fusion
  42.7 0.1 pad_maximum_fusion.5
  42.7 3.8 %collective-permute-done.12.refs_8_ = bf16[96,1024]{1,0:T(8,128)(2,1)S(1)} collective-permute-done((bf16[96,1024]{1,0:T(8,128)(2,1)S(1)}, bf16[96,1024]{1,0:T(8,128)(2,1)S(1)}, u32[]{:S(2)}, u32[]{:S(2)}) %collective-permute-start.12) | collective-permute-done | bytes 196640 | tf_op jit(solution)/shard_map/ppermute | solution.py:96
  46.6 0.6 collective-permute-start.13
  47.1 3.5 %collective-permute-done.10.refs_12_ = bf16[96,1024]{1,0:T(8,128)(2,1)S(1)} collective-permute-done((bf16[96,1024]{1,0:T(8,128)(2,1)S(1)}, bf16[96,1024]{1,0:T(8,128)(2,1)S(1)}, u32[]{:S(2)}, u32[]{:S(2)}) %collective-permute-start.10) | collective-permute-done | bytes 196640 | tf_op jit(solution)/shard_map/ppermute | solution.py:96
  50.6 1.1 %collective-permute-start.19 = (bf16[96,1024]{1,0:T(8,128)(2,1)S(1)}, bf16[96,1024]{1,0:T(8,128)(2,1)S(1)}, u32[]{:S(2)}, u32[]{:S(2)}) collective-permute-start(bf16[96,1024]{1,0:T(8,128)(2,1)S(1)} %collective-permute-done.10.refs_12_), channel_id=1, source_target_pairs={{0,4},{4,8},{8,12},{12,0},{1,5},{5,9},{9,13},{13,1},{2,6},{6,10},{... | collective-permute-start | bytes 589832 | tf_op jit(solution)/shard_map/ppermute | solution.py:96
  51.8 0.6 collective-permute-start.17
  52.3 0.1 add_rsqrt_fusion
  52.4 0.1 fusion.5
  52.5 0.2 broadcast_select_fusion.1
  52.7 0.1 fusion.3
  52.8 0.1 collective-permute-start.14
  52.9 2.8 %collective-permute-done.15.refs_0_ = bf16[96,1024]{1,0:T(8,128)(2,1)S(1)} collective-permute-done((bf16[96,1024]{1,0:T(8,128)(2,1)S(1)}, bf16[96,1024]{1,0:T(8,128)(2,1)S(1)}, u32[]{:S(2)}, u32[]{:S(2)}) %collective-permute-start.15) | collective-permute-done | bytes 196640 | tf_op jit(solution)/shard_map/ppermute | solution.py:96
  55.7 2.6 %collective-permute-done.19.refs_4_ = bf16[96,1024]{1,0:T(8,128)(2,1)S(1)} collective-permute-done((bf16[96,1024]{1,0:T(8,128)(2,1)S(1)}, bf16[96,1024]{1,0:T(8,128)(2,1)S(1)}, u32[]{:S(2)}, u32[]{:S(2)}) %collective-permute-start.19) | collective-permute-done | bytes 196640 | tf_op jit(solution)/shard_map/ppermute | solution.py:96
  58.3 0.1 collective-permute-start.20
  58.4 0.3 collective-permute-start.22
  58.6 2.3 %shard_map.63 = (f32[944,512]{1,0:T(8,128)S(1)}, f32[944,512]{1,0:T(8,128)S(1)}) custom-call(s32[5]{0:T(128)S(1)} %stack.18.where, bf16[96,1024]{1,0:T(8,128)(2,1)S(1)} %select_convert_fusion.1.refs_0_, bf16[192,1024]{1,0:T(8,128)(2,1)S(1)} %collective-permute-done.9.refs_1_.refs_5_, bf16[192,864]{1,0:T(8,128)(2,1)S(1)} %copy.7.mine.refs_2_.refs_6_, ...), custom_call_target="tpu_custom_call" | custom-call | flops 1000 | bytes 1000 | tf_op jit(solution)/shard_map/pallas_call | solution.py:115
  60.9 3.5 %collective-permute-done.16.refs_0_ = bf16[96,1024]{1,0:T(8,128)(2,1)S(1)} collective-permute-done((bf16[96,1024]{1,0:T(8,128)(2,1)S(1)}, bf16[96,1024]{1,0:T(8,128)(2,1)S(1)}, u32[]{:S(2)}, u32[]{:S(2)}) %collective-permute-start.16) | collective-permute-done | bytes 196640 | tf_op jit(solution)/shard_map/ppermute | solution.py:96
  64.4 1.1 %collective-permute-start.18 = (bf16[96,512]{1,0:T(8,128)(2,1)S(1)}, bf16[96,512]{1,0:T(8,128)(2,1)S(1)}, u32[]{:S(2)}, u32[]{:S(2)}) collective-permute-start(bf16[96,512]{1,0:T(8,128)(2,1)S(1)} %constant_dynamic-slice_fusion.3), channel_id=1, source_target_pairs={{0,1},{1,0},{2,3},{3,2},{4,5},{5,4},{6,7},{7,6},{8,9},{9,8},{10,11... | collective-permute-start | bytes 294920 | tf_op jit(solution)/shard_map/ppermute | solution.py:91
  65.5 1.0 %collective-permute-done.20.refs_4_ = bf16[96,1024]{1,0:T(8,128)(2,1)S(1)} collective-permute-done((bf16[96,1024]{1,0:T(8,128)(2,1)S(1)}, bf16[96,1024]{1,0:T(8,128)(2,1)S(1)}, u32[]{:S(2)}, u32[]{:S(2)}) %collective-permute-start.20) | collective-permute-done | bytes 196640 | tf_op jit(solution)/shard_map/ppermute | solution.py:96
  66.5 1.3 %collective-permute-start.21 = (bf16[96,512]{1,0:T(8,128)(2,1)S(1)}, bf16[96,512]{1,0:T(8,128)(2,1)S(1)}, u32[]{:S(2)}, u32[]{:S(2)}) collective-permute-start(bf16[96,512]{1,0:T(8,128)(2,1)S(1)} %constant_dynamic-slice_fusion.2), channel_id=1, source_target_pairs={{0,1},{1,0},{2,3},{3,2},{4,5},{5,4},{6,7},{7,6},{8,9},{9,8},{10,11... | collective-permute-start | bytes 294920 | tf_op jit(solution)/shard_map/ppermute | solution.py:91
  67.8 1.2 %maximum_select_fusion = bf16[384,1024]{1,0:T(8,128)(2,1)} fusion(bf16[192,1024]{1,0:T(8,128)(2,1)S(1)} %collective-permute-done.14, bf16[192,512]{1,0:T(8,128)(2,1)S(1)} %get-tuple-element.69, bf16[192,512]{1,0:T(8,128)(2,1)S(1)} %get-tuple-element.57, pred[]{:T(512)S(6)} %eq.18), kind=kLoop, calls=%fused_computation | loop fusion | flops 5111808 | bytes 1572865 | tf_op jit(solution)/shard_map/jit(_where)/select_n | solution.py:344
  69.0 1.6 %shard_map.64 = (f32[944,512]{1,0:T(8,128)S(1)}, f32[944,512]{1,0:T(8,128)S(1)}) custom-call(s32[5]{0:T(128)S(1)} %stack.18.where, bf16[96,1024]{1,0:T(8,128)(2,1)S(1)} %collective-permute-done.15.refs_0_, bf16[192,512]{1,0:T(8,128)(2,1)S(1)} %collective-permute-done.22.refs_1_.refs_5_, bf16[192,864]{1,0:T(8,128)(2,1)S(1)} %collective-permute-done.7.refs_2_.refs_6_, ...), custom_call_target="tpu_custom_call" | custom-call | flops 1000 | bytes 1000 | tf_op jit(solution)/shard_map/pallas_call | solution.py:115
  70.6 0.6 collective-permute-done.21.refs_5_
  71.2 1.3 %shard_map.65 = bf16[944,512]{1,0:T(8,128)(2,1)S(1)} custom-call(s32[5]{0:T(128)S(1)} %stack.18.where, bf16[96,1024]{1,0:T(8,128)(2,1)S(1)} %collective-permute-done.16.refs_0_, bf16[96,512]{1,0:T(8,128)(2,1)S(1)} %collective-permute-done.18.refs_1_, bf16[192,864]{1,0:T(8,128)(2,1)S(1)} %collective-permute-done.11.refs_2_.refs_6_, f32[1,192]{1,0:T(1,128)S(1)} %bitcast.11, ...), custom_call_target="tpu_custom_call" | custom-call | flops 1000 | bytes 1000 | tf_op jit(solution)/shard_map/pallas_call | solution.py:115
  72.4 0.1 collective-permute-start.23
  72.5 1.3 %shard_map.66.kept = f32[944,512]{1,0:T(8,128)S(1)} custom-call(s32[5]{0:T(128)S(1)} %stack.18.where, bf16[96,1024]{1,0:T(8,128)(2,1)S(1)} %collective-permute-done.16.refs_0_, bf16[96,512]{1,0:T(8,128)(2,1)S(1)} %collective-permute-done.18.refs_1_, bf16[192,864]{1,0:T(8,128)(2,1)S(1)} %collective-permute-done.11.refs_2_.refs_6_, f32[1,192]{1,0:T(1,128)S(1)} %bitcast.13, ...), custom_call_target="tpu_custom_call" | custom-call | flops 1000 | bytes 1000 | tf_op jit(solution)/shard_map/pallas_call | solution.py:115
  73.8 1.3 %collective-permute-done.23.sent = bf16[944,512]{1,0:T(8,128)(2,1)S(1)} collective-permute-done((bf16[944,512]{1,0:T(8,128)(2,1)S(1)}, bf16[944,512]{1,0:T(8,128)(2,1)S(1)}, u32[]{:S(2)}, u32[]{:S(2)}) %collective-permute-start.23) | collective-permute-done | bytes 966688 | tf_op jit(solution)/shard_map/ppermute | solution.py:91
  75.1 1.4 %shard_map.67 = (f32[512,512]{1,0:T(8,128)}, f32[864,256]{1,0:T(8,128)}) custom-call(s32[1]{0:T(128)} %bitcast._.where, f32[944,512]{1,0:T(8,128)S(1)} %shard_map.66.kept, bf16[944,512]{1,0:T(8,128)(2,1)S(1)} %collective-permute-done.23.sent), custom_call_target="tpu_custom_call" | custom-call | flops 1000 | bytes 1000 | tf_op jit(solution)/shard_map/pallas_call | solution.py:115
  (31 shorter events, 0.2 us)
Async XLA Ops:
  0.6 1.1 %copy-start = (bf16[384,864]{0,1:T(8,128)(2,1)S(1)}, bf16[384,864]{0,1:T(8,128)(2,1)}, u32[]{:S(2)}) copy-start(bf16[384,864]{0,1:T(8,128)(2,1)} %param.3) | copy-start | bytes 1990660
  0.6 9.4 %collective-permute-start.1 = (bf16[864,1024]{1,0:T(8,128)(2,1)}, bf16[864,1024]{1,0:T(8,128)(2,1)S(1)}, u32[]{:S(2)}, u32[]{:S(2)}) collective-permute-start(bf16[864,1024]{1,0:T(8,128)(2,1)} %own.3), channel_id=1, source_target_pairs={{0,2},{2,0},{1,3},{3,1},{4,6},{6,4},{5,7},{7,5},{8,10},{10,8},{9,1... | collective-permute-start | bytes 5308424 | tf_op jit(solution)/shard_map/ppermute | solution.py:91
  1.9 6.9 %copy-start.3 = (f32[1024]{0:T(1024)S(1)}, f32[1024]{0:T(1024)}, u32[]{:S(2)}) copy-start(f32[1024]{0:T(1024)} %param.5) | copy-start | bytes 12292
  2.1 1.5 %copy-start.1 = (bf16[864,1024]{1,0:T(8,128)(2,1)S(1)}, bf16[864,1024]{1,0:T(8,128)(2,1)}, u32[]{:S(2)}) copy-start(bf16[864,1024]{1,0:T(8,128)(2,1)} %own.3) | copy-start | bytes 5308420
  4.2 15.2 %collective-permute-start = (bf16[192,1024]{1,0:T(8,128)(2,1)S(1)}, bf16[192,1024]{1,0:T(8,128)(2,1)}, u32[]{:S(2)}, u32[]{:S(2)}) collective-permute-start(bf16[192,1024]{1,0:T(8,128)(2,1)S(1)} %shard_map.58.part), channel_id=1, source_target_pairs={{0,1},{1,0},{2,3},{3,2},{4,5},{5,4},{6,7},{7,6},{8,9},{9,8},{10,11... | collective-permute-start | bytes 1179656 | tf_op jit(solution)/shard_map/ppermute | solution.py:91
  7.2 11.4 %collective-permute-start.5 = (bf16[192,864]{1,0:T(8,128)(2,1)S(1)}, bf16[192,864]{1,0:T(8,128)(2,1)S(1)}, u32[]{:S(2)}, u32[]{:S(2)}) collective-permute-start(bf16[192,864]{1,0:T(8,128)(2,1)S(1)} %copy.7.mine.refs_2_.refs_6_), channel_id=1, source_target_pairs={{0,4},{4,8},{8,12},{12,0},{1,5},{5,9},{9,13},{13,1},{2,6},{6,10},{... | collective-permute-start | bytes 995336 | tf_op jit(solution)/shard_map/ppermute | solution.py:96
  8.8 1.2 %collective-permute-start.4 = (f32[1,1024]{1,0:T(1,128)S(1)}, f32[1,1024]{1,0:T(1,128)S(1)}, u32[]{:S(2)}, u32[]{:S(2)}) collective-permute-start(f32[1,1024]{1,0:T(1,128)S(1)} %bitcast.22), channel_id=1, source_target_pairs={{0,2},{2,0},{1,3},{3,1},{4,6},{6,4},{5,7},{7,5},{8,10},{10,8},{9,1... | collective-permute-start | bytes 12296 | tf_op jit(solution)/shard_map/ppermute | solution.py:91
  9.0 8.3 %collective-permute-start.3 = (f32[192]{0:T(256)S(1)}, f32[192]{0:T(256)S(1)}, u32[]{:S(2)}, u32[]{:S(2)}) collective-permute-start(f32[192]{0:T(256)S(1)} %multiply_reduce_fusion.3), channel_id=1, source_target_pairs={{0,1},{1,0},{2,3},{3,2},{4,5},{5,4},{6,7},{7,6},{8,9},{9,8},{10,11... | collective-permute-start | bytes 2312 | tf_op jit(solution)/shard_map/ppermute | solution.py:91
  10.6 14.2 %collective-permute-start.2 = (bf16[192,1024]{1,0:T(8,128)(2,1)S(1)}, bf16[192,1024]{1,0:T(8,128)(2,1)S(1)}, u32[]{:S(2)}, u32[]{:S(2)}) collective-permute-start(bf16[192,1024]{1,0:T(8,128)(2,1)S(1)} %shard_map.59.part2), channel_id=1, source_target_pairs={{0,1},{1,0},{2,3},{3,2},{4,5},{5,4},{6,7},{7,6},{8,9},{9,8},{10,11... | collective-permute-start | bytes 1179656 | tf_op jit(solution)/shard_map/ppermute | solution.py:91
  11.9 12.9 %copy-start.2 = (bf16[864,1024]{1,0:T(8,128)(2,1)S(1)}, bf16[864,1024]{1,0:T(8,128)(2,1)}, u32[]{:S(2)}) copy-start(bf16[864,1024]{1,0:T(8,128)(2,1)} %own.3) | copy-start | bytes 5308420
  18.6 11.1 %collective-permute-start.7 = (bf16[192,864]{1,0:T(8,128)(2,1)S(1)}, bf16[192,864]{1,0:T(8,128)(2,1)S(1)}, u32[]{:S(2)}, u32[]{:S(2)}) collective-permute-start(bf16[192,864]{1,0:T(8,128)(2,1)S(1)} %collective-permute-done.5.refs_10_.refs_14_), channel_id=1, source_target_pairs={{0,4},{4,8},{8,12},{12,0},{1,5},{5,9},{9,13},{13,1},{2,6},{6,10},{... | collective-permute-start | bytes 995336 | tf_op jit(solution)/shard_map/ppermute | solution.py:96
  27.7 7.5 %collective-permute-start.6 = (bf16[96,1024]{1,0:T(8,128)(2,1)S(1)}, bf16[96,1024]{1,0:T(8,128)(2,1)S(1)}, u32[]{:S(2)}, u32[]{:S(2)}) collective-permute-start(bf16[96,1024]{1,0:T(8,128)(2,1)S(1)} %get-tuple-element.35), channel_id=1, source_target_pairs={{0,1},{1,0},{2,3},{3,2},{4,5},{5,4},{6,7},{7,6},{8,9},{9,8},{10,11... | collective-permute-start | bytes 589832 | tf_op jit(solution)/shard_map/ppermute | solution.py:91
  29.7 12.8 %collective-permute-start.11 = (bf16[192,864]{1,0:T(8,128)(2,1)S(1)}, bf16[192,864]{1,0:T(8,128)(2,1)S(1)}, u32[]{:S(2)}, u32[]{:S(2)}) collective-permute-start(bf16[192,864]{1,0:T(8,128)(2,1)S(1)} %collective-permute-done.7.refs_2_.refs_6_), channel_id=1, source_target_pairs={{0,4},{4,8},{8,12},{12,0},{1,5},{5,9},{9,13},{13,1},{2,6},{6,10},{... | collective-permute-start | bytes 995336 | tf_op jit(solution)/shard_map/ppermute | solution.py:96
  31.4 6.6 %collective-permute-start.8 = (bf16[96,1024]{1,0:T(8,128)(2,1)S(1)}, bf16[96,1024]{1,0:T(8,128)(2,1)S(1)}, u32[]{:S(2)}, u32[]{:S(2)}) collective-permute-start(bf16[96,1024]{1,0:T(8,128)(2,1)S(1)} %get-tuple-element.38), channel_id=1, source_target_pairs={{0,1},{1,0},{2,3},{3,2},{4,5},{5,4},{6,7},{7,6},{8,9},{9,8},{10,11... | collective-permute-start | bytes 589832 | tf_op jit(solution)/shard_map/ppermute | solution.py:91
  35.3 11.2 %collective-permute-start.12 = (bf16[96,1024]{1,0:T(8,128)(2,1)S(1)}, bf16[96,1024]{1,0:T(8,128)(2,1)S(1)}, u32[]{:S(2)}, u32[]{:S(2)}) collective-permute-start(bf16[96,1024]{1,0:T(8,128)(2,1)S(1)} %select_convert_fusion.1.refs_0_), channel_id=1, source_target_pairs={{0,4},{4,8},{8,12},{12,0},{1,5},{5,9},{9,13},{13,1},{2,6},{6,10},{... | collective-permute-start | bytes 589832 | tf_op jit(solution)/shard_map/ppermute | solution.py:96
  38.2 12.4 %collective-permute-start.10 = (bf16[96,1024]{1,0:T(8,128)(2,1)S(1)}, bf16[96,1024]{1,0:T(8,128)(2,1)S(1)}, u32[]{:S(2)}, u32[]{:S(2)}) collective-permute-start(bf16[96,1024]{1,0:T(8,128)(2,1)S(1)} %select_convert_fusion.refs_4_), channel_id=1, source_target_pairs={{0,4},{4,8},{8,12},{12,0},{1,5},{5,9},{9,13},{13,1},{2,6},{6,10},{... | collective-permute-start | bytes 589832 | tf_op jit(solution)/shard_map/ppermute | solution.py:96
  39.8 12.7 %collective-permute-start.9 = (bf16[192,1024]{1,0:T(8,128)(2,1)S(1)}, bf16[192,1024]{1,0:T(8,128)(2,1)S(1)}, u32[]{:S(2)}, u32[]{:S(2)}) collective-permute-start(bf16[192,1024]{1,0:T(8,128)(2,1)S(1)} %pad_maximum_fusion), channel_id=1, source_target_pairs={{0,1},{1,0},{2,3},{3,2},{4,5},{5,4},{6,7},{7,6},{8,9},{9,8},{10,11... | collective-permute-start | bytes 1179656 | tf_op jit(solution)/shard_map/ppermute | solution.py:91
  46.5 9.1 %collective-permute-start.15 = (bf16[96,1024]{1,0:T(8,128)(2,1)S(1)}, bf16[96,1024]{1,0:T(8,128)(2,1)S(1)}, u32[]{:S(2)}, u32[]{:S(2)}) collective-permute-start(bf16[96,1024]{1,0:T(8,128)(2,1)S(1)} %collective-permute-done.12.refs_8_), channel_id=1, source_target_pairs={{0,4},{4,8},{8,12},{12,0},{1,5},{5,9},{9,13},{13,1},{2,6},{6,10},{... | collective-permute-start | bytes 589832 | tf_op jit(solution)/shard_map/ppermute | solution.py:96
  46.6 4.0 %collective-permute-start.13 = (f32[576]{0:T(1024)S(1)}, f32[576]{0:T(1024)S(1)}, u32[]{:S(2)}, u32[]{:S(2)}) collective-permute-start(f32[576]{0:T(1024)S(1)} %pad_maximum_fusion.5), channel_id=1, source_target_pairs={{0,1},{1,0},{2,3},{3,2},{4,5},{5,4},{6,7},{7,6},{8,9},{9,8},{10,11... | collective-permute-start | bytes 6920 | tf_op jit(solution)/shard_map/ppermute | solution.py:91
  50.6 7.7 %collective-permute-start.19 = (bf16[96,1024]{1,0:T(8,128)(2,1)S(1)}, bf16[96,1024]{1,0:T(8,128)(2,1)S(1)}, u32[]{:S(2)}, u32[]{:S(2)}) collective-permute-start(bf16[96,1024]{1,0:T(8,128)(2,1)S(1)} %collective-permute-done.10.refs_12_), channel_id=1, source_target_pairs={{0,4},{4,8},{8,12},{12,0},{1,5},{5,9},{9,13},{13,1},{2,6},{6,10},{... | collective-permute-start | bytes 589832 | tf_op jit(solution)/shard_map/ppermute | solution.py:96
  51.8 6.9 %collective-permute-start.17 = (bf16[192,512]{1,0:T(8,128)(2,1)S(1)}, bf16[192,512]{1,0:T(8,128)(2,1)S(1)}, u32[]{:S(2)}, u32[]{:S(2)}) collective-permute-start(bf16[192,512]{1,0:T(8,128)(2,1)S(1)} %pad_maximum_fusion.2), channel_id=1, source_target_pairs={{0,1},{1,0},{2,3},{3,2},{4,5},{5,4},{6,7},{7,6},{8,9},{9,8},{10,11... | collective-permute-start | bytes 589832 | tf_op jit(solution)/shard_map/ppermute | solution.py:91
  52.8 15.0 %collective-permute-start.14 = (bf16[192,1024]{1,0:T(8,128)(2,1)S(1)}, bf16[192,1024]{1,0:T(8,128)(2,1)S(1)}, u32[]{:S(2)}, u32[]{:S(2)}) collective-permute-start(bf16[192,1024]{1,0:T(8,128)(2,1)S(1)} %pad_maximum_fusion.1), channel_id=1, source_target_pairs={{0,2},{2,0},{1,3},{3,1},{4,6},{6,4},{5,7},{7,5},{8,10},{10,8},{9,1... | collective-permute-start | bytes 1179656 | tf_op jit(solution)/shard_map/ppermute | solution.py:91
  55.7 8.7 %collective-permute-start.16 = (bf16[96,1024]{1,0:T(8,128)(2,1)S(1)}, bf16[96,1024]{1,0:T(8,128)(2,1)S(1)}, u32[]{:S(2)}, u32[]{:S(2)}) collective-permute-start(bf16[96,1024]{1,0:T(8,128)(2,1)S(1)} %collective-permute-done.15.refs_0_), channel_id=1, source_target_pairs={{0,4},{4,8},{8,12},{12,0},{1,5},{5,9},{9,13},{13,1},{2,6},{6,10},{... | collective-permute-start | bytes 589832 | tf_op jit(solution)/shard_map/ppermute | solution.py:96
  58.3 8.2 %collective-permute-start.20 = (bf16[96,1024]{1,0:T(8,128)(2,1)S(1)}, bf16[96,1024]{1,0:T(8,128)(2,1)S(1)}, u32[]{:S(2)}, u32[]{:S(2)}) collective-permute-start(bf16[96,1024]{1,0:T(8,128)(2,1)S(1)} %collective-permute-done.19.refs_4_), channel_id=1, source_target_pairs={{0,4},{4,8},{8,12},{12,0},{1,5},{5,9},{9,13},{13,1},{2,6},{6,10},{... | collective-permute-start | bytes 589832 | tf_op jit(solution)/shard_map/ppermute | solution.py:96
  58.4 10.6 %collective-permute-start.22 = (bf16[192,512]{1,0:T(8,128)(2,1)S(1)}, bf16[192,512]{1,0:T(8,128)(2,1)S(1)}, u32[]{:S(2)}, u32[]{:S(2)}) collective-permute-start(bf16[192,512]{1,0:T(8,128)(2,1)S(1)} %pad_maximum_fusion.3), channel_id=1, source_target_pairs={{0,1},{1,0},{2,3},{3,2},{4,5},{5,4},{6,7},{7,6},{8,9},{9,8},{10,11... | collective-permute-start | bytes 589832 | tf_op jit(solution)/shard_map/ppermute | solution.py:91
  64.4 6.2 %collective-permute-start.18 = (bf16[96,512]{1,0:T(8,128)(2,1)S(1)}, bf16[96,512]{1,0:T(8,128)(2,1)S(1)}, u32[]{:S(2)}, u32[]{:S(2)}) collective-permute-start(bf16[96,512]{1,0:T(8,128)(2,1)S(1)} %constant_dynamic-slice_fusion.3), channel_id=1, source_target_pairs={{0,1},{1,0},{2,3},{3,2},{4,5},{5,4},{6,7},{7,6},{8,9},{9,8},{10,11... | collective-permute-start | bytes 294920 | tf_op jit(solution)/shard_map/ppermute | solution.py:91
  66.5 4.7 %collective-permute-start.21 = (bf16[96,512]{1,0:T(8,128)(2,1)S(1)}, bf16[96,512]{1,0:T(8,128)(2,1)S(1)}, u32[]{:S(2)}, u32[]{:S(2)}) collective-permute-start(bf16[96,512]{1,0:T(8,128)(2,1)S(1)} %constant_dynamic-slice_fusion.2), channel_id=1, source_target_pairs={{0,1},{1,0},{2,3},{3,2},{4,5},{5,4},{6,7},{7,6},{8,9},{9,8},{10,11... | collective-permute-start | bytes 294920 | tf_op jit(solution)/shard_map/ppermute | solution.py:91
  72.4 2.6 %collective-permute-start.23 = (bf16[944,512]{1,0:T(8,128)(2,1)S(1)}, bf16[944,512]{1,0:T(8,128)(2,1)S(1)}, u32[]{:S(2)}, u32[]{:S(2)}) collective-permute-start(bf16[944,512]{1,0:T(8,128)(2,1)S(1)} %shard_map.65), channel_id=1, source_target_pairs={{0,2},{2,0},{1,3},{3,1},{4,6},{6,4},{5,7},{7,5},{8,10},{10,8},{9,1... | collective-permute-start | bytes 2899976 | tf_op jit(solution)/shard_map/ppermute | solution.py:91

commit v9 on v8

--- a/solution.py
+++ b/solution.py
@@ -377,16 +377,16 @@
     there2 = tie("qb in", there2)
     ring3[0] = tie("z3a in", ring3[0])
     there3 = [send("qc", own_block(ring3[:1]), over_feat)]
-    second = [(2, 0, there2, 0), (2, 1, there2, step)]
+    second = [(2, 0, there2, 0), (2, 1, there2, step), (3, 0, there3[0], 0)]
     totals = add_products("sums2", second, {False: f32, True: f32}, totals)
     ring3[1] = tie("z3b in", ring3[1])
     there3.append(send("qd", own_block(ring3[1:]), over_feat))
     there3[0] = tie("qc in", there3[0])
     there3[1] = tie("qd in", there3[1])
-    third = [(3, 0, there3[0], 0), (3, 1, there3[1], 0)]
+    third = [(3, 1, there3[1], 0)]
     (total,) = add_products("sums3", third, {False: bf16}, totals[:1])
     sent = tie("sent in", send("sent", total, over_cores))
-    third = [(3, 0, after(there3[0], total), 0), (3, 1, there3[1], 0)]
+    third = [(3, 1, after(there3[1], total), 0)]
     (kept,) = add_products("sums4", third, {True: f32}, totals[1:])
     gram, cross = run(
         functools.partial(add_body, count),

time: 76.7 us -> 76.6 us (level)
  transfers between devices with their start and end apart: 24 -> 24, of which waited for: 15 -> 16; matrix products, arithmetic and copies ran while one was open for 4% -> 4% of each run, Pallas kernels for 13% -> 13%
where the time goes in v9:
time: 76.6 us; the launch traced here: 76.4 us
  waiting for transfers between devices  36.1 us (47%)
  starting transfers between devices  21.5 us (28%)
  Pallas kernels  12.6 us (16%)
  local copies, waits for them, and re-layouts  2.71 us (4%)
  other arithmetic  2.52 us (3%)
  between operations  0.87 us (1%)
    ppermute x9, waiting for transfers between devices, shift(): return lax.ppermute(value, 'patch', [(i, (i + by) % n) for i in range(n)])  19.7 us
    ppermute x15, waiting for transfers between devices, swap(): return lax.ppermute(value, axis, [(0, 1), (1, 0)])  16.4 us
    ppermute x15, starting transfers between devices, swap(): return lax.ppermute(value, axis, [(0, 1), (1, 0)])  13.2 us
    pallas_call x10, Pallas kernels, run(): pl.pallas_call(body, out_shape=outs, in_specs=[slow] + [fast] * len(array...  12.6 us
    ppermute x9, starting transfers between devices, shift(): return lax.ppermute(value, 'patch', [(i, (i + by) % n) for i in range(n)])  8.35 us
    unnamed x8, local copies, waits for them, and re-layouts  2.05 us
  transfers between devices with their start and end apart: 24, of which 16 were waited for; matrix products, arithmetic and copies ran while one was open for 4% of the time, Pallas kernels for 13%

profile of v9, /device:TPU:0, one launch (start us, length us, event | category | flops | bytes accessed | tf_op | source)
XLA Modules:
  0.0 76.4 jit_solution(12807644423679760883)
XLA Ops:
  0.6 0.5 collective-permute-start.1
  1.2 0.6 copy-done
  1.7 0.2 constant_dynamic-slice_fusion.6
  1.9 0.2 copy.7.mine.refs_2_.refs_6_
  2.2 1.5 %copy-done.1 = bf16[864,1024]{1,0:T(8,128)(2,1)S(1)} copy-done((bf16[864,1024]{1,0:T(8,128)(2,1)S(1)}, bf16[864,1024]{1,0:T(8,128)(2,1)}, u32[]{:S(2)}) %copy-start.1) | copy-done | bytes 1769496
  3.6 0.6 shard_map.58.part
  4.2 3.0 %collective-permute-start = (bf16[192,1024]{1,0:T(8,128)(2,1)S(1)}, bf16[192,1024]{1,0:T(8,128)(2,1)}, u32[]{:S(2)}, u32[]{:S(2)}) collective-permute-start(bf16[192,1024]{1,0:T(8,128)(2,1)S(1)} %shard_map.58.part), channel_id=1, source_target_pairs={{0,1},{1,0},{2,3},{3,2},{4,5},{5,4},{6,7},{7,6},{8,9},{9,8},{10,11... | collective-permute-start | bytes 1179656 | tf_op jit(solution)/shard_map/ppermute | solution.py:91
  7.2 1.6 %collective-permute-start.5 = (bf16[192,864]{1,0:T(8,128)(2,1)S(1)}, bf16[192,864]{1,0:T(8,128)(2,1)S(1)}, u32[]{:S(2)}, u32[]{:S(2)}) collective-permute-start(bf16[192,864]{1,0:T(8,128)(2,1)S(1)} %copy.7.mine.refs_2_.refs_6_), channel_id=1, source_target_pairs={{0,4},{4,8},{8,12},{12,0},{1,5},{5,9},{9,13},{13,1},{2,6},{6,10},{... | collective-permute-start | bytes 995336 | tf_op jit(solution)/shard_map/ppermute | solution.py:96
  8.8 0.2 multiply_reduce_fusion.3
  9.0 0.6 collective-permute-start.3
  9.6 0.1 stack.18.where
  9.6 0.3 collective-permute-done.4
  10.0 0.6 shard_map.59.part2
  10.6 1.2 %collective-permute-start.2 = (bf16[192,1024]{1,0:T(8,128)(2,1)S(1)}, bf16[192,1024]{1,0:T(8,128)(2,1)S(1)}, u32[]{:S(2)}, u32[]{:S(2)}) collective-permute-start(bf16[192,1024]{1,0:T(8,128)(2,1)S(1)} %shard_map.59.part2), channel_id=1, source_target_pairs={{0,1},{1,0},{2,3},{3,2},{4,5},{5,4},{6,7},{7,6},{8,9},{9,8},{10,11... | collective-permute-start | bytes 1179656 | tf_op jit(solution)/shard_map/ppermute | solution.py:91
  11.9 0.1 shard_map.60.other
  12.0 5.3 %collective-permute-done.3 = f32[192]{0:T(256)S(1)} collective-permute-done((f32[192]{0:T(256)S(1)}, f32[192]{0:T(256)S(1)}, u32[]{:S(2)}, u32[]{:S(2)}) %collective-permute-start.3) | collective-permute-done | bytes 800 | tf_op jit(solution)/shard_map/ppermute | solution.py:91
  17.3 1.3 %collective-permute-done.5.refs_10_.refs_14_ = bf16[192,864]{1,0:T(8,128)(2,1)S(1)} collective-permute-done((bf16[192,864]{1,0:T(8,128)(2,1)S(1)}, bf16[192,864]{1,0:T(8,128)(2,1)S(1)}, u32[]{:S(2)}, u32[]{:S(2)}) %collective-permute-start.5) | collective-permute-done | bytes 331808 | tf_op jit(solution)/shard_map/ppermute | solution.py:96
  18.6 0.8 %collective-permute-start.7 = (bf16[192,864]{1,0:T(8,128)(2,1)S(1)}, bf16[192,864]{1,0:T(8,128)(2,1)S(1)}, u32[]{:S(2)}, u32[]{:S(2)}) collective-permute-start(bf16[192,864]{1,0:T(8,128)(2,1)S(1)} %collective-permute-done.5.refs_10_.refs_14_), channel_id=1, source_target_pairs={{0,4},{4,8},{8,12},{12,0},{1,5},{5,9},{9,13},{13,1},{2,6},{6,10},{... | collective-permute-start | bytes 995336 | tf_op jit(solution)/shard_map/ppermute | solution.py:96
  19.4 5.4 %collective-permute-done.2.arrived2 = bf16[192,1024]{1,0:T(8,128)(2,1)S(1)} collective-permute-done((bf16[192,1024]{1,0:T(8,128)(2,1)S(1)}, bf16[192,1024]{1,0:T(8,128)(2,1)S(1)}, u32[]{:S(2)}, u32[]{:S(2)}) %collective-permute-start.2) | collective-permute-done | bytes 393248 | tf_op jit(solution)/shard_map/ppermute | solution.py:91
  24.8 2.9 %shard_map.61 = (bf16[96,1024]{1,0:T(8,128)(2,1)S(1)}, bf16[96,1024]{1,0:T(8,128)(2,1)S(1)}, bf16[192,864]{1,0:T(8,128)(2,1)S(1)}, bf16[192,2048]{1,0:T(8,128)(2,1)S(1)}) custom-call(s32[1]{0:T(128)} %bitcast._.where, bf16[192,1024]{1,0:T(8,128)(2,1)S(1)} %shard_map.58.part, bf16[192,1024]{1,0:T(8,128)(2,1)} %collective-permute-done.arrived, ...), custom_call_target="tpu_custom_call" | custom-call | flops 1000 | bytes 1000 | tf_op jit(solution)/shard_map/pallas_call | solution.py:115
  27.7 1.8 %collective-permute-start.6 = (bf16[96,1024]{1,0:T(8,128)(2,1)S(1)}, bf16[96,1024]{1,0:T(8,128)(2,1)S(1)}, u32[]{:S(2)}, u32[]{:S(2)}) collective-permute-start(bf16[96,1024]{1,0:T(8,128)(2,1)S(1)} %get-tuple-element.35), channel_id=1, source_target_pairs={{0,1},{1,0},{2,3},{3,2},{4,5},{5,4},{6,7},{7,6},{8,9},{9,8},{10,11... | collective-permute-start | bytes 589832 | tf_op jit(solution)/shard_map/ppermute | solution.py:91
  29.5 0.2 multiply_reduce_fusion.2
  29.7 1.6 %collective-permute-start.11 = (bf16[192,864]{1,0:T(8,128)(2,1)S(1)}, bf16[192,864]{1,0:T(8,128)(2,1)S(1)}, u32[]{:S(2)}, u32[]{:S(2)}) collective-permute-start(bf16[192,864]{1,0:T(8,128)(2,1)S(1)} %collective-permute-done.7.refs_2_.refs_6_), channel_id=1, source_target_pairs={{0,4},{4,8},{8,12},{12,0},{1,5},{5,9},{9,13},{13,1},{2,6},{6,10},{... | collective-permute-start | bytes 995336 | tf_op jit(solution)/shard_map/ppermute | solution.py:96
  31.3 0.2 multiply_reduce_fusion.1
  31.4 0.6 collective-permute-start.8
  32.1 0.6 shard_map.62
  32.7 2.6 %collective-permute-done.6 = bf16[96,1024]{1,0:T(8,128)(2,1)S(1)} collective-permute-done((bf16[96,1024]{1,0:T(8,128)(2,1)S(1)}, bf16[96,1024]{1,0:T(8,128)(2,1)S(1)}, u32[]{:S(2)}, u32[]{:S(2)}) %collective-permute-start.6) | collective-permute-done | bytes 196640 | tf_op jit(solution)/shard_map/ppermute | solution.py:91
  35.2 0.1 select_convert_fusion.1.refs_0_
  35.3 1.5 %collective-permute-start.12 = (bf16[96,1024]{1,0:T(8,128)(2,1)S(1)}, bf16[96,1024]{1,0:T(8,128)(2,1)S(1)}, u32[]{:S(2)}, u32[]{:S(2)}) collective-permute-start(bf16[96,1024]{1,0:T(8,128)(2,1)S(1)} %select_convert_fusion.1.refs_0_), channel_id=1, source_target_pairs={{0,4},{4,8},{8,12},{12,0},{1,5},{5,9},{9,13},{13,1},{2,6},{6,10},{... | collective-permute-start | bytes 589832 | tf_op jit(solution)/shard_map/ppermute | solution.py:96
  36.9 1.2 %collective-permute-done.8 = bf16[96,1024]{1,0:T(8,128)(2,1)S(1)} collective-permute-done((bf16[96,1024]{1,0:T(8,128)(2,1)S(1)}, bf16[96,1024]{1,0:T(8,128)(2,1)S(1)}, u32[]{:S(2)}, u32[]{:S(2)}) %collective-permute-start.8) | collective-permute-done | bytes 196640 | tf_op jit(solution)/shard_map/ppermute | solution.py:91
  38.1 0.1 select_convert_fusion.refs_4_
  38.2 1.6 %collective-permute-start.10 = (bf16[96,1024]{1,0:T(8,128)(2,1)S(1)}, bf16[96,1024]{1,0:T(8,128)(2,1)S(1)}, u32[]{:S(2)}, u32[]{:S(2)}) collective-permute-start(bf16[96,1024]{1,0:T(8,128)(2,1)S(1)} %select_convert_fusion.refs_4_), channel_id=1, source_target_pairs={{0,4},{4,8},{8,12},{12,0},{1,5},{5,9},{9,13},{13,1},{2,6},{6,10},{... | collective-permute-start | bytes 589832 | tf_op jit(solution)/shard_map/ppermute | solution.py:96
  39.8 1.5 %collective-permute-start.9 = (bf16[192,1024]{1,0:T(8,128)(2,1)S(1)}, bf16[192,1024]{1,0:T(8,128)(2,1)S(1)}, u32[]{:S(2)}, u32[]{:S(2)}) collective-permute-start(bf16[192,1024]{1,0:T(8,128)(2,1)S(1)} %pad_maximum_fusion), channel_id=1, source_target_pairs={{0,1},{1,0},{2,3},{3,2},{4,5},{5,4},{6,7},{7,6},{8,9},{9,8},{10,11... | collective-permute-start | bytes 1179656 | tf_op jit(solution)/shard_map/ppermute | solution.py:91
  41.3 1.2 %collective-permute-done.11.refs_10_.refs_2_ = bf16[192,864]{1,0:T(8,128)(2,1)S(1)} collective-permute-done((bf16[192,864]{1,0:T(8,128)(2,1)S(1)}, bf16[192,864]{1,0:T(8,128)(2,1)S(1)}, u32[]{:S(2)}, u32[]{:S(2)}) %collective-permute-start.11) | collective-permute-done | bytes 331808 | tf_op jit(solution)/shard_map/ppermute | solution.py:96
  42.5 0.2 multiply_reduce_fusion
  42.7 0.1 pad_maximum_fusion.5
  42.7 3.8 %collective-permute-done.12.refs_8_ = bf16[96,1024]{1,0:T(8,128)(2,1)S(1)} collective-permute-done((bf16[96,1024]{1,0:T(8,128)(2,1)S(1)}, bf16[96,1024]{1,0:T(8,128)(2,1)S(1)}, u32[]{:S(2)}, u32[]{:S(2)}) %collective-permute-start.12) | collective-permute-done | bytes 196640 | tf_op jit(solution)/shard_map/ppermute | solution.py:96
  46.6 0.6 collective-permute-start.13
  47.1 3.5 %collective-permute-done.10.refs_12_ = bf16[96,1024]{1,0:T(8,128)(2,1)S(1)} collective-permute-done((bf16[96,1024]{1,0:T(8,128)(2,1)S(1)}, bf16[96,1024]{1,0:T(8,128)(2,1)S(1)}, u32[]{:S(2)}, u32[]{:S(2)}) %collective-permute-start.10) | collective-permute-done | bytes 196640 | tf_op jit(solution)/shard_map/ppermute | solution.py:96
  50.6 1.2 %collective-permute-start.15 = (bf16[96,1024]{1,0:T(8,128)(2,1)S(1)}, bf16[96,1024]{1,0:T(8,128)(2,1)S(1)}, u32[]{:S(2)}, u32[]{:S(2)}) collective-permute-start(bf16[96,1024]{1,0:T(8,128)(2,1)S(1)} %collective-permute-done.10.refs_12_), channel_id=1, source_target_pairs={{0,4},{4,8},{8,12},{12,0},{1,5},{5,9},{9,13},{13,1},{2,6},{6,10},{... | collective-permute-start | bytes 589832 | tf_op jit(solution)/shard_map/ppermute | solution.py:96
  51.8 0.6 collective-permute-start.17
  52.4 0.1 add_rsqrt_fusion
  52.5 0.1 fusion.5
  52.5 0.2 broadcast_select_fusion.1
  52.7 0.1 fusion.3
  52.9 0.1 collective-permute-start.14
  52.9 2.8 %collective-permute-done.19.refs_0_ = bf16[96,1024]{1,0:T(8,128)(2,1)S(1)} collective-permute-done((bf16[96,1024]{1,0:T(8,128)(2,1)S(1)}, bf16[96,1024]{1,0:T(8,128)(2,1)S(1)}, u32[]{:S(2)}, u32[]{:S(2)}) %collective-permute-start.19) | collective-permute-done | bytes 196640 | tf_op jit(solution)/shard_map/ppermute | solution.py:96
  55.8 2.6 %collective-permute-done.15.refs_4_ = bf16[96,1024]{1,0:T(8,128)(2,1)S(1)} collective-permute-done((bf16[96,1024]{1,0:T(8,128)(2,1)S(1)}, bf16[96,1024]{1,0:T(8,128)(2,1)S(1)}, u32[]{:S(2)}, u32[]{:S(2)}) %collective-permute-start.15) | collective-permute-done | bytes 196640 | tf_op jit(solution)/shard_map/ppermute | solution.py:96
  58.4 0.1 collective-permute-start.16
  58.5 0.3 collective-permute-start.20
  58.7 2.2 %shard_map.63 = (f32[944,512]{1,0:T(8,128)S(1)}, f32[944,512]{1,0:T(8,128)S(1)}) custom-call(s32[5]{0:T(128)S(1)} %stack.18.where, bf16[96,1024]{1,0:T(8,128)(2,1)S(1)} %select_convert_fusion.1.refs_0_, bf16[192,1024]{1,0:T(8,128)(2,1)S(1)} %collective-permute-done.9.refs_1_.refs_5_, bf16[192,864]{1,0:T(8,128)(2,1)S(1)} %copy.7.mine.refs_2_.refs_6_, ...), custom_call_target="tpu_custom_call" | custom-call | flops 1000 | bytes 1000 | tf_op jit(solution)/shard_map/pallas_call | solution.py:115
  61.0 3.5 %collective-permute-done.21.refs_8_ = bf16[96,1024]{1,0:T(8,128)(2,1)S(1)} collective-permute-done((bf16[96,1024]{1,0:T(8,128)(2,1)S(1)}, bf16[96,1024]{1,0:T(8,128)(2,1)S(1)}, u32[]{:S(2)}, u32[]{:S(2)}) %collective-permute-start.21) | collective-permute-done | bytes 196640 | tf_op jit(solution)/shard_map/ppermute | solution.py:96
  64.5 1.1 %collective-permute-start.22 = (bf16[96,512]{1,0:T(8,128)(2,1)S(1)}, bf16[96,512]{1,0:T(8,128)(2,1)S(1)}, u32[]{:S(2)}, u32[]{:S(2)}) collective-permute-start(bf16[96,512]{1,0:T(8,128)(2,1)S(1)} %constant_dynamic-slice_fusion), channel_id=1, source_target_pairs={{0,1},{1,0},{2,3},{3,2},{4,5},{5,4},{6,7},{7,6},{8,9},{9,8},{10,11... | collective-permute-start | bytes 294920 | tf_op jit(solution)/shard_map/ppermute | solution.py:91
  65.5 1.0 %collective-permute-done.16.refs_0_ = bf16[96,1024]{1,0:T(8,128)(2,1)S(1)} collective-permute-done((bf16[96,1024]{1,0:T(8,128)(2,1)S(1)}, bf16[96,1024]{1,0:T(8,128)(2,1)S(1)}, u32[]{:S(2)}, u32[]{:S(2)}) %collective-permute-start.16) | collective-permute-done | bytes 196640 | tf_op jit(solution)/shard_map/ppermute | solution.py:96
  66.6 1.3 %collective-permute-start.18 = (bf16[96,512]{1,0:T(8,128)(2,1)S(1)}, bf16[96,512]{1,0:T(8,128)(2,1)S(1)}, u32[]{:S(2)}, u32[]{:S(2)}) collective-permute-start(bf16[96,512]{1,0:T(8,128)(2,1)S(1)} %constant_dynamic-slice_fusion.3), channel_id=1, source_target_pairs={{0,1},{1,0},{2,3},{3,2},{4,5},{5,4},{6,7},{7,6},{8,9},{9,8},{10,11... | collective-permute-start | bytes 294920 | tf_op jit(solution)/shard_map/ppermute | solution.py:91
  67.8 1.2 %maximum_select_fusion = bf16[384,1024]{1,0:T(8,128)(2,1)} fusion(bf16[192,1024]{1,0:T(8,128)(2,1)S(1)} %collective-permute-done.14, bf16[192,512]{1,0:T(8,128)(2,1)S(1)} %get-tuple-element.69, bf16[192,512]{1,0:T(8,128)(2,1)S(1)} %get-tuple-element.57, pred[]{:T(512)S(6)} %eq.18), kind=kLoop, calls=%fused_computation | loop fusion | flops 5111808 | bytes 1572865 | tf_op jit(solution)/shard_map/jit(_where)/select_n | solution.py:344
  69.0 0.1 collective-permute-done.22.refs_9_
  69.1 2.0 %shard_map.64 = (f32[944,512]{1,0:T(8,128)S(1)}, f32[944,512]{1,0:T(8,128)S(1)}) custom-call(s32[5]{0:T(128)S(1)} %stack.18.where, bf16[96,1024]{1,0:T(8,128)(2,1)S(1)} %collective-permute-done.19.refs_0_, bf16[192,512]{1,0:T(8,128)(2,1)S(1)} %collective-permute-done.20.refs_1_.refs_5_, bf16[192,864]{1,0:T(8,128)(2,1)S(1)} %collective-permute-done.7.refs_2_.refs_6_, ...), custom_call_target="tpu_custom_call" | custom-call | flops 1000 | bytes 1000 | tf_op jit(solution)/shard_map/pallas_call | solution.py:115
  71.2 0.1 collective-permute-done.18.refs_1_
  71.2 1.1 %shard_map.65 = bf16[944,512]{1,0:T(8,128)(2,1)S(1)} custom-call(s32[5]{0:T(128)S(1)} %stack.18.where, bf16[96,1024]{1,0:T(8,128)(2,1)S(1)} %collective-permute-done.16.refs_0_, bf16[96,512]{1,0:T(8,128)(2,1)S(1)} %collective-permute-done.18.refs_1_, bf16[192,864]{1,0:T(8,128)(2,1)S(1)} %collective-permute-done.11.refs_10_.refs_2_, f32[1,192]{1,0:T(1,128)S(1)} %bitcast.15, ...), custom_call_target="tpu_custom_call" | custom-call | flops 1000 | bytes 1000 | tf_op jit(solution)/shard_map/pallas_call | solution.py:115
  72.3 0.1 collective-permute-start.23
  72.4 1.1 %shard_map.66.kept = f32[944,512]{1,0:T(8,128)S(1)} custom-call(s32[5]{0:T(128)S(1)} %stack.18.where, bf16[96,1024]{1,0:T(8,128)(2,1)S(1)} %collective-permute-done.16.refs_0_, bf16[96,512]{1,0:T(8,128)(2,1)S(1)} %collective-permute-done.18.refs_1_, bf16[192,864]{1,0:T(8,128)(2,1)S(1)} %collective-permute-done.11.refs_10_.refs_2_, f32[1,192]{1,0:T(1,128)S(1)} %bitcast.16, ...), custom_call_target="tpu_custom_call" | custom-call | flops 1000 | bytes 1000 | tf_op jit(solution)/shard_map/pallas_call | solution.py:115
  73.5 1.4 %collective-permute-done.23.sent = bf16[944,512]{1,0:T(8,128)(2,1)S(1)} collective-permute-done((bf16[944,512]{1,0:T(8,128)(2,1)S(1)}, bf16[944,512]{1,0:T(8,128)(2,1)S(1)}, u32[]{:S(2)}, u32[]{:S(2)}) %collective-permute-start.23) | collective-permute-done | bytes 966688 | tf_op jit(solution)/shard_map/ppermute | solution.py:91
  74.9 1.4 %shard_map.67 = (f32[512,512]{1,0:T(8,128)}, f32[864,256]{1,0:T(8,128)}) custom-call(s32[1]{0:T(128)} %bitcast._.where, f32[944,512]{1,0:T(8,128)S(1)} %shard_map.66.kept, bf16[944,512]{1,0:T(8,128)(2,1)S(1)} %collective-permute-done.23.sent), custom_call_target="tpu_custom_call" | custom-call | flops 1000 | bytes 1000 | tf_op jit(solution)/shard_map/pallas_call | solution.py:115
  (31 shorter events, 0.2 us)
Async XLA Ops:
  0.6 1.1 %copy-start = (bf16[384,864]{0,1:T(8,128)(2,1)S(1)}, bf16[384,864]{0,1:T(8,128)(2,1)}, u32[]{:S(2)}) copy-start(bf16[384,864]{0,1:T(8,128)(2,1)} %param.3) | copy-start | bytes 1990660
  0.6 9.4 %collective-permute-start.1 = (bf16[864,1024]{1,0:T(8,128)(2,1)}, bf16[864,1024]{1,0:T(8,128)(2,1)S(1)}, u32[]{:S(2)}, u32[]{:S(2)}) collective-permute-start(bf16[864,1024]{1,0:T(8,128)(2,1)} %own.3), channel_id=1, source_target_pairs={{0,2},{2,0},{1,3},{3,1},{4,6},{6,4},{5,7},{7,5},{8,10},{10,8},{9,1... | collective-permute-start | bytes 5308424 | tf_op jit(solution)/shard_map/ppermute | solution.py:91
  1.9 6.9 %copy-start.3 = (f32[1024]{0:T(1024)S(1)}, f32[1024]{0:T(1024)}, u32[]{:S(2)}) copy-start(f32[1024]{0:T(1024)} %param.5) | copy-start | bytes 12292
  2.1 1.5 %copy-start.1 = (bf16[864,1024]{1,0:T(8,128)(2,1)S(1)}, bf16[864,1024]{1,0:T(8,128)(2,1)}, u32[]{:S(2)}) copy-start(bf16[864,1024]{1,0:T(8,128)(2,1)} %own.3) | copy-start | bytes 5308420
  4.2 15.2 %collective-permute-start = (bf16[192,1024]{1,0:T(8,128)(2,1)S(1)}, bf16[192,1024]{1,0:T(8,128)(2,1)}, u32[]{:S(2)}, u32[]{:S(2)}) collective-permute-start(bf16[192,1024]{1,0:T(8,128)(2,1)S(1)} %shard_map.58.part), channel_id=1, source_target_pairs={{0,1},{1,0},{2,3},{3,2},{4,5},{5,4},{6,7},{7,6},{8,9},{9,8},{10,11... | collective-permute-start | bytes 1179656 | tf_op jit(solution)/shard_map/ppermute | solution.py:91
  7.2 11.4 %collective-permute-start.5 = (bf16[192,864]{1,0:T(8,128)(2,1)S(1)}, bf16[192,864]{1,0:T(8,128)(2,1)S(1)}, u32[]{:S(2)}, u32[]{:S(2)}) collective-permute-start(bf16[192,864]{1,0:T(8,128)(2,1)S(1)} %copy.7.mine.refs_2_.refs_6_), channel_id=1, source_target_pairs={{0,4},{4,8},{8,12},{12,0},{1,5},{5,9},{9,13},{13,1},{2,6},{6,10},{... | collective-permute-start | bytes 995336 | tf_op jit(solution)/shard_map/ppermute | solution.py:96
  8.8 1.2 %collective-permute-start.4 = (f32[1,1024]{1,0:T(1,128)S(1)}, f32[1,1024]{1,0:T(1,128)S(1)}, u32[]{:S(2)}, u32[]{:S(2)}) collective-permute-start(f32[1,1024]{1,0:T(1,128)S(1)} %bitcast.21), channel_id=1, source_target_pairs={{0,2},{2,0},{1,3},{3,1},{4,6},{6,4},{5,7},{7,5},{8,10},{10,8},{9,1... | collective-permute-start | bytes 12296 | tf_op jit(solution)/shard_map/ppermute | solution.py:91
  9.0 8.3 %collective-permute-start.3 = (f32[192]{0:T(256)S(1)}, f32[192]{0:T(256)S(1)}, u32[]{:S(2)}, u32[]{:S(2)}) collective-permute-start(f32[192]{0:T(256)S(1)} %multiply_reduce_fusion.3), channel_id=1, source_target_pairs={{0,1},{1,0},{2,3},{3,2},{4,5},{5,4},{6,7},{7,6},{8,9},{9,8},{10,11... | collective-permute-start | bytes 2312 | tf_op jit(solution)/shard_map/ppermute | solution.py:91
  10.6 14.2 %collective-permute-start.2 = (bf16[192,1024]{1,0:T(8,128)(2,1)S(1)}, bf16[192,1024]{1,0:T(8,128)(2,1)S(1)}, u32[]{:S(2)}, u32[]{:S(2)}) collective-permute-start(bf16[192,1024]{1,0:T(8,128)(2,1)S(1)} %shard_map.59.part2), channel_id=1, source_target_pairs={{0,1},{1,0},{2,3},{3,2},{4,5},{5,4},{6,7},{7,6},{8,9},{9,8},{10,11... | collective-permute-start | bytes 1179656 | tf_op jit(solution)/shard_map/ppermute | solution.py:91
  11.9 12.9 %copy-start.2 = (bf16[864,1024]{1,0:T(8,128)(2,1)S(1)}, bf16[864,1024]{1,0:T(8,128)(2,1)}, u32[]{:S(2)}) copy-start(bf16[864,1024]{1,0:T(8,128)(2,1)} %own.3) | copy-start | bytes 5308420
  18.6 11.1 %collective-permute-start.7 = (bf16[192,864]{1,0:T(8,128)(2,1)S(1)}, bf16[192,864]{1,0:T(8,128)(2,1)S(1)}, u32[]{:S(2)}, u32[]{:S(2)}) collective-permute-start(bf16[192,864]{1,0:T(8,128)(2,1)S(1)} %collective-permute-done.5.refs_10_.refs_14_), channel_id=1, source_target_pairs={{0,4},{4,8},{8,12},{12,0},{1,5},{5,9},{9,13},{13,1},{2,6},{6,10},{... | collective-permute-start | bytes 995336 | tf_op jit(solution)/shard_map/ppermute | solution.py:96
  27.7 7.5 %collective-permute-start.6 = (bf16[96,1024]{1,0:T(8,128)(2,1)S(1)}, bf16[96,1024]{1,0:T(8,128)(2,1)S(1)}, u32[]{:S(2)}, u32[]{:S(2)}) collective-permute-start(bf16[96,1024]{1,0:T(8,128)(2,1)S(1)} %get-tuple-element.35), channel_id=1, source_target_pairs={{0,1},{1,0},{2,3},{3,2},{4,5},{5,4},{6,7},{7,6},{8,9},{9,8},{10,11... | collective-permute-start | bytes 589832 | tf_op jit(solution)/shard_map/ppermute | solution.py:91
  29.7 12.8 %collective-permute-start.11 = (bf16[192,864]{1,0:T(8,128)(2,1)S(1)}, bf16[192,864]{1,0:T(8,128)(2,1)S(1)}, u32[]{:S(2)}, u32[]{:S(2)}) collective-permute-start(bf16[192,864]{1,0:T(8,128)(2,1)S(1)} %collective-permute-done.7.refs_2_.refs_6_), channel_id=1, source_target_pairs={{0,4},{4,8},{8,12},{12,0},{1,5},{5,9},{9,13},{13,1},{2,6},{6,10},{... | collective-permute-start | bytes 995336 | tf_op jit(solution)/shard_map/ppermute | solution.py:96
  31.4 6.6 %collective-permute-start.8 = (bf16[96,1024]{1,0:T(8,128)(2,1)S(1)}, bf16[96,1024]{1,0:T(8,128)(2,1)S(1)}, u32[]{:S(2)}, u32[]{:S(2)}) collective-permute-start(bf16[96,1024]{1,0:T(8,128)(2,1)S(1)} %get-tuple-element.38), channel_id=1, source_target_pairs={{0,1},{1,0},{2,3},{3,2},{4,5},{5,4},{6,7},{7,6},{8,9},{9,8},{10,11... | collective-permute-start | bytes 589832 | tf_op jit(solution)/shard_map/ppermute | solution.py:91
  35.3 11.2 %collective-permute-start.12 = (bf16[96,1024]{1,0:T(8,128)(2,1)S(1)}, bf16[96,1024]{1,0:T(8,128)(2,1)S(1)}, u32[]{:S(2)}, u32[]{:S(2)}) collective-permute-start(bf16[96,1024]{1,0:T(8,128)(2,1)S(1)} %select_convert_fusion.1.refs_0_), channel_id=1, source_target_pairs={{0,4},{4,8},{8,12},{12,0},{1,5},{5,9},{9,13},{13,1},{2,6},{6,10},{... | collective-permute-start | bytes 589832 | tf_op jit(solution)/shard_map/ppermute | solution.py:96
  38.2 12.4 %collective-permute-start.10 = (bf16[96,1024]{1,0:T(8,128)(2,1)S(1)}, bf16[96,1024]{1,0:T(8,128)(2,1)S(1)}, u32[]{:S(2)}, u32[]{:S(2)}) collective-permute-start(bf16[96,1024]{1,0:T(8,128)(2,1)S(1)} %select_convert_fusion.refs_4_), channel_id=1, source_target_pairs={{0,4},{4,8},{8,12},{12,0},{1,5},{5,9},{9,13},{13,1},{2,6},{6,10},{... | collective-permute-start | bytes 589832 | tf_op jit(solution)/shard_map/ppermute | solution.py:96
  39.8 12.7 %collective-permute-start.9 = (bf16[192,1024]{1,0:T(8,128)(2,1)S(1)}, bf16[192,1024]{1,0:T(8,128)(2,1)S(1)}, u32[]{:S(2)}, u32[]{:S(2)}) collective-permute-start(bf16[192,1024]{1,0:T(8,128)(2,1)S(1)} %pad_maximum_fusion), channel_id=1, source_target_pairs={{0,1},{1,0},{2,3},{3,2},{4,5},{5,4},{6,7},{7,6},{8,9},{9,8},{10,11... | collective-permute-start | bytes 1179656 | tf_op jit(solution)/shard_map/ppermute | solution.py:91
  46.5 9.2 %collective-permute-start.19 = (bf16[96,1024]{1,0:T(8,128)(2,1)S(1)}, bf16[96,1024]{1,0:T(8,128)(2,1)S(1)}, u32[]{:S(2)}, u32[]{:S(2)}) collective-permute-start(bf16[96,1024]{1,0:T(8,128)(2,1)S(1)} %collective-permute-done.12.refs_8_), channel_id=1, source_target_pairs={{0,4},{4,8},{8,12},{12,0},{1,5},{5,9},{9,13},{13,1},{2,6},{6,10},{... | collective-permute-start | bytes 589832 | tf_op jit(solution)/shard_map/ppermute | solution.py:96
  46.6 4.0 %collective-permute-start.13 = (f32[576]{0:T(1024)S(1)}, f32[576]{0:T(1024)S(1)}, u32[]{:S(2)}, u32[]{:S(2)}) collective-permute-start(f32[576]{0:T(1024)S(1)} %pad_maximum_fusion.5), channel_id=1, source_target_pairs={{0,1},{1,0},{2,3},{3,2},{4,5},{5,4},{6,7},{7,6},{8,9},{9,8},{10,11... | collective-permute-start | bytes 6920 | tf_op jit(solution)/shard_map/ppermute | solution.py:91
  50.6 7.8 %collective-permute-start.15 = (bf16[96,1024]{1,0:T(8,128)(2,1)S(1)}, bf16[96,1024]{1,0:T(8,128)(2,1)S(1)}, u32[]{:S(2)}, u32[]{:S(2)}) collective-permute-start(bf16[96,1024]{1,0:T(8,128)(2,1)S(1)} %collective-permute-done.10.refs_12_), channel_id=1, source_target_pairs={{0,4},{4,8},{8,12},{12,0},{1,5},{5,9},{9,13},{13,1},{2,6},{6,10},{... | collective-permute-start | bytes 589832 | tf_op jit(solution)/shard_map/ppermute | solution.py:96
  51.8 6.9 %collective-permute-start.17 = (bf16[192,512]{1,0:T(8,128)(2,1)S(1)}, bf16[192,512]{1,0:T(8,128)(2,1)S(1)}, u32[]{:S(2)}, u32[]{:S(2)}) collective-permute-start(bf16[192,512]{1,0:T(8,128)(2,1)S(1)} %pad_maximum_fusion.2), channel_id=1, source_target_pairs={{0,1},{1,0},{2,3},{3,2},{4,5},{5,4},{6,7},{7,6},{8,9},{9,8},{10,11... | collective-permute-start | bytes 589832 | tf_op jit(solution)/shard_map/ppermute | solution.py:91
  52.9 15.0 %collective-permute-start.14 = (bf16[192,1024]{1,0:T(8,128)(2,1)S(1)}, bf16[192,1024]{1,0:T(8,128)(2,1)S(1)}, u32[]{:S(2)}, u32[]{:S(2)}) collective-permute-start(bf16[192,1024]{1,0:T(8,128)(2,1)S(1)} %pad_maximum_fusion.1), channel_id=1, source_target_pairs={{0,2},{2,0},{1,3},{3,1},{4,6},{6,4},{5,7},{7,5},{8,10},{10,8},{9,1... | collective-permute-start | bytes 1179656 | tf_op jit(solution)/shard_map/ppermute | solution.py:91
  55.8 8.7 %collective-permute-start.21 = (bf16[96,1024]{1,0:T(8,128)(2,1)S(1)}, bf16[96,1024]{1,0:T(8,128)(2,1)S(1)}, u32[]{:S(2)}, u32[]{:S(2)}) collective-permute-start(bf16[96,1024]{1,0:T(8,128)(2,1)S(1)} %collective-permute-done.19.refs_0_), channel_id=1, source_target_pairs={{0,4},{4,8},{8,12},{12,0},{1,5},{5,9},{9,13},{13,1},{2,6},{6,10},{... | collective-permute-start | bytes 589832 | tf_op jit(solution)/shard_map/ppermute | solution.py:96
  58.4 8.2 %collective-permute-start.16 = (bf16[96,1024]{1,0:T(8,128)(2,1)S(1)}, bf16[96,1024]{1,0:T(8,128)(2,1)S(1)}, u32[]{:S(2)}, u32[]{:S(2)}) collective-permute-start(bf16[96,1024]{1,0:T(8,128)(2,1)S(1)} %collective-permute-done.15.refs_4_), channel_id=1, source_target_pairs={{0,4},{4,8},{8,12},{12,0},{1,5},{5,9},{9,13},{13,1},{2,6},{6,10},{... | collective-permute-start | bytes 589832 | tf_op jit(solution)/shard_map/ppermute | solution.py:96
  58.5 10.6 %collective-permute-start.20 = (bf16[192,512]{1,0:T(8,128)(2,1)S(1)}, bf16[192,512]{1,0:T(8,128)(2,1)S(1)}, u32[]{:S(2)}, u32[]{:S(2)}) collective-permute-start(bf16[192,512]{1,0:T(8,128)(2,1)S(1)} %pad_maximum_fusion.3), channel_id=1, source_target_pairs={{0,1},{1,0},{2,3},{3,2},{4,5},{5,4},{6,7},{7,6},{8,9},{9,8},{10,11... | collective-permute-start | bytes 589832 | tf_op jit(solution)/shard_map/ppermute | solution.py:91
  64.5 4.7 %collective-permute-start.22 = (bf16[96,512]{1,0:T(8,128)(2,1)S(1)}, bf16[96,512]{1,0:T(8,128)(2,1)S(1)}, u32[]{:S(2)}, u32[]{:S(2)}) collective-permute-start(bf16[96,512]{1,0:T(8,128)(2,1)S(1)} %constant_dynamic-slice_fusion), channel_id=1, source_target_pairs={{0,1},{1,0},{2,3},{3,2},{4,5},{5,4},{6,7},{7,6},{8,9},{9,8},{10,11... | collective-permute-start | bytes 294920 | tf_op jit(solution)/shard_map/ppermute | solution.py:91
  66.6 4.7 %collective-permute-start.18 = (bf16[96,512]{1,0:T(8,128)(2,1)S(1)}, bf16[96,512]{1,0:T(8,128)(2,1)S(1)}, u32[]{:S(2)}, u32[]{:S(2)}) collective-permute-start(bf16[96,512]{1,0:T(8,128)(2,1)S(1)} %constant_dynamic-slice_fusion.3), channel_id=1, source_target_pairs={{0,1},{1,0},{2,3},{3,2},{4,5},{5,4},{6,7},{7,6},{8,9},{9,8},{10,11... | collective-permute-start | bytes 294920 | tf_op jit(solution)/shard_map/ppermute | solution.py:91
  72.3 2.6 %collective-permute-start.23 = (bf16[944,512]{1,0:T(8,128)(2,1)S(1)}, bf16[944,512]{1,0:T(8,128)(2,1)S(1)}, u32[]{:S(2)}, u32[]{:S(2)}) collective-permute-start(bf16[944,512]{1,0:T(8,128)(2,1)S(1)} %shard_map.65), channel_id=1, source_target_pairs={{0,2},{2,0},{1,3},{3,1},{4,6},{6,4},{5,7},{7,5},{8,10},{10,8},{9,1... | collective-permute-start | bytes 2899976 | tf_op jit(solution)/shard_map/ppermute | solution.py:91
